TPU v7x, 128 devices: a whole 4x4x4 slice. The times are simulated.
128 devices in a mesh: ctx: 16 (over y, x_lo, core), db: 8 (over x_hi, z).
Axes of the slice: x: 4 (x_hi: 2, x_lo: 2; x = x_hi * 2 + x_lo), y: 4, z: 4, core: 2. Of those that a mesh axis runs over, the one named last changes fastest.
Arguments:
- queries: bfloat16 [8, 4096, 2048], P('db', 'ctx'), may hold values from -6 to 6
- keys: bfloat16 [8, 4096, 2048], P('db', 'ctx'), may hold values from -6 to 6
- values: bfloat16 [8, 4096, 2048], P('db', 'ctx'), may hold values from -6 to 6
- doc_ids: int32 [8, 4096], P('db', 'ctx'), may hold values from 0 to 3, never falling along the last dimension, each value on 1 to 3072 neighbouring positions
- nbr_owner: int32 [8, 64, 2], P('db', 'ctx'), may hold values from 0 to 7, all different within a row; in each aligned block of 4 rows (0 to 3, 4 to 7, ..., all dimensions but the last counted through in order) at most 2 rows name the same one
- nbr_local: int32 [8, 64, 2], P('db', 'ctx'), may hold values from 0 to 7
- db_keys: bfloat16 [8, 128, 64, 2048], P('db', 'ctx'), may hold values from -6 to 6
- db_values: bfloat16 [8, 128, 64, 2048], P('db', 'ctx'), may hold values from -6 to 6
Outputs:
- self_out: bfloat16 [8, 4096, 2048], P('db', 'ctx')
- cross_out: bfloat16 [8, 4096, 2048], P('db', 'ctx')
Inputs may be any that keep to these rules, and one draw needn't show every extreme that they name: `nbr_owner`: the 2 neighbours of a query span lie in different shards. Among the 4 query spans of one device (aligned blocks of 4 spans) no shard is named more than 2 times, and on some devices one shard is named exactly 2 times. `nbr_local`: A neighbour of query span n lies among the 8 spans n // 4 * 8 to n // 4 * 8 + 7 of its shard. `doc_ids`: never falls along a sequence; at most 4 documents, the longest 3 * 1024 tokens.
All inputs are finite; a program needn't handle non-finite values.
Results may differ from a plain program's by a relative error of at most 0.0045.
Values may be sent and summed in bfloat16 or wider, within the bound.
No kernel may reach another device: no remote copies, remote signals or barrier semaphores. Data moves between devices by JAX's collectives and lax.ppermute only.
A program may use at most 256 MiB of HBM per device.

v0:
```python
import math

import jax
import jax.numpy as jnp
from jax import lax
from jax.sharding import PartitionSpec as P

DH = 128
CH = 64
KN = 2
CAP = 2


neg_fill = -1e30


def per_device(queries, keys, values, doc_ids, nbr_owner, nbr_local, db_keys, db_values):
    query_rows = queries[0]
    tok_rows = query_rows.shape[0]
    row_width = query_rows.shape[1]
    head_count = row_width // DH
    score_scale = 1.0 / math.sqrt(DH)
    all_docs = lax.all_gather(doc_ids, "ctx", axis=1, tiled=True)[0]
    first_pos = lax.axis_index("ctx") * tok_rows
    own_pos = first_pos + jnp.arange(tok_rows, dtype=jnp.int32)
    own_docs = doc_ids[0]
    query_split = query_rows.reshape(tok_rows, head_count, DH)
    start_state = (
        jnp.zeros((tok_rows, head_count, DH), jnp.float32),
        jnp.full((head_count, tok_rows), neg_fill, jnp.float32),
        jnp.zeros((head_count, tok_rows), jnp.float32),
    )
    key_block = lax.all_gather(keys[0], "ctx", axis=0, tiled=True)
    value_block = lax.all_gather(values[0], "ctx", axis=0, tiled=True)
    block_rows = key_block.shape[0]

    def update(unused):
        running_out, running_top, running_sum = start_state
        key_pos = jnp.arange(block_rows, dtype=jnp.int32)
        allowed = (key_pos[None, :] <= own_pos[:, None]) & (all_docs[None, :] == own_docs[:, None])
        scores = (
            jnp.einsum(
                "thd,shd->hts",
                query_split,
                key_block.reshape(block_rows, head_count, DH),
                preferred_element_type=jnp.float32,
            )
            * score_scale
        )
        scores = jnp.where(allowed[None], scores, neg_fill)
        new_top = jnp.maximum(running_top, jnp.max(scores, axis=2))
        expo = jnp.where(allowed[None], jnp.exp(scores - new_top[:, :, None]), 0.0)
        shrink = jnp.exp(running_top - new_top)
        new_sum = jnp.sum(expo, axis=2)
        contrib = jnp.einsum(
            "hts,shd->thd",
            expo.astype(jnp.bfloat16),
            value_block.reshape(block_rows, head_count, DH),
            preferred_element_type=jnp.float32,
        )
        new_out = running_out * jnp.swapaxes(shrink, 0, 1)[:, :, None] + contrib
        return (new_out, new_top, new_sum)

    def keep_state(unused):
        return start_state

    running_out, running_top, running_sum = lax.cond(
        jnp.int32(0) <= first_pos + tok_rows - 1, update, keep_state, 0
    )
    self_rows = (
        (running_out / jnp.swapaxes(running_sum, 0, 1)[:, :, None])
        .astype(jnp.bfloat16)
        .reshape(tok_rows, row_width)
    )
    owner_ids = nbr_owner[0].reshape(-1)
    local_ids = nbr_local[0].reshape(-1)
    shard_count = lax.axis_size("db")
    request_count = owner_ids.shape[0]
    shard_hits = (owner_ids[:, None] == jnp.arange(shard_count, dtype=jnp.int32)[None, :]).astype(
        jnp.int32
    )
    earlier = jnp.tril(jnp.ones((request_count, request_count), jnp.int32), -1)
    slot_ranks = jnp.sum(jnp.dot(earlier, shard_hits) * shard_hits, axis=1)
    slot_match = shard_hits[:, :, None] * (
        slot_ranks[:, None, None] == jnp.arange(CAP, dtype=jnp.int32)[None, None, :]
    ).astype(jnp.int32)
    request_table = jnp.sum(slot_match * local_ids[:, None, None], axis=0)
    wanted = lax.all_to_all(request_table, "db", split_axis=0, concat_axis=0, tiled=True)
    span_keys = db_keys[0][wanted]
    span_values = db_values[0][wanted]
    got_keys = lax.all_to_all(span_keys, "db", split_axis=0, concat_axis=0, tiled=True)
    got_values = lax.all_to_all(span_values, "db", split_axis=0, concat_axis=0, tiled=True)
    flat_slot = owner_ids * CAP + slot_ranks
    span_count = tok_rows // CH
    near_keys = got_keys.reshape(shard_count * CAP, CH, row_width)[flat_slot].reshape(
        span_count, KN * CH, head_count, DH
    )
    near_values = got_values.reshape(shard_count * CAP, CH, row_width)[flat_slot].reshape(
        span_count, KN * CH, head_count, DH
    )
    span_queries = query_rows.reshape(span_count, CH, head_count, DH)
    scores = (
        jnp.einsum("cthd,cshd->chts", span_queries, near_keys, preferred_element_type=jnp.float32)
        * score_scale
    )
    row_top = jnp.max(scores, axis=3)
    expo = jnp.exp(scores - row_top[..., None])
    running_sum = jnp.sum(expo, axis=3)
    mixed = jnp.einsum(
        "chts,cshd->cthd",
        expo.astype(jnp.bfloat16),
        near_values,
        preferred_element_type=jnp.float32,
    )
    cross_rows = (
        (mixed / jnp.swapaxes(running_sum, 1, 2)[..., None])
        .astype(jnp.bfloat16)
        .reshape(tok_rows, row_width)
    )
    return (self_rows[None], cross_rows[None])


def solution(mesh):
    placed = (
        P("db", "ctx", None),
        P("db", "ctx", None),
        P("db", "ctx", None),
        P("db", "ctx"),
        P("db", "ctx", None),
        P("db", "ctx", None),
        P("db", "ctx", None, None),
        P("db", "ctx", None, None),
    )
    return jax.shard_map(
        per_device,
        mesh=mesh,
        in_specs=placed,
        out_specs=(P("db", "ctx", None), P("db", "ctx", None)),
        check_vma=False,
    )
```

profile of v0, /device:TPU:1, one launch (start us, length us, event | category | flops | bytes accessed | tf_op | source)
XLA Modules:
  0.0 371.8 jit_solution(7283561359122738542)
XLA Ops:
  7.2 0.0 copy-start
  7.2 0.0 all-gather.5.cloned.1.call-start
  7.2 0.7 all-gather.5.cloned.1.call-update
  7.9 0.0 all-gather.7.cloned.1.call-start
  8.0 0.7 all-gather.7.cloned.1.call-update
  8.7 0.8 copy.54
  9.4 0.1 mul.64
  9.5 0.8 copy.52
  10.3 0.1 eq.58
  10.4 0.1 copy.53
  10.5 0.1 fusion.30
  10.6 0.1 multiply_reduce_fusion
  10.7 0.1 copy.55
  10.8 14.6 %all_to_all.22 = s32[8,1,2]{2,1,0:T(1,128)S(1)} all-to-all(s32[8,1,2]{2,1,0:T(1,128)S(1)} %copy.55), channel_id=1, replica_groups=mesh['ctx'=16,'db'=8] {'db'}, dimensions={0} | all-to-all | bytes 128 | tf_op jit(solution)/shard_map/all_to_all | solution.py:88
  25.4 0.1 copy.56
  25.5 0.1 copy.57
  25.6 0.1 reshape.191
  25.7 2.8 gather_fusion
  28.4 4.7 %all-to-all-start.1 = ((bf16[8,2,64,2048]{3,2,1,0:T(8,128)(2,1)}), bf16[8,2,64,2048]{3,2,1,0:T(8,128)(2,1)}, u32[]{:S(2)}, u32[]{:S(2)}) async-start(bf16[8,2,64,2048]{3,2,1,0:T(8,128)(2,1)} %bitcast.79), calls=%async_computation.1 | async-start | bytes 8388608 | tf_op jit(solution)/shard_map/all_to_all | solution.py:92
  33.2 2.7 gather_fusion.2
  35.9 90.7 %all-to-all-done.1 = bf16[8,2,64,2048]{3,2,1,0:T(8,128)(2,1)} async-done(((bf16[8,2,64,2048]{3,2,1,0:T(8,128)(2,1)}), bf16[8,2,64,2048]{3,2,1,0:T(8,128)(2,1)}, u32[]{:S(2)}, u32[]{:S(2)}) %all-to-all-start.1) | async-done | bytes 4194336 | tf_op jit(solution)/shard_map/all_to_all | solution.py:92
  126.6 4.7 %all-to-all-start.2 = ((bf16[8,2,64,2048]{3,2,1,0:T(8,128)(2,1)}), bf16[8,2,64,2048]{3,2,1,0:T(8,128)(2,1)}, u32[]{:S(2)}, u32[]{:S(2)}) async-start(bf16[8,2,64,2048]{3,2,1,0:T(8,128)(2,1)} %bitcast.78), calls=%async_computation.2 | async-start | bytes 8388608 | tf_op jit(solution)/shard_map/all_to_all | solution.py:91
  131.3 0.1 copy.58
  131.4 0.1 mul.68
  131.5 0.2 copy.67
  131.8 91.4 %all_gather.9 = s32[1,4096]{1,0:T(1,128)S(1)} all-gather(s32[1,256]{1,0:T(1,128)S(1)} %copy-done.7), channel_id=1, replica_groups=mesh['ctx'=16,'db'=8] {'ctx'}, dimensions={1}, use_global_device_ids=true | all-gather | bytes 17408 | tf_op jit(solution)/shard_map/all_gather | solution.py:23
  223.2 3.0 gather_fusion.1
  226.2 2.0 copy.68
  228.1 0.0 all-to-all-done.2
  228.1 2.9 gather_fusion.3
  231.0 0.6 copy.66
  231.7 1.6 bitcast_reduce_fusion
  233.3 1.3 fusion.26
  234.6 1.5 fusion.20
  236.1 0.0 copy-start.4
  236.1 0.7 copy.62
  236.8 1.3 broadcast_in_dim_reshape.7
  238.1 35.4 %all-gather.7.cloned.1.call-done = bf16[1,4096,2048]{2,1,0:T(8,128)(2,1)} async-done(((bf16[1,256,2048]{2,1,0:T(8,128)(2,1)}), bf16[1,4096,2048]{2,1,0:T(8,128)(2,1)}) %all-gather.7.cloned.1.call-update) | async-done | bytes 16777232 | tf_op jit(solution)/shard_map/all_gather | solution.py:34
  273.5 87.4 %conditional.1 = (f32[256,16,128]{2,0,1:T(8,128)}, f32[16,256]{1,0:T(8,128)S(1)}) conditional(s32[]{:T(128)} %convert_element_type.30, () %tuple.16, (s32[]{:T(128)}, s32[256]{0:T(256)S(1)}, s32[1,4096]{1,0:T(1,128)S(1)}, s32[1,256]{1,0:T(1,128)S(1)}, bf16[1,256,2048]{2,1,0:T(8,128)(2,1)S(1)}, /*index=5*/bf16[4096,2048]{1,0:T(8,128)(2,1)}, ...), branch_computations={%region_0.0_spmd, %region_1.4_spmd} | conditional | flops 8811712512 | bytes 244469776 | solution.py:67
  273.5 1.0 fusion.11
  274.5 0.2 copy.65
  274.7 30.6 %fusion = (f32[16,256]{1,0:T(8,128)S(1)}, f32[16,256,4096]{2,1,0:T(8,128)}) fusion(pred[256,4096]{1,0:T(8,128)(4,1)S(1)} %fusion.11, bf16[256,16,128]{2,1,0:T(8,128)(2,1)S(1)} %bitcast.84, bf16[4096,2048]{1,0:T(8,128)(2,1)} %get-tuple-element.22), kind=kOutput, calls=%fused_computation.6 | convolution fusion | flops 4345294848 | bytes 85999616 | tf_op jit(solution)/shard_map/cond/branch_1_fun/thd,shd->hts/dot_general | solution.py:42
  305.3 31.4 %bitcast_add_fusion = f32[256,16,128]{2,0,1:T(8,128)} fusion(f32[16,256,4096]{2,1,0:T(8,128)} %get-tuple-element.33, f32[16,256]{1,0:T(8,128)S(1)} %get-tuple-element.31, pred[256,4096]{1,0:T(8,128)(4,1)S(1)} %fusion.11, f32[256,16]{0,1:T(8,128)S(1)} %get-tuple-element.30, bf16[4096,2048]{1,0:T(8,128)(2,1)} %get-tuple-element.23), kind=kOutput, calls=%fused_computation.18 | convolution fusion | flops 4379377664 | bytes 87064576 | tf_op jit(solution)/shard_map/cond/branch_1_fun/hts,shd->thd/dot_general | solution.py:55
  336.8 24.2 %fusion.1 = f32[16,256]{1,0:T(8,128)S(1)} fusion(f32[16,256,4096]{2,1,0:T(8,128)} %get-tuple-element.33, f32[16,256]{1,0:T(8,128)S(1)} %get-tuple-element.31, pred[256,4096]{1,0:T(8,128)(4,1)S(1)} %fusion.11), kind=kLoop, calls=%fused_computation.7 | loop fusion | flops 83881984 | bytes 68190208 | tf_op jit(solution)/shard_map/cond/branch_1_fun/reduce_sum | solution.py:54
  360.9 0.0 copy-start.1
  360.9 2.1 divide_convert_fusion
  363.0 0.7 copy.51
  363.7 1.3 broadcast_in_dim_reshape.6
  (25 shorter events, 0.1 us)
Async XLA Ops:
  7.2 18.5 %copy-start = (bf16[1,8,64,2048]{3,2,1,0:T(8,128)(2,1)S(1)}, bf16[1,8,64,2048]{3,2,1,0:T(8,128)(2,1)}, u32[]{:S(2)}) copy-start(bf16[1,8,64,2048]{3,2,1,0:T(8,128)(2,1)} %param.17) | copy-start | bytes 6291460
  7.2 230.9 %all-gather.5.cloned.1.call-start = ((), (), s32[]{:S(2)}) async-start(), calls=%async_computation.3 | async-start | bytes 17825792 | tf_op jit(solution)/shard_map/all_gather | solution.py:33
  7.9 265.6 %all-gather.7.cloned.1.call-start = ((), (), s32[]{:S(2)}) async-start(), calls=%async_computation.4 | async-start | bytes 17825792 | tf_op jit(solution)/shard_map/all_gather | solution.py:34
  28.4 4.7 %copy-start.2 = (bf16[1,8,64,2048]{3,2,1,0:T(8,128)(2,1)S(1)}, bf16[1,8,64,2048]{3,2,1,0:T(8,128)(2,1)}, u32[]{:S(2)}) copy-start(bf16[1,8,64,2048]{3,2,1,0:T(8,128)(2,1)} %param.16) | copy-start | bytes 6291460
  28.4 98.1 %all-to-all-start.1 = ((bf16[8,2,64,2048]{3,2,1,0:T(8,128)(2,1)}), bf16[8,2,64,2048]{3,2,1,0:T(8,128)(2,1)}, u32[]{:S(2)}, u32[]{:S(2)}) async-start(bf16[8,2,64,2048]{3,2,1,0:T(8,128)(2,1)} %bitcast.79), calls=%async_computation.1 | async-start | bytes 8388608 | tf_op jit(solution)/shard_map/all_to_all | solution.py:92
  126.6 4.8 %copy-start.6 = (s32[1,4,2]{1,2,0:T(2,128)S(1)}, s32[1,4,2]{1,2,0:T(2,128)}, u32[]{:S(2)}) copy-start(s32[1,4,2]{1,2,0:T(2,128)} %param.14) | copy-start | bytes 100
  126.6 5.0 %copy-start.3 = (bf16[1,256,2048]{2,1,0:T(8,128)(2,1)S(1)}, bf16[1,256,2048]{2,1,0:T(8,128)(2,1)}, u32[]{:S(2)}) copy-start(bf16[1,256,2048]{2,1,0:T(8,128)(2,1)} %param.10) | copy-start | bytes 3145732
  126.6 5.2 %copy-start.7 = (s32[1,256]{1,0:T(1,128)S(1)}, s32[1,256]{1,0:T(1,128)}, u32[]{:S(2)}) copy-start(s32[1,256]{1,0:T(1,128)} %param.13) | copy-start | bytes 3076
  126.6 101.6 %all-to-all-start.2 = ((bf16[8,2,64,2048]{3,2,1,0:T(8,128)(2,1)}), bf16[8,2,64,2048]{3,2,1,0:T(8,128)(2,1)}, u32[]{:S(2)}, u32[]{:S(2)}) async-start(bf16[8,2,64,2048]{3,2,1,0:T(8,128)(2,1)} %bitcast.78), calls=%async_computation.2 | async-start | bytes 8388608 | tf_op jit(solution)/shard_map/all_to_all | solution.py:91
  231.7 3.0 copy-start.5
  236.1 37.4 %copy-start.4 = (bf16[1,256,2048]{2,1,0:T(8,128)(2,1)S(1)}, bf16[1,256,2048]{2,1,0:T(8,128)(2,1)}, u32[]{:S(2)}) copy-start(bf16[1,256,2048]{2,1,0:T(8,128)(2,1)} %param.10) | copy-start | bytes 3145732
  360.9 4.1 %copy-start.1 = (bf16[1,8,64,2048]{3,2,1,0:T(8,128)(2,1)S(1)}, bf16[1,8,64,2048]{3,2,1,0:T(8,128)(2,1)}, u32[]{:S(2)}) copy-start(bf16[1,8,64,2048]{3,2,1,0:T(8,128)(2,1)} %param.17) | copy-start | bytes 6291460
Sparse Core Ops, SparseCore 0:
  9.7 154.0 all-gather.4
  165.5 107.8 all-gather.6
where the time goes:
time: 372 us
  waiting for transfers between devices  127 us (34%)
  blocking collectives  106 us (28%)
  matrix products  65.2 us (18%)
  other arithmetic  28.7 us (8%)
  local copies, waits for them, and re-layouts  20.6 us (6%)
  between operations  14.2 us (4%)
  starting transfers between devices  9.51 us (3%)
    all_gather x1, blocking collectives, per_device(): all_docs = lax.all_gather(doc_ids, 'ctx', axis=1, tiled=True)[0]  91.4 us
    all_to_all x1, waiting for transfers between devices, per_device(): lax.all_to_all(span_values, 'db', split_axis=0, concat_axis=0, tiled=True)  90.7 us
    all_gather x1, waiting for transfers between devices, per_device(): value_block = lax.all_gather(values[0], 'ctx', axis=0, tiled=True)  35.4 us
    dot_general x1, matrix products, update(): jnp.einsum('hts,shd->thd', expo.astype(jnp.bfloat16), value_block.reshape...  31.4 us
    dot_general x1, matrix products, update(): jnp.einsum('thd,shd->hts', query_split, key_block.reshape(block_rows, hea...  30.6 us
    reduce_sum x1, other arithmetic, update(): new_sum = jnp.sum(expo, axis=2)  24.2 us
    all_to_all x1, blocking collectives, per_device(): lax.all_to_all(request_table, 'db', split_axis=0, concat_axis=0, tiled=True)  14.6 us
  transfers between devices with their start and end apart: 4, of which 2 were waited for; matrix products, arithmetic and copies ran while one was open for 6% of the time, Pallas kernels for 0%

commit v1 on v0

v1 whole, which is shorter than its diff:
```python
import functools
import math

import jax
import jax.numpy as jnp
from jax import lax
from jax.experimental import pallas as pl
from jax.experimental.pallas import tpu as pltpu
from jax.sharding import PartitionSpec as P

DH = 128
CH = 64
NH = 16
TOK = 256
HD = 2048
NZ = 4
NC = 16
QT = 512
CHUNK = 3 * TOK + 16
NEG = -1e30
SCALE = math.log2(math.e) / math.sqrt(DH)
VMEM = 48 << 20

f32, bf16, i32 = jnp.float32, jnp.bfloat16, jnp.int32


def params():
    return pltpu.CompilerParams(vmem_limit_bytes=VMEM)


def cost(flops, nbytes):
    return pl.CostEstimate(flops=flops, bytes_accessed=nbytes, transcendentals=0)


def pack_heads_kernel(docs_ref, q_ref, k_ref, v_ref, out_ref):
    row = lax.broadcasted_iota(i32, (16, DH), 0)
    docs = docs_ref[...]
    left = jnp.broadcast_to(docs[:, :DH], (16, DH))
    right = jnp.broadcast_to(docs[:, DH:], (16, DH))
    packed = jnp.where(row == 0, left, jnp.where(row == 1, right, 4)).astype(f32).astype(bf16)
    for h in range(4):
        cols = slice(h * DH, (h + 1) * DH)
        out_ref[h, 0:TOK, :] = q_ref[:, cols]
        out_ref[h, TOK : 2 * TOK, :] = k_ref[:, cols]
        out_ref[h, 2 * TOK : 3 * TOK, :] = v_ref[:, cols]
        out_ref[h, 3 * TOK : CHUNK, :] = packed


def pack_heads(docs, q, k, v):
    wide = pl.BlockSpec((TOK, 4 * DH), lambda i: (0, i))
    return pl.pallas_call(
        pack_heads_kernel,
        grid=(4,),
        in_specs=[pl.BlockSpec((1, TOK), lambda i: (0, 0)), wide, wide, wide],
        out_specs=pl.BlockSpec((4, CHUNK, DH), lambda i: (i, 0, 0)),
        out_shape=jax.ShapeDtypeStruct((NC, CHUNK, DH), bf16),
        compiler_params=params(),
        cost_estimate=cost(0, 6 << 20),
        name="pack_heads",
    )(docs, q, k, v)


def unpack_heads_kernel(x_ref, out_ref):
    for h in range(4):
        out_ref[:, h * DH : (h + 1) * DH] = x_ref[h]


def unpack_heads(x):
    return pl.pallas_call(
        unpack_heads_kernel,
        grid=(4,),
        in_specs=[pl.BlockSpec((4, TOK, DH), lambda i: (i, 0, 0))],
        out_specs=pl.BlockSpec((TOK, 4 * DH), lambda i: (0, i)),
        out_shape=jax.ShapeDtypeStruct((TOK, HD), bf16),
        compiler_params=params(),
        cost_estimate=cost(0, 2 << 20),
        name="unpack_heads",
    )(x)


def self_kernel(x_ref, o_ref):
    docs = x_ref[:, 3 * TOK : CHUNK, :].astype(f32)
    ends = [jnp.sum(jnp.where(docs < d - 0.5, 1.0, 0.0)).astype(i32) for d in (1, 2, 3)]

    def start_of(p):
        s = jnp.where(p >= ends[0], ends[0], 0)
        s = jnp.maximum(s, jnp.where(p >= ends[1], ends[1], 0))
        return jnp.maximum(s, jnp.where(p >= ends[2], ends[2], 0))

    def rows(j, part):
        return x_ref[pl.ds(2 * j, 2), part * TOK : (part + 1) * TOK, :].reshape(QT, DH)

    local = lax.broadcasted_iota(i32, (QT, QT), 1)
    column = lax.broadcasted_iota(i32, (QT, 1), 0)

    def scores(q, j):
        s = lax.dot_general(q, rows(j, 1), (((1,), (1,)), ((), ())), preferred_element_type=f32)
        return s * SCALE

    def lanes(p):
        return (p[:, :DH] + p[:, DH : 2 * DH]) + (p[:, 2 * DH : 3 * DH] + p[:, 3 * DH :])

    def mix(p, j):
        return jnp.dot(p.astype(bf16), rows(j, 2), preferred_element_type=f32)

    def query_tile(i, carry):
        base = i * QT
        q = rows(i, 0)
        first = start_of(base + column)
        lo = start_of(base) // QT
        mid = jnp.minimum((start_of(base + QT - 1) + QT - 1) // QT, i)

        s = scores(q, i)
        s = jnp.where((local <= column) & (local >= first - base), s, NEG)
        top = jnp.max(s, axis=1, keepdims=True)
        p = jnp.exp2(s - top)
        state = (mix(p, i), top, lanes(p))

        def step(j, state, masked):
            acc, top, total = state
            s = scores(q, j)
            if masked:
                s = jnp.where(local >= first - j * QT, s, NEG)
            new = jnp.maximum(top, jnp.max(s, axis=1, keepdims=True))
            p = jnp.exp2(s - new)
            fade = jnp.exp2(top - new)
            return acc * fade + mix(p, j), new, total * fade + lanes(p)

        state = lax.fori_loop(lo, mid, functools.partial(step, masked=True), state)
        acc, top, total = lax.fori_loop(mid, i, functools.partial(step, masked=False), state)
        out = acc / jnp.sum(total, axis=1, keepdims=True)
        o_ref[pl.ds(2 * i, 2)] = out.astype(bf16).reshape(2, TOK, DH)
        return carry

    lax.fori_loop(0, NC * TOK // QT, query_tile, 0)


def self_attention(x):
    return pl.pallas_call(
        self_kernel,
        in_specs=[pl.BlockSpec(memory_space=pltpu.VMEM)],
        out_specs=pl.BlockSpec(memory_space=pltpu.VMEM),
        out_shape=jax.ShapeDtypeStruct((NC, TOK, DH), bf16),
        compiler_params=params(),
        cost_estimate=cost(16 << 30, 4 << 20),
        name="self_attention",
    )(x)


def pack_spans_kernel(tab_ref, keys_ref, values_ref, *refs):
    outs, sems = refs[:8], refs[8]
    me = lax.axis_index("db")
    plane, z = me // NZ, me % NZ
    copies = []
    for far in (1, 0):
        side = 1 - plane if far else plane
        for k in (1, 3, 2, 0):
            asker = side * NZ + (z + k) % NZ
            first, second, seen = jnp.int32(0), jnp.int32(0), jnp.int32(0)
            for r in range(8):
                hit = tab_ref[asker, r] == me
                span = tab_ref[asker, 8 + r]
                first = jnp.where(hit & (seen == 0), span, first)
                second = jnp.where(hit & (seen == 1), span, second)
                seen = seen + jnp.where(hit, 1, 0)
            for slot, span in ((0, first), (1, second)):
                for kind, src in ((0, keys_ref), (1, values_ref)):
                    copy = pltpu.make_async_copy(
                        src.at[span], outs[far * 4 + k].at[slot, kind], sems.at[far * 4 + k, slot, kind]
                    )
                    copy.start()
                    copies.append(copy)
    for copy in copies:
        copy.wait()


def pack_spans(table, keys, values):
    spec = pl.BlockSpec(memory_space=pl.ANY)
    return pl.pallas_call(
        pack_spans_kernel,
        in_specs=[pl.BlockSpec(memory_space=pltpu.SMEM), spec, spec],
        out_specs=[spec] * 8,
        out_shape=[jax.ShapeDtypeStruct((2, 2, CH, HD), bf16)] * 8,
        scratch_shapes=[pltpu.SemaphoreType.DMA((8, 2, 2))],
        compiler_params=params(),
        cost_estimate=cost(0, 16 << 20),
        name="pack_spans",
    )(table, keys, values)


def cross_kernel(far, tab_ref, q_ref, *refs):
    got = refs[:4]
    if far:
        out_ref, lse_ref, kbuf, vbuf, sems = refs[4:]
    else:
        part_ref, part_lse_ref, out_ref, kbuf, vbuf, sems = refs[4:]
    me = lax.axis_index("db")
    plane, z = me // NZ, me % NZ
    row = (1 - plane) * NZ + z if far else me
    here = []
    for r in range(8):
        owner = tab_ref[row, r]
        slot = jnp.int32(0)
        for earlier in range(r):
            slot = slot + jnp.where(tab_ref[row, earlier] == owner, 1, 0)
        here.append(jnp.where(owner // NZ == plane, 1, 0))
        shift = (z - owner % NZ + NZ) % NZ
        place = pl.ds((r % 2) * CH, CH)
        for k in range(4):

            @pl.when(shift == k)
            def _(k=k, slot=slot, place=place, r=r):
                pltpu.make_async_copy(got[k].at[slot, 0], kbuf.at[r // 2, place], sems.at[r, 0]).start()
                pltpu.make_async_copy(got[k].at[slot, 1], vbuf.at[r // 2, place], sems.at[r, 1]).start()

    lane = lax.broadcasted_iota(i32, (1, DH), 1)
    for n in range(4):
        for r in (2 * n, 2 * n + 1):
            place = pl.ds((r % 2) * CH, CH)
            pltpu.make_async_copy(got[0].at[0, 0], kbuf.at[n, place], sems.at[r, 0]).wait()
            pltpu.make_async_copy(got[0].at[0, 1], vbuf.at[n, place], sems.at[r, 1]).wait()
        mine = jnp.where(lane < CH, here[2 * n], here[2 * n + 1]) > 0
        toks = slice(n * CH, (n + 1) * CH)
        heads = [slice(h * DH, (h + 1) * DH) for h in range(NH)]
        s = [
            lax.dot_general(
                q_ref[toks, c], kbuf[n, :, c], (((1,), (1,)), ((), ())), preferred_element_type=f32
            )
            for c in heads
        ]
        s = [jnp.where(mine, x * SCALE, NEG) for x in s]
        top = [jnp.max(x, axis=1, keepdims=True) for x in s]
        p = [jnp.where(mine, jnp.exp2(x - t), 0.0) for x, t in zip(s, top)]
        total = [jnp.sum(x, axis=1, keepdims=True) for x in p]
        o = [jnp.dot(x.astype(bf16), vbuf[n, :, c], preferred_element_type=f32) for x, c in zip(p, heads)]
        if far:
            stats = jnp.full((CH, DH), NEG, f32)
            for h, c in enumerate(heads):
                safe = jnp.maximum(total[h], 1e-30)
                out_ref[toks, c] = (o[h] / safe).astype(bf16)
                lse = jnp.where(total[h] > 0, top[h] + jnp.log2(safe), NEG)
                stats = jnp.where(lane == h, lse, stats)
            lse_ref[toks, :] = stats
        else:
            for h, c in enumerate(heads):
                other = part_lse_ref[toks, h : h + 1]
                high = jnp.maximum(top[h], other)
                a, b = jnp.exp2(top[h] - high), jnp.exp2(other - high)
                mixed = o[h] * a + part_ref[toks, c].astype(f32) * b
                out_ref[toks, c] = (mixed / (total[h] * a + b)).astype(bf16)


def cross(far, table, q, got, part=()):
    vmem = pl.BlockSpec(memory_space=pltpu.VMEM)
    rows = jax.ShapeDtypeStruct((TOK, HD), bf16)
    stats = jax.ShapeDtypeStruct((TOK, DH), f32)
    return pl.pallas_call(
        functools.partial(cross_kernel, far),
        in_specs=[pl.BlockSpec(memory_space=pltpu.SMEM), vmem]
        + [pl.BlockSpec(memory_space=pl.ANY)] * 4
        + [vmem] * len(part),
        out_specs=[vmem, vmem] if far else vmem,
        out_shape=[rows, stats] if far else rows,
        scratch_shapes=[
            pltpu.VMEM((4, 2 * CH, HD), bf16),
            pltpu.VMEM((4, 2 * CH, HD), bf16),
            pltpu.SemaphoreType.DMA((8, 2)),
        ],
        compiler_params=params(),
        cost_estimate=cost(4 << 30, 6 << 20),
        name="cross_far" if far else "cross_near",
    )(table, q, *got, *part)


def per_device(queries, keys, values, doc_ids, nbr_owner, nbr_local, db_keys, db_values):
    q = queries[0]
    swap = [(d, (d + NZ) % 8) for d in range(8)]
    turn = lambda k: [(s * NZ + z, s * NZ + (z + k) % NZ) for s in range(2) for z in range(NZ)]
    far_q = lax.ppermute(q, "db", swap)

    asked = jnp.concatenate([nbr_owner[0].reshape(1, 8), nbr_local[0].reshape(1, 8)], axis=1)
    table = lax.all_gather(asked, "db", axis=0, tiled=True)
    packed = pack_spans(table, db_keys[0], db_values[0])
    near, far = list(packed[:4]), list(packed[4:])

    heads = pack_heads(doc_ids, q, keys[0], values[0])
    heads, far = lax.optimization_barrier((heads, far))
    far_got = [far[0]] + [lax.ppermute(far[k], "db", turn(k)) for k in (1, 2, 3)]
    heads = lax.all_to_all(heads, "ctx", split_axis=0, concat_axis=0, tiled=True)

    near, far_got = lax.optimization_barrier((near, far_got))
    near_got = [near[0]] + [lax.ppermute(near[k], "db", turn(k)) for k in (1, 2, 3)]
    part, lse = cross(True, table, far_q, far_got)
    part = lax.ppermute(part, "db", swap)
    lse = lax.ppermute(lse, "db", swap)

    self_rows = self_attention(heads)
    self_rows = lax.all_to_all(self_rows, "ctx", split_axis=0, concat_axis=0, tiled=True)
    self_rows = unpack_heads(self_rows)

    cross_rows = cross(False, table, q, near_got, (part, lse))
    return self_rows[None], cross_rows[None]


def solution(mesh):
    rows = P("db", "ctx", None)
    spans = P("db", "ctx", None, None)
    return jax.shard_map(
        per_device,
        mesh=mesh,
        in_specs=(rows, rows, rows, P("db", "ctx"), rows, rows, spans, spans),
        out_specs=(rows, rows),
        check_vma=False,
    )
```

time: 372 us -> 364 us (0.978)
  Pallas kernels: 0 us -> 238 us
  blocking collectives: 106 us -> 21.5 us
  matrix products: 65.2 us -> 0 us
  waiting for transfers between devices: 127 us -> 71.8 us
  other arithmetic: 28.7 us -> 0.08 us
  local copies, waits for them, and re-layouts: 20.6 us -> 6.52 us
  starting transfers between devices: 9.51 us -> 23 us
  between operations: 14.2 us -> 0.81 us
    pallas_call x0 -> x6, Pallas kernels: none -> 238 us  [the longest x1 193 us: pack_spans(): pl.pallas_call(pack_spans_kernel, in_specs=[pl.BlockSpec(memory_space=plt...]
    all_to_all x2, waiting for transfers between devices: 90.7 us -> 0.01 us  [the longest x1 0.01 us: per_device(): lax.all_to_all(heads, 'ctx', split_axis=0, concat_axis=0, tiled=True)]
    ppermute x0 -> x9, waiting for transfers between devices: none -> 71.8 us  [the longest x3 44.4 us: per_device(): lax.ppermute(far[k], 'db', turn(k))]
    all_gather x1, blocking collectives: 91.4 us -> 21.5 us  [per_device(): table = lax.all_gather(asked, 'db', axis=0, tiled=True)]
    dot_general x5 -> x0, matrix products: 65.2 us -> none  [the longest x1 31.4 us: update(): jnp.einsum('hts,shd->thd', expo.astype(jnp.bfloat16), value_block.reshape...]
    all_gather x2 -> x0, waiting for transfers between devices: 35.4 us -> none  [the longest x1 35.4 us: per_device(): value_block = lax.all_gather(values[0], 'ctx', axis=0, tiled=True)]
    reduce_sum x3 -> x0, other arithmetic: 25.6 us -> none  [the longest x1 24.2 us: update(): new_sum = jnp.sum(expo, axis=2)]
    all_to_all x1 -> x0, blocking collectives: 14.6 us -> none  [per_device(): lax.all_to_all(request_table, 'db', split_axis=0, concat_axis=0, tiled=True)]
  transfers between devices with their start and end apart: 4 -> 11, of which waited for: 2 -> 4; matrix products, arithmetic and copies ran while one was open for 6% -> 0% of each run, Pallas kernels for 0% -> 11%
where the time goes in v1:
time: 364 us; the launch traced here: 362 us
  Pallas kernels  238 us (65%)
  waiting for transfers between devices  71.8 us (20%)
  starting transfers between devices  23 us (6%)
  blocking collectives  21.5 us (6%)
  local copies, waits for them, and re-layouts  6.52 us (2%)
    pallas_call x1, Pallas kernels, pack_spans(): pl.pallas_call(pack_spans_kernel, in_specs=[pl.BlockSpec(memory_space=plt...  193 us
    ppermute x3, waiting for transfers between devices, per_device(): lax.ppermute(far[k], 'db', turn(k))  44.4 us
    pallas_call x1, Pallas kernels, self_attention(): pl.pallas_call(self_kernel, in_specs=[pl.BlockSpec(memory_space=pltpu.VME...  24.7 us
    all_gather x1, blocking collectives, per_device(): table = lax.all_gather(asked, 'db', axis=0, tiled=True)  21.5 us
    pallas_call x2, Pallas kernels, cross(): pl.pallas_call(functools.partial(cross_kernel, far), in_specs=[pl.BlockSp...  16.1 us
    ppermute x1, waiting for transfers between devices, per_device(): lse = lax.ppermute(lse, 'db', swap)  15 us
    ppermute x1, waiting for transfers between devices, per_device(): far_q = lax.ppermute(q, 'db', swap)  12.5 us
    all_to_all x1, starting transfers between devices, per_device(): lax.all_to_all(heads, 'ctx', split_axis=0, concat_axis=0, tiled=True)  8.94 us
  transfers between devices with their start and end apart: 11, of which 4 were waited for; matrix products, arithmetic and copies ran while one was open for 0% of the time, Pallas kernels for 11%

profile of v1, /device:TPU:1, one launch (start us, length us, event | category | flops | bytes accessed | tf_op | source)
XLA Modules:
  0.0 361.7 jit_solution(1226551896929942318)
XLA Ops:
  0.6 0.0 copy-start.3
  0.6 0.0 copy-start.1
  0.7 0.0 copy-start.2
  0.7 0.0 copy-start.5
  0.7 0.9 copy.14
  1.6 0.1 reshape_squeeze.6
  1.7 0.8 copy.15
  2.4 0.1 reshape_squeeze.7
  2.5 0.1 add_bitcast_fusion
  2.6 21.5 %all-gather = s32[8,1,16]{2,1,0:T(1,128)S(1)} all-gather(s32[1,1,16]{2,1,0:T(1,128)S(1)} %add_bitcast_fusion), channel_id=1, replica_groups=mesh['ctx'=16,'db'=8] {'db'}, dimensions={0}, use_global_device_ids=true | all-gather | bytes 576 | tf_op jit(solution)/shard_map/all_gather | solution.py:282
  24.1 192.6 %pack_spans.1 = (bf16[2,2,64,2048]{3,2,1,0:T(8,128)(2,1)S(1)}, bf16[2,2,64,2048]{3,2,1,0:T(8,128)(2,1)}, bf16[2,2,64,2048]{3,2,1,0:T(8,128)(2,1)}, bf16[2,2,64,2...) custom-call(s32[8,16]{1,0:T(8,128)S(1)} %bitcast.15, ...), custom_call_target="tpu_custom_call" | custom-call | bytes 16777216 | tf_op jit(solution)/shard_map/pack_spans/pallas_call | solution.py:179
  216.8 0.0 copy-start.6
  216.8 0.0 copy-start.8
  216.8 0.0 copy-done.3
  216.8 0.0 copy-done.1
  216.8 2.8 pack_heads.1
  219.6 8.9 %all-to-all-start = ((bf16[16,784,128]{2,1,0:T(8,128)(2,1)}), bf16[16,784,128]{2,1,0:T(8,128)(2,1)S(1)}, u32[]{:S(2)}, u32[]{:S(2)}) async-start(bf16[16,784,128]{2,1,0:T(8,128)(2,1)} %pack_heads.1), calls=%async_computation | async-start | bytes 6422528 | tf_op jit(solution)/shard_map/all_to_all | solution.py:289
  228.6 0.0 collective-permute-start
  228.6 0.1 collective-permute-start.1
  228.7 2.6 collective-permute-start.2
  231.2 1.7 collective-permute-start.6
  233.0 44.1 %collective-permute-done.refs_1_ = bf16[2,2,64,2048]{3,2,1,0:T(8,128)(2,1)S(1)} collective-permute-done((bf16[2,2,64,2048]{3,2,1,0:T(8,128)(2,1)}, bf16[2,2,64,2048]{3,2,1,0:T(8,128)(2,1)S(1)}, u32[]{:S(2)}, u32[]{:S(2)}) %collective-permute-start) | collective-permute-done | bytes 1048608 | tf_op jit(solution)/shard_map/ppermute | solution.py:288
  277.1 0.0 collective-permute-done.1.refs_2_
  277.1 0.3 collective-permute-done.2.refs_3_
  277.4 12.5 %collective-permute-done.6.q_ref = bf16[256,2048]{1,0:T(8,128)(2,1)S(1)} collective-permute-done((bf16[256,2048]{1,0:T(8,128)(2,1)}, bf16[256,2048]{1,0:T(8,128)(2,1)S(1)}, u32[]{:S(2)}, u32[]{:S(2)}) %collective-permute-start.6) | collective-permute-done | bytes 1048608 | tf_op jit(solution)/shard_map/ppermute | solution.py:279
  289.8 1.2 copy-done.9
  291.1 5.7 %cross_far.1 = (bf16[256,2048]{1,0:T(8,128)(2,1)}, f32[256,128]{1,0:T(8,128)S(1)}) custom-call(s32[8,16]{1,0:T(8,128)S(1)} %bitcast.16, bf16[256,2048]{1,0:T(8,128)(2,1)S(1)} %collective-permute-done.6.q_ref, bf16[2,2,64,2048]{3,2,1,0:T(8,128)(2,1)S(1)} %copy-done.9, bf16[2,2,64,2048]{3,2,1,0:T(8,128)(2,1)S(1)} %collective-permute-done.refs_1_, ...), custom_call_target="tpu_custom_call" | custom-call | flops 4294967296 | bytes 6291456 | tf_op jit(solution)/shard_map/cross_far/pallas_call | solution.py:257
  296.8 1.5 collective-permute-start.7
  298.3 0.0 collective-permute-start.3
  298.3 0.0 collective-permute-start.4
  298.3 2.7 collective-permute-start.5
  301.0 0.0 all-to-all-done.x_ref
  301.0 24.7 %self_attention.1 = bf16[16,256,128]{2,1,0:T(8,128)(2,1)S(1)} custom-call(bf16[16,784,128]{2,1,0:T(8,128)(2,1)S(1)} %all-to-all-done.x_ref), custom_call_target="tpu_custom_call" | custom-call | flops 17179869184 | bytes 4194304 | tf_op jit(solution)/shard_map/self_attention/pallas_call | solution.py:139
  325.7 0.0 copy-start
  325.7 1.0 copy-done
  326.6 5.5 %all-to-all-start.1 = ((bf16[16,256,128]{2,1,0:T(8,128)(2,1)}), bf16[16,256,128]{2,1,0:T(8,128)(2,1)S(1)}, u32[]{:S(2)}, u32[]{:S(2)}) async-start(bf16[16,256,128]{2,1,0:T(8,128)(2,1)} %copy-done), calls=%async_computation.1 | async-start | bytes 2097152 | tf_op jit(solution)/shard_map/all_to_all | solution.py:298
  332.2 0.0 collective-permute-start.8
  332.2 15.0 %collective-permute-done.8.refs_5_ = f32[256,128]{1,0:T(8,128)S(1)} collective-permute-done((f32[256,128]{1,0:T(8,128)S(1)}, f32[256,128]{1,0:T(8,128)S(1)}, u32[]{:S(2)}, u32[]{:S(2)}) %collective-permute-start.8) | collective-permute-done | bytes 131104 | tf_op jit(solution)/shard_map/ppermute | solution.py:295
  347.1 0.0 collective-permute-done.7.refs_4_
  347.1 0.0 collective-permute-done.3.refs_1_
  347.1 0.0 collective-permute-done.4.refs_2_
  347.1 0.0 collective-permute-done.5.refs_3_
  347.2 0.0 copy-start.4
  347.2 1.2 copy-done.4
  348.4 1.2 copy-done.7
  349.6 10.4 %cross_near.1 = bf16[256,2048]{1,0:T(8,128)(2,1)} custom-call(s32[8,16]{1,0:T(8,128)S(1)} %bitcast.17, bf16[256,2048]{1,0:T(8,128)(2,1)S(1)} %bitcast.14, bf16[2,2,64,2048]{3,2,1,0:T(8,128)(2,1)S(1)} %copy-done.7, bf16[2,2,64,2048]{3,2,1,0:T(8,128)(2,1)} %collective-permute-done.3.refs_1_, bf16[2,2,64,2048]{3,2,1,0:T(8,128)(2,1)} %collective-permute-done.4.refs_2_, ...), custom_call_target="tpu_custom_call" | custom-call | flops 4294967296 | bytes 6291456 | tf_op jit(solution)/shard_map/cross_near/pallas_call | solution.py:257
  360.0 0.0 all-to-all-done.1.x_ref
  360.0 1.6 unpack_heads.1
  (8 shorter events, 0.0 us)
Async XLA Ops:
  0.6 216.2 %copy-start.3 = (bf16[1,256,2048]{2,1,0:T(8,128)(2,1)S(1)}, bf16[1,256,2048]{2,1,0:T(8,128)(2,1)}, u32[]{:S(2)}) copy-start(bf16[1,256,2048]{2,1,0:T(8,128)(2,1)} %param.8) | copy-start | bytes 3145732
  0.6 216.2 %copy-start.1 = (bf16[1,256,2048]{2,1,0:T(8,128)(2,1)S(1)}, bf16[1,256,2048]{2,1,0:T(8,128)(2,1)}, u32[]{:S(2)}) copy-start(bf16[1,256,2048]{2,1,0:T(8,128)(2,1)} %param.9) | copy-start | bytes 3145732
  0.7 216.2 %copy-start.2 = (bf16[1,256,2048]{2,1,0:T(8,128)(2,1)S(1)}, bf16[1,256,2048]{2,1,0:T(8,128)(2,1)}, u32[]{:S(2)}) copy-start(bf16[1,256,2048]{2,1,0:T(8,128)(2,1)} %param.10) | copy-start | bytes 3145732
  0.7 216.2 %copy-start.5 = (s32[1,256]{1,0:T(1,128)S(1)}, s32[1,256]{1,0:T(1,128)}, u32[]{:S(2)}) copy-start(s32[1,256]{1,0:T(1,128)} %docs_ref.1) | copy-start | bytes 3076
  216.8 2.8 copy-start.6
  216.8 2.8 copy-start.8
  219.6 81.3 %all-to-all-start = ((bf16[16,784,128]{2,1,0:T(8,128)(2,1)}), bf16[16,784,128]{2,1,0:T(8,128)(2,1)S(1)}, u32[]{:S(2)}, u32[]{:S(2)}) async-start(bf16[16,784,128]{2,1,0:T(8,128)(2,1)} %pack_heads.1), calls=%async_computation | async-start | bytes 6422528 | tf_op jit(solution)/shard_map/all_to_all | solution.py:289
  228.6 48.5 %collective-permute-start = (bf16[2,2,64,2048]{3,2,1,0:T(8,128)(2,1)}, bf16[2,2,64,2048]{3,2,1,0:T(8,128)(2,1)S(1)}, u32[]{:S(2)}, u32[]{:S(2)}) collective-permute-start(bf16[2,2,64,2048]{3,2,1,0:T(8,128)(2,1)} %get-tuple-element.35), channel_id=1, source_target_pairs={{0,1},{1,2},{2,3},{3,0},{4,5},{5,6},{6,7},{7,4},{8,9},{9,10},{10,1... | collective-permute-start | bytes 3145736 | tf_op jit(solution)/shard_map/ppermute | solution.py:288
  228.6 48.5 %collective-permute-start.1 = (bf16[2,2,64,2048]{3,2,1,0:T(8,128)(2,1)}, bf16[2,2,64,2048]{3,2,1,0:T(8,128)(2,1)S(1)}, u32[]{:S(2)}, u32[]{:S(2)}) collective-permute-start(bf16[2,2,64,2048]{3,2,1,0:T(8,128)(2,1)} %get-tuple-element.36), channel_id=1, source_target_pairs={{0,2},{1,3},{2,0},{3,1},{4,6},{5,7},{6,4},{7,5},{8,10},{9,11},{10,... | collective-permute-start | bytes 3145736 | tf_op jit(solution)/shard_map/ppermute | solution.py:288
  228.7 48.7 %collective-permute-start.2 = (bf16[2,2,64,2048]{3,2,1,0:T(8,128)(2,1)}, bf16[2,2,64,2048]{3,2,1,0:T(8,128)(2,1)S(1)}, u32[]{:S(2)}, u32[]{:S(2)}) collective-permute-start(bf16[2,2,64,2048]{3,2,1,0:T(8,128)(2,1)} %get-tuple-element.37), channel_id=1, source_target_pairs={{0,3},{1,0},{2,1},{3,2},{4,7},{5,4},{6,5},{7,6},{8,11},{9,8},{10,9... | collective-permute-start | bytes 3145736 | tf_op jit(solution)/shard_map/ppermute | solution.py:288
  231.2 58.6 %collective-permute-start.6 = (bf16[256,2048]{1,0:T(8,128)(2,1)}, bf16[256,2048]{1,0:T(8,128)(2,1)S(1)}, u32[]{:S(2)}, u32[]{:S(2)}) collective-permute-start(bf16[256,2048]{1,0:T(8,128)(2,1)} %bitcast.12), channel_id=1, source_target_pairs={{0,4},{1,5},{2,6},{3,7},{4,0},{5,1},{6,2},{7,3},{8,12},{9,13},{10,... | collective-permute-start | bytes 3145736 | tf_op jit(solution)/shard_map/ppermute | solution.py:279
  277.4 12.5 %copy-start.10 = (bf16[2,2,64,2048]{3,2,1,0:T(8,128)(2,1)}, bf16[2,2,64,2048]{3,2,1,0:T(8,128)(2,1)S(1)}, u32[]{:S(2)}) copy-start(bf16[2,2,64,2048]{3,2,1,0:T(8,128)(2,1)S(1)} %collective-permute-done.2.refs_3_) | copy-start | bytes 3145732
  289.8 1.2 copy-start.9
  296.8 50.3 %collective-permute-start.7 = (bf16[256,2048]{1,0:T(8,128)(2,1)}, bf16[256,2048]{1,0:T(8,128)(2,1)}, u32[]{:S(2)}, u32[]{:S(2)}) collective-permute-start(bf16[256,2048]{1,0:T(8,128)(2,1)} %get-tuple-element.46), channel_id=1, source_target_pairs={{0,4},{1,5},{2,6},{3,7},{4,0},{5,1},{6,2},{7,3},{8,12},{9,13},{10,... | collective-permute-start | bytes 3145736 | tf_op jit(solution)/shard_map/ppermute | solution.py:294
  298.3 48.9 %collective-permute-start.3 = (bf16[2,2,64,2048]{3,2,1,0:T(8,128)(2,1)}, bf16[2,2,64,2048]{3,2,1,0:T(8,128)(2,1)}, u32[]{:S(2)}, u32[]{:S(2)}) collective-permute-start(bf16[2,2,64,2048]{3,2,1,0:T(8,128)(2,1)} %get-tuple-element.39), channel_id=1, source_target_pairs={{0,1},{1,2},{2,3},{3,0},{4,5},{5,6},{6,7},{7,4},{8,9},{9,10},{10,1... | collective-permute-start | bytes 3145736 | tf_op jit(solution)/shard_map/ppermute | solution.py:292
  298.3 48.9 %collective-permute-start.4 = (bf16[2,2,64,2048]{3,2,1,0:T(8,128)(2,1)}, bf16[2,2,64,2048]{3,2,1,0:T(8,128)(2,1)}, u32[]{:S(2)}, u32[]{:S(2)}) collective-permute-start(bf16[2,2,64,2048]{3,2,1,0:T(8,128)(2,1)} %get-tuple-element.40), channel_id=1, source_target_pairs={{0,2},{1,3},{2,0},{3,1},{4,6},{5,7},{6,4},{7,5},{8,10},{9,11},{10,... | collective-permute-start | bytes 3145736 | tf_op jit(solution)/shard_map/ppermute | solution.py:292
  298.3 48.9 %collective-permute-start.5 = (bf16[2,2,64,2048]{3,2,1,0:T(8,128)(2,1)}, bf16[2,2,64,2048]{3,2,1,0:T(8,128)(2,1)}, u32[]{:S(2)}, u32[]{:S(2)}) collective-permute-start(bf16[2,2,64,2048]{3,2,1,0:T(8,128)(2,1)} %get-tuple-element.41), channel_id=1, source_target_pairs={{0,3},{1,0},{2,1},{3,2},{4,7},{5,4},{6,5},{7,6},{8,11},{9,8},{10,9... | collective-permute-start | bytes 3145736 | tf_op jit(solution)/shard_map/ppermute | solution.py:292
  325.7 1.0 copy-start
  326.6 33.4 %all-to-all-start.1 = ((bf16[16,256,128]{2,1,0:T(8,128)(2,1)}), bf16[16,256,128]{2,1,0:T(8,128)(2,1)S(1)}, u32[]{:S(2)}, u32[]{:S(2)}) async-start(bf16[16,256,128]{2,1,0:T(8,128)(2,1)} %copy-done), calls=%async_computation.1 | async-start | bytes 2097152 | tf_op jit(solution)/shard_map/all_to_all | solution.py:298
  332.2 15.0 %collective-permute-start.8 = (f32[256,128]{1,0:T(8,128)S(1)}, f32[256,128]{1,0:T(8,128)S(1)}, u32[]{:S(2)}, u32[]{:S(2)}) collective-permute-start(f32[256,128]{1,0:T(8,128)S(1)} %get-tuple-element.47), channel_id=1, source_target_pairs={{0,4},{1,5},{2,6},{3,7},{4,0},{5,1},{6,2},{7,3},{8,12},{9,13},{10,... | collective-permute-start | bytes 393224 | tf_op jit(solution)/shard_map/ppermute | solution.py:295
  347.2 1.2 copy-start.4
  348.4 1.2 copy-start.7

commit v2 on v1

--- a/solution.py
+++ b/solution.py
@@ -29,7 +29,7 @@
 
 
 def cost(flops, nbytes):
-    return pl.CostEstimate(flops=flops, bytes_accessed=nbytes, transcendentals=0)
+    return pl.CostEstimate(flops=flops // 64, bytes_accessed=nbytes // 16, transcendentals=0)
 
 
 def pack_heads_kernel(docs_ref, q_ref, k_ref, v_ref, out_ref):
@@ -147,78 +147,87 @@
     )(x)
 
 
-def pack_spans_kernel(tab_ref, keys_ref, values_ref, *refs):
-    outs, sems = refs[:8], refs[8]
+SHIFTS = (1, 3, 2)
+
+
+def pack_spans_kernel(far, tab_ref, keys_ref, values_ref, *refs):
+    outs, sems = refs[:3], refs[3]
     me = lax.axis_index("db")
     plane, z = me // NZ, me % NZ
+    side = 1 - plane if far else plane
     copies = []
-    for far in (1, 0):
-        side = 1 - plane if far else plane
-        for k in (1, 3, 2, 0):
-            asker = side * NZ + (z + k) % NZ
-            first, second, seen = jnp.int32(0), jnp.int32(0), jnp.int32(0)
-            for r in range(8):
-                hit = tab_ref[asker, r] == me
-                span = tab_ref[asker, 8 + r]
-                first = jnp.where(hit & (seen == 0), span, first)
-                second = jnp.where(hit & (seen == 1), span, second)
-                seen = seen + jnp.where(hit, 1, 0)
-            for slot, span in ((0, first), (1, second)):
-                for kind, src in ((0, keys_ref), (1, values_ref)):
-                    copy = pltpu.make_async_copy(
-                        src.at[span], outs[far * 4 + k].at[slot, kind], sems.at[far * 4 + k, slot, kind]
-                    )
-                    copy.start()
-                    copies.append(copy)
+    for i, k in enumerate(SHIFTS):
+        asker = side * NZ + (z + k) % NZ
+        first, second, seen = jnp.int32(0), jnp.int32(0), jnp.int32(0)
+        for r in range(8):
+            hit = tab_ref[asker, r // 2, r % 2] == me
+            span = tab_ref[asker, r // 2, 2 + r % 2]
+            first = jnp.where(hit & (seen == 0), span, first)
+            second = jnp.where(hit & (seen == 1), span, second)
+            seen = seen + jnp.where(hit, 1, 0)
+        for slot, span in ((0, first), (1, second)):
+            for kind, src in ((0, keys_ref), (1, values_ref)):
+                copy = pltpu.make_async_copy(src.at[span], outs[i].at[slot, kind], sems.at[i, slot, kind])
+                copy.start()
+                copies.append(copy)
     for copy in copies:
         copy.wait()
 
 
-def pack_spans(table, keys, values):
-    spec = pl.BlockSpec(memory_space=pl.ANY)
-    return pl.pallas_call(
-        pack_spans_kernel,
-        in_specs=[pl.BlockSpec(memory_space=pltpu.SMEM), spec, spec],
-        out_specs=[spec] * 8,
-        out_shape=[jax.ShapeDtypeStruct((2, 2, CH, HD), bf16)] * 8,
-        scratch_shapes=[pltpu.SemaphoreType.DMA((8, 2, 2))],
-        compiler_params=params(),
-        cost_estimate=cost(0, 16 << 20),
-        name="pack_spans",
+def pack_spans(far, table, keys, values):
+    anywhere = pl.BlockSpec(memory_space=pl.ANY)
+    vmem = pl.BlockSpec(memory_space=pltpu.VMEM)
+    return pl.pallas_call(
+        functools.partial(pack_spans_kernel, far),
+        in_specs=[pl.BlockSpec(memory_space=pltpu.SMEM), vmem, vmem],
+        out_specs=[anywhere] * 3,
+        out_shape=[jax.ShapeDtypeStruct((2, 2, CH, HD), bf16)] * 3,
+        scratch_shapes=[pltpu.SemaphoreType.DMA((3, 2, 2))],
+        compiler_params=params(),
+        cost_estimate=cost(0, 7 << 20),
+        name="pack_far" if far else "pack_near",
     )(table, keys, values)
 
 
 def cross_kernel(far, tab_ref, q_ref, *refs):
-    got = refs[:4]
+    keys_ref, values_ref = refs[:2]
+    got = refs[2:5]
     if far:
-        out_ref, lse_ref, kbuf, vbuf, sems = refs[4:]
+        out_ref, kbuf, vbuf, sems = refs[5:]
     else:
-        part_ref, part_lse_ref, out_ref, kbuf, vbuf, sems = refs[4:]
+        part_ref, out_ref, kbuf, vbuf, sems = refs[5:]
     me = lax.axis_index("db")
     plane, z = me // NZ, me % NZ
     row = (1 - plane) * NZ + z if far else me
     here = []
     for r in range(8):
-        owner = tab_ref[row, r]
+        owner = tab_ref[row, r // 2, r % 2]
         slot = jnp.int32(0)
         for earlier in range(r):
-            slot = slot + jnp.where(tab_ref[row, earlier] == owner, 1, 0)
+            slot = slot + jnp.where(tab_ref[row, earlier // 2, earlier % 2] == owner, 1, 0)
         here.append(jnp.where(owner // NZ == plane, 1, 0))
         shift = (z - owner % NZ + NZ) % NZ
         place = pl.ds((r % 2) * CH, CH)
-        for k in range(4):
+        span = tab_ref[row, r // 2, 2 + r % 2]
+
+        @pl.when(shift == 0)
+        def _(span=span, place=place, r=r):
+            pltpu.make_async_copy(keys_ref.at[span], kbuf.at[r // 2, place], sems.at[r, 0]).start()
+            pltpu.make_async_copy(values_ref.at[span], vbuf.at[r // 2, place], sems.at[r, 1]).start()
+
+        for i, k in enumerate(SHIFTS):
 
             @pl.when(shift == k)
-            def _(k=k, slot=slot, place=place, r=r):
-                pltpu.make_async_copy(got[k].at[slot, 0], kbuf.at[r // 2, place], sems.at[r, 0]).start()
-                pltpu.make_async_copy(got[k].at[slot, 1], vbuf.at[r // 2, place], sems.at[r, 1]).start()
+            def _(i=i, slot=slot, place=place, r=r):
+                pltpu.make_async_copy(got[i].at[slot, 0], kbuf.at[r // 2, place], sems.at[r, 0]).start()
+                pltpu.make_async_copy(got[i].at[slot, 1], vbuf.at[r // 2, place], sems.at[r, 1]).start()
 
     lane = lax.broadcasted_iota(i32, (1, DH), 1)
     for n in range(4):
         for r in (2 * n, 2 * n + 1):
             place = pl.ds((r % 2) * CH, CH)
-            pltpu.make_async_copy(got[0].at[0, 0], kbuf.at[n, place], sems.at[r, 0]).wait()
-            pltpu.make_async_copy(got[0].at[0, 1], vbuf.at[n, place], sems.at[r, 1]).wait()
+            pltpu.make_async_copy(keys_ref.at[0], kbuf.at[n, place], sems.at[r, 0]).wait()
+            pltpu.make_async_copy(values_ref.at[0], vbuf.at[n, place], sems.at[r, 1]).wait()
         mine = jnp.where(lane < CH, here[2 * n], here[2 * n + 1]) > 0
         toks = slice(n * CH, (n + 1) * CH)
         heads = [slice(h * DH, (h + 1) * DH) for h in range(NH)]
@@ -239,28 +248,32 @@
                 safe = jnp.maximum(total[h], 1e-30)
                 out_ref[toks, c] = (o[h] / safe).astype(bf16)
                 lse = jnp.where(total[h] > 0, top[h] + jnp.log2(safe), NEG)
-                stats = jnp.where(lane == h, lse, stats)
-            lse_ref[toks, :] = stats
+                stats = jnp.where(lane % NH == h, lse, stats)
+            high = stats.astype(bf16).astype(f32)
+            low = (stats - high).astype(bf16).astype(f32)
+            rest = stats - high - low
+            stats = jnp.where(lane < NH, high, jnp.where(lane < 2 * NH, low, rest))
+            out_ref[toks, HD:] = stats.astype(bf16)
         else:
+            stats = part_ref[toks, HD:].astype(f32)
+            lse = (stats[:, :NH] + stats[:, NH : 2 * NH]) + stats[:, 2 * NH : 3 * NH]
             for h, c in enumerate(heads):
-                other = part_lse_ref[toks, h : h + 1]
+                other = lse[:, h : h + 1]
                 high = jnp.maximum(top[h], other)
                 a, b = jnp.exp2(top[h] - high), jnp.exp2(other - high)
                 mixed = o[h] * a + part_ref[toks, c].astype(f32) * b
                 out_ref[toks, c] = (mixed / (total[h] * a + b)).astype(bf16)
 
 
-def cross(far, table, q, got, part=()):
+def cross(far, table, q, keys, values, got, part=()):
     vmem = pl.BlockSpec(memory_space=pltpu.VMEM)
-    rows = jax.ShapeDtypeStruct((TOK, HD), bf16)
-    stats = jax.ShapeDtypeStruct((TOK, DH), f32)
     return pl.pallas_call(
         functools.partial(cross_kernel, far),
         in_specs=[pl.BlockSpec(memory_space=pltpu.SMEM), vmem]
-        + [pl.BlockSpec(memory_space=pl.ANY)] * 4
+        + [pl.BlockSpec(memory_space=pl.ANY)] * 5
         + [vmem] * len(part),
-        out_specs=[vmem, vmem] if far else vmem,
-        out_shape=[rows, stats] if far else rows,
+        out_specs=vmem,
+        out_shape=jax.ShapeDtypeStruct((TOK, HD + DH if far else HD), bf16),
         scratch_shapes=[
             pltpu.VMEM((4, 2 * CH, HD), bf16),
             pltpu.VMEM((4, 2 * CH, HD), bf16),
@@ -269,36 +282,36 @@
         compiler_params=params(),
         cost_estimate=cost(4 << 30, 6 << 20),
         name="cross_far" if far else "cross_near",
-    )(table, q, *got, *part)
+    )(table, q, keys, values, *got, *part)
 
 
 def per_device(queries, keys, values, doc_ids, nbr_owner, nbr_local, db_keys, db_values):
-    q = queries[0]
+    q, db_k, db_v = queries[0], db_keys[0], db_values[0]
     swap = [(d, (d + NZ) % 8) for d in range(8)]
     turn = lambda k: [(s * NZ + z, s * NZ + (z + k) % NZ) for s in range(2) for z in range(NZ)]
     far_q = lax.ppermute(q, "db", swap)
 
-    asked = jnp.concatenate([nbr_owner[0].reshape(1, 8), nbr_local[0].reshape(1, 8)], axis=1)
-    table = lax.all_gather(asked, "db", axis=0, tiled=True)
-    packed = pack_spans(table, db_keys[0], db_values[0])
-    near, far = list(packed[:4]), list(packed[4:])
+    asked = jnp.concatenate([nbr_owner, nbr_local], axis=2)
+    mine = lax.broadcasted_iota(i32, (8, 4, 4), 0) == lax.axis_index("db")
+    table = lax.psum(jnp.where(mine, asked, 0), "db")
+    far = pack_spans(True, table, db_k, db_v)
+    far_got = [lax.ppermute(x, "db", turn(k)) for x, k in zip(far, SHIFTS)]
 
     heads = pack_heads(doc_ids, q, keys[0], values[0])
-    heads, far = lax.optimization_barrier((heads, far))
-    far_got = [far[0]] + [lax.ppermute(far[k], "db", turn(k)) for k in (1, 2, 3)]
     heads = lax.all_to_all(heads, "ctx", split_axis=0, concat_axis=0, tiled=True)
 
-    near, far_got = lax.optimization_barrier((near, far_got))
-    near_got = [near[0]] + [lax.ppermute(near[k], "db", turn(k)) for k in (1, 2, 3)]
-    part, lse = cross(True, table, far_q, far_got)
-    part = lax.ppermute(part, "db", swap)
-    lse = lax.ppermute(lse, "db", swap)
+    near = list(pack_spans(False, table, db_k, db_v))
+    near_got = []
+    for i, k in enumerate(SHIFTS):
+        near[i], far_got[i] = lax.optimization_barrier((near[i], far_got[i]))
+        near_got.append(lax.ppermute(near[i], "db", turn(k)))
+    part = lax.ppermute(cross(True, table, far_q, db_k, db_v, far_got), "db", swap)
 
     self_rows = self_attention(heads)
     self_rows = lax.all_to_all(self_rows, "ctx", split_axis=0, concat_axis=0, tiled=True)
     self_rows = unpack_heads(self_rows)
 
-    cross_rows = cross(False, table, q, near_got, (part, lse))
+    cross_rows = cross(False, table, q, db_k, db_v, near_got, (part,))
     return self_rows[None], cross_rows[None]
 
 

time: 364 us -> 192 us (0.53)
  Pallas kernels: 238 us -> 52.7 us
  blocking collectives: 21.5 us -> 64.6 us
  waiting for transfers between devices: 71.8 us -> 37.2 us
  starting transfers between devices: 23 us -> 32.3 us
    pallas_call x1 -> x2, Pallas kernels: 193 us -> 5.55 us  [pack_spans(): pl.pallas_call(functools.partial(pack_spans_kernel, far), in_specs=[pl.Bl...]
    psum x0 -> x1, blocking collectives: none -> 64.6 us  [per_device(): table = lax.psum(jnp.where(mine, asked, 0), 'db')]
    ppermute x8 -> x7, waiting for transfers between devices: 59.4 us -> 35.3 us  [the longest x3 31.3 us: per_device(): far_got = [lax.ppermute(x, 'db', turn(k)) for x, k in zip(far, SHIFTS)]]
    all_gather x1 -> x0, blocking collectives: 21.5 us -> none  [per_device(): table = lax.all_gather(asked, 'db', axis=0, tiled=True)]
    ppermute x1, waiting for transfers between devices: 12.5 us -> 0.01 us  [per_device(): far_q = lax.ppermute(q, 'db', swap)]
    all_to_all x1, starting transfers between devices: 5.51 us -> 13 us  [per_device(): lax.all_to_all(self_rows, 'ctx', split_axis=0, concat_axis=0, tiled=True)]
    ppermute x8 -> x7, starting transfers between devices: 6.84 us -> 10.3 us  [the longest x3 5.81 us: per_device(): near_got.append(lax.ppermute(near[i], 'db', turn(k)))]
  transfers between devices with their start and end apart: 11 -> 10, of which waited for: 4 -> 4; matrix products, arithmetic and copies ran while one was open for 0% -> 0% of each run, Pallas kernels for 11% -> 25%
where the time goes in v2:
time: 192 us
  blocking collectives  64.6 us (34%)
  Pallas kernels  52.7 us (27%)
  waiting for transfers between devices  37.2 us (19%)
  starting transfers between devices  32.3 us (17%)
  local copies, waits for them, and re-layouts  4.45 us (2%)
    psum x1, blocking collectives, per_device(): table = lax.psum(jnp.where(mine, asked, 0), 'db')  64.6 us
    ppermute x3, waiting for transfers between devices, per_device(): far_got = [lax.ppermute(x, 'db', turn(k)) for x, k in zip(far, SHIFTS)]  31.3 us
    pallas_call x1, Pallas kernels, self_attention(): pl.pallas_call(self_kernel, in_specs=[pl.BlockSpec(memory_space=pltpu.VME...  27.6 us
    pallas_call x2, Pallas kernels, cross(): pl.pallas_call(functools.partial(cross_kernel, far), in_specs=[pl.BlockSp...  15.4 us
    all_to_all x1, starting transfers between devices, per_device(): lax.all_to_all(self_rows, 'ctx', split_axis=0, concat_axis=0, tiled=True)  13 us
    all_to_all x1, starting transfers between devices, per_device(): lax.all_to_all(heads, 'ctx', split_axis=0, concat_axis=0, tiled=True)  7.05 us
    ppermute x3, starting transfers between devices, per_device(): near_got.append(lax.ppermute(near[i], 'db', turn(k)))  5.81 us
    pallas_call x2, Pallas kernels, pack_spans(): pl.pallas_call(functools.partial(pack_spans_kernel, far), in_specs=[pl.Bl...  5.55 us
  transfers between devices with their start and end apart: 10, of which 4 were waited for; matrix products, arithmetic and copies ran while one was open for 0% of the time, Pallas kernels for 25%

profile of v2, /device:TPU:1, one launch (start us, length us, event | category | flops | bytes accessed | tf_op | source)
XLA Modules:
  0.0 192.0 jit_solution(1957419016546826398)
XLA Ops:
  0.6 0.0 copy-start.1
  0.6 1.2 copy-done.1
  1.9 0.0 copy-start.3
  1.9 1.2 copy-done.3
  3.1 0.0 copy-start.4
  3.1 1.2 copy-done.4
  4.3 0.0 copy-start.5
  4.3 0.7 copy-done.5
  5.0 2.6 %pack_heads.1 = bf16[16,784,128]{2,1,0:T(8,128)(2,1)} custom-call(s32[1,256]{1,0:T(1,128)S(1)} %copy-done.5, bf16[256,2048]{1,0:T(8,128)(2,1)S(1)} %bitcast.12, bf16[256,2048]{1,0:T(8,128)(2,1)S(1)} %bitcast.15, bf16[256,2048]{1,0:T(8,128)(2,1)S(1)} %bitcast.16), custom_call_target="tpu_custom_call" | custom-call | bytes 393216 | tf_op jit(solution)/shard_map/pack_heads/pallas_call | solution.py:51
  7.6 0.0 copy-start.6
  7.6 0.0 copy-start.7
  7.6 0.0 copy-start
  7.6 7.0 %all-to-all-start = ((bf16[16,784,128]{2,1,0:T(8,128)(2,1)}), bf16[16,784,128]{2,1,0:T(8,128)(2,1)}, u32[]{:S(2)}, u32[]{:S(2)}) async-start(bf16[16,784,128]{2,1,0:T(8,128)(2,1)} %pack_heads.1), calls=%async_computation | async-start | bytes 6422528 | tf_op jit(solution)/shard_map/all_to_all | solution.py:301
  14.6 0.0 copy-done.6
  14.6 0.0 copy-done.7
  14.6 0.1 copy.10
  14.7 0.1 broadcast_select_fusion
  14.8 64.6 %psum.7.tab_ref = s32[8,4,4]{2,1,0:T(4,128)S(1)} all-reduce(s32[8,4,4]{2,1,0:T(4,128)S(1)} %broadcast_select_fusion), channel_id=1, replica_groups=mesh['ctx'=16,'db'=8] {'db'}, use_global_device_ids=true, to_apply=%region_0.1 | all-reduce | flops 128 | bytes 1024 | tf_op jit(solution)/shard_map/psum | solution.py:296
  79.4 0.0 copy-done
  79.4 0.0 copy-start.2
  79.4 2.2 %pack_far.1 = (bf16[2,2,64,2048]{3,2,1,0:T(8,128)(2,1)S(1)}, bf16[2,2,64,2048]{3,2,1,0:T(8,128)(2,1)S(1)}, bf16[2,2,64,2048]{3,2,1,0:T(8,128)(2,1)S(1)}) custom-call(s32[8,4,4]{2,1,0:T(4,128)S(1)} %psum.7.tab_ref, bf16[8,64,2048]{2,1,0:T(8,128)(2,1)S(1)} %bitcast.10, bf16[8,64,2048]{2,1,0:T(8,128)(2,1)} %bitcast.17), custom_call_target="tpu_custom_call" | custom-call | bytes 458752 | tf_op jit(solution)/shard_map/pack_far/pallas_call | solution.py:180
  81.5 0.1 collective-permute-start
  81.6 2.7 %collective-permute-start.2 = (bf16[2,2,64,2048]{3,2,1,0:T(8,128)(2,1)S(1)}, bf16[2,2,64,2048]{3,2,1,0:T(8,128)(2,1)S(1)}, u32[]{:S(2)}, u32[]{:S(2)}) collective-permute-start(bf16[2,2,64,2048]{3,2,1,0:T(8,128)(2,1)S(1)} %get-tuple-element.18), channel_id=1, source_target_pairs={{0,3},{1,0},{2,1},{3,2},{4,7},{5,4},{6,5},{7,6},{8,11},{9,8},{10,9... | collective-permute-start | bytes 3145736 | tf_op jit(solution)/shard_map/ppermute | solution.py:298
  84.3 0.0 collective-permute-start.4
  84.3 0.0 copy-done.2
  84.3 2.0 %collective-permute-start.6 = (bf16[256,2048]{1,0:T(8,128)(2,1)S(1)}, bf16[256,2048]{1,0:T(8,128)(2,1)S(1)}, u32[]{:S(2)}, u32[]{:S(2)}) collective-permute-start(bf16[256,2048]{1,0:T(8,128)(2,1)S(1)} %bitcast.13), channel_id=1, source_target_pairs={{0,4},{1,5},{2,6},{3,7},{4,0},{5,1},{6,2},{7,3},{8,12},{9,13},{10,... | collective-permute-start | bytes 3145736 | tf_op jit(solution)/shard_map/ppermute | solution.py:292
  86.3 3.4 %pack_near.1 = (bf16[2,2,64,2048]{3,2,1,0:T(8,128)(2,1)}, bf16[2,2,64,2048]{3,2,1,0:T(8,128)(2,1)}, bf16[2,2,64,2048]{3,2,1,0:T(8,128)(2,1)}) custom-call(s32[8,4,4]{2,1,0:T(4,128)S(1)} %psum.7.tab_ref, bf16[8,64,2048]{2,1,0:T(8,128)(2,1)S(1)} %bitcast.11, bf16[8,64,2048]{2,1,0:T(8,128)(2,1)} %bitcast.18), custom_call_target="tpu_custom_call" | custom-call | bytes 458752 | tf_op jit(solution)/shard_map/pack_near/pallas_call | solution.py:180
  89.7 13.4 %collective-permute-done.refs_2_ = bf16[2,2,64,2048]{3,2,1,0:T(8,128)(2,1)S(1)} collective-permute-done((bf16[2,2,64,2048]{3,2,1,0:T(8,128)(2,1)S(1)}, bf16[2,2,64,2048]{3,2,1,0:T(8,128)(2,1)S(1)}, u32[]{:S(2)}, u32[]{:S(2)}) %collective-permute-start) | collective-permute-done | bytes 1048608 | tf_op jit(solution)/shard_map/ppermute | solution.py:298
  103.1 0.0 collective-permute-done.2.refs_3_
  103.1 18.0 %collective-permute-done.4.refs_4_ = bf16[2,2,64,2048]{3,2,1,0:T(8,128)(2,1)S(1)} collective-permute-done((bf16[2,2,64,2048]{3,2,1,0:T(8,128)(2,1)S(1)}, bf16[2,2,64,2048]{3,2,1,0:T(8,128)(2,1)S(1)}, u32[]{:S(2)}, u32[]{:S(2)}) %collective-permute-start.4) | collective-permute-done | bytes 1048608 | tf_op jit(solution)/shard_map/ppermute | solution.py:298
  121.0 0.0 collective-permute-done.6.q_ref
  121.0 5.4 %cross_far.1 = bf16[256,2176]{1,0:T(8,128)(2,1)} custom-call(s32[8,4,4]{2,1,0:T(4,128)S(1)} %psum.7.tab_ref, bf16[256,2048]{1,0:T(8,128)(2,1)S(1)} %collective-permute-done.6.q_ref, bf16[8,64,2048]{2,1,0:T(8,128)(2,1)} %bitcast.8, bf16[8,64,2048]{2,1,0:T(8,128)(2,1)} %bitcast.19, bf16[2,2,64,2048]{3,2,1,0:T(8,128)(2,1)S(1)} %collective-permute-done.refs_2_, ...), custom_call_target="tpu_custom_call" | custom-call | flops 67108864 | bytes 393216 | tf_op jit(solution)/shard_map/cross_far/pallas_call | solution.py:270
  126.5 1.7 collective-permute-start.7
  128.2 3.5 %collective-permute-start.5 = (bf16[2,2,64,2048]{3,2,1,0:T(8,128)(2,1)}, bf16[2,2,64,2048]{3,2,1,0:T(8,128)(2,1)S(1)}, u32[]{:S(2)}, u32[]{:S(2)}) collective-permute-start(bf16[2,2,64,2048]{3,2,1,0:T(8,128)(2,1)} %get-tuple-element.22), channel_id=1, source_target_pairs={{0,2},{1,3},{2,0},{3,1},{4,6},{5,7},{6,4},{7,5},{8,10},{9,11},{10,... | collective-permute-start | bytes 3145736 | tf_op jit(solution)/shard_map/ppermute | solution.py:307
  131.7 2.3 %collective-permute-start.3 = (bf16[2,2,64,2048]{3,2,1,0:T(8,128)(2,1)}, bf16[2,2,64,2048]{3,2,1,0:T(8,128)(2,1)}, u32[]{:S(2)}, u32[]{:S(2)}) collective-permute-start(bf16[2,2,64,2048]{3,2,1,0:T(8,128)(2,1)} %get-tuple-element.19), channel_id=1, source_target_pairs={{0,3},{1,0},{2,1},{3,2},{4,7},{5,4},{6,5},{7,6},{8,11},{9,8},{10,9... | collective-permute-start | bytes 3145736 | tf_op jit(solution)/shard_map/ppermute | solution.py:307
  134.0 0.0 collective-permute-start.1
  134.0 0.0 all-to-all-done.x_ref
  134.0 27.6 %self_attention.1 = bf16[16,256,128]{2,1,0:T(8,128)(2,1)} custom-call(bf16[16,784,128]{2,1,0:T(8,128)(2,1)} %all-to-all-done.x_ref), custom_call_target="tpu_custom_call" | custom-call | flops 268435456 | bytes 262144 | tf_op jit(solution)/shard_map/self_attention/pallas_call | solution.py:139
  161.6 13.0 %all-to-all-start.1 = ((bf16[16,256,128]{2,1,0:T(8,128)(2,1)}), bf16[16,256,128]{2,1,0:T(8,128)(2,1)S(1)}, u32[]{:S(2)}, u32[]{:S(2)}) async-start(bf16[16,256,128]{2,1,0:T(8,128)(2,1)} %self_attention.1), calls=%async_computation.1 | async-start | bytes 2097152 | tf_op jit(solution)/shard_map/all_to_all | solution.py:311
  174.6 0.0 collective-permute-done.5.refs_4_
  174.6 3.9 %collective-permute-done.3.refs_3_ = bf16[2,2,64,2048]{3,2,1,0:T(8,128)(2,1)} collective-permute-done((bf16[2,2,64,2048]{3,2,1,0:T(8,128)(2,1)}, bf16[2,2,64,2048]{3,2,1,0:T(8,128)(2,1)}, u32[]{:S(2)}, u32[]{:S(2)}) %collective-permute-start.3) | collective-permute-done | bytes 1048608 | tf_op jit(solution)/shard_map/ppermute | solution.py:307
  178.5 0.0 collective-permute-done.1.refs_2_
  178.5 0.0 collective-permute-done.7.refs_5_
  178.5 10.0 %cross_near.1 = bf16[256,2048]{1,0:T(8,128)(2,1)} custom-call(s32[8,4,4]{2,1,0:T(4,128)S(1)} %psum.7.tab_ref, bf16[256,2048]{1,0:T(8,128)(2,1)S(1)} %bitcast.14, bf16[8,64,2048]{2,1,0:T(8,128)(2,1)} %bitcast.9, bf16[8,64,2048]{2,1,0:T(8,128)(2,1)} %bitcast.20, bf16[2,2,64,2048]{3,2,1,0:T(8,128)(2,1)} %collective-permute-done.1.refs_2_, ...), custom_call_target="tpu_custom_call" | custom-call | flops 67108864 | bytes 393216 | tf_op jit(solution)/shard_map/cross_near/pallas_call | solution.py:270
  188.5 1.9 all-to-all-done.1.x_ref
  190.4 1.6 unpack_heads.1
  (2 shorter events, 0.0 us)
Async XLA Ops:
  0.6 1.2 copy-start.1
  1.9 1.2 copy-start.3
  3.1 1.2 copy-start.4
  4.3 0.7 copy-start.5
  7.6 7.1 %copy-start.6 = (s32[1,4,2]{1,2,0:T(2,128)S(1)}, s32[1,4,2]{1,2,0:T(2,128)}, u32[]{:S(2)}) copy-start(s32[1,4,2]{1,2,0:T(2,128)} %param.13) | copy-start | bytes 100
  7.6 7.1 %copy-start.7 = (s32[1,4,2]{1,2,0:T(2,128)S(1)}, s32[1,4,2]{1,2,0:T(2,128)}, u32[]{:S(2)}) copy-start(s32[1,4,2]{1,2,0:T(2,128)} %param.12) | copy-start | bytes 100
  7.6 71.8 %copy-start = (bf16[1,8,64,2048]{3,2,1,0:T(8,128)(2,1)S(1)}, bf16[1,8,64,2048]{3,2,1,0:T(8,128)(2,1)}, u32[]{:S(2)}) copy-start(bf16[1,8,64,2048]{3,2,1,0:T(8,128)(2,1)} %param.14) | copy-start | bytes 6291460
  7.6 126.5 %all-to-all-start = ((bf16[16,784,128]{2,1,0:T(8,128)(2,1)}), bf16[16,784,128]{2,1,0:T(8,128)(2,1)}, u32[]{:S(2)}, u32[]{:S(2)}) async-start(bf16[16,784,128]{2,1,0:T(8,128)(2,1)} %pack_heads.1), calls=%async_computation | async-start | bytes 6422528 | tf_op jit(solution)/shard_map/all_to_all | solution.py:301
  79.4 4.9 %copy-start.2 = (bf16[1,256,2048]{2,1,0:T(8,128)(2,1)S(1)}, bf16[1,256,2048]{2,1,0:T(8,128)(2,1)}, u32[]{:S(2)}) copy-start(bf16[1,256,2048]{2,1,0:T(8,128)(2,1)} %param.8) | copy-start | bytes 3145732
  81.5 21.5 %collective-permute-start = (bf16[2,2,64,2048]{3,2,1,0:T(8,128)(2,1)S(1)}, bf16[2,2,64,2048]{3,2,1,0:T(8,128)(2,1)S(1)}, u32[]{:S(2)}, u32[]{:S(2)}) collective-permute-start(bf16[2,2,64,2048]{3,2,1,0:T(8,128)(2,1)S(1)} %get-tuple-element.15), channel_id=1, source_target_pairs={{0,1},{1,2},{2,3},{3,0},{4,5},{5,6},{6,7},{7,4},{8,9},{9,10},{10,1... | collective-permute-start | bytes 3145736 | tf_op jit(solution)/shard_map/ppermute | solution.py:298
  81.6 21.4 %collective-permute-start.2 = (bf16[2,2,64,2048]{3,2,1,0:T(8,128)(2,1)S(1)}, bf16[2,2,64,2048]{3,2,1,0:T(8,128)(2,1)S(1)}, u32[]{:S(2)}, u32[]{:S(2)}) collective-permute-start(bf16[2,2,64,2048]{3,2,1,0:T(8,128)(2,1)S(1)} %get-tuple-element.18), channel_id=1, source_target_pairs={{0,3},{1,0},{2,1},{3,2},{4,7},{5,4},{6,5},{7,6},{8,11},{9,8},{10,9... | collective-permute-start | bytes 3145736 | tf_op jit(solution)/shard_map/ppermute | solution.py:298
  84.3 36.7 %collective-permute-start.4 = (bf16[2,2,64,2048]{3,2,1,0:T(8,128)(2,1)S(1)}, bf16[2,2,64,2048]{3,2,1,0:T(8,128)(2,1)S(1)}, u32[]{:S(2)}, u32[]{:S(2)}) collective-permute-start(bf16[2,2,64,2048]{3,2,1,0:T(8,128)(2,1)S(1)} %get-tuple-element.21), channel_id=1, source_target_pairs={{0,2},{1,3},{2,0},{3,1},{4,6},{5,7},{6,4},{7,5},{8,10},{9,11},{10,... | collective-permute-start | bytes 3145736 | tf_op jit(solution)/shard_map/ppermute | solution.py:298
  84.3 36.7 %collective-permute-start.6 = (bf16[256,2048]{1,0:T(8,128)(2,1)S(1)}, bf16[256,2048]{1,0:T(8,128)(2,1)S(1)}, u32[]{:S(2)}, u32[]{:S(2)}) collective-permute-start(bf16[256,2048]{1,0:T(8,128)(2,1)S(1)} %bitcast.13), channel_id=1, source_target_pairs={{0,4},{1,5},{2,6},{3,7},{4,0},{5,1},{6,2},{7,3},{8,12},{9,13},{10,... | collective-permute-start | bytes 3145736 | tf_op jit(solution)/shard_map/ppermute | solution.py:292
  126.5 52.0 %collective-permute-start.7 = (bf16[256,2176]{1,0:T(8,128)(2,1)}, bf16[256,2176]{1,0:T(8,128)(2,1)}, u32[]{:S(2)}, u32[]{:S(2)}) collective-permute-start(bf16[256,2176]{1,0:T(8,128)(2,1)} %cross_far.1), channel_id=1, source_target_pairs={{0,4},{1,5},{2,6},{3,7},{4,0},{5,1},{6,2},{7,3},{8,12},{9,13},{10,... | collective-permute-start | bytes 3342344 | tf_op jit(solution)/shard_map/ppermute | solution.py:308
  128.2 46.4 %collective-permute-start.5 = (bf16[2,2,64,2048]{3,2,1,0:T(8,128)(2,1)}, bf16[2,2,64,2048]{3,2,1,0:T(8,128)(2,1)S(1)}, u32[]{:S(2)}, u32[]{:S(2)}) collective-permute-start(bf16[2,2,64,2048]{3,2,1,0:T(8,128)(2,1)} %get-tuple-element.22), channel_id=1, source_target_pairs={{0,2},{1,3},{2,0},{3,1},{4,6},{5,7},{6,4},{7,5},{8,10},{9,11},{10,... | collective-permute-start | bytes 3145736 | tf_op jit(solution)/shard_map/ppermute | solution.py:307
  131.7 46.8 %collective-permute-start.3 = (bf16[2,2,64,2048]{3,2,1,0:T(8,128)(2,1)}, bf16[2,2,64,2048]{3,2,1,0:T(8,128)(2,1)}, u32[]{:S(2)}, u32[]{:S(2)}) collective-permute-start(bf16[2,2,64,2048]{3,2,1,0:T(8,128)(2,1)} %get-tuple-element.19), channel_id=1, source_target_pairs={{0,3},{1,0},{2,1},{3,2},{4,7},{5,4},{6,5},{7,6},{8,11},{9,8},{10,9... | collective-permute-start | bytes 3145736 | tf_op jit(solution)/shard_map/ppermute | solution.py:307
  134.0 44.5 %collective-permute-start.1 = (bf16[2,2,64,2048]{3,2,1,0:T(8,128)(2,1)}, bf16[2,2,64,2048]{3,2,1,0:T(8,128)(2,1)}, u32[]{:S(2)}, u32[]{:S(2)}) collective-permute-start(bf16[2,2,64,2048]{3,2,1,0:T(8,128)(2,1)} %get-tuple-element.16), channel_id=1, source_target_pairs={{0,1},{1,2},{2,3},{3,0},{4,5},{5,6},{6,7},{7,4},{8,9},{9,10},{10,1... | collective-permute-start | bytes 3145736 | tf_op jit(solution)/shard_map/ppermute | solution.py:307
  161.6 28.8 %all-to-all-start.1 = ((bf16[16,256,128]{2,1,0:T(8,128)(2,1)}), bf16[16,256,128]{2,1,0:T(8,128)(2,1)S(1)}, u32[]{:S(2)}, u32[]{:S(2)}) async-start(bf16[16,256,128]{2,1,0:T(8,128)(2,1)} %self_attention.1), calls=%async_computation.1 | async-start | bytes 2097152 | tf_op jit(solution)/shard_map/all_to_all | solution.py:311

commit v3 on v2

--- a/solution.py
+++ b/solution.py
@@ -32,7 +32,7 @@
     return pl.CostEstimate(flops=flops // 64, bytes_accessed=nbytes // 16, transcendentals=0)
 
 
-def pack_heads_kernel(docs_ref, q_ref, k_ref, v_ref, out_ref):
+def pack_heads_kernel(token_ref, docs_ref, q_ref, k_ref, v_ref, out_ref):
     row = lax.broadcasted_iota(i32, (16, DH), 0)
     docs = docs_ref[...]
     left = jnp.broadcast_to(docs[:, :DH], (16, DH))
@@ -46,18 +46,24 @@
         out_ref[h, 3 * TOK : CHUNK, :] = packed
 
 
-def pack_heads(docs, q, k, v):
+def pack_heads(token, docs, q, k, v):
     wide = pl.BlockSpec((TOK, 4 * DH), lambda i: (0, i))
     return pl.pallas_call(
         pack_heads_kernel,
         grid=(4,),
-        in_specs=[pl.BlockSpec((1, TOK), lambda i: (0, 0)), wide, wide, wide],
+        in_specs=[
+            pl.BlockSpec((8, DH), lambda i: (0, 0)),
+            pl.BlockSpec((1, TOK), lambda i: (0, 0)),
+            wide,
+            wide,
+            wide,
+        ],
         out_specs=pl.BlockSpec((4, CHUNK, DH), lambda i: (i, 0, 0)),
         out_shape=jax.ShapeDtypeStruct((NC, CHUNK, DH), bf16),
         compiler_params=params(),
         cost_estimate=cost(0, 6 << 20),
         name="pack_heads",
-    )(docs, q, k, v)
+    )(token, docs, q, k, v)
 
 
 def unpack_heads_kernel(x_ref, out_ref):
@@ -151,7 +157,8 @@
 
 
 def pack_spans_kernel(far, tab_ref, keys_ref, values_ref, *refs):
-    outs, sems = refs[:3], refs[3]
+    outs, token_ref, sems = refs[:3], refs[3], refs[4]
+    token_ref[...] = jnp.zeros_like(token_ref)
     me = lax.axis_index("db")
     plane, z = me // NZ, me % NZ
     side = 1 - plane if far else plane
@@ -180,8 +187,8 @@
     return pl.pallas_call(
         functools.partial(pack_spans_kernel, far),
         in_specs=[pl.BlockSpec(memory_space=pltpu.SMEM), vmem, vmem],
-        out_specs=[anywhere] * 3,
-        out_shape=[jax.ShapeDtypeStruct((2, 2, CH, HD), bf16)] * 3,
+        out_specs=[anywhere] * 3 + [vmem],
+        out_shape=[jax.ShapeDtypeStruct((2, 2, CH, HD), bf16)] * 3 + [jax.ShapeDtypeStruct((8, DH), i32)],
         scratch_shapes=[pltpu.SemaphoreType.DMA((3, 2, 2))],
         compiler_params=params(),
         cost_estimate=cost(0, 7 << 20),
@@ -285,6 +292,24 @@
     )(table, q, keys, values, *got, *part)
 
 
+def arrived_kernel(*refs):
+    pass
+
+
+def arrived(xs):
+    anywhere = pl.BlockSpec(memory_space=pl.ANY)
+    return pl.pallas_call(
+        arrived_kernel,
+        in_specs=[anywhere] * len(xs),
+        out_specs=[anywhere] * len(xs),
+        out_shape=[jax.ShapeDtypeStruct(x.shape, x.dtype) for x in xs],
+        input_output_aliases={i: i for i in range(len(xs))},
+        compiler_params=params(),
+        cost_estimate=pl.CostEstimate(flops=32 << 30, bytes_accessed=0, transcendentals=0),
+        name="arrived",
+    )(*xs)
+
+
 def per_device(queries, keys, values, doc_ids, nbr_owner, nbr_local, db_keys, db_values):
     q, db_k, db_v = queries[0], db_keys[0], db_values[0]
     swap = [(d, (d + NZ) % 8) for d in range(8)]
@@ -294,13 +319,13 @@
     asked = jnp.concatenate([nbr_owner, nbr_local], axis=2)
     mine = lax.broadcasted_iota(i32, (8, 4, 4), 0) == lax.axis_index("db")
     table = lax.psum(jnp.where(mine, asked, 0), "db")
-    far = pack_spans(True, table, db_k, db_v)
+    *far, token = pack_spans(True, table, db_k, db_v)
     far_got = [lax.ppermute(x, "db", turn(k)) for x, k in zip(far, SHIFTS)]
 
-    heads = pack_heads(doc_ids, q, keys[0], values[0])
+    heads = pack_heads(token, doc_ids, q, keys[0], values[0])
     heads = lax.all_to_all(heads, "ctx", split_axis=0, concat_axis=0, tiled=True)
 
-    near = list(pack_spans(False, table, db_k, db_v))
+    near = list(pack_spans(False, table, db_k, db_v)[:3])
     near_got = []
     for i, k in enumerate(SHIFTS):
         near[i], far_got[i] = lax.optimization_barrier((near[i], far_got[i]))
@@ -311,6 +336,7 @@
     self_rows = lax.all_to_all(self_rows, "ctx", split_axis=0, concat_axis=0, tiled=True)
     self_rows = unpack_heads(self_rows)
 
+    near_got = arrived(near_got)
     cross_rows = cross(False, table, q, db_k, db_v, near_got, (part,))
     return self_rows[None], cross_rows[None]
 

time: 192 us -> 176 us (0.917); the launches traced: 192 us -> 174 us
  blocking collectives: 64.6 us -> 36.7 us
  waiting for transfers between devices: 37.2 us -> 55.8 us
  starting transfers between devices: 32.3 us -> 26.3 us
  Pallas kernels: 52.7 us -> 48.8 us
    psum x1, blocking collectives: 64.6 us -> 36.7 us  [per_device(): table = lax.psum(jnp.where(mine, asked, 0), 'db')]
    ppermute x1, waiting for transfers between devices: 0.01 us -> 9.83 us  [per_device(): far_q = lax.ppermute(q, 'db', swap)]
    ppermute x3, waiting for transfers between devices: 31.3 us -> 40.1 us  [per_device(): far_got = [lax.ppermute(x, 'db', turn(k)) for x, k in zip(far, SHIFTS)]]
    all_to_all x1, starting transfers between devices: 13 us -> 4.96 us  [per_device(): lax.all_to_all(self_rows, 'ctx', split_axis=0, concat_axis=0, tiled=True)]
    all_to_all x1, starting transfers between devices: 7.05 us -> 12.5 us  [per_device(): lax.all_to_all(heads, 'ctx', split_axis=0, concat_axis=0, tiled=True)]
    pallas_call x1, Pallas kernels: 27.6 us -> 22.6 us  [self_attention(): pl.pallas_call(self_kernel, in_specs=[pl.BlockSpec(memory_space=pltpu.VME...]
    ppermute x3, starting transfers between devices: 5.81 us -> 2.97 us  [per_device(): near_got.append(lax.ppermute(near[i], 'db', turn(k)))]
    all_to_all x1, waiting for transfers between devices: 1.9 us -> 4.41 us  [per_device(): lax.all_to_all(self_rows, 'ctx', split_axis=0, concat_axis=0, tiled=True)]
  transfers between devices with their start and end apart: 10 -> 10, of which waited for: 4 -> 5; matrix products, arithmetic and copies ran while one was open for 0% -> 0% of each run, Pallas kernels for 25% -> 24%
where the time goes in v3:
time: 176 us; the launch traced here: 174 us
  waiting for transfers between devices  55.8 us (32%)
  Pallas kernels  48.8 us (28%)
  blocking collectives  36.7 us (21%)
  starting transfers between devices  26.3 us (15%)
  local copies, waits for them, and re-layouts  4.7 us (3%)
    ppermute x3, waiting for transfers between devices, per_device(): far_got = [lax.ppermute(x, 'db', turn(k)) for x, k in zip(far, SHIFTS)]  40.1 us
    psum x1, blocking collectives, per_device(): table = lax.psum(jnp.where(mine, asked, 0), 'db')  36.7 us
    pallas_call x1, Pallas kernels, self_attention(): pl.pallas_call(self_kernel, in_specs=[pl.BlockSpec(memory_space=pltpu.VME...  22.6 us
    pallas_call x2, Pallas kernels, cross(): pl.pallas_call(functools.partial(cross_kernel, far), in_specs=[pl.BlockSp...  15.8 us
    all_to_all x1, starting transfers between devices, per_device(): lax.all_to_all(heads, 'ctx', split_axis=0, concat_axis=0, tiled=True)  12.5 us
    ppermute x1, waiting for transfers between devices, per_device(): far_q = lax.ppermute(q, 'db', swap)  9.83 us
    pallas_call x2, Pallas kernels, pack_spans(): pl.pallas_call(functools.partial(pack_spans_kernel, far), in_specs=[pl.Bl...  6.21 us
    all_to_all x1, starting transfers between devices, per_device(): lax.all_to_all(self_rows, 'ctx', split_axis=0, concat_axis=0, tiled=True)  4.96 us
  transfers between devices with their start and end apart: 10, of which 5 were waited for; matrix products, arithmetic and copies ran while one was open for 0% of the time, Pallas kernels for 24%

profile of v3, /device:TPU:1, one launch (start us, length us, event | category | flops | bytes accessed | tf_op | source)
XLA Modules:
  0.0 173.9 jit_solution(9599739720444987859)
XLA Ops:
  0.6 0.7 pad_add_fusion
  1.4 0.1 copy.13
  1.4 0.1 broadcast_select_fusion
  1.5 36.7 %psum.7.tab_ref = s32[8,4,4]{2,1,0:T(4,128)S(1)} all-reduce(s32[8,4,4]{2,1,0:T(4,128)S(1)} %broadcast_select_fusion), channel_id=1, replica_groups=mesh['ctx'=16,'db'=8] {'db'}, use_global_device_ids=true, to_apply=%region_0.1 | all-reduce | flops 128 | bytes 1024 | tf_op jit(solution)/shard_map/psum | solution.py:321
  38.2 0.0 copy-start
  38.2 1.6 copy-done
  39.8 0.0 copy-start.3
  39.8 0.0 copy-start.4
  39.8 0.0 copy-start.5
  39.8 2.2 %pack_far.1 = (bf16[2,2,64,2048]{3,2,1,0:T(8,128)(2,1)S(1)}, bf16[2,2,64,2048]{3,2,1,0:T(8,128)(2,1)S(1)}, bf16[2,2,64,2048]{3,2,1,0:T(8,128)(2,1)S(1)}, s32[8,128]{1,0:T(8,128)S(1)}) custom-call(s32[8,4,4]{2,1,0:T(4,128)S(1)} %psum.7.tab_ref, bf16[8,64,2048]{2,1,0:T(8,128)(2,1)S(1)} %bitcast.10, bf16[8,64,2048]{2,1,0:T(8,128)(2,1)} %bitcast.17), custom_call_target="tpu_custom_call" | custom-call | bytes 458752 | tf_op jit(solution)/shard_map/pack_far/pallas_call | solution.py:187
  42.0 0.0 copy-start.6
  42.0 0.9 copy-done.6
  43.0 0.0 copy-start.7
  43.0 1.1 copy-done.7
  44.1 0.0 copy-start.8
  44.1 1.0 copy-done.8
  45.0 0.0 copy-done.2
  45.0 0.0 copy-done.3
  45.0 0.0 copy-done.4
  45.0 0.0 copy-done.5
  45.0 2.6 %pack_heads.1 = bf16[16,784,128]{2,1,0:T(8,128)(2,1)} custom-call(s32[8,128]{1,0:T(8,128)S(1)} %get-tuple-element.18.token_ref, s32[1,256]{1,0:T(1,128)S(1)} %copy-done.5, bf16[256,2048]{1,0:T(8,128)(2,1)S(1)} %bitcast.12, bf16[256,2048]{1,0:T(8,128)(2,1)S(1)} %bitcast.15, bf16[256,2048]{1,0:T(8,128)(2,1)S(1)} %bitcast.16), custom_call_target="tpu_custom_call" | custom-call | bytes 393216 | tf_op jit(solution)/shard_map/pack_heads/pallas_call | solution.py:51
  47.6 0.0 copy-start.1
  47.6 12.5 %all-to-all-start = ((bf16[16,784,128]{2,1,0:T(8,128)(2,1)}), bf16[16,784,128]{2,1,0:T(8,128)(2,1)}, u32[]{:S(2)}, u32[]{:S(2)}) async-start(bf16[16,784,128]{2,1,0:T(8,128)(2,1)} %pack_heads.1), calls=%async_computation | async-start | bytes 6422528 | tf_op jit(solution)/shard_map/all_to_all | solution.py:326
  60.2 0.0 collective-permute-start
  60.2 2.7 %collective-permute-start.2 = (bf16[2,2,64,2048]{3,2,1,0:T(8,128)(2,1)}, bf16[2,2,64,2048]{3,2,1,0:T(8,128)(2,1)S(1)}, u32[]{:S(2)}, u32[]{:S(2)}) collective-permute-start(bf16[2,2,64,2048]{3,2,1,0:T(8,128)(2,1)} %copy-done.7), channel_id=1, source_target_pairs={{0,3},{1,0},{2,1},{3,2},{4,7},{5,4},{6,5},{7,6},{8,11},{9,8},{10,9... | collective-permute-start | bytes 3145736 | tf_op jit(solution)/shard_map/ppermute | solution.py:323
  62.8 0.0 collective-permute-start.4
  62.8 1.7 collective-permute-start.6
  64.5 0.0 copy-done.1
  64.5 4.0 %pack_near.1 = (bf16[2,2,64,2048]{3,2,1,0:T(8,128)(2,1)}, bf16[2,2,64,2048]{3,2,1,0:T(8,128)(2,1)}, bf16[2,2,64,2048]{3,2,1,0:T(8,128)(2,1)}, s32[8,128]{1,0:T(8,128)}) custom-call(s32[8,4,4]{2,1,0:T(4,128)S(1)} %psum.7.tab_ref, bf16[8,64,2048]{2,1,0:T(8,128)(2,1)S(1)} %bitcast.11, bf16[8,64,2048]{2,1,0:T(8,128)(2,1)} %bitcast.18), custom_call_target="tpu_custom_call" | custom-call | bytes 458752 | tf_op jit(solution)/shard_map/pack_near/pallas_call | solution.py:187
  68.5 40.1 %collective-permute-done.refs_2_ = bf16[2,2,64,2048]{3,2,1,0:T(8,128)(2,1)S(1)} collective-permute-done((bf16[2,2,64,2048]{3,2,1,0:T(8,128)(2,1)}, bf16[2,2,64,2048]{3,2,1,0:T(8,128)(2,1)S(1)}, u32[]{:S(2)}, u32[]{:S(2)}) %collective-permute-start) | collective-permute-done | bytes 1048608 | tf_op jit(solution)/shard_map/ppermute | solution.py:323
  108.6 0.0 collective-permute-done.2.refs_3_
  108.6 0.0 collective-permute-done.4.refs_4_
  108.6 0.6 collective-permute-start.5
  109.2 2.4 %collective-permute-start.3 = (bf16[2,2,64,2048]{3,2,1,0:T(8,128)(2,1)}, bf16[2,2,64,2048]{3,2,1,0:T(8,128)(2,1)}, u32[]{:S(2)}, u32[]{:S(2)}) collective-permute-start(bf16[2,2,64,2048]{3,2,1,0:T(8,128)(2,1)} %get-tuple-element.24), channel_id=1, source_target_pairs={{0,3},{1,0},{2,1},{3,2},{4,7},{5,4},{6,5},{7,6},{8,11},{9,8},{10,9... | collective-permute-start | bytes 3145736 | tf_op jit(solution)/shard_map/ppermute | solution.py:332
  111.6 0.0 collective-permute-start.1
  111.6 9.8 %collective-permute-done.6.q_ref = bf16[256,2048]{1,0:T(8,128)(2,1)S(1)} collective-permute-done((bf16[256,2048]{1,0:T(8,128)(2,1)S(1)}, bf16[256,2048]{1,0:T(8,128)(2,1)S(1)}, u32[]{:S(2)}, u32[]{:S(2)}) %collective-permute-start.6) | collective-permute-done | bytes 1048608 | tf_op jit(solution)/shard_map/ppermute | solution.py:317
  121.4 5.9 %cross_far.1 = bf16[256,2176]{1,0:T(8,128)(2,1)} custom-call(s32[8,4,4]{2,1,0:T(4,128)S(1)} %psum.7.tab_ref, bf16[256,2048]{1,0:T(8,128)(2,1)S(1)} %collective-permute-done.6.q_ref, bf16[8,64,2048]{2,1,0:T(8,128)(2,1)} %bitcast.8, bf16[8,64,2048]{2,1,0:T(8,128)(2,1)} %bitcast.19, bf16[2,2,64,2048]{3,2,1,0:T(8,128)(2,1)S(1)} %collective-permute-done.refs_2_, ...), custom_call_target="tpu_custom_call" | custom-call | flops 67108864 | bytes 393216 | tf_op jit(solution)/shard_map/cross_far/pallas_call | solution.py:277
  127.3 1.5 collective-permute-start.7
  128.9 0.0 all-to-all-done.x_ref
  128.9 22.6 %self_attention.1 = bf16[16,256,128]{2,1,0:T(8,128)(2,1)} custom-call(bf16[16,784,128]{2,1,0:T(8,128)(2,1)} %all-to-all-done.x_ref), custom_call_target="tpu_custom_call" | custom-call | flops 268435456 | bytes 262144 | tf_op jit(solution)/shard_map/self_attention/pallas_call | solution.py:145
  151.5 5.0 %all-to-all-start.1 = ((bf16[16,256,128]{2,1,0:T(8,128)(2,1)}), bf16[16,256,128]{2,1,0:T(8,128)(2,1)S(1)}, u32[]{:S(2)}, u32[]{:S(2)}) async-start(bf16[16,256,128]{2,1,0:T(8,128)(2,1)} %self_attention.1), calls=%async_computation.1 | async-start | bytes 2097152 | tf_op jit(solution)/shard_map/all_to_all | solution.py:336
  156.5 0.0 collective-permute-done.5.refs_2_
  156.5 0.5 collective-permute-done.3.refs_1_
  156.9 1.1 collective-permute-done.1.refs_0_
  158.0 0.0 collective-permute-done.7.refs_5_
  158.0 9.9 %cross_near.1 = bf16[256,2048]{1,0:T(8,128)(2,1)} custom-call(s32[8,4,4]{2,1,0:T(4,128)S(1)} %psum.7.tab_ref, bf16[256,2048]{1,0:T(8,128)(2,1)S(1)} %bitcast.14, bf16[8,64,2048]{2,1,0:T(8,128)(2,1)} %bitcast.9, bf16[8,64,2048]{2,1,0:T(8,128)(2,1)} %bitcast.20, bf16[2,2,64,2048]{3,2,1,0:T(8,128)(2,1)} %get-tuple-element.28.refs_2_, ...), custom_call_target="tpu_custom_call" | custom-call | flops 67108864 | bytes 393216 | tf_op jit(solution)/shard_map/cross_near/pallas_call | solution.py:277
  167.9 4.4 %all-to-all-done.1.x_ref = bf16[16,256,128]{2,1,0:T(8,128)(2,1)S(1)} async-done(((bf16[16,256,128]{2,1,0:T(8,128)(2,1)}), bf16[16,256,128]{2,1,0:T(8,128)(2,1)S(1)}, u32[]{:S(2)}, u32[]{:S(2)}) %all-to-all-start.1) | async-done | bytes 1048608 | tf_op jit(solution)/shard_map/all_to_all | solution.py:336
  172.3 1.6 unpack_heads.1
  (3 shorter events, 0.0 us)
Async XLA Ops:
  38.2 1.6 copy-start
  39.8 5.3 %copy-start.2 = (bf16[1,256,2048]{2,1,0:T(8,128)(2,1)S(1)}, bf16[1,256,2048]{2,1,0:T(8,128)(2,1)}, u32[]{:S(2)}) copy-start(bf16[1,256,2048]{2,1,0:T(8,128)(2,1)} %param.8) | copy-start | bytes 3145732
  39.8 5.3 %copy-start.3 = (bf16[1,256,2048]{2,1,0:T(8,128)(2,1)S(1)}, bf16[1,256,2048]{2,1,0:T(8,128)(2,1)}, u32[]{:S(2)}) copy-start(bf16[1,256,2048]{2,1,0:T(8,128)(2,1)} %param.9) | copy-start | bytes 3145732
  39.8 5.3 %copy-start.4 = (bf16[1,256,2048]{2,1,0:T(8,128)(2,1)S(1)}, bf16[1,256,2048]{2,1,0:T(8,128)(2,1)}, u32[]{:S(2)}) copy-start(bf16[1,256,2048]{2,1,0:T(8,128)(2,1)} %param.10) | copy-start | bytes 3145732
  39.8 5.3 %copy-start.5 = (s32[1,256]{1,0:T(1,128)S(1)}, s32[1,256]{1,0:T(1,128)}, u32[]{:S(2)}) copy-start(s32[1,256]{1,0:T(1,128)} %docs_ref.1) | copy-start | bytes 3076
  42.0 1.0 copy-start.6
  43.0 1.1 copy-start.7
  44.1 1.0 copy-start.8
  47.6 16.9 %copy-start.1 = (bf16[1,8,64,2048]{3,2,1,0:T(8,128)(2,1)S(1)}, bf16[1,8,64,2048]{3,2,1,0:T(8,128)(2,1)}, u32[]{:S(2)}) copy-start(bf16[1,8,64,2048]{3,2,1,0:T(8,128)(2,1)} %param.14) | copy-start | bytes 6291460
  47.6 81.2 %all-to-all-start = ((bf16[16,784,128]{2,1,0:T(8,128)(2,1)}), bf16[16,784,128]{2,1,0:T(8,128)(2,1)}, u32[]{:S(2)}, u32[]{:S(2)}) async-start(bf16[16,784,128]{2,1,0:T(8,128)(2,1)} %pack_heads.1), calls=%async_computation | async-start | bytes 6422528 | tf_op jit(solution)/shard_map/all_to_all | solution.py:326
  60.2 48.4 %collective-permute-start = (bf16[2,2,64,2048]{3,2,1,0:T(8,128)(2,1)}, bf16[2,2,64,2048]{3,2,1,0:T(8,128)(2,1)S(1)}, u32[]{:S(2)}, u32[]{:S(2)}) collective-permute-start(bf16[2,2,64,2048]{3,2,1,0:T(8,128)(2,1)} %copy-done.8), channel_id=1, source_target_pairs={{0,1},{1,2},{2,3},{3,0},{4,5},{5,6},{6,7},{7,4},{8,9},{9,10},{10,1... | collective-permute-start | bytes 3145736 | tf_op jit(solution)/shard_map/ppermute | solution.py:323
  60.2 48.4 %collective-permute-start.2 = (bf16[2,2,64,2048]{3,2,1,0:T(8,128)(2,1)}, bf16[2,2,64,2048]{3,2,1,0:T(8,128)(2,1)S(1)}, u32[]{:S(2)}, u32[]{:S(2)}) collective-permute-start(bf16[2,2,64,2048]{3,2,1,0:T(8,128)(2,1)} %copy-done.7), channel_id=1, source_target_pairs={{0,3},{1,0},{2,1},{3,2},{4,7},{5,4},{6,5},{7,6},{8,11},{9,8},{10,9... | collective-permute-start | bytes 3145736 | tf_op jit(solution)/shard_map/ppermute | solution.py:323
  62.8 45.8 %collective-permute-start.4 = (bf16[2,2,64,2048]{3,2,1,0:T(8,128)(2,1)}, bf16[2,2,64,2048]{3,2,1,0:T(8,128)(2,1)S(1)}, u32[]{:S(2)}, u32[]{:S(2)}) collective-permute-start(bf16[2,2,64,2048]{3,2,1,0:T(8,128)(2,1)} %copy-done.6), channel_id=1, source_target_pairs={{0,2},{1,3},{2,0},{3,1},{4,6},{5,7},{6,4},{7,5},{8,10},{9,11},{10,... | collective-permute-start | bytes 3145736 | tf_op jit(solution)/shard_map/ppermute | solution.py:323
  62.8 58.6 %collective-permute-start.6 = (bf16[256,2048]{1,0:T(8,128)(2,1)S(1)}, bf16[256,2048]{1,0:T(8,128)(2,1)S(1)}, u32[]{:S(2)}, u32[]{:S(2)}) collective-permute-start(bf16[256,2048]{1,0:T(8,128)(2,1)S(1)} %bitcast.13), channel_id=1, source_target_pairs={{0,4},{1,5},{2,6},{3,7},{4,0},{5,1},{6,2},{7,3},{8,12},{9,13},{10,... | collective-permute-start | bytes 3145736 | tf_op jit(solution)/shard_map/ppermute | solution.py:317
  108.6 47.9 %collective-permute-start.5 = (bf16[2,2,64,2048]{3,2,1,0:T(8,128)(2,1)}, bf16[2,2,64,2048]{3,2,1,0:T(8,128)(2,1)S(1)}, u32[]{:S(2)}, u32[]{:S(2)}) collective-permute-start(bf16[2,2,64,2048]{3,2,1,0:T(8,128)(2,1)} %get-tuple-element.27), channel_id=1, source_target_pairs={{0,2},{1,3},{2,0},{3,1},{4,6},{5,7},{6,4},{7,5},{8,10},{9,11},{10,... | collective-permute-start | bytes 3145736 | tf_op jit(solution)/shard_map/ppermute | solution.py:332
  109.2 47.7 %collective-permute-start.3 = (bf16[2,2,64,2048]{3,2,1,0:T(8,128)(2,1)}, bf16[2,2,64,2048]{3,2,1,0:T(8,128)(2,1)}, u32[]{:S(2)}, u32[]{:S(2)}) collective-permute-start(bf16[2,2,64,2048]{3,2,1,0:T(8,128)(2,1)} %get-tuple-element.24), channel_id=1, source_target_pairs={{0,3},{1,0},{2,1},{3,2},{4,7},{5,4},{6,5},{7,6},{8,11},{9,8},{10,9... | collective-permute-start | bytes 3145736 | tf_op jit(solution)/shard_map/ppermute | solution.py:332
  111.6 46.4 %collective-permute-start.1 = (bf16[2,2,64,2048]{3,2,1,0:T(8,128)(2,1)}, bf16[2,2,64,2048]{3,2,1,0:T(8,128)(2,1)}, u32[]{:S(2)}, u32[]{:S(2)}) collective-permute-start(bf16[2,2,64,2048]{3,2,1,0:T(8,128)(2,1)} %get-tuple-element.21), channel_id=1, source_target_pairs={{0,1},{1,2},{2,3},{3,0},{4,5},{5,6},{6,7},{7,4},{8,9},{9,10},{10,1... | collective-permute-start | bytes 3145736 | tf_op jit(solution)/shard_map/ppermute | solution.py:332
  127.3 30.6 %collective-permute-start.7 = (bf16[256,2176]{1,0:T(8,128)(2,1)}, bf16[256,2176]{1,0:T(8,128)(2,1)}, u32[]{:S(2)}, u32[]{:S(2)}) collective-permute-start(bf16[256,2176]{1,0:T(8,128)(2,1)} %cross_far.1), channel_id=1, source_target_pairs={{0,4},{1,5},{2,6},{3,7},{4,0},{5,1},{6,2},{7,3},{8,12},{9,13},{10,... | collective-permute-start | bytes 3342344 | tf_op jit(solution)/shard_map/ppermute | solution.py:333
  151.5 20.8 %all-to-all-start.1 = ((bf16[16,256,128]{2,1,0:T(8,128)(2,1)}), bf16[16,256,128]{2,1,0:T(8,128)(2,1)S(1)}, u32[]{:S(2)}, u32[]{:S(2)}) async-start(bf16[16,256,128]{2,1,0:T(8,128)(2,1)} %self_attention.1), calls=%async_computation.1 | async-start | bytes 2097152 | tf_op jit(solution)/shard_map/all_to_all | solution.py:336

commit v4 on v3

--- a/solution.py
+++ b/solution.py
@@ -156,19 +156,17 @@
 SHIFTS = (1, 3, 2)
 
 
-def pack_spans_kernel(far, tab_ref, keys_ref, values_ref, *refs):
-    outs, token_ref, sems = refs[:3], refs[3], refs[4]
+def pack_spans_kernel(far, *refs):
+    tabs, keys_ref, values_ref = refs[:3], refs[3], refs[4]
+    outs, token_ref, sems = refs[5:8], refs[8], refs[9]
     token_ref[...] = jnp.zeros_like(token_ref)
     me = lax.axis_index("db")
-    plane, z = me // NZ, me % NZ
-    side = 1 - plane if far else plane
     copies = []
-    for i, k in enumerate(SHIFTS):
-        asker = side * NZ + (z + k) % NZ
+    for i in range(3):
         first, second, seen = jnp.int32(0), jnp.int32(0), jnp.int32(0)
         for r in range(8):
-            hit = tab_ref[asker, r // 2, r % 2] == me
-            span = tab_ref[asker, r // 2, 2 + r % 2]
+            hit = tabs[i][far, r // 2, r % 2] == me
+            span = tabs[i][far, r // 2, 2 + r % 2]
             first = jnp.where(hit & (seen == 0), span, first)
             second = jnp.where(hit & (seen == 1), span, second)
             seen = seen + jnp.where(hit, 1, 0)
@@ -181,19 +179,19 @@
         copy.wait()
 
 
-def pack_spans(far, table, keys, values):
+def pack_spans(far, tables, keys, values):
     anywhere = pl.BlockSpec(memory_space=pl.ANY)
     vmem = pl.BlockSpec(memory_space=pltpu.VMEM)
     return pl.pallas_call(
-        functools.partial(pack_spans_kernel, far),
-        in_specs=[pl.BlockSpec(memory_space=pltpu.SMEM), vmem, vmem],
+        functools.partial(pack_spans_kernel, int(far)),
+        in_specs=[pl.BlockSpec(memory_space=pltpu.SMEM)] * 3 + [vmem, vmem],
         out_specs=[anywhere] * 3 + [vmem],
         out_shape=[jax.ShapeDtypeStruct((2, 2, CH, HD), bf16)] * 3 + [jax.ShapeDtypeStruct((8, DH), i32)],
         scratch_shapes=[pltpu.SemaphoreType.DMA((3, 2, 2))],
         compiler_params=params(),
         cost_estimate=cost(0, 7 << 20),
         name="pack_far" if far else "pack_near",
-    )(table, keys, values)
+    )(*tables, keys, values)
 
 
 def cross_kernel(far, tab_ref, q_ref, *refs):
@@ -205,7 +203,7 @@
         part_ref, out_ref, kbuf, vbuf, sems = refs[5:]
     me = lax.axis_index("db")
     plane, z = me // NZ, me % NZ
-    row = (1 - plane) * NZ + z if far else me
+    row = 1 if far else 0
     here = []
     for r in range(8):
         owner = tab_ref[row, r // 2, r % 2]
@@ -287,7 +285,7 @@
             pltpu.SemaphoreType.DMA((8, 2)),
         ],
         compiler_params=params(),
-        cost_estimate=cost(4 << 30, 6 << 20),
+        cost_estimate=pl.CostEstimate(flops=32 << 30 if far else 1 << 26, bytes_accessed=0, transcendentals=0),
         name="cross_far" if far else "cross_near",
     )(table, q, keys, values, *got, *part)
 
@@ -317,15 +315,15 @@
     far_q = lax.ppermute(q, "db", swap)
 
     asked = jnp.concatenate([nbr_owner, nbr_local], axis=2)
-    mine = lax.broadcasted_iota(i32, (8, 4, 4), 0) == lax.axis_index("db")
-    table = lax.psum(jnp.where(mine, asked, 0), "db")
-    *far, token = pack_spans(True, table, db_k, db_v)
+    table = jnp.concatenate([asked, lax.ppermute(asked, "db", swap)], axis=0)
+    tables = [lax.ppermute(table, "db", turn(NZ - k)) for k in SHIFTS]
+    *far, token = pack_spans(True, tables, db_k, db_v)
     far_got = [lax.ppermute(x, "db", turn(k)) for x, k in zip(far, SHIFTS)]
 
     heads = pack_heads(token, doc_ids, q, keys[0], values[0])
     heads = lax.all_to_all(heads, "ctx", split_axis=0, concat_axis=0, tiled=True)
 
-    near = list(pack_spans(False, table, db_k, db_v)[:3])
+    near = list(pack_spans(False, tables, db_k, db_v)[:3])
     near_got = []
     for i, k in enumerate(SHIFTS):
         near[i], far_got[i] = lax.optimization_barrier((near[i], far_got[i]))

time: 176 us -> 145 us (0.82)
  the two profiles are of different devices: /device:TPU:1 before, /device:TPU:96 now
where the time goes in v4:
time: 145 us; the launch traced here: 142 us
  Pallas kernels  56.3 us (39%)
  waiting for transfers between devices  54.9 us (38%)
  starting transfers between devices  27.2 us (19%)
  local copies, waits for them, and re-layouts  3.14 us (2%)
    ppermute x3, waiting for transfers between devices, per_device(): far_got = [lax.ppermute(x, 'db', turn(k)) for x, k in zip(far, SHIFTS)]  41.8 us
    pallas_call x1, Pallas kernels, self_attention(): pl.pallas_call(self_kernel, in_specs=[pl.BlockSpec(memory_space=pltpu.VME...  27.6 us
    pallas_call x2, Pallas kernels, cross(): pl.pallas_call(functools.partial(cross_kernel, far), in_specs=[pl.BlockSp...  17 us
    pallas_call x2, Pallas kernels, pack_spans(): pl.pallas_call(functools.partial(pack_spans_kernel, int(far)), in_specs=[...  7.56 us
    all_to_all x1, waiting for transfers between devices, per_device(): lax.all_to_all(self_rows, 'ctx', split_axis=0, concat_axis=0, tiled=True)  6.19 us
    ppermute x3, waiting for transfers between devices, per_device(): tables = [lax.ppermute(table, 'db', turn(NZ - k)) for k in SHIFTS]  4.81 us
    all_to_all x1, starting transfers between devices, per_device(): lax.all_to_all(heads, 'ctx', split_axis=0, concat_axis=0, tiled=True)  4.78 us
    all_to_all x1, starting transfers between devices, per_device(): lax.all_to_all(self_rows, 'ctx', split_axis=0, concat_axis=0, tiled=True)  4.46 us
  transfers between devices with their start and end apart: 14, of which 6 were waited for; matrix products, arithmetic and copies ran while one was open for 0% of the time, Pallas kernels for 36%

profile of v4, /device:TPU:96, one launch (start us, length us, event | category | flops | bytes accessed | tf_op | source)
XLA Modules:
  0.0 142.4 jit_solution(5759744301046336484)
XLA Ops:
  0.6 0.8 copy.13
  1.4 0.8 copy.14
  2.2 0.1 pad_add_fusion.1
  2.2 3.0 %collective-permute-start = (s32[1,4,4]{2,1,0:T(4,128)S(1)}, s32[1,4,4]{2,1,0:T(4,128)S(1)}, u32[]{:S(2)}, u32[]{:S(2)}) collective-permute-start(s32[1,4,4]{2,1,0:T(4,128)S(1)} %pad_add_fusion.1), channel_id=1, source_target_pairs={{0,4},{1,5},{2,6},{3,7},{4,0},{5,1},{6,2},{7,3},{8,12},{9,13},{10,... | collective-permute-start | bytes 200 | tf_op jit(solution)/shard_map/ppermute | solution.py:318
  5.3 2.1 %collective-permute-done = s32[1,4,4]{2,1,0:T(4,128)S(1)} collective-permute-done((s32[1,4,4]{2,1,0:T(4,128)S(1)}, s32[1,4,4]{2,1,0:T(4,128)S(1)}, u32[]{:S(2)}, u32[]{:S(2)}) %collective-permute-start) | collective-permute-done | bytes 96 | tf_op jit(solution)/shard_map/ppermute | solution.py:318
  7.3 0.1 pad_add_fusion.tab_ref
  7.4 0.6 collective-permute-start.3
  8.0 2.5 %collective-permute-start.2 = (s32[2,4,4]{2,1,0:T(4,128)S(1)}, s32[2,4,4]{2,1,0:T(4,128)S(1)}, u32[]{:S(2)}, u32[]{:S(2)}) collective-permute-start(s32[2,4,4]{2,1,0:T(4,128)S(1)} %pad_add_fusion.tab_ref), channel_id=1, source_target_pairs={{0,1},{1,2},{2,3},{3,0},{4,5},{5,6},{6,7},{7,4},{8,9},{9,10},{10,1... | collective-permute-start | bytes 392 | tf_op jit(solution)/shard_map/ppermute | solution.py:319
  10.5 0.0 collective-permute-start.1
  10.5 2.0 %collective-permute-done.3.refs_2_ = s32[2,4,4]{2,1,0:T(4,128)S(1)} collective-permute-done((s32[2,4,4]{2,1,0:T(4,128)S(1)}, s32[2,4,4]{2,1,0:T(4,128)S(1)}, u32[]{:S(2)}, u32[]{:S(2)}) %collective-permute-start.3) | collective-permute-done | bytes 160 | tf_op jit(solution)/shard_map/ppermute | solution.py:319
  12.5 0.0 collective-permute-done.2.refs_1_
  12.5 2.8 %collective-permute-done.1.refs_0_ = s32[2,4,4]{2,1,0:T(4,128)S(1)} collective-permute-done((s32[2,4,4]{2,1,0:T(4,128)S(1)}, s32[2,4,4]{2,1,0:T(4,128)S(1)}, u32[]{:S(2)}, u32[]{:S(2)}) %collective-permute-start.1) | collective-permute-done | bytes 160 | tf_op jit(solution)/shard_map/ppermute | solution.py:319
  15.3 0.0 copy-start
  15.3 1.6 %copy-done = bf16[1,8,64,2048]{3,2,1,0:T(8,128)(2,1)S(1)} copy-done((bf16[1,8,64,2048]{3,2,1,0:T(8,128)(2,1)S(1)}, bf16[1,8,64,2048]{3,2,1,0:T(8,128)(2,1)}, u32[]{:S(2)}) %copy-start) | copy-done | bytes 2097176
  16.9 0.0 copy-start.2
  16.9 0.0 copy-start.3
  16.9 3.5 %pack_far.1 = (bf16[2,2,64,2048]{3,2,1,0:T(8,128)(2,1)}, bf16[2,2,64,2048]{3,2,1,0:T(8,128)(2,1)}, bf16[2,2,64,2048]{3,2,1,0:T(8,128)(2,1)}, s32[8,128]{1,0:T(8,128)S(1)}) custom-call(s32[2,4,4]{2,1,0:T(4,128)S(1)} %collective-permute-done.1.refs_0_, s32[2,4,4]{2,1,0:T(4,128)S(1)} %collective-permute-done.2.refs_1_, ...), custom_call_target="tpu_custom_call" | custom-call | bytes 458752 | tf_op jit(solution)/shard_map/pack_far/pallas_call | solution.py:185
  20.5 0.1 collective-permute-start.4
  20.6 2.0 %collective-permute-start.6 = (bf16[2,2,64,2048]{3,2,1,0:T(8,128)(2,1)}, bf16[2,2,64,2048]{3,2,1,0:T(8,128)(2,1)}, u32[]{:S(2)}, u32[]{:S(2)}) collective-permute-start(bf16[2,2,64,2048]{3,2,1,0:T(8,128)(2,1)} %get-tuple-element.23), channel_id=1, source_target_pairs={{0,3},{1,0},{2,1},{3,2},{4,7},{5,4},{6,5},{7,6},{8,11},{9,8},{10,9... | collective-permute-start | bytes 3145736 | tf_op jit(solution)/shard_map/ppermute | solution.py:321
  22.6 0.0 collective-permute-start.8
  22.6 0.0 copy-done.2
  22.6 3.0 %collective-permute-start.10 = (bf16[256,2048]{1,0:T(8,128)(2,1)S(1)}, bf16[256,2048]{1,0:T(8,128)(2,1)}, u32[]{:S(2)}, u32[]{:S(2)}) collective-permute-start(bf16[256,2048]{1,0:T(8,128)(2,1)S(1)} %bitcast.11), channel_id=1, source_target_pairs={{0,4},{1,5},{2,6},{3,7},{4,0},{5,1},{6,2},{7,3},{8,12},{9,13},{10,... | collective-permute-start | bytes 3145736 | tf_op jit(solution)/shard_map/ppermute | solution.py:315
  25.6 0.0 copy-done.3
  25.6 0.0 copy-done.4
  25.6 0.0 copy-done.5
  25.6 2.6 %pack_heads.1 = bf16[16,784,128]{2,1,0:T(8,128)(2,1)} custom-call(s32[8,128]{1,0:T(8,128)S(1)} %get-tuple-element.18.token_ref, s32[1,256]{1,0:T(1,128)S(1)} %copy-done.5, bf16[256,2048]{1,0:T(8,128)(2,1)S(1)} %bitcast.12, bf16[256,2048]{1,0:T(8,128)(2,1)S(1)} %bitcast.14, bf16[256,2048]{1,0:T(8,128)(2,1)S(1)} %bitcast.15), custom_call_target="tpu_custom_call" | custom-call | bytes 393216 | tf_op jit(solution)/shard_map/pack_heads/pallas_call | solution.py:51
  28.2 4.8 %all-to-all-start = ((bf16[16,784,128]{2,1,0:T(8,128)(2,1)}), bf16[16,784,128]{2,1,0:T(8,128)(2,1)}, u32[]{:S(2)}, u32[]{:S(2)}) async-start(bf16[16,784,128]{2,1,0:T(8,128)(2,1)} %pack_heads.1), calls=%async_computation | async-start | bytes 6422528 | tf_op jit(solution)/shard_map/all_to_all | solution.py:324
  33.0 0.0 copy-done.1
  33.0 4.0 %pack_near.1 = (bf16[2,2,64,2048]{3,2,1,0:T(8,128)(2,1)}, bf16[2,2,64,2048]{3,2,1,0:T(8,128)(2,1)}, bf16[2,2,64,2048]{3,2,1,0:T(8,128)(2,1)}, s32[8,128]{1,0:T(8,128)}) custom-call(s32[2,4,4]{2,1,0:T(4,128)S(1)} %collective-permute-done.1.refs_0_, s32[2,4,4]{2,1,0:T(4,128)S(1)} %collective-permute-done.2.refs_1_, ...), custom_call_target="tpu_custom_call" | custom-call | bytes 458752 | tf_op jit(solution)/shard_map/pack_near/pallas_call | solution.py:185
  37.0 9.9 %collective-permute-done.4.refs_2_ = bf16[2,2,64,2048]{3,2,1,0:T(8,128)(2,1)} collective-permute-done((bf16[2,2,64,2048]{3,2,1,0:T(8,128)(2,1)}, bf16[2,2,64,2048]{3,2,1,0:T(8,128)(2,1)}, u32[]{:S(2)}, u32[]{:S(2)}) %collective-permute-start.4) | collective-permute-done | bytes 1048608 | tf_op jit(solution)/shard_map/ppermute | solution.py:321
  47.0 31.9 %collective-permute-done.6.refs_3_ = bf16[2,2,64,2048]{3,2,1,0:T(8,128)(2,1)} collective-permute-done((bf16[2,2,64,2048]{3,2,1,0:T(8,128)(2,1)}, bf16[2,2,64,2048]{3,2,1,0:T(8,128)(2,1)}, u32[]{:S(2)}, u32[]{:S(2)}) %collective-permute-start.6) | collective-permute-done | bytes 1048608 | tf_op jit(solution)/shard_map/ppermute | solution.py:321
  78.9 0.0 collective-permute-done.8.refs_4_
  78.9 0.0 collective-permute-start.9
  78.9 0.4 collective-permute-start.7
  79.3 2.8 %collective-permute-start.5 = (bf16[2,2,64,2048]{3,2,1,0:T(8,128)(2,1)}, bf16[2,2,64,2048]{3,2,1,0:T(8,128)(2,1)}, u32[]{:S(2)}, u32[]{:S(2)}) collective-permute-start(bf16[2,2,64,2048]{3,2,1,0:T(8,128)(2,1)} %get-tuple-element.21), channel_id=1, source_target_pairs={{0,1},{1,2},{2,3},{3,0},{4,5},{5,6},{6,7},{7,4},{8,9},{9,10},{10,1... | collective-permute-start | bytes 3145736 | tf_op jit(solution)/shard_map/ppermute | solution.py:330
  82.1 0.0 collective-permute-done.10.q_ref
  82.1 6.6 %cross_far.1 = bf16[256,2176]{1,0:T(8,128)(2,1)} custom-call(s32[2,4,4]{2,1,0:T(4,128)S(1)} %pad_add_fusion.tab_ref, bf16[256,2048]{1,0:T(8,128)(2,1)} %collective-permute-done.10.q_ref, bf16[8,64,2048]{2,1,0:T(8,128)(2,1)} %bitcast.7, bf16[8,64,2048]{2,1,0:T(8,128)(2,1)} %bitcast.18, bf16[2,2,64,2048]{3,2,1,0:T(8,128)(2,1)} %collective-permute-done.4.refs_2_, ...), custom_call_target="tpu_custom_call" | custom-call | flops 34359738368 | tf_op jit(solution)/shard_map/cross_far/pallas_call | solution.py:275
  88.8 3.5 %collective-permute-start.11 = (bf16[256,2176]{1,0:T(8,128)(2,1)}, bf16[256,2176]{1,0:T(8,128)(2,1)}, u32[]{:S(2)}, u32[]{:S(2)}) collective-permute-start(bf16[256,2176]{1,0:T(8,128)(2,1)} %cross_far.1), channel_id=1, source_target_pairs={{0,4},{1,5},{2,6},{3,7},{4,0},{5,1},{6,2},{7,3},{8,12},{9,13},{10,... | collective-permute-start | bytes 3342344 | tf_op jit(solution)/shard_map/ppermute | solution.py:331
  92.2 0.0 all-to-all-done.x_ref
  92.2 27.6 %self_attention.1 = bf16[16,256,128]{2,1,0:T(8,128)(2,1)} custom-call(bf16[16,784,128]{2,1,0:T(8,128)(2,1)} %all-to-all-done.x_ref), custom_call_target="tpu_custom_call" | custom-call | flops 268435456 | bytes 262144 | tf_op jit(solution)/shard_map/self_attention/pallas_call | solution.py:145
  119.8 4.5 %all-to-all-start.1 = ((bf16[16,256,128]{2,1,0:T(8,128)(2,1)}), bf16[16,256,128]{2,1,0:T(8,128)(2,1)S(1)}, u32[]{:S(2)}, u32[]{:S(2)}) async-start(bf16[16,256,128]{2,1,0:T(8,128)(2,1)} %self_attention.1), calls=%async_computation.1 | async-start | bytes 2097152 | tf_op jit(solution)/shard_map/all_to_all | solution.py:334
  124.3 0.0 collective-permute-done.9.refs_2_
  124.3 0.0 collective-permute-done.7.refs_1_
  124.3 0.0 collective-permute-done.5.refs_0_
  124.3 0.0 collective-permute-done.11.refs_5_
  124.3 10.4 %cross_near.1 = bf16[256,2048]{1,0:T(8,128)(2,1)} custom-call(s32[2,4,4]{2,1,0:T(4,128)S(1)} %pad_add_fusion.tab_ref, bf16[256,2048]{1,0:T(8,128)(2,1)S(1)} %bitcast.13, bf16[8,64,2048]{2,1,0:T(8,128)(2,1)} %bitcast.8, bf16[8,64,2048]{2,1,0:T(8,128)(2,1)} %bitcast.19, bf16[2,2,64,2048]{3,2,1,0:T(8,128)(2,1)} %get-tuple-element.28.refs_2_, ...), custom_call_target="tpu_custom_call" | custom-call | flops 67108864 | tf_op jit(solution)/shard_map/cross_near/pallas_call | solution.py:275
  134.7 6.2 %all-to-all-done.1.x_ref = bf16[16,256,128]{2,1,0:T(8,128)(2,1)S(1)} async-done(((bf16[16,256,128]{2,1,0:T(8,128)(2,1)}), bf16[16,256,128]{2,1,0:T(8,128)(2,1)S(1)}, u32[]{:S(2)}, u32[]{:S(2)}) %all-to-all-start.1) | async-done | bytes 1048608 | tf_op jit(solution)/shard_map/all_to_all | solution.py:334
  140.9 1.6 %unpack_heads.1 = bf16[256,2048]{1,0:T(8,128)(2,1)} custom-call(bf16[16,256,128]{2,1,0:T(8,128)(2,1)S(1)} %all-to-all-done.1.x_ref), custom_call_target="tpu_custom_call" | custom-call | bytes 131072 | tf_op jit(solution)/shard_map/unpack_heads/pallas_call | solution.py:75
  (4 shorter events, 0.0 us)
Async XLA Ops:
  2.2 5.1 %collective-permute-start = (s32[1,4,4]{2,1,0:T(4,128)S(1)}, s32[1,4,4]{2,1,0:T(4,128)S(1)}, u32[]{:S(2)}, u32[]{:S(2)}) collective-permute-start(s32[1,4,4]{2,1,0:T(4,128)S(1)} %pad_add_fusion.1), channel_id=1, source_target_pairs={{0,4},{1,5},{2,6},{3,7},{4,0},{5,1},{6,2},{7,3},{8,12},{9,13},{10,... | collective-permute-start | bytes 200 | tf_op jit(solution)/shard_map/ppermute | solution.py:318
  7.4 5.1 %collective-permute-start.3 = (s32[2,4,4]{2,1,0:T(4,128)S(1)}, s32[2,4,4]{2,1,0:T(4,128)S(1)}, u32[]{:S(2)}, u32[]{:S(2)}) collective-permute-start(s32[2,4,4]{2,1,0:T(4,128)S(1)} %pad_add_fusion.tab_ref), channel_id=1, source_target_pairs={{0,2},{1,3},{2,0},{3,1},{4,6},{5,7},{6,4},{7,5},{8,10},{9,11},{10,... | collective-permute-start | bytes 392 | tf_op jit(solution)/shard_map/ppermute | solution.py:319
  8.0 4.6 %collective-permute-start.2 = (s32[2,4,4]{2,1,0:T(4,128)S(1)}, s32[2,4,4]{2,1,0:T(4,128)S(1)}, u32[]{:S(2)}, u32[]{:S(2)}) collective-permute-start(s32[2,4,4]{2,1,0:T(4,128)S(1)} %pad_add_fusion.tab_ref), channel_id=1, source_target_pairs={{0,1},{1,2},{2,3},{3,0},{4,5},{5,6},{6,7},{7,4},{8,9},{9,10},{10,1... | collective-permute-start | bytes 392 | tf_op jit(solution)/shard_map/ppermute | solution.py:319
  10.5 4.8 %collective-permute-start.1 = (s32[2,4,4]{2,1,0:T(4,128)S(1)}, s32[2,4,4]{2,1,0:T(4,128)S(1)}, u32[]{:S(2)}, u32[]{:S(2)}) collective-permute-start(s32[2,4,4]{2,1,0:T(4,128)S(1)} %pad_add_fusion.tab_ref), channel_id=1, source_target_pairs={{0,3},{1,0},{2,1},{3,2},{4,7},{5,4},{6,5},{7,6},{8,11},{9,8},{10,9... | collective-permute-start | bytes 392 | tf_op jit(solution)/shard_map/ppermute | solution.py:319
  15.3 1.6 %copy-start = (bf16[1,8,64,2048]{3,2,1,0:T(8,128)(2,1)S(1)}, bf16[1,8,64,2048]{3,2,1,0:T(8,128)(2,1)}, u32[]{:S(2)}) copy-start(bf16[1,8,64,2048]{3,2,1,0:T(8,128)(2,1)} %param.14) | copy-start | bytes 6291460
  16.9 5.7 %copy-start.2 = (bf16[1,256,2048]{2,1,0:T(8,128)(2,1)S(1)}, bf16[1,256,2048]{2,1,0:T(8,128)(2,1)}, u32[]{:S(2)}) copy-start(bf16[1,256,2048]{2,1,0:T(8,128)(2,1)} %param.8) | copy-start | bytes 3145732
  16.9 8.7 %copy-start.3 = (bf16[1,256,2048]{2,1,0:T(8,128)(2,1)S(1)}, bf16[1,256,2048]{2,1,0:T(8,128)(2,1)}, u32[]{:S(2)}) copy-start(bf16[1,256,2048]{2,1,0:T(8,128)(2,1)} %param.9) | copy-start | bytes 3145732
  16.9 8.7 %copy-start.4 = (bf16[1,256,2048]{2,1,0:T(8,128)(2,1)S(1)}, bf16[1,256,2048]{2,1,0:T(8,128)(2,1)}, u32[]{:S(2)}) copy-start(bf16[1,256,2048]{2,1,0:T(8,128)(2,1)} %param.10) | copy-start | bytes 3145732
  16.9 8.7 %copy-start.5 = (s32[1,256]{1,0:T(1,128)S(1)}, s32[1,256]{1,0:T(1,128)}, u32[]{:S(2)}) copy-start(s32[1,256]{1,0:T(1,128)} %docs_ref.1) | copy-start | bytes 3076
  20.5 26.5 %collective-permute-start.4 = (bf16[2,2,64,2048]{3,2,1,0:T(8,128)(2,1)}, bf16[2,2,64,2048]{3,2,1,0:T(8,128)(2,1)}, u32[]{:S(2)}, u32[]{:S(2)}) collective-permute-start(bf16[2,2,64,2048]{3,2,1,0:T(8,128)(2,1)} %get-tuple-element.20), channel_id=1, source_target_pairs={{0,1},{1,2},{2,3},{3,0},{4,5},{5,6},{6,7},{7,4},{8,9},{9,10},{10,1... | collective-permute-start | bytes 3145736 | tf_op jit(solution)/shard_map/ppermute | solution.py:321
  20.6 58.3 %collective-permute-start.6 = (bf16[2,2,64,2048]{3,2,1,0:T(8,128)(2,1)}, bf16[2,2,64,2048]{3,2,1,0:T(8,128)(2,1)}, u32[]{:S(2)}, u32[]{:S(2)}) collective-permute-start(bf16[2,2,64,2048]{3,2,1,0:T(8,128)(2,1)} %get-tuple-element.23), channel_id=1, source_target_pairs={{0,3},{1,0},{2,1},{3,2},{4,7},{5,4},{6,5},{7,6},{8,11},{9,8},{10,9... | collective-permute-start | bytes 3145736 | tf_op jit(solution)/shard_map/ppermute | solution.py:321
  22.6 56.3 %collective-permute-start.8 = (bf16[2,2,64,2048]{3,2,1,0:T(8,128)(2,1)}, bf16[2,2,64,2048]{3,2,1,0:T(8,128)(2,1)}, u32[]{:S(2)}, u32[]{:S(2)}) collective-permute-start(bf16[2,2,64,2048]{3,2,1,0:T(8,128)(2,1)} %get-tuple-element.26), channel_id=1, source_target_pairs={{0,2},{1,3},{2,0},{3,1},{4,6},{5,7},{6,4},{7,5},{8,10},{9,11},{10,... | collective-permute-start | bytes 3145736 | tf_op jit(solution)/shard_map/ppermute | solution.py:321
  22.6 59.6 %collective-permute-start.10 = (bf16[256,2048]{1,0:T(8,128)(2,1)S(1)}, bf16[256,2048]{1,0:T(8,128)(2,1)}, u32[]{:S(2)}, u32[]{:S(2)}) collective-permute-start(bf16[256,2048]{1,0:T(8,128)(2,1)S(1)} %bitcast.11), channel_id=1, source_target_pairs={{0,4},{1,5},{2,6},{3,7},{4,0},{5,1},{6,2},{7,3},{8,12},{9,13},{10,... | collective-permute-start | bytes 3145736 | tf_op jit(solution)/shard_map/ppermute | solution.py:315
  28.2 4.8 %copy-start.1 = (bf16[1,8,64,2048]{3,2,1,0:T(8,128)(2,1)S(1)}, bf16[1,8,64,2048]{3,2,1,0:T(8,128)(2,1)}, u32[]{:S(2)}) copy-start(bf16[1,8,64,2048]{3,2,1,0:T(8,128)(2,1)} %param.14) | copy-start | bytes 6291460
  28.2 64.0 %all-to-all-start = ((bf16[16,784,128]{2,1,0:T(8,128)(2,1)}), bf16[16,784,128]{2,1,0:T(8,128)(2,1)}, u32[]{:S(2)}, u32[]{:S(2)}) async-start(bf16[16,784,128]{2,1,0:T(8,128)(2,1)} %pack_heads.1), calls=%async_computation | async-start | bytes 6422528 | tf_op jit(solution)/shard_map/all_to_all | solution.py:324
  78.9 45.4 %collective-permute-start.9 = (bf16[2,2,64,2048]{3,2,1,0:T(8,128)(2,1)}, bf16[2,2,64,2048]{3,2,1,0:T(8,128)(2,1)S(1)}, u32[]{:S(2)}, u32[]{:S(2)}) collective-permute-start(bf16[2,2,64,2048]{3,2,1,0:T(8,128)(2,1)} %get-tuple-element.27), channel_id=1, source_target_pairs={{0,2},{1,3},{2,0},{3,1},{4,6},{5,7},{6,4},{7,5},{8,10},{9,11},{10,... | collective-permute-start | bytes 3145736 | tf_op jit(solution)/shard_map/ppermute | solution.py:330
  78.9 45.4 %collective-permute-start.7 = (bf16[2,2,64,2048]{3,2,1,0:T(8,128)(2,1)}, bf16[2,2,64,2048]{3,2,1,0:T(8,128)(2,1)}, u32[]{:S(2)}, u32[]{:S(2)}) collective-permute-start(bf16[2,2,64,2048]{3,2,1,0:T(8,128)(2,1)} %get-tuple-element.24), channel_id=1, source_target_pairs={{0,3},{1,0},{2,1},{3,2},{4,7},{5,4},{6,5},{7,6},{8,11},{9,8},{10,9... | collective-permute-start | bytes 3145736 | tf_op jit(solution)/shard_map/ppermute | solution.py:330
  79.3 45.0 %collective-permute-start.5 = (bf16[2,2,64,2048]{3,2,1,0:T(8,128)(2,1)}, bf16[2,2,64,2048]{3,2,1,0:T(8,128)(2,1)}, u32[]{:S(2)}, u32[]{:S(2)}) collective-permute-start(bf16[2,2,64,2048]{3,2,1,0:T(8,128)(2,1)} %get-tuple-element.21), channel_id=1, source_target_pairs={{0,1},{1,2},{2,3},{3,0},{4,5},{5,6},{6,7},{7,4},{8,9},{9,10},{10,1... | collective-permute-start | bytes 3145736 | tf_op jit(solution)/shard_map/ppermute | solution.py:330
  88.8 35.6 %collective-permute-start.11 = (bf16[256,2176]{1,0:T(8,128)(2,1)}, bf16[256,2176]{1,0:T(8,128)(2,1)}, u32[]{:S(2)}, u32[]{:S(2)}) collective-permute-start(bf16[256,2176]{1,0:T(8,128)(2,1)} %cross_far.1), channel_id=1, source_target_pairs={{0,4},{1,5},{2,6},{3,7},{4,0},{5,1},{6,2},{7,3},{8,12},{9,13},{10,... | collective-permute-start | bytes 3342344 | tf_op jit(solution)/shard_map/ppermute | solution.py:331
  119.8 21.1 %all-to-all-start.1 = ((bf16[16,256,128]{2,1,0:T(8,128)(2,1)}), bf16[16,256,128]{2,1,0:T(8,128)(2,1)S(1)}, u32[]{:S(2)}, u32[]{:S(2)}) async-start(bf16[16,256,128]{2,1,0:T(8,128)(2,1)} %self_attention.1), calls=%async_computation.1 | async-start | bytes 2097152 | tf_op jit(solution)/shard_map/all_to_all | solution.py:334

commit v5 on v4

--- a/solution.py
+++ b/solution.py
@@ -15,7 +15,7 @@
 HD = 2048
 NZ = 4
 NC = 16
-QT = 512
+QT = 1024
 CHUNK = 3 * TOK + 16
 NEG = -1e30
 SCALE = math.log2(math.e) / math.sqrt(DH)
@@ -52,7 +52,7 @@
         pack_heads_kernel,
         grid=(4,),
         in_specs=[
-            pl.BlockSpec((8, DH), lambda i: (0, 0)),
+            pl.BlockSpec((2, 4, 4), lambda i: (0, 0, 0)),
             pl.BlockSpec((1, TOK), lambda i: (0, 0)),
             wide,
             wide,
@@ -87,6 +87,7 @@
 def self_kernel(x_ref, o_ref):
     docs = x_ref[:, 3 * TOK : CHUNK, :].astype(f32)
     ends = [jnp.sum(jnp.where(docs < d - 0.5, 1.0, 0.0)).astype(i32) for d in (1, 2, 3)]
+    per = QT // TOK
 
     def start_of(p):
         s = jnp.where(p >= ends[0], ends[0], 0)
@@ -94,48 +95,54 @@
         return jnp.maximum(s, jnp.where(p >= ends[2], ends[2], 0))
 
     def rows(j, part):
-        return x_ref[pl.ds(2 * j, 2), part * TOK : (part + 1) * TOK, :].reshape(QT, DH)
-
-    local = lax.broadcasted_iota(i32, (QT, QT), 1)
-    column = lax.broadcasted_iota(i32, (QT, 1), 0)
-
-    def scores(q, j):
-        s = lax.dot_general(q, rows(j, 1), (((1,), (1,)), ((), ())), preferred_element_type=f32)
-        return s * SCALE
+        return x_ref[pl.ds(per * j, per), part * TOK : (part + 1) * TOK, :].reshape(QT, DH)
 
     def lanes(p):
-        return (p[:, :DH] + p[:, DH : 2 * DH]) + (p[:, 2 * DH : 3 * DH] + p[:, 3 * DH :])
-
-    def mix(p, j):
-        return jnp.dot(p.astype(bf16), rows(j, 2), preferred_element_type=f32)
+        return sum(p[:, c : c + DH] for c in range(0, p.shape[1], DH))
 
     def query_tile(i, carry):
         base = i * QT
-        q = rows(i, 0)
-        first = start_of(base + column)
+        qs = [x_ref[per * i + u, 0:TOK, :] for u in range(per)]
+        columns = [lax.broadcasted_iota(i32, (TOK, 1), 0) + u * TOK for u in range(per)]
+        firsts = [start_of(base + c) for c in columns]
         lo = start_of(base) // QT
         mid = jnp.minimum((start_of(base + QT - 1) + QT - 1) // QT, i)
 
-        s = scores(q, i)
-        s = jnp.where((local <= column) & (local >= first - base), s, NEG)
-        top = jnp.max(s, axis=1, keepdims=True)
-        p = jnp.exp2(s - top)
-        state = (mix(p, i), top, lanes(p))
-
-        def step(j, state, masked):
-            acc, top, total = state
-            s = scores(q, j)
-            if masked:
-                s = jnp.where(local >= first - j * QT, s, NEG)
-            new = jnp.maximum(top, jnp.max(s, axis=1, keepdims=True))
-            p = jnp.exp2(s - new)
-            fade = jnp.exp2(top - new)
-            return acc * fade + mix(p, j), new, total * fade + lanes(p)
-
-        state = lax.fori_loop(lo, mid, functools.partial(step, masked=True), state)
-        acc, top, total = lax.fori_loop(mid, i, functools.partial(step, masked=False), state)
-        out = acc / jnp.sum(total, axis=1, keepdims=True)
-        o_ref[pl.ds(2 * i, 2)] = out.astype(bf16).reshape(2, TOK, DH)
+        def step(j, state, kind):
+            k, v = rows(j, 1), rows(j, 2)
+            ss = []
+            for u in range(per):
+                width = (u + 1) * TOK if kind == "diagonal" else QT
+                s = lax.dot_general(qs[u], k[:width], (((1,), (1,)), ((), ())), preferred_element_type=f32)
+                s = s * SCALE
+                if kind != "open":
+                    local = lax.broadcasted_iota(i32, (TOK, width), 1)
+                    seen = local >= firsts[u] - j * QT
+                    if kind == "diagonal":
+                        seen = seen & (local <= columns[u])
+                    s = jnp.where(seen, s, NEG)
+                ss.append(s)
+            out = []
+            for u, s in enumerate(ss):
+                new = jnp.max(s, axis=1, keepdims=True)
+                if state is not None:
+                    acc, top, total = state[u]
+                    new = jnp.maximum(top, new)
+                p = jnp.exp2(s - new)
+                mixed = jnp.dot(p.astype(bf16), v[: s.shape[1]], preferred_element_type=f32)
+                weight = lanes(p)
+                if state is not None:
+                    fade = jnp.exp2(top - new)
+                    mixed = acc * fade + mixed
+                    weight = total * fade + weight
+                out.append((mixed, new, weight))
+            return tuple(out)
+
+        state = step(i, None, "diagonal")
+        state = lax.fori_loop(lo, mid, functools.partial(step, kind="masked"), state)
+        state = lax.fori_loop(mid, i, functools.partial(step, kind="open"), state)
+        for u, (acc, top, total) in enumerate(state):
+            o_ref[per * i + u] = (acc / jnp.sum(total, axis=1, keepdims=True)).astype(bf16)
         return carry
 
     lax.fori_loop(0, NC * TOK // QT, query_tile, 0)
@@ -261,13 +268,20 @@
             out_ref[toks, HD:] = stats.astype(bf16)
         else:
             stats = part_ref[toks, HD:].astype(f32)
-            lse = (stats[:, :NH] + stats[:, NH : 2 * NH]) + stats[:, 2 * NH : 3 * NH]
+            other = (stats[:, :NH] + stats[:, NH : 2 * NH]) + stats[:, 2 * NH : 3 * NH]
+            tops = jnp.full((CH, NH), NEG, f32)
+            sums = jnp.zeros((CH, NH), f32)
+            slot = lax.broadcasted_iota(i32, (1, NH), 1)
+            for h in range(NH):
+                tops = jnp.where(slot == h, top[h], tops)
+                sums = jnp.where(slot == h, total[h], sums)
+            high = jnp.maximum(tops, other)
+            a, b = jnp.exp2(tops - high), jnp.exp2(other - high)
+            inverse = 1.0 / (sums * a + b)
+            a, b = a * inverse, b * inverse
             for h, c in enumerate(heads):
-                other = lse[:, h : h + 1]
-                high = jnp.maximum(top[h], other)
-                a, b = jnp.exp2(top[h] - high), jnp.exp2(other - high)
-                mixed = o[h] * a + part_ref[toks, c].astype(f32) * b
-                out_ref[toks, c] = (mixed / (total[h] * a + b)).astype(bf16)
+                mixed = o[h] * a[:, h : h + 1] + part_ref[toks, c].astype(f32) * b[:, h : h + 1]
+                out_ref[toks, c] = mixed.astype(bf16)
 
 
 def cross(far, table, q, keys, values, got, part=()):
@@ -320,13 +334,12 @@
     *far, token = pack_spans(True, tables, db_k, db_v)
     far_got = [lax.ppermute(x, "db", turn(k)) for x, k in zip(far, SHIFTS)]
 
-    heads = pack_heads(token, doc_ids, q, keys[0], values[0])
+    heads = pack_heads(table, doc_ids, q, keys[0], values[0])
     heads = lax.all_to_all(heads, "ctx", split_axis=0, concat_axis=0, tiled=True)
 
     near = list(pack_spans(False, tables, db_k, db_v)[:3])
     near_got = []
     for i, k in enumerate(SHIFTS):
-        near[i], far_got[i] = lax.optimization_barrier((near[i], far_got[i]))
         near_got.append(lax.ppermute(near[i], "db", turn(k)))
     part = lax.ppermute(cross(True, table, far_q, db_k, db_v, far_got), "db", swap)
 

time: 145 us -> 131 us (0.903)
  the two profiles are of different devices: /device:TPU:96 before, /device:TPU:1 now
where the time goes in v5:
time: 131 us; the launch traced here: 130 us
  Pallas kernels  50.1 us (38%)
  starting transfers between devices  41.9 us (32%)
  waiting for transfers between devices  34.4 us (26%)
  local copies, waits for them, and re-layouts  3.14 us (2%)
    ppermute x3, waiting for transfers between devices, per_device(): far_got = [lax.ppermute(x, 'db', turn(k)) for x, k in zip(far, SHIFTS)]  24.1 us
    pallas_call x1, Pallas kernels, self_attention(): pl.pallas_call(self_kernel, in_specs=[pl.BlockSpec(memory_space=pltpu.VME...  23.5 us
    pallas_call x2, Pallas kernels, cross(): pl.pallas_call(functools.partial(cross_kernel, far), in_specs=[pl.BlockSp...  14.3 us
    all_to_all x1, starting transfers between devices, per_device(): lax.all_to_all(self_rows, 'ctx', split_axis=0, concat_axis=0, tiled=True)  12.9 us
    all_to_all x1, starting transfers between devices, per_device(): lax.all_to_all(heads, 'ctx', split_axis=0, concat_axis=0, tiled=True)  9.24 us
    pallas_call x2, Pallas kernels, pack_spans(): pl.pallas_call(functools.partial(pack_spans_kernel, int(far)), in_specs=[...  8.09 us
    all_to_all x1, waiting for transfers between devices, per_device(): lax.all_to_all(self_rows, 'ctx', split_axis=0, concat_axis=0, tiled=True)  8 us
    ppermute x3, starting transfers between devices, per_device(): tables = [lax.ppermute(table, 'db', turn(NZ - k)) for k in SHIFTS]  6.51 us
  transfers between devices with their start and end apart: 14, of which 5 were waited for; matrix products, arithmetic and copies ran while one was open for 0% of the time, Pallas kernels for 37%

profile of v5, /device:TPU:1, one launch (start us, length us, event | category | flops | bytes accessed | tf_op | source)
XLA Modules:
  0.0 130.5 jit_solution(2685642119865134347)
XLA Ops:
  0.6 0.8 copy.13
  1.4 0.8 copy.14
  2.2 0.1 pad_add_fusion.1
  2.2 3.6 %collective-permute-start = (s32[1,4,4]{2,1,0:T(4,128)S(1)}, s32[1,4,4]{2,1,0:T(4,128)S(1)}, u32[]{:S(2)}, u32[]{:S(2)}) collective-permute-start(s32[1,4,4]{2,1,0:T(4,128)S(1)} %pad_add_fusion.1), channel_id=1, source_target_pairs={{0,4},{1,5},{2,6},{3,7},{4,0},{5,1},{6,2},{7,3},{8,12},{9,13},{10,... | collective-permute-start | bytes 200 | tf_op jit(solution)/shard_map/ppermute | solution.py:332
  5.8 0.1 collective-permute-start.7
  5.9 0.9 collective-permute-done
  6.8 0.1 pad_add_fusion.token_ref.tab_ref
  6.9 3.8 %collective-permute-start.3 = (s32[2,4,4]{2,1,0:T(4,128)S(1)}, s32[2,4,4]{2,1,0:T(4,128)S(1)}, u32[]{:S(2)}, u32[]{:S(2)}) collective-permute-start(s32[2,4,4]{2,1,0:T(4,128)S(1)} %pad_add_fusion.token_ref.tab_ref), channel_id=1, source_target_pairs={{0,2},{1,3},{2,0},{3,1},{4,6},{5,7},{6,4},{7,5},{8,10},{9,11},{10,... | collective-permute-start | bytes 392 | tf_op jit(solution)/shard_map/ppermute | solution.py:333
  10.7 0.7 collective-permute-start.2
  11.4 1.9 %collective-permute-start.1 = (s32[2,4,4]{2,1,0:T(4,128)S(1)}, s32[2,4,4]{2,1,0:T(4,128)S(1)}, u32[]{:S(2)}, u32[]{:S(2)}) collective-permute-start(s32[2,4,4]{2,1,0:T(4,128)S(1)} %pad_add_fusion.token_ref.tab_ref), channel_id=1, source_target_pairs={{0,3},{1,0},{2,1},{3,2},{4,7},{5,4},{6,5},{7,6},{8,11},{9,8},{10,9... | collective-permute-start | bytes 392 | tf_op jit(solution)/shard_map/ppermute | solution.py:333
  13.4 0.0 collective-permute-done.3.refs_2_
  13.4 1.4 %collective-permute-done.2.refs_1_ = s32[2,4,4]{2,1,0:T(4,128)S(1)} collective-permute-done((s32[2,4,4]{2,1,0:T(4,128)S(1)}, s32[2,4,4]{2,1,0:T(4,128)S(1)}, u32[]{:S(2)}, u32[]{:S(2)}) %collective-permute-start.2) | collective-permute-done | bytes 160 | tf_op jit(solution)/shard_map/ppermute | solution.py:333
  14.8 0.0 collective-permute-done.1.refs_0_
  14.8 0.0 copy-start
  14.8 1.6 %copy-done = bf16[1,8,64,2048]{3,2,1,0:T(8,128)(2,1)S(1)} copy-done((bf16[1,8,64,2048]{3,2,1,0:T(8,128)(2,1)S(1)}, bf16[1,8,64,2048]{3,2,1,0:T(8,128)(2,1)}, u32[]{:S(2)}) %copy-start) | copy-done | bytes 2097176
  16.4 0.0 copy-start.2
  16.4 0.0 copy-start.3
  16.4 4.1 %pack_far.1 = (bf16[2,2,64,2048]{3,2,1,0:T(8,128)(2,1)}, bf16[2,2,64,2048]{3,2,1,0:T(8,128)(2,1)}, bf16[2,2,64,2048]{3,2,1,0:T(8,128)(2,1)}, s32[8,128]{1,0:T(8,128)}) custom-call(s32[2,4,4]{2,1,0:T(4,128)S(1)} %collective-permute-done.1.refs_0_, s32[2,4,4]{2,1,0:T(4,128)S(1)} %collective-permute-done.2.refs_1_, ...), custom_call_target="tpu_custom_call" | custom-call | bytes 458752 | tf_op jit(solution)/shard_map/pack_far/pallas_call | solution.py:192
  20.5 0.1 collective-permute-start.8
  20.6 2.7 %collective-permute-start.9 = (bf16[2,2,64,2048]{3,2,1,0:T(8,128)(2,1)}, bf16[2,2,64,2048]{3,2,1,0:T(8,128)(2,1)}, u32[]{:S(2)}, u32[]{:S(2)}) collective-permute-start(bf16[2,2,64,2048]{3,2,1,0:T(8,128)(2,1)} %get-tuple-element.18), channel_id=1, source_target_pairs={{0,3},{1,0},{2,1},{3,2},{4,7},{5,4},{6,5},{7,6},{8,11},{9,8},{10,9... | collective-permute-start | bytes 3145736 | tf_op jit(solution)/shard_map/ppermute | solution.py:335
  23.3 1.1 collective-permute-start.10
  24.4 0.0 copy-done.2
  24.4 0.0 copy-done.3
  24.4 0.0 copy-done.4
  24.4 0.0 copy-done.5
  24.4 2.6 %pack_heads.1 = bf16[16,784,128]{2,1,0:T(8,128)(2,1)} custom-call(s32[2,4,4]{2,1,0:T(4,128)S(1)} %pad_add_fusion.token_ref.tab_ref, s32[1,256]{1,0:T(1,128)S(1)} %copy-done.5, bf16[256,2048]{1,0:T(8,128)(2,1)S(1)} %bitcast.12, bf16[256,2048]{1,0:T(8,128)(2,1)S(1)} %bitcast.14, bf16[256,2048]{1,0:T(8,128)(2,1)S(1)} %bitcast.15), custom_call_target="tpu_custom_call" | custom-call | bytes 393216 | tf_op jit(solution)/shard_map/pack_heads/pallas_call | solution.py:51
  27.1 9.2 %all-to-all-start = ((bf16[16,784,128]{2,1,0:T(8,128)(2,1)}), bf16[16,784,128]{2,1,0:T(8,128)(2,1)}, u32[]{:S(2)}, u32[]{:S(2)}) async-start(bf16[16,784,128]{2,1,0:T(8,128)(2,1)} %pack_heads.1), calls=%async_computation | async-start | bytes 6422528 | tf_op jit(solution)/shard_map/all_to_all | solution.py:338
  36.3 0.0 copy-done.1
  36.3 4.0 %pack_near.1 = (bf16[2,2,64,2048]{3,2,1,0:T(8,128)(2,1)}, bf16[2,2,64,2048]{3,2,1,0:T(8,128)(2,1)}, bf16[2,2,64,2048]{3,2,1,0:T(8,128)(2,1)}, s32[8,128]{1,0:T(8,128)}) custom-call(s32[2,4,4]{2,1,0:T(4,128)S(1)} %collective-permute-done.1.refs_0_, s32[2,4,4]{2,1,0:T(4,128)S(1)} %collective-permute-done.2.refs_1_, ...), custom_call_target="tpu_custom_call" | custom-call | bytes 458752 | tf_op jit(solution)/shard_map/pack_near/pallas_call | solution.py:192
  40.3 1.2 collective-permute-start.4
  41.5 0.0 collective-permute-done.7.q_ref
  41.5 1.5 %collective-permute-start.5 = (bf16[2,2,64,2048]{3,2,1,0:T(8,128)(2,1)}, bf16[2,2,64,2048]{3,2,1,0:T(8,128)(2,1)}, u32[]{:S(2)}, u32[]{:S(2)}) collective-permute-start(bf16[2,2,64,2048]{3,2,1,0:T(8,128)(2,1)} %get-tuple-element.12), channel_id=1, source_target_pairs={{0,3},{1,0},{2,1},{3,2},{4,7},{5,4},{6,5},{7,6},{8,11},{9,8},{10,9... | collective-permute-start | bytes 3145736 | tf_op jit(solution)/shard_map/ppermute | solution.py:343
  43.0 0.9 collective-permute-done.8.refs_2_
  43.9 0.2 collective-permute-start.6
  44.1 0.0 collective-permute-done.9.refs_3_
  44.1 23.2 %collective-permute-done.10.refs_4_ = bf16[2,2,64,2048]{3,2,1,0:T(8,128)(2,1)} collective-permute-done((bf16[2,2,64,2048]{3,2,1,0:T(8,128)(2,1)}, bf16[2,2,64,2048]{3,2,1,0:T(8,128)(2,1)}, u32[]{:S(2)}, u32[]{:S(2)}) %collective-permute-start.10) | collective-permute-done | bytes 1048608 | tf_op jit(solution)/shard_map/ppermute | solution.py:335
  67.3 6.6 %cross_far.1 = bf16[256,2176]{1,0:T(8,128)(2,1)} custom-call(s32[2,4,4]{2,1,0:T(4,128)S(1)} %pad_add_fusion.token_ref.tab_ref, bf16[256,2048]{1,0:T(8,128)(2,1)} %collective-permute-done.7.q_ref, bf16[8,64,2048]{2,1,0:T(8,128)(2,1)} %bitcast.7, bf16[8,64,2048]{2,1,0:T(8,128)(2,1)} %bitcast.18, bf16[2,2,64,2048]{3,2,1,0:T(8,128)(2,1)} %collective-permute-done.8.refs_2_, ...), custom_call_target="tpu_custom_call" | custom-call | flops 34359738368 | tf_op jit(solution)/shard_map/cross_far/pallas_call | solution.py:289
  73.9 2.8 %collective-permute-start.11 = (bf16[256,2176]{1,0:T(8,128)(2,1)}, bf16[256,2176]{1,0:T(8,128)(2,1)}, u32[]{:S(2)}, u32[]{:S(2)}) collective-permute-start(bf16[256,2176]{1,0:T(8,128)(2,1)} %cross_far.1), channel_id=1, source_target_pairs={{0,4},{1,5},{2,6},{3,7},{4,0},{5,1},{6,2},{7,3},{8,12},{9,13},{10,... | collective-permute-start | bytes 3342344 | tf_op jit(solution)/shard_map/ppermute | solution.py:344
  76.7 0.0 all-to-all-done.x_ref
  76.7 23.5 %self_attention.1 = bf16[16,256,128]{2,1,0:T(8,128)(2,1)} custom-call(bf16[16,784,128]{2,1,0:T(8,128)(2,1)} %all-to-all-done.x_ref), custom_call_target="tpu_custom_call" | custom-call | flops 268435456 | bytes 262144 | tf_op jit(solution)/shard_map/self_attention/pallas_call | solution.py:152
  100.2 12.9 %all-to-all-start.1 = ((bf16[16,256,128]{2,1,0:T(8,128)(2,1)}), bf16[16,256,128]{2,1,0:T(8,128)(2,1)S(1)}, u32[]{:S(2)}, u32[]{:S(2)}) async-start(bf16[16,256,128]{2,1,0:T(8,128)(2,1)} %self_attention.1), calls=%async_computation.1 | async-start | bytes 2097152 | tf_op jit(solution)/shard_map/all_to_all | solution.py:347
  113.1 0.0 collective-permute-done.4.refs_0_
  113.1 0.0 collective-permute-done.5.refs_1_
  113.1 0.0 collective-permute-done.6.refs_2_
  113.1 0.0 collective-permute-done.11.refs_5_
  113.1 7.8 %cross_near.1 = bf16[256,2048]{1,0:T(8,128)(2,1)} custom-call(s32[2,4,4]{2,1,0:T(4,128)S(1)} %pad_add_fusion.token_ref.tab_ref, bf16[256,2048]{1,0:T(8,128)(2,1)S(1)} %bitcast.13, bf16[8,64,2048]{2,1,0:T(8,128)(2,1)} %bitcast.8, bf16[8,64,2048]{2,1,0:T(8,128)(2,1)} %bitcast.19, bf16[2,2,64,2048]{3,2,1,0:T(8,128)(2,1)S(1)} %get-tuple-element.14.refs_2_, ...), custom_call_target="tpu_custom_call" | custom-call | flops 67108864 | tf_op jit(solution)/shard_map/cross_near/pallas_call | solution.py:289
  120.9 8.0 %all-to-all-done.1.x_ref = bf16[16,256,128]{2,1,0:T(8,128)(2,1)S(1)} async-done(((bf16[16,256,128]{2,1,0:T(8,128)(2,1)}), bf16[16,256,128]{2,1,0:T(8,128)(2,1)S(1)}, u32[]{:S(2)}, u32[]{:S(2)}) %all-to-all-start.1) | async-done | bytes 1048608 | tf_op jit(solution)/shard_map/all_to_all | solution.py:347
  128.9 1.6 %unpack_heads.1 = bf16[256,2048]{1,0:T(8,128)(2,1)} custom-call(bf16[16,256,128]{2,1,0:T(8,128)(2,1)S(1)} %all-to-all-done.1.x_ref), custom_call_target="tpu_custom_call" | custom-call | bytes 131072 | tf_op jit(solution)/shard_map/unpack_heads/pallas_call | solution.py:75
  (4 shorter events, 0.0 us)
Async XLA Ops:
  2.2 4.6 %collective-permute-start = (s32[1,4,4]{2,1,0:T(4,128)S(1)}, s32[1,4,4]{2,1,0:T(4,128)S(1)}, u32[]{:S(2)}, u32[]{:S(2)}) collective-permute-start(s32[1,4,4]{2,1,0:T(4,128)S(1)} %pad_add_fusion.1), channel_id=1, source_target_pairs={{0,4},{1,5},{2,6},{3,7},{4,0},{5,1},{6,2},{7,3},{8,12},{9,13},{10,... | collective-permute-start | bytes 200 | tf_op jit(solution)/shard_map/ppermute | solution.py:332
  5.8 35.7 %collective-permute-start.7 = (bf16[256,2048]{1,0:T(8,128)(2,1)}, bf16[256,2048]{1,0:T(8,128)(2,1)}, u32[]{:S(2)}, u32[]{:S(2)}) collective-permute-start(bf16[256,2048]{1,0:T(8,128)(2,1)} %bitcast.11), channel_id=1, source_target_pairs={{0,4},{1,5},{2,6},{3,7},{4,0},{5,1},{6,2},{7,3},{8,12},{9,13},{10,... | collective-permute-start | bytes 3145736 | tf_op jit(solution)/shard_map/ppermute | solution.py:329
  6.9 6.5 %collective-permute-start.3 = (s32[2,4,4]{2,1,0:T(4,128)S(1)}, s32[2,4,4]{2,1,0:T(4,128)S(1)}, u32[]{:S(2)}, u32[]{:S(2)}) collective-permute-start(s32[2,4,4]{2,1,0:T(4,128)S(1)} %pad_add_fusion.token_ref.tab_ref), channel_id=1, source_target_pairs={{0,2},{1,3},{2,0},{3,1},{4,6},{5,7},{6,4},{7,5},{8,10},{9,11},{10,... | collective-permute-start | bytes 392 | tf_op jit(solution)/shard_map/ppermute | solution.py:333
  10.7 4.1 %collective-permute-start.2 = (s32[2,4,4]{2,1,0:T(4,128)S(1)}, s32[2,4,4]{2,1,0:T(4,128)S(1)}, u32[]{:S(2)}, u32[]{:S(2)}) collective-permute-start(s32[2,4,4]{2,1,0:T(4,128)S(1)} %pad_add_fusion.token_ref.tab_ref), channel_id=1, source_target_pairs={{0,1},{1,2},{2,3},{3,0},{4,5},{5,6},{6,7},{7,4},{8,9},{9,10},{10,1... | collective-permute-start | bytes 392 | tf_op jit(solution)/shard_map/ppermute | solution.py:333
  11.4 3.3 %collective-permute-start.1 = (s32[2,4,4]{2,1,0:T(4,128)S(1)}, s32[2,4,4]{2,1,0:T(4,128)S(1)}, u32[]{:S(2)}, u32[]{:S(2)}) collective-permute-start(s32[2,4,4]{2,1,0:T(4,128)S(1)} %pad_add_fusion.token_ref.tab_ref), channel_id=1, source_target_pairs={{0,3},{1,0},{2,1},{3,2},{4,7},{5,4},{6,5},{7,6},{8,11},{9,8},{10,9... | collective-permute-start | bytes 392 | tf_op jit(solution)/shard_map/ppermute | solution.py:333
  14.8 1.6 %copy-start = (bf16[1,8,64,2048]{3,2,1,0:T(8,128)(2,1)S(1)}, bf16[1,8,64,2048]{3,2,1,0:T(8,128)(2,1)}, u32[]{:S(2)}) copy-start(bf16[1,8,64,2048]{3,2,1,0:T(8,128)(2,1)} %param.14) | copy-start | bytes 6291460
  16.4 8.1 %copy-start.2 = (bf16[1,256,2048]{2,1,0:T(8,128)(2,1)S(1)}, bf16[1,256,2048]{2,1,0:T(8,128)(2,1)}, u32[]{:S(2)}) copy-start(bf16[1,256,2048]{2,1,0:T(8,128)(2,1)} %param.8) | copy-start | bytes 3145732
  16.4 8.1 %copy-start.3 = (bf16[1,256,2048]{2,1,0:T(8,128)(2,1)S(1)}, bf16[1,256,2048]{2,1,0:T(8,128)(2,1)}, u32[]{:S(2)}) copy-start(bf16[1,256,2048]{2,1,0:T(8,128)(2,1)} %param.9) | copy-start | bytes 3145732
  16.4 8.1 %copy-start.4 = (bf16[1,256,2048]{2,1,0:T(8,128)(2,1)S(1)}, bf16[1,256,2048]{2,1,0:T(8,128)(2,1)}, u32[]{:S(2)}) copy-start(bf16[1,256,2048]{2,1,0:T(8,128)(2,1)} %param.10) | copy-start | bytes 3145732
  16.4 8.1 %copy-start.5 = (s32[1,256]{1,0:T(1,128)S(1)}, s32[1,256]{1,0:T(1,128)}, u32[]{:S(2)}) copy-start(s32[1,256]{1,0:T(1,128)} %docs_ref.1) | copy-start | bytes 3076
  20.5 23.4 %collective-permute-start.8 = (bf16[2,2,64,2048]{3,2,1,0:T(8,128)(2,1)}, bf16[2,2,64,2048]{3,2,1,0:T(8,128)(2,1)}, u32[]{:S(2)}, u32[]{:S(2)}) collective-permute-start(bf16[2,2,64,2048]{3,2,1,0:T(8,128)(2,1)} %get-tuple-element.17), channel_id=1, source_target_pairs={{0,1},{1,2},{2,3},{3,0},{4,5},{5,6},{6,7},{7,4},{8,9},{9,10},{10,1... | collective-permute-start | bytes 3145736 | tf_op jit(solution)/shard_map/ppermute | solution.py:335
  20.6 23.5 %collective-permute-start.9 = (bf16[2,2,64,2048]{3,2,1,0:T(8,128)(2,1)}, bf16[2,2,64,2048]{3,2,1,0:T(8,128)(2,1)}, u32[]{:S(2)}, u32[]{:S(2)}) collective-permute-start(bf16[2,2,64,2048]{3,2,1,0:T(8,128)(2,1)} %get-tuple-element.18), channel_id=1, source_target_pairs={{0,3},{1,0},{2,1},{3,2},{4,7},{5,4},{6,5},{7,6},{8,11},{9,8},{10,9... | collective-permute-start | bytes 3145736 | tf_op jit(solution)/shard_map/ppermute | solution.py:335
  23.3 44.0 %collective-permute-start.10 = (bf16[2,2,64,2048]{3,2,1,0:T(8,128)(2,1)}, bf16[2,2,64,2048]{3,2,1,0:T(8,128)(2,1)}, u32[]{:S(2)}, u32[]{:S(2)}) collective-permute-start(bf16[2,2,64,2048]{3,2,1,0:T(8,128)(2,1)} %get-tuple-element.19), channel_id=1, source_target_pairs={{0,2},{1,3},{2,0},{3,1},{4,6},{5,7},{6,4},{7,5},{8,10},{9,11},{10,... | collective-permute-start | bytes 3145736 | tf_op jit(solution)/shard_map/ppermute | solution.py:335
  27.1 9.2 %copy-start.1 = (bf16[1,8,64,2048]{3,2,1,0:T(8,128)(2,1)S(1)}, bf16[1,8,64,2048]{3,2,1,0:T(8,128)(2,1)}, u32[]{:S(2)}) copy-start(bf16[1,8,64,2048]{3,2,1,0:T(8,128)(2,1)} %param.14) | copy-start | bytes 6291460
  27.1 49.6 %all-to-all-start = ((bf16[16,784,128]{2,1,0:T(8,128)(2,1)}), bf16[16,784,128]{2,1,0:T(8,128)(2,1)}, u32[]{:S(2)}, u32[]{:S(2)}) async-start(bf16[16,784,128]{2,1,0:T(8,128)(2,1)} %pack_heads.1), calls=%async_computation | async-start | bytes 6422528 | tf_op jit(solution)/shard_map/all_to_all | solution.py:338
  40.3 72.8 %collective-permute-start.4 = (bf16[2,2,64,2048]{3,2,1,0:T(8,128)(2,1)}, bf16[2,2,64,2048]{3,2,1,0:T(8,128)(2,1)S(1)}, u32[]{:S(2)}, u32[]{:S(2)}) collective-permute-start(bf16[2,2,64,2048]{3,2,1,0:T(8,128)(2,1)} %get-tuple-element.11), channel_id=1, source_target_pairs={{0,1},{1,2},{2,3},{3,0},{4,5},{5,6},{6,7},{7,4},{8,9},{9,10},{10,1... | collective-permute-start | bytes 3145736 | tf_op jit(solution)/shard_map/ppermute | solution.py:343
  41.5 71.6 %collective-permute-start.5 = (bf16[2,2,64,2048]{3,2,1,0:T(8,128)(2,1)}, bf16[2,2,64,2048]{3,2,1,0:T(8,128)(2,1)}, u32[]{:S(2)}, u32[]{:S(2)}) collective-permute-start(bf16[2,2,64,2048]{3,2,1,0:T(8,128)(2,1)} %get-tuple-element.12), channel_id=1, source_target_pairs={{0,3},{1,0},{2,1},{3,2},{4,7},{5,4},{6,5},{7,6},{8,11},{9,8},{10,9... | collective-permute-start | bytes 3145736 | tf_op jit(solution)/shard_map/ppermute | solution.py:343
  43.9 69.2 %collective-permute-start.6 = (bf16[2,2,64,2048]{3,2,1,0:T(8,128)(2,1)}, bf16[2,2,64,2048]{3,2,1,0:T(8,128)(2,1)}, u32[]{:S(2)}, u32[]{:S(2)}) collective-permute-start(bf16[2,2,64,2048]{3,2,1,0:T(8,128)(2,1)} %get-tuple-element.13), channel_id=1, source_target_pairs={{0,2},{1,3},{2,0},{3,1},{4,6},{5,7},{6,4},{7,5},{8,10},{9,11},{10,... | collective-permute-start | bytes 3145736 | tf_op jit(solution)/shard_map/ppermute | solution.py:343
  73.9 39.2 %collective-permute-start.11 = (bf16[256,2176]{1,0:T(8,128)(2,1)}, bf16[256,2176]{1,0:T(8,128)(2,1)}, u32[]{:S(2)}, u32[]{:S(2)}) collective-permute-start(bf16[256,2176]{1,0:T(8,128)(2,1)} %cross_far.1), channel_id=1, source_target_pairs={{0,4},{1,5},{2,6},{3,7},{4,0},{5,1},{6,2},{7,3},{8,12},{9,13},{10,... | collective-permute-start | bytes 3342344 | tf_op jit(solution)/shard_map/ppermute | solution.py:344
  100.2 28.7 %all-to-all-start.1 = ((bf16[16,256,128]{2,1,0:T(8,128)(2,1)}), bf16[16,256,128]{2,1,0:T(8,128)(2,1)S(1)}, u32[]{:S(2)}, u32[]{:S(2)}) async-start(bf16[16,256,128]{2,1,0:T(8,128)(2,1)} %self_attention.1), calls=%async_computation.1 | async-start | bytes 2097152 | tf_op jit(solution)/shard_map/all_to_all | solution.py:347

commit v6 on v5

--- a/solution.py
+++ b/solution.py
@@ -15,7 +15,7 @@
 HD = 2048
 NZ = 4
 NC = 16
-QT = 1024
+QT = 2048
 CHUNK = 3 * TOK + 16
 NEG = -1e30
 SCALE = math.log2(math.e) / math.sqrt(DH)
@@ -52,7 +52,7 @@
         pack_heads_kernel,
         grid=(4,),
         in_specs=[
-            pl.BlockSpec((2, 4, 4), lambda i: (0, 0, 0)),
+            pl.BlockSpec((2, 4, 2), lambda i: (0, 0, 0)),
             pl.BlockSpec((1, TOK), lambda i: (0, 0)),
             wide,
             wide,
@@ -165,36 +165,43 @@
 
 def pack_spans_kernel(far, *refs):
     tabs, keys_ref, values_ref = refs[:3], refs[3], refs[4]
-    outs, token_ref, sems = refs[5:8], refs[8], refs[9]
-    token_ref[...] = jnp.zeros_like(token_ref)
+    outs, hold, loads, stores = refs[5:8], refs[8], refs[9], refs[10]
     me = lax.axis_index("db")
-    copies = []
+    moves = []
     for i in range(3):
         first, second, seen = jnp.int32(0), jnp.int32(0), jnp.int32(0)
         for r in range(8):
-            hit = tabs[i][far, r // 2, r % 2] == me
-            span = tabs[i][far, r // 2, 2 + r % 2]
+            entry = tabs[i][far, r // 2, r % 2]
+            hit = entry // 8 == me
+            span = entry % 8
             first = jnp.where(hit & (seen == 0), span, first)
             second = jnp.where(hit & (seen == 1), span, second)
             seen = seen + jnp.where(hit, 1, 0)
         for slot, span in ((0, first), (1, second)):
             for kind, src in ((0, keys_ref), (1, values_ref)):
-                copy = pltpu.make_async_copy(src.at[span], outs[i].at[slot, kind], sems.at[i, slot, kind])
-                copy.start()
-                copies.append(copy)
-    for copy in copies:
-        copy.wait()
+                at = (i, slot, kind)
+                load = pltpu.make_async_copy(src.at[span], hold.at[at], loads.at[at])
+                load.start()
+                moves.append((load, pltpu.make_async_copy(hold.at[at], outs[i].at[slot, kind], stores.at[at])))
+    for load, store in moves:
+        load.wait()
+        store.start()
+    for load, store in moves:
+        store.wait()
 
 
 def pack_spans(far, tables, keys, values):
     anywhere = pl.BlockSpec(memory_space=pl.ANY)
-    vmem = pl.BlockSpec(memory_space=pltpu.VMEM)
     return pl.pallas_call(
         functools.partial(pack_spans_kernel, int(far)),
-        in_specs=[pl.BlockSpec(memory_space=pltpu.SMEM)] * 3 + [vmem, vmem],
-        out_specs=[anywhere] * 3 + [vmem],
-        out_shape=[jax.ShapeDtypeStruct((2, 2, CH, HD), bf16)] * 3 + [jax.ShapeDtypeStruct((8, DH), i32)],
-        scratch_shapes=[pltpu.SemaphoreType.DMA((3, 2, 2))],
+        in_specs=[pl.BlockSpec(memory_space=pltpu.SMEM)] * 3 + [anywhere, anywhere],
+        out_specs=[anywhere] * 3,
+        out_shape=[jax.ShapeDtypeStruct((2, 2, CH, HD), bf16)] * 3,
+        scratch_shapes=[
+            pltpu.VMEM((3, 2, 2, CH, HD), bf16),
+            pltpu.SemaphoreType.DMA((3, 2, 2)),
+            pltpu.SemaphoreType.DMA((3, 2, 2)),
+        ],
         compiler_params=params(),
         cost_estimate=cost(0, 7 << 20),
         name="pack_far" if far else "pack_near",
@@ -213,14 +220,14 @@
     row = 1 if far else 0
     here = []
     for r in range(8):
-        owner = tab_ref[row, r // 2, r % 2]
+        owner = tab_ref[row, r // 2, r % 2] // 8
         slot = jnp.int32(0)
         for earlier in range(r):
-            slot = slot + jnp.where(tab_ref[row, earlier // 2, earlier % 2] == owner, 1, 0)
+            slot = slot + jnp.where(tab_ref[row, earlier // 2, earlier % 2] // 8 == owner, 1, 0)
         here.append(jnp.where(owner // NZ == plane, 1, 0))
         shift = (z - owner % NZ + NZ) % NZ
         place = pl.ds((r % 2) * CH, CH)
-        span = tab_ref[row, r // 2, 2 + r % 2]
+        span = tab_ref[row, r // 2, r % 2] % 8
 
         @pl.when(shift == 0)
         def _(span=span, place=place, r=r):
@@ -328,16 +335,16 @@
     turn = lambda k: [(s * NZ + z, s * NZ + (z + k) % NZ) for s in range(2) for z in range(NZ)]
     far_q = lax.ppermute(q, "db", swap)
 
-    asked = jnp.concatenate([nbr_owner, nbr_local], axis=2)
+    asked = lax.optimization_barrier(nbr_owner * 8 + nbr_local)
     table = jnp.concatenate([asked, lax.ppermute(asked, "db", swap)], axis=0)
     tables = [lax.ppermute(table, "db", turn(NZ - k)) for k in SHIFTS]
-    *far, token = pack_spans(True, tables, db_k, db_v)
+    far = pack_spans(True, tables, db_k, db_v)
     far_got = [lax.ppermute(x, "db", turn(k)) for x, k in zip(far, SHIFTS)]
 
     heads = pack_heads(table, doc_ids, q, keys[0], values[0])
     heads = lax.all_to_all(heads, "ctx", split_axis=0, concat_axis=0, tiled=True)
 
-    near = list(pack_spans(False, tables, db_k, db_v)[:3])
+    near = pack_spans(False, tables, db_k, db_v)
     near_got = []
     for i, k in enumerate(SHIFTS):
         near_got.append(lax.ppermute(near[i], "db", turn(k)))

time: 131 us -> 129 us (0.985)
  Pallas kernels: 50.1 us -> 48.4 us
    pallas_call x1, Pallas kernels: 23.5 us -> 21.4 us  [self_attention(): pl.pallas_call(self_kernel, in_specs=[pl.BlockSpec(memory_space=pltpu.VME...]
  transfers between devices with their start and end apart: 14 -> 14, of which waited for: 5 -> 6; matrix products, arithmetic and copies ran while one was open for 0% -> 0% of each run, Pallas kernels for 37% -> 36%
where the time goes in v6:
time: 129 us; the launch traced here: 128 us
  Pallas kernels  48.4 us (38%)
  starting transfers between devices  42.4 us (33%)
  waiting for transfers between devices  33.7 us (26%)
  local copies, waits for them, and re-layouts  3.14 us (2%)
    ppermute x3, waiting for transfers between devices, per_device(): far_got = [lax.ppermute(x, 'db', turn(k)) for x, k in zip(far, SHIFTS)]  23.5 us
    pallas_call x1, Pallas kernels, self_attention(): pl.pallas_call(self_kernel, in_specs=[pl.BlockSpec(memory_space=pltpu.VME...  21.4 us
    pallas_call x2, Pallas kernels, cross(): pl.pallas_call(functools.partial(cross_kernel, far), in_specs=[pl.BlockSp...  14.6 us
    all_to_all x1, starting transfers between devices, per_device(): lax.all_to_all(self_rows, 'ctx', split_axis=0, concat_axis=0, tiled=True)  12.9 us
    all_to_all x1, starting transfers between devices, per_device(): lax.all_to_all(heads, 'ctx', split_axis=0, concat_axis=0, tiled=True)  9.24 us
    pallas_call x2, Pallas kernels, pack_spans(): pl.pallas_call(functools.partial(pack_spans_kernel, int(far)), in_specs=[...  8.24 us
    all_to_all x1, waiting for transfers between devices, per_device(): lax.all_to_all(self_rows, 'ctx', split_axis=0, concat_axis=0, tiled=True)  7.43 us
    ppermute x3, starting transfers between devices, per_device(): tables = [lax.ppermute(table, 'db', turn(NZ - k)) for k in SHIFTS]  6.5 us
  transfers between devices with their start and end apart: 14, of which 6 were waited for; matrix products, arithmetic and copies ran while one was open for 0% of the time, Pallas kernels for 36%

profile of v6, /device:TPU:1, one launch (start us, length us, event | category | flops | bytes accessed | tf_op | source)
XLA Modules:
  0.0 128.3 jit_solution(18346571440378064944)
XLA Ops:
  0.6 0.8 copy.13
  1.4 0.8 copy.14
  2.2 3.6 %collective-permute-start = (s32[1,4,2]{2,1,0:T(4,128)S(1)}, s32[1,4,2]{2,1,0:T(4,128)S(1)}, u32[]{:S(2)}, u32[]{:S(2)}) collective-permute-start(s32[1,4,2]{2,1,0:T(4,128)S(1)} %multiply_add_fusion), channel_id=1, source_target_pairs={{0,4},{1,5},{2,6},{3,7},{4,0},{5,1},{6,2},{7,3},{8,12},{9,13},{10,... | collective-permute-start | bytes 104 | tf_op jit(solution)/shard_map/ppermute | solution.py:339
  5.7 0.1 collective-permute-start.7
  5.8 0.9 collective-permute-done
  6.7 3.8 %collective-permute-start.3 = (s32[2,4,2]{2,1,0:T(4,128)S(1)}, s32[2,4,2]{2,1,0:T(4,128)S(1)}, u32[]{:S(2)}, u32[]{:S(2)}) collective-permute-start(s32[2,4,2]{2,1,0:T(4,128)S(1)} %pad_add_fusion.token_ref.tab_ref), channel_id=1, source_target_pairs={{0,2},{1,3},{2,0},{3,1},{4,6},{5,7},{6,4},{7,5},{8,10},{9,11},{10,... | collective-permute-start | bytes 200 | tf_op jit(solution)/shard_map/ppermute | solution.py:340
  10.5 0.7 collective-permute-start.2
  11.3 1.9 %collective-permute-start.1 = (s32[2,4,2]{2,1,0:T(4,128)S(1)}, s32[2,4,2]{2,1,0:T(4,128)S(1)}, u32[]{:S(2)}, u32[]{:S(2)}) collective-permute-start(s32[2,4,2]{2,1,0:T(4,128)S(1)} %pad_add_fusion.token_ref.tab_ref), channel_id=1, source_target_pairs={{0,3},{1,0},{2,1},{3,2},{4,7},{5,4},{6,5},{7,6},{8,11},{9,8},{10,9... | collective-permute-start | bytes 200 | tf_op jit(solution)/shard_map/ppermute | solution.py:340
  13.2 0.0 collective-permute-done.3.refs_2_
  13.2 1.4 %collective-permute-done.2.refs_1_ = s32[2,4,2]{2,1,0:T(4,128)S(1)} collective-permute-done((s32[2,4,2]{2,1,0:T(4,128)S(1)}, s32[2,4,2]{2,1,0:T(4,128)S(1)}, u32[]{:S(2)}, u32[]{:S(2)}) %collective-permute-start.2) | collective-permute-done | bytes 96 | tf_op jit(solution)/shard_map/ppermute | solution.py:340
  14.6 0.0 collective-permute-done.1.refs_0_
  14.6 0.0 copy-start
  14.6 1.6 %copy-done = bf16[1,8,64,2048]{3,2,1,0:T(8,128)(2,1)S(1)} copy-done((bf16[1,8,64,2048]{3,2,1,0:T(8,128)(2,1)S(1)}, bf16[1,8,64,2048]{3,2,1,0:T(8,128)(2,1)}, u32[]{:S(2)}) %copy-start) | copy-done | bytes 2097176
  16.2 0.0 copy-start.2
  16.2 0.0 copy-start.3
  16.2 0.0 copy-start.4
  16.2 0.0 copy-start.5
  16.2 4.2 %pack_far.1 = (bf16[2,2,64,2048]{3,2,1,0:T(8,128)(2,1)}, bf16[2,2,64,2048]{3,2,1,0:T(8,128)(2,1)}, bf16[2,2,64,2048]{3,2,1,0:T(8,128)(2,1)}) custom-call(s32[2,4,2]{2,1,0:T(4,128)S(1)} %collective-permute-done.1.refs_0_, s32[2,4,2]{2,1,0:T(4,128)S(1)} %collective-permute-done.2.refs_1_, s32[2,4,2]{2,1,0:T(4,128)S(1)} %collective-permute-done.3.refs_2_, ...), custom_call_target="tpu_custom_call" | custom-call | bytes 458752 | tf_op jit(solution)/shard_map/pack_far/pallas_call | solution.py:195
  20.4 0.1 collective-permute-start.8
  20.5 2.7 %collective-permute-start.9 = (bf16[2,2,64,2048]{3,2,1,0:T(8,128)(2,1)}, bf16[2,2,64,2048]{3,2,1,0:T(8,128)(2,1)}, u32[]{:S(2)}, u32[]{:S(2)}) collective-permute-start(bf16[2,2,64,2048]{3,2,1,0:T(8,128)(2,1)} %get-tuple-element.18), channel_id=1, source_target_pairs={{0,3},{1,0},{2,1},{3,2},{4,7},{5,4},{6,5},{7,6},{8,11},{9,8},{10,9... | collective-permute-start | bytes 3145736 | tf_op jit(solution)/shard_map/ppermute | solution.py:342
  23.2 0.7 collective-permute-start.10
  23.8 0.0 copy-done.2
  23.8 0.0 copy-done.3
  23.8 0.0 copy-done.4
  23.8 0.0 copy-done.5
  23.8 2.6 %pack_heads.1 = bf16[16,784,128]{2,1,0:T(8,128)(2,1)} custom-call(s32[2,4,2]{2,1,0:T(4,128)S(1)} %pad_add_fusion.token_ref.tab_ref, s32[1,256]{1,0:T(1,128)S(1)} %copy-done.5, bf16[256,2048]{1,0:T(8,128)(2,1)S(1)} %bitcast.12, bf16[256,2048]{1,0:T(8,128)(2,1)S(1)} %bitcast.14, bf16[256,2048]{1,0:T(8,128)(2,1)S(1)} %bitcast.15), custom_call_target="tpu_custom_call" | custom-call | bytes 393216 | tf_op jit(solution)/shard_map/pack_heads/pallas_call | solution.py:51
  26.5 9.2 %all-to-all-start = ((bf16[16,784,128]{2,1,0:T(8,128)(2,1)}), bf16[16,784,128]{2,1,0:T(8,128)(2,1)}, u32[]{:S(2)}, u32[]{:S(2)}) async-start(bf16[16,784,128]{2,1,0:T(8,128)(2,1)} %pack_heads.1), calls=%async_computation | async-start | bytes 6422528 | tf_op jit(solution)/shard_map/all_to_all | solution.py:345
  35.7 0.0 copy-done.1
  35.7 4.0 %pack_near.1 = (bf16[2,2,64,2048]{3,2,1,0:T(8,128)(2,1)}, bf16[2,2,64,2048]{3,2,1,0:T(8,128)(2,1)}, bf16[2,2,64,2048]{3,2,1,0:T(8,128)(2,1)}) custom-call(s32[2,4,2]{2,1,0:T(4,128)S(1)} %collective-permute-done.1.refs_0_, s32[2,4,2]{2,1,0:T(4,128)S(1)} %collective-permute-done.2.refs_1_, s32[2,4,2]{2,1,0:T(4,128)S(1)} %collective-permute-done.3.refs_2_, ...), custom_call_target="tpu_custom_call" | custom-call | bytes 458752 | tf_op jit(solution)/shard_map/pack_near/pallas_call | solution.py:195
  39.7 1.4 %collective-permute-start.4 = (bf16[2,2,64,2048]{3,2,1,0:T(8,128)(2,1)}, bf16[2,2,64,2048]{3,2,1,0:T(8,128)(2,1)S(1)}, u32[]{:S(2)}, u32[]{:S(2)}) collective-permute-start(bf16[2,2,64,2048]{3,2,1,0:T(8,128)(2,1)} %get-tuple-element.11), channel_id=1, source_target_pairs={{0,1},{1,2},{2,3},{3,0},{4,5},{5,6},{6,7},{7,4},{8,9},{9,10},{10,1... | collective-permute-start | bytes 3145736 | tf_op jit(solution)/shard_map/ppermute | solution.py:350
  41.1 0.0 collective-permute-done.7.q_ref
  41.1 1.4 %collective-permute-start.5 = (bf16[2,2,64,2048]{3,2,1,0:T(8,128)(2,1)}, bf16[2,2,64,2048]{3,2,1,0:T(8,128)(2,1)}, u32[]{:S(2)}, u32[]{:S(2)}) collective-permute-start(bf16[2,2,64,2048]{3,2,1,0:T(8,128)(2,1)} %get-tuple-element.12), channel_id=1, source_target_pairs={{0,3},{1,0},{2,1},{3,2},{4,7},{5,4},{6,5},{7,6},{8,11},{9,8},{10,9... | collective-permute-start | bytes 3145736 | tf_op jit(solution)/shard_map/ppermute | solution.py:350
  42.5 1.2 collective-permute-done.8.refs_2_
  43.7 0.4 collective-permute-start.6
  44.1 0.0 collective-permute-done.9.refs_3_
  44.1 22.3 %collective-permute-done.10.refs_4_ = bf16[2,2,64,2048]{3,2,1,0:T(8,128)(2,1)} collective-permute-done((bf16[2,2,64,2048]{3,2,1,0:T(8,128)(2,1)}, bf16[2,2,64,2048]{3,2,1,0:T(8,128)(2,1)}, u32[]{:S(2)}, u32[]{:S(2)}) %collective-permute-start.10) | collective-permute-done | bytes 1048608 | tf_op jit(solution)/shard_map/ppermute | solution.py:342
  66.4 6.6 %cross_far.1 = bf16[256,2176]{1,0:T(8,128)(2,1)} custom-call(s32[2,4,2]{2,1,0:T(4,128)S(1)} %pad_add_fusion.token_ref.tab_ref, bf16[256,2048]{1,0:T(8,128)(2,1)} %collective-permute-done.7.q_ref, bf16[8,64,2048]{2,1,0:T(8,128)(2,1)} %bitcast.7, bf16[8,64,2048]{2,1,0:T(8,128)(2,1)} %bitcast.18, bf16[2,2,64,2048]{3,2,1,0:T(8,128)(2,1)} %collective-permute-done.8.refs_2_, ...), custom_call_target="tpu_custom_call" | custom-call | flops 34359738368 | tf_op jit(solution)/shard_map/cross_far/pallas_call | solution.py:296
  73.0 3.5 %collective-permute-start.11 = (bf16[256,2176]{1,0:T(8,128)(2,1)}, bf16[256,2176]{1,0:T(8,128)(2,1)}, u32[]{:S(2)}, u32[]{:S(2)}) collective-permute-start(bf16[256,2176]{1,0:T(8,128)(2,1)} %cross_far.1), channel_id=1, source_target_pairs={{0,4},{1,5},{2,6},{3,7},{4,0},{5,1},{6,2},{7,3},{8,12},{9,13},{10,... | collective-permute-start | bytes 3342344 | tf_op jit(solution)/shard_map/ppermute | solution.py:351
  76.5 0.0 all-to-all-done.x_ref
  76.5 21.4 %self_attention.1 = bf16[16,256,128]{2,1,0:T(8,128)(2,1)} custom-call(bf16[16,784,128]{2,1,0:T(8,128)(2,1)} %all-to-all-done.x_ref), custom_call_target="tpu_custom_call" | custom-call | flops 268435456 | bytes 262144 | tf_op jit(solution)/shard_map/self_attention/pallas_call | solution.py:152
  97.9 12.9 %all-to-all-start.1 = ((bf16[16,256,128]{2,1,0:T(8,128)(2,1)}), bf16[16,256,128]{2,1,0:T(8,128)(2,1)S(1)}, u32[]{:S(2)}, u32[]{:S(2)}) async-start(bf16[16,256,128]{2,1,0:T(8,128)(2,1)} %self_attention.1), calls=%async_computation.1 | async-start | bytes 2097152 | tf_op jit(solution)/shard_map/all_to_all | solution.py:354
  110.9 0.0 collective-permute-done.4.refs_0_
  110.9 0.0 collective-permute-done.5.refs_1_
  110.9 0.4 collective-permute-done.6.refs_2_
  111.3 0.0 collective-permute-done.11.refs_5_
  111.3 7.9 %cross_near.1 = bf16[256,2048]{1,0:T(8,128)(2,1)} custom-call(s32[2,4,2]{2,1,0:T(4,128)S(1)} %pad_add_fusion.token_ref.tab_ref, bf16[256,2048]{1,0:T(8,128)(2,1)S(1)} %bitcast.13, bf16[8,64,2048]{2,1,0:T(8,128)(2,1)} %bitcast.8, bf16[8,64,2048]{2,1,0:T(8,128)(2,1)} %bitcast.19, bf16[2,2,64,2048]{3,2,1,0:T(8,128)(2,1)S(1)} %get-tuple-element.14.refs_2_, ...), custom_call_target="tpu_custom_call" | custom-call | flops 67108864 | tf_op jit(solution)/shard_map/cross_near/pallas_call | solution.py:296
  119.3 7.4 %all-to-all-done.1.x_ref = bf16[16,256,128]{2,1,0:T(8,128)(2,1)S(1)} async-done(((bf16[16,256,128]{2,1,0:T(8,128)(2,1)}), bf16[16,256,128]{2,1,0:T(8,128)(2,1)S(1)}, u32[]{:S(2)}, u32[]{:S(2)}) %all-to-all-start.1) | async-done | bytes 1048608 | tf_op jit(solution)/shard_map/all_to_all | solution.py:354
  126.7 1.6 %unpack_heads.1 = bf16[256,2048]{1,0:T(8,128)(2,1)} custom-call(bf16[16,256,128]{2,1,0:T(8,128)(2,1)S(1)} %all-to-all-done.1.x_ref), custom_call_target="tpu_custom_call" | custom-call | bytes 131072 | tf_op jit(solution)/shard_map/unpack_heads/pallas_call | solution.py:75
  (4 shorter events, 0.0 us)
Async XLA Ops:
  2.2 4.5 %collective-permute-start = (s32[1,4,2]{2,1,0:T(4,128)S(1)}, s32[1,4,2]{2,1,0:T(4,128)S(1)}, u32[]{:S(2)}, u32[]{:S(2)}) collective-permute-start(s32[1,4,2]{2,1,0:T(4,128)S(1)} %multiply_add_fusion), channel_id=1, source_target_pairs={{0,4},{1,5},{2,6},{3,7},{4,0},{5,1},{6,2},{7,3},{8,12},{9,13},{10,... | collective-permute-start | bytes 104 | tf_op jit(solution)/shard_map/ppermute | solution.py:339
  5.7 35.4 %collective-permute-start.7 = (bf16[256,2048]{1,0:T(8,128)(2,1)}, bf16[256,2048]{1,0:T(8,128)(2,1)}, u32[]{:S(2)}, u32[]{:S(2)}) collective-permute-start(bf16[256,2048]{1,0:T(8,128)(2,1)} %bitcast.11), channel_id=1, source_target_pairs={{0,4},{1,5},{2,6},{3,7},{4,0},{5,1},{6,2},{7,3},{8,12},{9,13},{10,... | collective-permute-start | bytes 3145736 | tf_op jit(solution)/shard_map/ppermute | solution.py:336
  6.7 6.5 %collective-permute-start.3 = (s32[2,4,2]{2,1,0:T(4,128)S(1)}, s32[2,4,2]{2,1,0:T(4,128)S(1)}, u32[]{:S(2)}, u32[]{:S(2)}) collective-permute-start(s32[2,4,2]{2,1,0:T(4,128)S(1)} %pad_add_fusion.token_ref.tab_ref), channel_id=1, source_target_pairs={{0,2},{1,3},{2,0},{3,1},{4,6},{5,7},{6,4},{7,5},{8,10},{9,11},{10,... | collective-permute-start | bytes 200 | tf_op jit(solution)/shard_map/ppermute | solution.py:340
  10.5 4.1 %collective-permute-start.2 = (s32[2,4,2]{2,1,0:T(4,128)S(1)}, s32[2,4,2]{2,1,0:T(4,128)S(1)}, u32[]{:S(2)}, u32[]{:S(2)}) collective-permute-start(s32[2,4,2]{2,1,0:T(4,128)S(1)} %pad_add_fusion.token_ref.tab_ref), channel_id=1, source_target_pairs={{0,1},{1,2},{2,3},{3,0},{4,5},{5,6},{6,7},{7,4},{8,9},{9,10},{10,1... | collective-permute-start | bytes 200 | tf_op jit(solution)/shard_map/ppermute | solution.py:340
  11.3 3.3 %collective-permute-start.1 = (s32[2,4,2]{2,1,0:T(4,128)S(1)}, s32[2,4,2]{2,1,0:T(4,128)S(1)}, u32[]{:S(2)}, u32[]{:S(2)}) collective-permute-start(s32[2,4,2]{2,1,0:T(4,128)S(1)} %pad_add_fusion.token_ref.tab_ref), channel_id=1, source_target_pairs={{0,3},{1,0},{2,1},{3,2},{4,7},{5,4},{6,5},{7,6},{8,11},{9,8},{10,9... | collective-permute-start | bytes 200 | tf_op jit(solution)/shard_map/ppermute | solution.py:340
  14.6 1.6 %copy-start = (bf16[1,8,64,2048]{3,2,1,0:T(8,128)(2,1)S(1)}, bf16[1,8,64,2048]{3,2,1,0:T(8,128)(2,1)}, u32[]{:S(2)}) copy-start(bf16[1,8,64,2048]{3,2,1,0:T(8,128)(2,1)} %param.14) | copy-start | bytes 6291460
  16.2 7.6 %copy-start.2 = (bf16[1,256,2048]{2,1,0:T(8,128)(2,1)S(1)}, bf16[1,256,2048]{2,1,0:T(8,128)(2,1)}, u32[]{:S(2)}) copy-start(bf16[1,256,2048]{2,1,0:T(8,128)(2,1)} %param.8) | copy-start | bytes 3145732
  16.2 7.6 %copy-start.3 = (bf16[1,256,2048]{2,1,0:T(8,128)(2,1)S(1)}, bf16[1,256,2048]{2,1,0:T(8,128)(2,1)}, u32[]{:S(2)}) copy-start(bf16[1,256,2048]{2,1,0:T(8,128)(2,1)} %param.9) | copy-start | bytes 3145732
  16.2 7.6 %copy-start.4 = (bf16[1,256,2048]{2,1,0:T(8,128)(2,1)S(1)}, bf16[1,256,2048]{2,1,0:T(8,128)(2,1)}, u32[]{:S(2)}) copy-start(bf16[1,256,2048]{2,1,0:T(8,128)(2,1)} %param.10) | copy-start | bytes 3145732
  16.2 7.6 %copy-start.5 = (s32[1,256]{1,0:T(1,128)S(1)}, s32[1,256]{1,0:T(1,128)}, u32[]{:S(2)}) copy-start(s32[1,256]{1,0:T(1,128)} %docs_ref.1) | copy-start | bytes 3076
  20.4 23.3 %collective-permute-start.8 = (bf16[2,2,64,2048]{3,2,1,0:T(8,128)(2,1)}, bf16[2,2,64,2048]{3,2,1,0:T(8,128)(2,1)}, u32[]{:S(2)}, u32[]{:S(2)}) collective-permute-start(bf16[2,2,64,2048]{3,2,1,0:T(8,128)(2,1)} %get-tuple-element.17), channel_id=1, source_target_pairs={{0,1},{1,2},{2,3},{3,0},{4,5},{5,6},{6,7},{7,4},{8,9},{9,10},{10,1... | collective-permute-start | bytes 3145736 | tf_op jit(solution)/shard_map/ppermute | solution.py:342
  20.5 23.6 %collective-permute-start.9 = (bf16[2,2,64,2048]{3,2,1,0:T(8,128)(2,1)}, bf16[2,2,64,2048]{3,2,1,0:T(8,128)(2,1)}, u32[]{:S(2)}, u32[]{:S(2)}) collective-permute-start(bf16[2,2,64,2048]{3,2,1,0:T(8,128)(2,1)} %get-tuple-element.18), channel_id=1, source_target_pairs={{0,3},{1,0},{2,1},{3,2},{4,7},{5,4},{6,5},{7,6},{8,11},{9,8},{10,9... | collective-permute-start | bytes 3145736 | tf_op jit(solution)/shard_map/ppermute | solution.py:342
  23.2 43.2 %collective-permute-start.10 = (bf16[2,2,64,2048]{3,2,1,0:T(8,128)(2,1)}, bf16[2,2,64,2048]{3,2,1,0:T(8,128)(2,1)}, u32[]{:S(2)}, u32[]{:S(2)}) collective-permute-start(bf16[2,2,64,2048]{3,2,1,0:T(8,128)(2,1)} %get-tuple-element.19), channel_id=1, source_target_pairs={{0,2},{1,3},{2,0},{3,1},{4,6},{5,7},{6,4},{7,5},{8,10},{9,11},{10,... | collective-permute-start | bytes 3145736 | tf_op jit(solution)/shard_map/ppermute | solution.py:342
  26.5 9.2 %copy-start.1 = (bf16[1,8,64,2048]{3,2,1,0:T(8,128)(2,1)S(1)}, bf16[1,8,64,2048]{3,2,1,0:T(8,128)(2,1)}, u32[]{:S(2)}) copy-start(bf16[1,8,64,2048]{3,2,1,0:T(8,128)(2,1)} %param.14) | copy-start | bytes 6291460
  26.5 50.1 %all-to-all-start = ((bf16[16,784,128]{2,1,0:T(8,128)(2,1)}), bf16[16,784,128]{2,1,0:T(8,128)(2,1)}, u32[]{:S(2)}, u32[]{:S(2)}) async-start(bf16[16,784,128]{2,1,0:T(8,128)(2,1)} %pack_heads.1), calls=%async_computation | async-start | bytes 6422528 | tf_op jit(solution)/shard_map/all_to_all | solution.py:345
  39.7 71.1 %collective-permute-start.4 = (bf16[2,2,64,2048]{3,2,1,0:T(8,128)(2,1)}, bf16[2,2,64,2048]{3,2,1,0:T(8,128)(2,1)S(1)}, u32[]{:S(2)}, u32[]{:S(2)}) collective-permute-start(bf16[2,2,64,2048]{3,2,1,0:T(8,128)(2,1)} %get-tuple-element.11), channel_id=1, source_target_pairs={{0,1},{1,2},{2,3},{3,0},{4,5},{5,6},{6,7},{7,4},{8,9},{9,10},{10,1... | collective-permute-start | bytes 3145736 | tf_op jit(solution)/shard_map/ppermute | solution.py:350
  41.1 69.8 %collective-permute-start.5 = (bf16[2,2,64,2048]{3,2,1,0:T(8,128)(2,1)}, bf16[2,2,64,2048]{3,2,1,0:T(8,128)(2,1)}, u32[]{:S(2)}, u32[]{:S(2)}) collective-permute-start(bf16[2,2,64,2048]{3,2,1,0:T(8,128)(2,1)} %get-tuple-element.12), channel_id=1, source_target_pairs={{0,3},{1,0},{2,1},{3,2},{4,7},{5,4},{6,5},{7,6},{8,11},{9,8},{10,9... | collective-permute-start | bytes 3145736 | tf_op jit(solution)/shard_map/ppermute | solution.py:350
  43.7 67.7 %collective-permute-start.6 = (bf16[2,2,64,2048]{3,2,1,0:T(8,128)(2,1)}, bf16[2,2,64,2048]{3,2,1,0:T(8,128)(2,1)}, u32[]{:S(2)}, u32[]{:S(2)}) collective-permute-start(bf16[2,2,64,2048]{3,2,1,0:T(8,128)(2,1)} %get-tuple-element.13), channel_id=1, source_target_pairs={{0,2},{1,3},{2,0},{3,1},{4,6},{5,7},{6,4},{7,5},{8,10},{9,11},{10,... | collective-permute-start | bytes 3145736 | tf_op jit(solution)/shard_map/ppermute | solution.py:350
  73.0 38.3 %collective-permute-start.11 = (bf16[256,2176]{1,0:T(8,128)(2,1)}, bf16[256,2176]{1,0:T(8,128)(2,1)}, u32[]{:S(2)}, u32[]{:S(2)}) collective-permute-start(bf16[256,2176]{1,0:T(8,128)(2,1)} %cross_far.1), channel_id=1, source_target_pairs={{0,4},{1,5},{2,6},{3,7},{4,0},{5,1},{6,2},{7,3},{8,12},{9,13},{10,... | collective-permute-start | bytes 3342344 | tf_op jit(solution)/shard_map/ppermute | solution.py:351
  97.9 28.8 %all-to-all-start.1 = ((bf16[16,256,128]{2,1,0:T(8,128)(2,1)}), bf16[16,256,128]{2,1,0:T(8,128)(2,1)S(1)}, u32[]{:S(2)}, u32[]{:S(2)}) async-start(bf16[16,256,128]{2,1,0:T(8,128)(2,1)} %self_attention.1), calls=%async_computation.1 | async-start | bytes 2097152 | tf_op jit(solution)/shard_map/all_to_all | solution.py:354

commit v7 on v6

--- a/solution.py
+++ b/solution.py
@@ -15,7 +15,7 @@
 HD = 2048
 NZ = 4
 NC = 16
-QT = 2048
+QT = 1024
 CHUNK = 3 * TOK + 16
 NEG = -1e30
 SCALE = math.log2(math.e) / math.sqrt(DH)
@@ -52,7 +52,7 @@
         pack_heads_kernel,
         grid=(4,),
         in_specs=[
-            pl.BlockSpec((2, 4, 2), lambda i: (0, 0, 0)),
+            pl.BlockSpec((4, 4, 2), lambda i: (0, 0, 0)),
             pl.BlockSpec((1, TOK), lambda i: (0, 0)),
             wide,
             wide,
@@ -163,20 +163,23 @@
 SHIFTS = (1, 3, 2)
 
 
-def pack_spans_kernel(far, *refs):
-    tabs, keys_ref, values_ref = refs[:3], refs[3], refs[4]
-    outs, hold, loads, stores = refs[5:8], refs[8], refs[9], refs[10]
+def asked_of(tab_ref, row, owner, value):
+    first, second, seen = jnp.int32(0), jnp.int32(0), jnp.int32(0)
+    for r in range(8):
+        entry = tab_ref[row, r // 2, r % 2]
+        hit = entry // 8 == owner
+        first = jnp.where(hit & (seen == 0), value(r, entry), first)
+        second = jnp.where(hit & (seen == 1), value(r, entry), second)
+        seen = seen + jnp.where(hit, 1, 0)
+    return first, second
+
+
+def pack_spans_kernel(tab_ref, keys_ref, values_ref, *refs):
+    outs, hold, loads, stores = refs[:3], refs[3], refs[4], refs[5]
     me = lax.axis_index("db")
     moves = []
     for i in range(3):
-        first, second, seen = jnp.int32(0), jnp.int32(0), jnp.int32(0)
-        for r in range(8):
-            entry = tabs[i][far, r // 2, r % 2]
-            hit = entry // 8 == me
-            span = entry % 8
-            first = jnp.where(hit & (seen == 0), span, first)
-            second = jnp.where(hit & (seen == 1), span, second)
-            seen = seen + jnp.where(hit, 1, 0)
+        first, second = asked_of(tab_ref, 1 + i, me, lambda r, entry: entry % 8)
         for slot, span in ((0, first), (1, second)):
             for kind, src in ((0, keys_ref), (1, values_ref)):
                 at = (i, slot, kind)
@@ -190,11 +193,11 @@
         store.wait()
 
 
-def pack_spans(far, tables, keys, values):
+def pack_spans(table, keys, values):
     anywhere = pl.BlockSpec(memory_space=pl.ANY)
     return pl.pallas_call(
-        functools.partial(pack_spans_kernel, int(far)),
-        in_specs=[pl.BlockSpec(memory_space=pltpu.SMEM)] * 3 + [anywhere, anywhere],
+        pack_spans_kernel,
+        in_specs=[pl.BlockSpec(memory_space=pltpu.SMEM), anywhere, anywhere],
         out_specs=[anywhere] * 3,
         out_shape=[jax.ShapeDtypeStruct((2, 2, CH, HD), bf16)] * 3,
         scratch_shapes=[
@@ -204,20 +207,156 @@
         ],
         compiler_params=params(),
         cost_estimate=cost(0, 7 << 20),
-        name="pack_far" if far else "pack_near",
-    )(*tables, keys, values)
-
-
-def cross_kernel(far, tab_ref, q_ref, *refs):
-    keys_ref, values_ref = refs[:2]
-    got = refs[2:5]
-    if far:
-        out_ref, kbuf, vbuf, sems = refs[5:]
-    else:
-        part_ref, out_ref, kbuf, vbuf, sems = refs[5:]
+        name="pack_far",
+    )(table, keys, values)
+
+
+def pack_queries_kernel(tab_ref, q_ref, *refs):
+    outs, sems = refs[:3], refs[3]
     me = lax.axis_index("db")
     plane, z = me // NZ, me % NZ
-    row = 1 if far else 0
+    copies = []
+    for i, k in enumerate(SHIFTS):
+        for slot, n in enumerate(asked_of(tab_ref, 0, plane * NZ + (z + k) % NZ, lambda r, entry: r // 2)):
+            src = q_ref.at[pl.ds(pl.multiple_of(n * CH, CH), CH)]
+            copy = pltpu.make_async_copy(src, outs[i].at[slot], sems.at[i, slot])
+            copy.start()
+            copies.append(copy)
+    for copy in copies:
+        copy.wait()
+
+
+def pack_queries(asked, q):
+    anywhere = pl.BlockSpec(memory_space=pl.ANY)
+    return pl.pallas_call(
+        pack_queries_kernel,
+        in_specs=[pl.BlockSpec(memory_space=pltpu.SMEM), pl.BlockSpec(memory_space=pltpu.VMEM)],
+        out_specs=[anywhere] * 3,
+        out_shape=[jax.ShapeDtypeStruct((2, CH, HD), bf16)] * 3,
+        scratch_shapes=[pltpu.SemaphoreType.DMA((3, 2))],
+        compiler_params=params(),
+        cost_estimate=cost(0, 3 << 20),
+        name="pack_queries",
+    )(asked, q)
+
+
+HEADS = [slice(h * DH, (h + 1) * DH) for h in range(NH)]
+
+
+def encode(stats, lane):
+    high = stats.astype(bf16).astype(f32)
+    low = (stats - high).astype(bf16).astype(f32)
+    rest = stats - high - low
+    return jnp.where(lane < NH, high, jnp.where(lane < 2 * NH, low, rest)).astype(bf16)
+
+
+def decode(stats):
+    stats = stats.astype(f32)
+    return (stats[:, :NH] + stats[:, NH : 2 * NH]) + stats[:, 2 * NH : 3 * NH]
+
+
+def serve_kernel(tab_ref, q_ref, keys_ref, values_ref, *refs):
+    got, outs = refs[:3], refs[3:7]
+    me = lax.axis_index("db")
+    lane = lax.broadcasted_iota(i32, (1, DH), 1)
+    for i in range(4):
+        row = 0 if i == 3 else 1 + SHIFTS.index(NZ - SHIFTS[i])
+        spans = asked_of(tab_ref, row, me, lambda r, entry: entry % 8)
+        if i == 3:
+            own = asked_of(tab_ref, row, me, lambda r, entry: r // 2)
+        for slot, span in enumerate(spans):
+            if i == 3:
+                toks = pl.ds(pl.multiple_of(own[slot] * CH, CH), CH)
+                q = [q_ref[toks, c] for c in HEADS]
+            else:
+                q = [got[i][slot, :, c] for c in HEADS]
+            k = [keys_ref[span, :, c] for c in HEADS]
+            s = [
+                lax.dot_general(x, y, (((1,), (1,)), ((), ())), preferred_element_type=f32) * SCALE
+                for x, y in zip(q, k)
+            ]
+            top = [jnp.max(x, axis=1, keepdims=True) for x in s]
+            p = [jnp.exp2(x - t) for x, t in zip(s, top)]
+            total = [jnp.sum(x, axis=1, keepdims=True) for x in p]
+            o = [
+                jnp.dot(x.astype(bf16), values_ref[span, :, c], preferred_element_type=f32)
+                for x, c in zip(p, HEADS)
+            ]
+            stats = jnp.zeros((CH, DH), f32)
+            for h, c in enumerate(HEADS):
+                outs[i][slot, :, c] = (o[h] / total[h]).astype(bf16)
+                stats = jnp.where(lane % NH == h, top[h] + jnp.log2(total[h]), stats)
+            outs[i][slot, :, HD:] = encode(stats, lane)
+
+
+def serve(table, q, keys, values, got):
+    vmem = pl.BlockSpec(memory_space=pltpu.VMEM)
+    return pl.pallas_call(
+        serve_kernel,
+        in_specs=[pl.BlockSpec(memory_space=pltpu.SMEM)] + [vmem] * 6,
+        out_specs=[vmem] * 4,
+        out_shape=[jax.ShapeDtypeStruct((2, CH, HD + DH), bf16)] * 4,
+        compiler_params=params(),
+        cost_estimate=cost(4 << 30, 6 << 20),
+        name="serve",
+    )(table, q, keys, values, *got)
+
+
+def combine_kernel(tab_ref, *refs):
+    got, part_ref, out_ref, hold, sems = refs[:4], refs[4], refs[5], refs[6], refs[7]
+    me = lax.axis_index("db")
+    plane, z = me // NZ, me % NZ
+    here = []
+    for r in range(8):
+        owner = tab_ref[0, r // 2, r % 2] // 8
+        slot = jnp.int32(0)
+        for earlier in range(r):
+            slot = slot + jnp.where(tab_ref[0, earlier // 2, earlier % 2] // 8 == owner, 1, 0)
+        here.append(jnp.where(owner // NZ == plane, 1, 0))
+        shift = (owner % NZ - z + NZ) % NZ
+        for i, k in enumerate(SHIFTS + (0,)):
+
+            @pl.when(shift == k)
+            def _(i=i, slot=slot, r=r):
+                pltpu.make_async_copy(got[i].at[slot], hold.at[r], sems.at[r]).start()
+
+    for n in range(4):
+        toks = slice(n * CH, (n + 1) * CH)
+        lse = [decode(part_ref[toks, HD:])]
+        for r in (2 * n, 2 * n + 1):
+            pltpu.make_async_copy(got[0].at[0], hold.at[r], sems.at[r]).wait()
+            lse.append(jnp.where(here[r] > 0, decode(hold[r, :, HD:]), NEG))
+        high = jnp.maximum(jnp.maximum(lse[0], lse[1]), lse[2])
+        w = [jnp.exp2(x - high) for x in lse]
+        inverse = 1.0 / (w[0] + w[1] + w[2])
+        w = [x * inverse for x in w]
+        for h, c in enumerate(HEADS):
+            a, b, d = (x[:, h : h + 1] for x in w)
+            mixed = part_ref[toks, c].astype(f32) * a
+            mixed = mixed + hold[2 * n, :, c].astype(f32) * b
+            mixed = mixed + hold[2 * n + 1, :, c].astype(f32) * d
+            out_ref[toks, c] = mixed.astype(bf16)
+
+
+def combine(asked, got, part):
+    vmem = pl.BlockSpec(memory_space=pltpu.VMEM)
+    return pl.pallas_call(
+        combine_kernel,
+        in_specs=[pl.BlockSpec(memory_space=pltpu.SMEM)] + [pl.BlockSpec(memory_space=pl.ANY)] * 4 + [vmem],
+        out_specs=vmem,
+        out_shape=jax.ShapeDtypeStruct((TOK, HD), bf16),
+        scratch_shapes=[pltpu.VMEM((8, CH, HD + DH), bf16), pltpu.SemaphoreType.DMA((8,))],
+        compiler_params=params(),
+        cost_estimate=cost(1 << 26, 4 << 20),
+        name="combine",
+    )(asked, *got, part)
+
+
+def cross_kernel(tab_ref, q_ref, keys_ref, values_ref, *refs):
+    got, out_ref, kbuf, vbuf, sems = refs[:3], refs[3], refs[4], refs[5], refs[6]
+    me = lax.axis_index("db")
+    plane, z = me // NZ, me % NZ
+    row = 0
     here = []
     for r in range(8):
         owner = tab_ref[row, r // 2, r % 2] // 8
@@ -261,54 +400,32 @@
         p = [jnp.where(mine, jnp.exp2(x - t), 0.0) for x, t in zip(s, top)]
         total = [jnp.sum(x, axis=1, keepdims=True) for x in p]
         o = [jnp.dot(x.astype(bf16), vbuf[n, :, c], preferred_element_type=f32) for x, c in zip(p, heads)]
-        if far:
-            stats = jnp.full((CH, DH), NEG, f32)
-            for h, c in enumerate(heads):
-                safe = jnp.maximum(total[h], 1e-30)
-                out_ref[toks, c] = (o[h] / safe).astype(bf16)
-                lse = jnp.where(total[h] > 0, top[h] + jnp.log2(safe), NEG)
-                stats = jnp.where(lane % NH == h, lse, stats)
-            high = stats.astype(bf16).astype(f32)
-            low = (stats - high).astype(bf16).astype(f32)
-            rest = stats - high - low
-            stats = jnp.where(lane < NH, high, jnp.where(lane < 2 * NH, low, rest))
-            out_ref[toks, HD:] = stats.astype(bf16)
-        else:
-            stats = part_ref[toks, HD:].astype(f32)
-            other = (stats[:, :NH] + stats[:, NH : 2 * NH]) + stats[:, 2 * NH : 3 * NH]
-            tops = jnp.full((CH, NH), NEG, f32)
-            sums = jnp.zeros((CH, NH), f32)
-            slot = lax.broadcasted_iota(i32, (1, NH), 1)
-            for h in range(NH):
-                tops = jnp.where(slot == h, top[h], tops)
-                sums = jnp.where(slot == h, total[h], sums)
-            high = jnp.maximum(tops, other)
-            a, b = jnp.exp2(tops - high), jnp.exp2(other - high)
-            inverse = 1.0 / (sums * a + b)
-            a, b = a * inverse, b * inverse
-            for h, c in enumerate(heads):
-                mixed = o[h] * a[:, h : h + 1] + part_ref[toks, c].astype(f32) * b[:, h : h + 1]
-                out_ref[toks, c] = mixed.astype(bf16)
-
-
-def cross(far, table, q, keys, values, got, part=()):
+        stats = jnp.full((CH, DH), NEG, f32)
+        for h, c in enumerate(heads):
+            safe = jnp.maximum(total[h], 1e-30)
+            out_ref[toks, c] = (o[h] / safe).astype(bf16)
+            lse = jnp.where(total[h] > 0, top[h] + jnp.log2(safe), NEG)
+            stats = jnp.where(lane % NH == h, lse, stats)
+        out_ref[toks, HD:] = encode(stats, lane)
+
+
+def cross(table, q, keys, values, got):
     vmem = pl.BlockSpec(memory_space=pltpu.VMEM)
     return pl.pallas_call(
-        functools.partial(cross_kernel, far),
+        cross_kernel,
         in_specs=[pl.BlockSpec(memory_space=pltpu.SMEM), vmem]
-        + [pl.BlockSpec(memory_space=pl.ANY)] * 5
-        + [vmem] * len(part),
+        + [pl.BlockSpec(memory_space=pl.ANY)] * 5,
         out_specs=vmem,
-        out_shape=jax.ShapeDtypeStruct((TOK, HD + DH if far else HD), bf16),
+        out_shape=jax.ShapeDtypeStruct((TOK, HD + DH), bf16),
         scratch_shapes=[
             pltpu.VMEM((4, 2 * CH, HD), bf16),
             pltpu.VMEM((4, 2 * CH, HD), bf16),
             pltpu.SemaphoreType.DMA((8, 2)),
         ],
         compiler_params=params(),
-        cost_estimate=pl.CostEstimate(flops=32 << 30 if far else 1 << 26, bytes_accessed=0, transcendentals=0),
-        name="cross_far" if far else "cross_near",
-    )(table, q, keys, values, *got, *part)
+        cost_estimate=pl.CostEstimate(flops=20 << 30, bytes_accessed=0, transcendentals=0),
+        name="cross_far",
+    )(table, q, keys, values, *got)
 
 
 def arrived_kernel(*refs):
@@ -333,29 +450,30 @@
     q, db_k, db_v = queries[0], db_keys[0], db_values[0]
     swap = [(d, (d + NZ) % 8) for d in range(8)]
     turn = lambda k: [(s * NZ + z, s * NZ + (z + k) % NZ) for s in range(2) for z in range(NZ)]
+
+    asked = lax.optimization_barrier(nbr_owner * 8 + nbr_local)
+    table = jnp.concatenate([asked] + [lax.ppermute(asked, "db", turn(NZ - k)) for k in SHIFTS], axis=0)
+    table = lax.optimization_barrier(table)
+    far_table = lax.ppermute(table, "db", swap)
     far_q = lax.ppermute(q, "db", swap)
-
-    asked = lax.optimization_barrier(nbr_owner * 8 + nbr_local)
-    table = jnp.concatenate([asked, lax.ppermute(asked, "db", swap)], axis=0)
-    tables = [lax.ppermute(table, "db", turn(NZ - k)) for k in SHIFTS]
-    far = pack_spans(True, tables, db_k, db_v)
-    far_got = [lax.ppermute(x, "db", turn(k)) for x, k in zip(far, SHIFTS)]
+    sent = pack_queries(asked, q)
+    sent = [lax.ppermute(x, "db", turn(k)) for x, k in zip(sent, SHIFTS)]
 
     heads = pack_heads(table, doc_ids, q, keys[0], values[0])
     heads = lax.all_to_all(heads, "ctx", split_axis=0, concat_axis=0, tiled=True)
 
-    near = pack_spans(False, tables, db_k, db_v)
-    near_got = []
-    for i, k in enumerate(SHIFTS):
-        near_got.append(lax.ppermute(near[i], "db", turn(k)))
-    part = lax.ppermute(cross(True, table, far_q, db_k, db_v, far_got), "db", swap)
+    far = pack_spans(far_table, db_k, db_v)
+    far_got = [lax.ppermute(x, "db", turn(k)) for x, k in zip(far, SHIFTS)]
+    *near, own = serve(table, q, db_k, db_v, sent)
+    near_got = [lax.ppermute(x, "db", turn(NZ - k)) for x, k in zip(near, SHIFTS)]
+    part = lax.ppermute(cross(far_table, far_q, db_k, db_v, far_got), "db", swap)
 
     self_rows = self_attention(heads)
     self_rows = lax.all_to_all(self_rows, "ctx", split_axis=0, concat_axis=0, tiled=True)
     self_rows = unpack_heads(self_rows)
 
     near_got = arrived(near_got)
-    cross_rows = cross(False, table, q, db_k, db_v, near_got, (part,))
+    cross_rows = combine(asked, list(near_got) + [own], part)
     return self_rows[None], cross_rows[None]
 
 

time: 129 us -> 157 us (1.22)
  the two profiles are of different devices: /device:TPU:1 before, /device:TPU:96 now
where the time goes in v7:
time: 157 us; the launch traced here: 156 us
  waiting for transfers between devices  62.1 us (40%)
  Pallas kernels  52.4 us (33%)
  starting transfers between devices  32 us (20%)
  local copies, waits for them, and re-layouts  8.6 us (5%)
    ppermute x3, waiting for transfers between devices, per_device(): sent = [lax.ppermute(x, 'db', turn(k)) for x, k in zip(sent, SHIFTS)]  41.7 us
    pallas_call x1, Pallas kernels, self_attention(): pl.pallas_call(self_kernel, in_specs=[pl.BlockSpec(memory_space=pltpu.VME...  20.6 us
    all_to_all x1, waiting for transfers between devices, per_device(): lax.all_to_all(self_rows, 'ctx', split_axis=0, concat_axis=0, tiled=True)  9.51 us
    ppermute x3, waiting for transfers between devices, per_device(): lax.ppermute(asked, 'db', turn(NZ - k))  9.23 us
    unnamed x22, local copies, waits for them, and re-layouts  8.6 us
    pallas_call x1, Pallas kernels, cross(): pl.pallas_call(cross_kernel, in_specs=[pl.BlockSpec(memory_space=pltpu.SM...  7.11 us
    pallas_call x1, Pallas kernels, serve(): pl.pallas_call(serve_kernel, in_specs=[pl.BlockSpec(memory_space=pltpu.SM...  6.86 us
    pallas_call x1, Pallas kernels, combine(): pl.pallas_call(combine_kernel, in_specs=[pl.BlockSpec(memory_space=pltpu....  6.02 us
  transfers between devices with their start and end apart: 17, of which 5 were waited for; matrix products, arithmetic and copies ran while one was open for 0% of the time, Pallas kernels for 31%

profile of v7, /device:TPU:96, one launch (start us, length us, event | category | flops | bytes accessed | tf_op | source)
XLA Modules:
  0.0 155.9 jit_solution(8647506073463863821)
XLA Ops:
  0.6 0.8 copy.13
  1.4 0.8 copy.14
  2.2 2.3 %pack_queries.1 = (bf16[2,64,2048]{2,1,0:T(8,128)(2,1)S(1)}, bf16[2,64,2048]{2,1,0:T(8,128)(2,1)}, bf16[2,64,2048]{2,1,0:T(8,128)(2,1)S(1)}) custom-call(s32[1,4,2]{2,1,0:T(4,128)S(1)} %multiply_add_fusion.tab_ref, bf16[256,2048]{1,0:T(8,128)(2,1)} %bitcast.q_ref), custom_call_target="tpu_custom_call" | custom-call | bytes 196608 | tf_op jit(solution)/shard_map/pack_queries/pallas_call | solution.py:231
  4.4 0.8 copy-done.9
  5.2 0.0 collective-permute-start.3
  5.2 2.0 %collective-permute-start = (s32[1,4,2]{2,1,0:T(4,128)S(1)}, s32[1,4,2]{2,1,0:T(4,128)S(1)}, u32[]{:S(2)}, u32[]{:S(2)}) collective-permute-start(s32[1,4,2]{2,1,0:T(4,128)S(1)} %multiply_add_fusion.tab_ref), channel_id=1, source_target_pairs={{0,3},{1,0},{2,1},{3,2},{4,7},{5,4},{6,5},{7,6},{8,11},{9,8},{10,9... | collective-permute-start | bytes 104 | tf_op jit(solution)/shard_map/ppermute | solution.py:455
  7.2 1.2 collective-permute-start.1
  8.5 1.3 collective-permute-start.2
  9.7 0.0 collective-permute-start.4
  9.7 0.3 collective-permute-done
  10.0 8.9 %collective-permute-done.1 = s32[1,4,2]{2,1,0:T(4,128)S(1)} collective-permute-done((s32[1,4,2]{2,1,0:T(4,128)S(1)}, s32[1,4,2]{2,1,0:T(4,128)S(1)}, u32[]{:S(2)}, u32[]{:S(2)}) %collective-permute-start.1) | collective-permute-done | bytes 64 | tf_op jit(solution)/shard_map/ppermute | solution.py:455
  18.9 0.0 collective-permute-done.2
  19.0 3.1 %collective-permute-start.9 = (s32[4,4,2]{2,1,0:T(4,128)S(1)}, s32[4,4,2]{2,1,0:T(4,128)S(1)}, u32[]{:S(2)}, u32[]{:S(2)}) collective-permute-start(s32[4,4,2]{2,1,0:T(4,128)S(1)} %pad_add_fusion.token_ref.tab_ref), channel_id=1, source_target_pairs={{0,4},{1,5},{2,6},{3,7},{4,0},{5,1},{6,2},{7,3},{8,12},{9,13},{10,... | collective-permute-start | bytes 392 | tf_op jit(solution)/shard_map/ppermute | solution.py:457
  22.1 0.5 collective-permute-start.10
  22.6 1.6 %collective-permute-done.9.tab_ref = s32[4,4,2]{2,1,0:T(4,128)S(1)} collective-permute-done((s32[4,4,2]{2,1,0:T(4,128)S(1)}, s32[4,4,2]{2,1,0:T(4,128)S(1)}, u32[]{:S(2)}, u32[]{:S(2)}) %collective-permute-start.9) | collective-permute-done | bytes 160 | tf_op jit(solution)/shard_map/ppermute | solution.py:457
  24.2 1.6 %copy-done = bf16[1,8,64,2048]{3,2,1,0:T(8,128)(2,1)S(1)} copy-done((bf16[1,8,64,2048]{3,2,1,0:T(8,128)(2,1)S(1)}, bf16[1,8,64,2048]{3,2,1,0:T(8,128)(2,1)}, u32[]{:S(2)}) %copy-start) | copy-done | bytes 2097176
  25.8 4.0 %pack_far.1 = (bf16[2,2,64,2048]{3,2,1,0:T(8,128)(2,1)}, bf16[2,2,64,2048]{3,2,1,0:T(8,128)(2,1)}, bf16[2,2,64,2048]{3,2,1,0:T(8,128)(2,1)}) custom-call(s32[4,4,2]{2,1,0:T(4,128)S(1)} %collective-permute-done.9.tab_ref, bf16[8,64,2048]{2,1,0:T(8,128)(2,1)S(1)} %bitcast.9, bf16[8,64,2048]{2,1,0:T(8,128)(2,1)} %bitcast.12), custom_call_target="tpu_custom_call" | custom-call | bytes 458752 | tf_op jit(solution)/shard_map/pack_far/pallas_call | solution.py:198
  29.8 2.2 %collective-permute-start.11 = (bf16[2,2,64,2048]{3,2,1,0:T(8,128)(2,1)}, bf16[2,2,64,2048]{3,2,1,0:T(8,128)(2,1)}, u32[]{:S(2)}, u32[]{:S(2)}) collective-permute-start(bf16[2,2,64,2048]{3,2,1,0:T(8,128)(2,1)} %get-tuple-element.25), channel_id=1, source_target_pairs={{0,1},{1,2},{2,3},{3,0},{4,5},{5,6},{6,7},{7,4},{8,9},{9,10},{10,1... | collective-permute-start | bytes 3145736 | tf_op jit(solution)/shard_map/ppermute | solution.py:466
  32.0 0.0 collective-permute-start.12
  32.0 0.0 collective-permute-done.3.refs_0_
  32.0 0.8 copy-done.6
  32.8 1.5 collective-permute-start.13
  34.4 4.0 %pack_heads.1 = bf16[16,784,128]{2,1,0:T(8,128)(2,1)} custom-call(s32[4,4,2]{2,1,0:T(4,128)S(1)} %pad_add_fusion.token_ref.tab_ref, s32[1,256]{1,0:T(1,128)S(1)} %copy-done.8, bf16[256,2048]{1,0:T(8,128)(2,1)} %bitcast.q_ref, bf16[256,2048]{1,0:T(8,128)(2,1)S(1)} %bitcast.10, bf16[256,2048]{1,0:T(8,128)(2,1)S(1)} %bitcast.11), custom_call_target="tpu_custom_call" | custom-call | bytes 393216 | tf_op jit(solution)/shard_map/pack_heads/pallas_call | solution.py:51
  38.4 5.9 %all-to-all-start = ((bf16[16,784,128]{2,1,0:T(8,128)(2,1)}), bf16[16,784,128]{2,1,0:T(8,128)(2,1)S(1)}, u32[]{:S(2)}, u32[]{:S(2)}) async-start(bf16[16,784,128]{2,1,0:T(8,128)(2,1)} %pack_heads.1), calls=%async_computation | async-start | bytes 6422528 | tf_op jit(solution)/shard_map/all_to_all | solution.py:463
  44.3 0.0 collective-permute-done.4.refs_1_
  44.3 2.1 %collective-permute-start.5 = (bf16[2,64,2048]{2,1,0:T(8,128)(2,1)}, bf16[2,64,2048]{2,1,0:T(8,128)(2,1)S(1)}, u32[]{:S(2)}, u32[]{:S(2)}) collective-permute-start(bf16[2,64,2048]{2,1,0:T(8,128)(2,1)} %copy-done.9), channel_id=1, source_target_pairs={{0,2},{1,3},{2,0},{3,1},{4,6},{5,7},{6,4},{7,5},{8,10},{9,11},{10,... | collective-permute-start | bytes 1572872 | tf_op jit(solution)/shard_map/ppermute | solution.py:460
  46.4 41.7 %collective-permute-done.5.refs_2_ = bf16[2,64,2048]{2,1,0:T(8,128)(2,1)S(1)} collective-permute-done((bf16[2,64,2048]{2,1,0:T(8,128)(2,1)}, bf16[2,64,2048]{2,1,0:T(8,128)(2,1)S(1)}, u32[]{:S(2)}, u32[]{:S(2)}) %collective-permute-start.5) | collective-permute-done | bytes 524320 | tf_op jit(solution)/shard_map/ppermute | solution.py:460
  88.1 1.0 copy-done.7
  89.1 6.9 %serve.1 = (bf16[2,64,2176]{2,1,0:T(8,128)(2,1)}, bf16[2,64,2176]{2,1,0:T(8,128)(2,1)}, bf16[2,64,2176]{2,1,0:T(8,128)(2,1)}, bf16[2,64,2176]{2,1,0:T(8,128)(2,1)S(1)}) custom-call(s32[4,4,2]{2,1,0:T(4,128)S(1)} %pad_add_fusion.token_ref.tab_ref, bf16[256,2048]{1,0:T(8,128)(2,1)} %bitcast.q_ref, bf16[8,64,2048]{2,1,0:T(8,128)(2,1)} %bitcast.7, ...), custom_call_target="tpu_custom_call" | custom-call | flops 67108864 | bytes 393216 | tf_op jit(solution)/shard_map/serve/pallas_call | solution.py:294
  96.0 0.9 copy-done.4
  96.9 0.0 collective-permute-start.6
  96.9 0.0 collective-permute-done.10.q_ref
  96.9 3.2 %collective-permute-start.7 = (bf16[2,64,2176]{2,1,0:T(8,128)(2,1)}, bf16[2,64,2176]{2,1,0:T(8,128)(2,1)}, u32[]{:S(2)}, u32[]{:S(2)}) collective-permute-start(bf16[2,64,2176]{2,1,0:T(8,128)(2,1)} %get-tuple-element.19), channel_id=1, source_target_pairs={{0,1},{1,2},{2,3},{3,0},{4,5},{5,6},{6,7},{7,4},{8,9},{9,10},{10,1... | collective-permute-start | bytes 1671176 | tf_op jit(solution)/shard_map/ppermute | solution.py:468
  100.1 0.0 collective-permute-done.11.refs_0_
  100.1 0.7 collective-permute-start.8
  100.8 0.0 collective-permute-done.12.refs_1_
  100.8 0.0 collective-permute-done.13.refs_2_
  100.8 7.1 %cross_far.1 = bf16[256,2176]{1,0:T(8,128)(2,1)} custom-call(s32[4,4,2]{2,1,0:T(4,128)S(1)} %collective-permute-done.9.tab_ref, bf16[256,2048]{1,0:T(8,128)(2,1)} %collective-permute-done.10.q_ref, bf16[8,64,2048]{2,1,0:T(8,128)(2,1)} %bitcast.8, bf16[8,64,2048]{2,1,0:T(8,128)(2,1)} %bitcast.14, bf16[2,2,64,2048]{3,2,1,0:T(8,128)(2,1)} %collective-permute-done.11.refs_0_, ...), custom_call_target="tpu_custom_call" | custom-call | flops 21474836480 | tf_op jit(solution)/shard_map/cross_far/pallas_call | solution.py:414
  107.9 3.8 %collective-permute-start.14 = (bf16[256,2176]{1,0:T(8,128)(2,1)}, bf16[256,2176]{1,0:T(8,128)(2,1)}, u32[]{:S(2)}, u32[]{:S(2)}) collective-permute-start(bf16[256,2176]{1,0:T(8,128)(2,1)} %cross_far.1), channel_id=1, source_target_pairs={{0,4},{1,5},{2,6},{3,7},{4,0},{5,1},{6,2},{7,3},{8,12},{9,13},{10,... | collective-permute-start | bytes 3342344 | tf_op jit(solution)/shard_map/ppermute | solution.py:469
  111.7 20.6 %self_attention.1 = bf16[16,256,128]{2,1,0:T(8,128)(2,1)S(1)} custom-call(bf16[16,784,128]{2,1,0:T(8,128)(2,1)S(1)} %all-to-all-done.x_ref), custom_call_target="tpu_custom_call" | custom-call | flops 268435456 | bytes 262144 | tf_op jit(solution)/shard_map/self_attention/pallas_call | solution.py:152
  132.3 0.0 copy-start.1
  132.3 1.0 copy-done.1
  133.3 4.5 %all-to-all-start.1 = ((bf16[16,256,128]{2,1,0:T(8,128)(2,1)}), bf16[16,256,128]{2,1,0:T(8,128)(2,1)S(1)}, u32[]{:S(2)}, u32[]{:S(2)}) async-start(bf16[16,256,128]{2,1,0:T(8,128)(2,1)} %copy-done.1), calls=%async_computation.1 | async-start | bytes 2097152 | tf_op jit(solution)/shard_map/all_to_all | solution.py:472
  137.8 0.0 collective-permute-done.8.refs_2_
  137.8 1.0 copy-done.5
  138.8 6.0 %combine.1 = bf16[256,2048]{1,0:T(8,128)(2,1)} custom-call(s32[1,4,2]{2,1,0:T(4,128)S(1)} %multiply_add_fusion.tab_ref, bf16[2,64,2176]{2,1,0:T(8,128)(2,1)} %get-tuple-element.21.refs_0_, bf16[2,64,2176]{2,1,0:T(8,128)(2,1)} %get-tuple-element.22.refs_1_, bf16[2,64,2176]{2,1,0:T(8,128)(2,1)} %get-tuple-element.23.refs_2_, ...), custom_call_target="tpu_custom_call" | custom-call | flops 1048576 | bytes 262144 | tf_op jit(solution)/shard_map/combine/pallas_call | solution.py:343
  144.9 9.5 %all-to-all-done.1.x_ref = bf16[16,256,128]{2,1,0:T(8,128)(2,1)S(1)} async-done(((bf16[16,256,128]{2,1,0:T(8,128)(2,1)}), bf16[16,256,128]{2,1,0:T(8,128)(2,1)S(1)}, u32[]{:S(2)}, u32[]{:S(2)}) %all-to-all-start.1) | async-done | bytes 1048608 | tf_op jit(solution)/shard_map/all_to_all | solution.py:472
  154.4 1.6 %unpack_heads.1 = bf16[256,2048]{1,0:T(8,128)(2,1)} custom-call(bf16[16,256,128]{2,1,0:T(8,128)(2,1)S(1)} %all-to-all-done.1.x_ref), custom_call_target="tpu_custom_call" | custom-call | bytes 131072 | tf_op jit(solution)/shard_map/unpack_heads/pallas_call | solution.py:75
  (19 shorter events, 0.0 us)
Async XLA Ops:
  4.4 0.8 copy-start.9
  5.2 26.8 %collective-permute-start.3 = (bf16[2,64,2048]{2,1,0:T(8,128)(2,1)S(1)}, bf16[2,64,2048]{2,1,0:T(8,128)(2,1)S(1)}, u32[]{:S(2)}, u32[]{:S(2)}) collective-permute-start(bf16[2,64,2048]{2,1,0:T(8,128)(2,1)S(1)} %get-tuple-element.15), channel_id=1, source_target_pairs={{0,1},{1,2},{2,3},{3,0},{4,5},{5,6},{6,7},{7,4},{8,9},{9,10},{10,1... | collective-permute-start | bytes 1572872 | tf_op jit(solution)/shard_map/ppermute | solution.py:460
  5.2 4.8 %collective-permute-start = (s32[1,4,2]{2,1,0:T(4,128)S(1)}, s32[1,4,2]{2,1,0:T(4,128)S(1)}, u32[]{:S(2)}, u32[]{:S(2)}) collective-permute-start(s32[1,4,2]{2,1,0:T(4,128)S(1)} %multiply_add_fusion.tab_ref), channel_id=1, source_target_pairs={{0,3},{1,0},{2,1},{3,2},{4,7},{5,4},{6,5},{7,6},{8,11},{9,8},{10,9... | collective-permute-start | bytes 104 | tf_op jit(solution)/shard_map/ppermute | solution.py:455
  7.2 11.7 %collective-permute-start.1 = (s32[1,4,2]{2,1,0:T(4,128)S(1)}, s32[1,4,2]{2,1,0:T(4,128)S(1)}, u32[]{:S(2)}, u32[]{:S(2)}) collective-permute-start(s32[1,4,2]{2,1,0:T(4,128)S(1)} %multiply_add_fusion.tab_ref), channel_id=1, source_target_pairs={{0,1},{1,2},{2,3},{3,0},{4,5},{5,6},{6,7},{7,4},{8,9},{9,10},{10,1... | collective-permute-start | bytes 104 | tf_op jit(solution)/shard_map/ppermute | solution.py:455
  8.5 10.5 %collective-permute-start.2 = (s32[1,4,2]{2,1,0:T(4,128)S(1)}, s32[1,4,2]{2,1,0:T(4,128)S(1)}, u32[]{:S(2)}, u32[]{:S(2)}) collective-permute-start(s32[1,4,2]{2,1,0:T(4,128)S(1)} %multiply_add_fusion.tab_ref), channel_id=1, source_target_pairs={{0,2},{1,3},{2,0},{3,1},{4,6},{5,7},{6,4},{7,5},{8,10},{9,11},{10,... | collective-permute-start | bytes 104 | tf_op jit(solution)/shard_map/ppermute | solution.py:455
  9.7 34.6 %collective-permute-start.4 = (bf16[2,64,2048]{2,1,0:T(8,128)(2,1)}, bf16[2,64,2048]{2,1,0:T(8,128)(2,1)}, u32[]{:S(2)}, u32[]{:S(2)}) collective-permute-start(bf16[2,64,2048]{2,1,0:T(8,128)(2,1)} %get-tuple-element.16), channel_id=1, source_target_pairs={{0,3},{1,0},{2,1},{3,2},{4,7},{5,4},{6,5},{7,6},{8,11},{9,8},{10,9... | collective-permute-start | bytes 1572872 | tf_op jit(solution)/shard_map/ppermute | solution.py:460
  19.0 5.2 %collective-permute-start.9 = (s32[4,4,2]{2,1,0:T(4,128)S(1)}, s32[4,4,2]{2,1,0:T(4,128)S(1)}, u32[]{:S(2)}, u32[]{:S(2)}) collective-permute-start(s32[4,4,2]{2,1,0:T(4,128)S(1)} %pad_add_fusion.token_ref.tab_ref), channel_id=1, source_target_pairs={{0,4},{1,5},{2,6},{3,7},{4,0},{5,1},{6,2},{7,3},{8,12},{9,13},{10,... | collective-permute-start | bytes 392 | tf_op jit(solution)/shard_map/ppermute | solution.py:457
  22.1 74.8 %collective-permute-start.10 = (bf16[256,2048]{1,0:T(8,128)(2,1)}, bf16[256,2048]{1,0:T(8,128)(2,1)}, u32[]{:S(2)}, u32[]{:S(2)}) collective-permute-start(bf16[256,2048]{1,0:T(8,128)(2,1)} %bitcast.q_ref), channel_id=1, source_target_pairs={{0,4},{1,5},{2,6},{3,7},{4,0},{5,1},{6,2},{7,3},{8,12},{9,13},{10,... | collective-permute-start | bytes 3145736 | tf_op jit(solution)/shard_map/ppermute | solution.py:458
  24.2 1.6 %copy-start = (bf16[1,8,64,2048]{3,2,1,0:T(8,128)(2,1)S(1)}, bf16[1,8,64,2048]{3,2,1,0:T(8,128)(2,1)}, u32[]{:S(2)}) copy-start(bf16[1,8,64,2048]{3,2,1,0:T(8,128)(2,1)} %param.14) | copy-start | bytes 6291460
  25.8 8.6 %copy-start.2 = (bf16[1,256,2048]{2,1,0:T(8,128)(2,1)S(1)}, bf16[1,256,2048]{2,1,0:T(8,128)(2,1)}, u32[]{:S(2)}) copy-start(bf16[1,256,2048]{2,1,0:T(8,128)(2,1)} %param.9) | copy-start | bytes 3145732
  25.8 8.6 %copy-start.3 = (bf16[1,256,2048]{2,1,0:T(8,128)(2,1)S(1)}, bf16[1,256,2048]{2,1,0:T(8,128)(2,1)}, u32[]{:S(2)}) copy-start(bf16[1,256,2048]{2,1,0:T(8,128)(2,1)} %param.10) | copy-start | bytes 3145732
  25.8 8.6 %copy-start.8 = (s32[1,256]{1,0:T(1,128)S(1)}, s32[1,256]{1,0:T(1,128)}, u32[]{:S(2)}) copy-start(s32[1,256]{1,0:T(1,128)} %docs_ref.1) | copy-start | bytes 3076
  29.8 70.3 %collective-permute-start.11 = (bf16[2,2,64,2048]{3,2,1,0:T(8,128)(2,1)}, bf16[2,2,64,2048]{3,2,1,0:T(8,128)(2,1)}, u32[]{:S(2)}, u32[]{:S(2)}) collective-permute-start(bf16[2,2,64,2048]{3,2,1,0:T(8,128)(2,1)} %get-tuple-element.25), channel_id=1, source_target_pairs={{0,1},{1,2},{2,3},{3,0},{4,5},{5,6},{6,7},{7,4},{8,9},{9,10},{10,1... | collective-permute-start | bytes 3145736 | tf_op jit(solution)/shard_map/ppermute | solution.py:466
  32.0 68.8 %collective-permute-start.12 = (bf16[2,2,64,2048]{3,2,1,0:T(8,128)(2,1)}, bf16[2,2,64,2048]{3,2,1,0:T(8,128)(2,1)}, u32[]{:S(2)}, u32[]{:S(2)}) collective-permute-start(bf16[2,2,64,2048]{3,2,1,0:T(8,128)(2,1)} %get-tuple-element.26), channel_id=1, source_target_pairs={{0,3},{1,0},{2,1},{3,2},{4,7},{5,4},{6,5},{7,6},{8,11},{9,8},{10,9... | collective-permute-start | bytes 3145736 | tf_op jit(solution)/shard_map/ppermute | solution.py:466
  32.0 0.8 copy-start.6
  32.8 68.0 %collective-permute-start.13 = (bf16[2,2,64,2048]{3,2,1,0:T(8,128)(2,1)}, bf16[2,2,64,2048]{3,2,1,0:T(8,128)(2,1)}, u32[]{:S(2)}, u32[]{:S(2)}) collective-permute-start(bf16[2,2,64,2048]{3,2,1,0:T(8,128)(2,1)} %get-tuple-element.27), channel_id=1, source_target_pairs={{0,2},{1,3},{2,0},{3,1},{4,6},{5,7},{6,4},{7,5},{8,10},{9,11},{10,... | collective-permute-start | bytes 3145736 | tf_op jit(solution)/shard_map/ppermute | solution.py:466
  38.4 73.3 %all-to-all-start = ((bf16[16,784,128]{2,1,0:T(8,128)(2,1)}), bf16[16,784,128]{2,1,0:T(8,128)(2,1)S(1)}, u32[]{:S(2)}, u32[]{:S(2)}) async-start(bf16[16,784,128]{2,1,0:T(8,128)(2,1)} %pack_heads.1), calls=%async_computation | async-start | bytes 6422528 | tf_op jit(solution)/shard_map/all_to_all | solution.py:463
  44.3 43.8 %collective-permute-start.5 = (bf16[2,64,2048]{2,1,0:T(8,128)(2,1)}, bf16[2,64,2048]{2,1,0:T(8,128)(2,1)S(1)}, u32[]{:S(2)}, u32[]{:S(2)}) collective-permute-start(bf16[2,64,2048]{2,1,0:T(8,128)(2,1)} %copy-done.9), channel_id=1, source_target_pairs={{0,2},{1,3},{2,0},{3,1},{4,6},{5,7},{6,4},{7,5},{8,10},{9,11},{10,... | collective-permute-start | bytes 1572872 | tf_op jit(solution)/shard_map/ppermute | solution.py:460
  88.1 1.0 copy-start.7
  96.0 0.9 copy-start.4
  96.9 40.9 %collective-permute-start.6 = (bf16[2,64,2176]{2,1,0:T(8,128)(2,1)}, bf16[2,64,2176]{2,1,0:T(8,128)(2,1)}, u32[]{:S(2)}, u32[]{:S(2)}) collective-permute-start(bf16[2,64,2176]{2,1,0:T(8,128)(2,1)} %get-tuple-element.18), channel_id=1, source_target_pairs={{0,3},{1,0},{2,1},{3,2},{4,7},{5,4},{6,5},{7,6},{8,11},{9,8},{10,9... | collective-permute-start | bytes 1671176 | tf_op jit(solution)/shard_map/ppermute | solution.py:468
  96.9 40.9 %collective-permute-start.7 = (bf16[2,64,2176]{2,1,0:T(8,128)(2,1)}, bf16[2,64,2176]{2,1,0:T(8,128)(2,1)}, u32[]{:S(2)}, u32[]{:S(2)}) collective-permute-start(bf16[2,64,2176]{2,1,0:T(8,128)(2,1)} %get-tuple-element.19), channel_id=1, source_target_pairs={{0,1},{1,2},{2,3},{3,0},{4,5},{5,6},{6,7},{7,4},{8,9},{9,10},{10,1... | collective-permute-start | bytes 1671176 | tf_op jit(solution)/shard_map/ppermute | solution.py:468
  100.1 37.7 %collective-permute-start.8 = (bf16[2,64,2176]{2,1,0:T(8,128)(2,1)}, bf16[2,64,2176]{2,1,0:T(8,128)(2,1)}, u32[]{:S(2)}, u32[]{:S(2)}) collective-permute-start(bf16[2,64,2176]{2,1,0:T(8,128)(2,1)} %get-tuple-element.20), channel_id=1, source_target_pairs={{0,2},{1,3},{2,0},{3,1},{4,6},{5,7},{6,4},{7,5},{8,10},{9,11},{10,... | collective-permute-start | bytes 1671176 | tf_op jit(solution)/shard_map/ppermute | solution.py:468
  107.9 29.9 %collective-permute-start.14 = (bf16[256,2176]{1,0:T(8,128)(2,1)}, bf16[256,2176]{1,0:T(8,128)(2,1)}, u32[]{:S(2)}, u32[]{:S(2)}) collective-permute-start(bf16[256,2176]{1,0:T(8,128)(2,1)} %cross_far.1), channel_id=1, source_target_pairs={{0,4},{1,5},{2,6},{3,7},{4,0},{5,1},{6,2},{7,3},{8,12},{9,13},{10,... | collective-permute-start | bytes 3342344 | tf_op jit(solution)/shard_map/ppermute | solution.py:469
  132.3 1.0 copy-start.1
  133.3 21.1 %all-to-all-start.1 = ((bf16[16,256,128]{2,1,0:T(8,128)(2,1)}), bf16[16,256,128]{2,1,0:T(8,128)(2,1)S(1)}, u32[]{:S(2)}, u32[]{:S(2)}) async-start(bf16[16,256,128]{2,1,0:T(8,128)(2,1)} %copy-done.1), calls=%async_computation.1 | async-start | bytes 2097152 | tf_op jit(solution)/shard_map/all_to_all | solution.py:472
  137.8 1.1 copy-start.5

commit v8 on v7

--- a/solution.py
+++ b/solution.py
@@ -52,7 +52,7 @@
         pack_heads_kernel,
         grid=(4,),
         in_specs=[
-            pl.BlockSpec((4, 4, 2), lambda i: (0, 0, 0)),
+            pl.BlockSpec(memory_space=pl.ANY),
             pl.BlockSpec((1, TOK), lambda i: (0, 0)),
             wide,
             wide,
@@ -174,7 +174,7 @@
     return first, second
 
 
-def pack_spans_kernel(tab_ref, keys_ref, values_ref, *refs):
+def pack_spans_kernel(tab_ref, keys_ref, values_ref, after_ref, *refs):
     outs, hold, loads, stores = refs[:3], refs[3], refs[4], refs[5]
     me = lax.axis_index("db")
     moves = []
@@ -193,11 +193,11 @@
         store.wait()
 
 
-def pack_spans(table, keys, values):
+def pack_spans(table, keys, values, after):
     anywhere = pl.BlockSpec(memory_space=pl.ANY)
     return pl.pallas_call(
         pack_spans_kernel,
-        in_specs=[pl.BlockSpec(memory_space=pltpu.SMEM), anywhere, anywhere],
+        in_specs=[pl.BlockSpec(memory_space=pltpu.SMEM), anywhere, anywhere, anywhere],
         out_specs=[anywhere] * 3,
         out_shape=[jax.ShapeDtypeStruct((2, 2, CH, HD), bf16)] * 3,
         scratch_shapes=[
@@ -208,7 +208,7 @@
         compiler_params=params(),
         cost_estimate=cost(0, 7 << 20),
         name="pack_far",
-    )(table, keys, values)
+    )(table, keys, values, after)
 
 
 def pack_queries_kernel(tab_ref, q_ref, *refs):
@@ -423,7 +423,7 @@
             pltpu.SemaphoreType.DMA((8, 2)),
         ],
         compiler_params=params(),
-        cost_estimate=pl.CostEstimate(flops=20 << 30, bytes_accessed=0, transcendentals=0),
+        cost_estimate=pl.CostEstimate(flops=18 << 30, bytes_accessed=0, transcendentals=0),
         name="cross_far",
     )(table, q, keys, values, *got)
 
@@ -455,14 +455,16 @@
     table = jnp.concatenate([asked] + [lax.ppermute(asked, "db", turn(NZ - k)) for k in SHIFTS], axis=0)
     table = lax.optimization_barrier(table)
     far_table = lax.ppermute(table, "db", swap)
-    far_q = lax.ppermute(q, "db", swap)
-    sent = pack_queries(asked, q)
+    sent = pack_queries(table, q)
+    swapped, far_table = lax.optimization_barrier((q, far_table))
+    far_q = lax.ppermute(swapped, "db", swap)
+    packed = pack_heads(sent[0], doc_ids, q, keys[0], values[0])
     sent = [lax.ppermute(x, "db", turn(k)) for x, k in zip(sent, SHIFTS)]
-
-    heads = pack_heads(table, doc_ids, q, keys[0], values[0])
-    heads = lax.all_to_all(heads, "ctx", split_axis=0, concat_axis=0, tiled=True)
-
-    far = pack_spans(far_table, db_k, db_v)
+    heads = lax.all_to_all(packed, "ctx", split_axis=0, concat_axis=0, tiled=True)
+
+    far = list(pack_spans(far_table, db_k, db_v, packed))
+    for i in range(3):
+        far[i], sent[i] = lax.optimization_barrier((far[i], sent[i]))
     far_got = [lax.ppermute(x, "db", turn(k)) for x, k in zip(far, SHIFTS)]
     *near, own = serve(table, q, db_k, db_v, sent)
     near_got = [lax.ppermute(x, "db", turn(NZ - k)) for x, k in zip(near, SHIFTS)]

time: 157 us -> 179 us (1.14)
  the two profiles are of different devices: /device:TPU:96 before, /device:TPU:100 now
where the time goes in v8:
time: 179 us; the launch traced here: 177 us
  waiting for transfers between devices  86.7 us (48%)
  Pallas kernels  47.5 us (27%)
  starting transfers between devices  30.3 us (17%)
  local copies, waits for them, and re-layouts  11.5 us (6%)
    ppermute x1, waiting for transfers between devices, per_device(): far_table = lax.ppermute(table, 'db', swap)  37.4 us
    ppermute x3, waiting for transfers between devices, per_device(): far_got = [lax.ppermute(x, 'db', turn(k)) for x, k in zip(far, SHIFTS)]  29.5 us
    pallas_call x1, Pallas kernels, self_attention(): pl.pallas_call(self_kernel, in_specs=[pl.BlockSpec(memory_space=pltpu.VME...  20.6 us
    unnamed x22, local copies, waits for them, and re-layouts  11.5 us
    all_to_all x1, waiting for transfers between devices, per_device(): lax.all_to_all(self_rows, 'ctx', split_axis=0, concat_axis=0, tiled=True)  9.54 us
    pallas_call x1, Pallas kernels, serve(): pl.pallas_call(serve_kernel, in_specs=[pl.BlockSpec(memory_space=pltpu.SM...  6.84 us
    pallas_call x1, Pallas kernels, combine(): pl.pallas_call(combine_kernel, in_specs=[pl.BlockSpec(memory_space=pltpu....  6 us
    pallas_call x1, Pallas kernels, cross(): pl.pallas_call(cross_kernel, in_specs=[pl.BlockSpec(memory_space=pltpu.SM...  5.59 us
  transfers between devices with their start and end apart: 17, of which 7 were waited for; matrix products, arithmetic and copies ran while one was open for 0% of the time, Pallas kernels for 25%

profile of v8, /device:TPU:100, one launch (start us, length us, event | category | flops | bytes accessed | tf_op | source)
XLA Modules:
  0.0 176.8 jit_solution(18147442892297920048)
XLA Ops:
  0.6 0.8 copy.14
  1.4 0.8 copy.13
  2.2 0.6 collective-permute-start.2
  2.7 2.5 %collective-permute-start.1 = (s32[1,4,2]{2,1,0:T(4,128)S(1)}, s32[1,4,2]{2,1,0:T(4,128)S(1)}, u32[]{:S(2)}, u32[]{:S(2)}) collective-permute-start(s32[1,4,2]{2,1,0:T(4,128)S(1)} %multiply_add_fusion.tab_ref), channel_id=1, source_target_pairs={{0,1},{1,2},{2,3},{3,0},{4,5},{5,6},{6,7},{7,4},{8,9},{9,10},{10,1... | collective-permute-start | bytes 104 | tf_op jit(solution)/shard_map/ppermute | solution.py:455
  5.2 2.0 %collective-permute-done.2 = s32[1,4,2]{2,1,0:T(4,128)S(1)} collective-permute-done((s32[1,4,2]{2,1,0:T(4,128)S(1)}, s32[1,4,2]{2,1,0:T(4,128)S(1)}, u32[]{:S(2)}, u32[]{:S(2)}) %collective-permute-start.2) | collective-permute-done | bytes 64 | tf_op jit(solution)/shard_map/ppermute | solution.py:455
  7.3 0.0 collective-permute-done.1
  7.3 2.8 %collective-permute-done = s32[1,4,2]{2,1,0:T(4,128)S(1)} collective-permute-done((s32[1,4,2]{2,1,0:T(4,128)S(1)}, s32[1,4,2]{2,1,0:T(4,128)S(1)}, u32[]{:S(2)}, u32[]{:S(2)}) %collective-permute-start) | collective-permute-done | bytes 64 | tf_op jit(solution)/shard_map/ppermute | solution.py:455
  10.0 1.2 copy-done
  11.3 1.9 %pack_queries.1 = (bf16[2,64,2048]{2,1,0:T(8,128)(2,1)}, bf16[2,64,2048]{2,1,0:T(8,128)(2,1)}, bf16[2,64,2048]{2,1,0:T(8,128)(2,1)}) custom-call(s32[4,4,2]{2,1,0:T(4,128)S(1)} %pad_add_fusion.tab_ref, bf16[256,2048]{1,0:T(8,128)(2,1)S(1)} %bitcast.8), custom_call_target="tpu_custom_call" | custom-call | bytes 196608 | tf_op jit(solution)/shard_map/pack_queries/pallas_call | solution.py:231
  13.2 0.1 collective-permute-start.4
  13.3 2.0 %collective-permute-start.5 = (bf16[2,64,2048]{2,1,0:T(8,128)(2,1)}, bf16[2,64,2048]{2,1,0:T(8,128)(2,1)}, u32[]{:S(2)}, u32[]{:S(2)}) collective-permute-start(bf16[2,64,2048]{2,1,0:T(8,128)(2,1)} %get-tuple-element.28), channel_id=1, source_target_pairs={{0,3},{1,0},{2,1},{3,2},{4,7},{5,4},{6,5},{7,6},{8,11},{9,8},{10,9... | collective-permute-start | bytes 1572872 | tf_op jit(solution)/shard_map/ppermute | solution.py:462
  15.3 0.0 collective-permute-start.6
  15.3 1.2 copy-done.1
  16.5 1.2 copy-done.5
  17.8 1.2 copy-done.6
  19.0 0.7 copy-done.9
  19.7 2.5 %pack_heads.1.after_ref = bf16[16,784,128]{2,1,0:T(8,128)(2,1)} custom-call(bf16[2,64,2048]{2,1,0:T(8,128)(2,1)} %get-tuple-element.23.token_ref, s32[1,256]{1,0:T(1,128)S(1)} %copy-done.9, bf16[256,2048]{1,0:T(8,128)(2,1)S(1)} %bitcast.9, bf16[256,2048]{1,0:T(8,128)(2,1)S(1)} %bitcast.14, bf16[256,2048]{1,0:T(8,128)(2,1)S(1)} %bitcast.15), custom_call_target="tpu_custom_call" | custom-call | bytes 393216 | tf_op jit(solution)/shard_map/pack_heads/pallas_call | solution.py:51
  22.2 5.2 %all-to-all-start = ((bf16[16,784,128]{2,1,0:T(8,128)(2,1)}), bf16[16,784,128]{2,1,0:T(8,128)(2,1)S(1)}, u32[]{:S(2)}, u32[]{:S(2)}) async-start(bf16[16,784,128]{2,1,0:T(8,128)(2,1)} %pack_heads.1.after_ref), calls=%async_computation | async-start | bytes 6422528 | tf_op jit(solution)/shard_map/all_to_all | solution.py:463
  27.4 0.9 collective-permute-start.3
  28.3 37.4 %collective-permute-done.3.tab_ref = s32[4,4,2]{2,1,0:T(4,128)S(1)} collective-permute-done((s32[4,4,2]{2,1,0:T(4,128)S(1)}, s32[4,4,2]{2,1,0:T(4,128)S(1)}, u32[]{:S(2)}, u32[]{:S(2)}) %collective-permute-start.3) | collective-permute-done | bytes 160 | tf_op jit(solution)/shard_map/ppermute | solution.py:457
  65.7 2.7 %collective-permute-start.10 = (bf16[256,2048]{1,0:T(8,128)(2,1)}, bf16[256,2048]{1,0:T(8,128)(2,1)S(1)}, u32[]{:S(2)}, u32[]{:S(2)}) collective-permute-start(bf16[256,2048]{1,0:T(8,128)(2,1)} %bitcast.7), channel_id=1, source_target_pairs={{0,4},{1,5},{2,6},{3,7},{4,0},{5,1},{6,2},{7,3},{8,12},{9,13},{10,... | collective-permute-start | bytes 3145736 | tf_op jit(solution)/shard_map/ppermute | solution.py:460
  68.4 1.6 copy-done.3
  70.0 2.4 %pack_far.1 = (bf16[2,2,64,2048]{3,2,1,0:T(8,128)(2,1)S(1)}, bf16[2,2,64,2048]{3,2,1,0:T(8,128)(2,1)S(1)}, bf16[2,2,64,2048]{3,2,1,0:T(8,128)(2,1)S(1)}) custom-call(s32[4,4,2]{2,1,0:T(4,128)S(1)} %collective-permute-done.3.tab_ref, bf16[8,64,2048]{2,1,0:T(8,128)(2,1)S(1)} %bitcast.13, bf16[8,64,2048]{2,1,0:T(8,128)(2,1)} %bitcast.16, ...), custom_call_target="tpu_custom_call" | custom-call | bytes 458752 | tf_op jit(solution)/shard_map/pack_far/pallas_call | solution.py:198
  72.4 0.0 collective-permute-done.4.refs_0_
  72.5 0.0 collective-permute-done.6.refs_2_
  72.5 2.7 %collective-permute-start.11 = (bf16[2,2,64,2048]{3,2,1,0:T(8,128)(2,1)S(1)}, bf16[2,2,64,2048]{3,2,1,0:T(8,128)(2,1)S(1)}, u32[]{:S(2)}, u32[]{:S(2)}) collective-permute-start(bf16[2,2,64,2048]{3,2,1,0:T(8,128)(2,1)S(1)} %get-tuple-element.41), channel_id=1, source_target_pairs={{0,1},{1,2},{2,3},{3,0},{4,5},{5,6},{6,7},{7,4},{8,9},{9,10},{10,1... | collective-permute-start | bytes 3145736 | tf_op jit(solution)/shard_map/ppermute | solution.py:468
  75.2 0.0 collective-permute-start.12
  75.2 2.9 %collective-permute-start.13 = (bf16[2,2,64,2048]{3,2,1,0:T(8,128)(2,1)S(1)}, bf16[2,2,64,2048]{3,2,1,0:T(8,128)(2,1)S(1)}, u32[]{:S(2)}, u32[]{:S(2)}) collective-permute-start(bf16[2,2,64,2048]{3,2,1,0:T(8,128)(2,1)S(1)} %get-tuple-element.43), channel_id=1, source_target_pairs={{0,2},{1,3},{2,0},{3,1},{4,6},{5,7},{6,4},{7,5},{8,10},{9,11},{10,... | collective-permute-start | bytes 3145736 | tf_op jit(solution)/shard_map/ppermute | solution.py:468
  78.0 6.8 %serve.1 = (bf16[2,64,2176]{2,1,0:T(8,128)(2,1)}, bf16[2,64,2176]{2,1,0:T(8,128)(2,1)}, bf16[2,64,2176]{2,1,0:T(8,128)(2,1)}, bf16[2,64,2176]{2,1,0:T(8,128)(2,1)S(1)}) custom-call(s32[4,4,2]{2,1,0:T(4,128)S(1)} %pad_add_fusion.tab_ref, bf16[256,2048]{1,0:T(8,128)(2,1)S(1)} %bitcast.10, bf16[8,64,2048]{2,1,0:T(8,128)(2,1)} %bitcast.11, ...), custom_call_target="tpu_custom_call" | custom-call | flops 67108864 | bytes 393216 | tf_op jit(solution)/shard_map/serve/pallas_call | solution.py:294
  84.9 0.8 copy-done.7
  85.7 1.2 collective-permute-start.7
  86.9 5.4 %collective-permute-done.10.q_ref = bf16[256,2048]{1,0:T(8,128)(2,1)S(1)} collective-permute-done((bf16[256,2048]{1,0:T(8,128)(2,1)}, bf16[256,2048]{1,0:T(8,128)(2,1)S(1)}, u32[]{:S(2)}, u32[]{:S(2)}) %collective-permute-start.10) | collective-permute-done | bytes 1048608 | tf_op jit(solution)/shard_map/ppermute | solution.py:460
  92.4 2.7 %collective-permute-start.8 = (bf16[2,64,2176]{2,1,0:T(8,128)(2,1)}, bf16[2,64,2176]{2,1,0:T(8,128)(2,1)}, u32[]{:S(2)}, u32[]{:S(2)}) collective-permute-start(bf16[2,64,2176]{2,1,0:T(8,128)(2,1)} %get-tuple-element.34), channel_id=1, source_target_pairs={{0,1},{1,2},{2,3},{3,0},{4,5},{5,6},{6,7},{7,4},{8,9},{9,10},{10,1... | collective-permute-start | bytes 1671176 | tf_op jit(solution)/shard_map/ppermute | solution.py:470
  95.1 26.1 %collective-permute-done.11.refs_0_ = bf16[2,2,64,2048]{3,2,1,0:T(8,128)(2,1)S(1)} collective-permute-done((bf16[2,2,64,2048]{3,2,1,0:T(8,128)(2,1)S(1)}, bf16[2,2,64,2048]{3,2,1,0:T(8,128)(2,1)S(1)}, u32[]{:S(2)}, u32[]{:S(2)}) %collective-permute-start.11) | collective-permute-done | bytes 1048608 | tf_op jit(solution)/shard_map/ppermute | solution.py:468
  121.1 0.4 collective-permute-start.9
  121.5 3.5 %collective-permute-done.12.refs_1_ = bf16[2,2,64,2048]{3,2,1,0:T(8,128)(2,1)S(1)} collective-permute-done((bf16[2,2,64,2048]{3,2,1,0:T(8,128)(2,1)S(1)}, bf16[2,2,64,2048]{3,2,1,0:T(8,128)(2,1)S(1)}, u32[]{:S(2)}, u32[]{:S(2)}) %collective-permute-start.12) | collective-permute-done | bytes 1048608 | tf_op jit(solution)/shard_map/ppermute | solution.py:468
  125.0 0.0 collective-permute-done.13.refs_2_
  125.0 5.6 %cross_far.1 = bf16[256,2176]{1,0:T(8,128)(2,1)} custom-call(s32[4,4,2]{2,1,0:T(4,128)S(1)} %collective-permute-done.3.tab_ref, bf16[256,2048]{1,0:T(8,128)(2,1)S(1)} %collective-permute-done.10.q_ref, bf16[8,64,2048]{2,1,0:T(8,128)(2,1)} %bitcast.12, bf16[8,64,2048]{2,1,0:T(8,128)(2,1)} %bitcast.18, ...), custom_call_target="tpu_custom_call" | custom-call | flops 19327352832 | tf_op jit(solution)/shard_map/cross_far/pallas_call | solution.py:414
  130.6 1.1 collective-permute-start.14
  131.7 20.6 %self_attention.1 = bf16[16,256,128]{2,1,0:T(8,128)(2,1)S(1)} custom-call(bf16[16,784,128]{2,1,0:T(8,128)(2,1)S(1)} %all-to-all-done.x_ref), custom_call_target="tpu_custom_call" | custom-call | flops 268435456 | bytes 262144 | tf_op jit(solution)/shard_map/self_attention/pallas_call | solution.py:152
  152.3 0.0 copy-start.4
  152.3 1.0 copy-done.4
  153.3 5.3 %all-to-all-start.1 = ((bf16[16,256,128]{2,1,0:T(8,128)(2,1)}), bf16[16,256,128]{2,1,0:T(8,128)(2,1)S(1)}, u32[]{:S(2)}, u32[]{:S(2)}) async-start(bf16[16,256,128]{2,1,0:T(8,128)(2,1)} %copy-done.4), calls=%async_computation.1 | async-start | bytes 2097152 | tf_op jit(solution)/shard_map/all_to_all | solution.py:474
  158.7 0.0 collective-permute-done.7.refs_0_
  158.7 1.0 copy-done.8
  159.7 6.0 %combine.1 = bf16[256,2048]{1,0:T(8,128)(2,1)} custom-call(s32[1,4,2]{2,1,0:T(4,128)S(1)} %multiply_add_fusion.tab_ref, bf16[2,64,2176]{2,1,0:T(8,128)(2,1)} %get-tuple-element.36.refs_0_, bf16[2,64,2176]{2,1,0:T(8,128)(2,1)} %get-tuple-element.37.refs_1_, bf16[2,64,2176]{2,1,0:T(8,128)(2,1)} %get-tuple-element.38.refs_2_, ...), custom_call_target="tpu_custom_call" | custom-call | flops 1048576 | bytes 262144 | tf_op jit(solution)/shard_map/combine/pallas_call | solution.py:343
  165.7 9.5 %all-to-all-done.1.x_ref = bf16[16,256,128]{2,1,0:T(8,128)(2,1)S(1)} async-done(((bf16[16,256,128]{2,1,0:T(8,128)(2,1)}), bf16[16,256,128]{2,1,0:T(8,128)(2,1)S(1)}, u32[]{:S(2)}, u32[]{:S(2)}) %all-to-all-start.1) | async-done | bytes 1048608 | tf_op jit(solution)/shard_map/all_to_all | solution.py:474
  175.2 1.6 unpack_heads.1
  (19 shorter events, 0.0 us)
Async XLA Ops:
  2.2 5.1 %collective-permute-start.2 = (s32[1,4,2]{2,1,0:T(4,128)S(1)}, s32[1,4,2]{2,1,0:T(4,128)S(1)}, u32[]{:S(2)}, u32[]{:S(2)}) collective-permute-start(s32[1,4,2]{2,1,0:T(4,128)S(1)} %multiply_add_fusion.tab_ref), channel_id=1, source_target_pairs={{0,2},{1,3},{2,0},{3,1},{4,6},{5,7},{6,4},{7,5},{8,10},{9,11},{10,... | collective-permute-start | bytes 104 | tf_op jit(solution)/shard_map/ppermute | solution.py:455
  2.7 4.5 %collective-permute-start.1 = (s32[1,4,2]{2,1,0:T(4,128)S(1)}, s32[1,4,2]{2,1,0:T(4,128)S(1)}, u32[]{:S(2)}, u32[]{:S(2)}) collective-permute-start(s32[1,4,2]{2,1,0:T(4,128)S(1)} %multiply_add_fusion.tab_ref), channel_id=1, source_target_pairs={{0,1},{1,2},{2,3},{3,0},{4,5},{5,6},{6,7},{7,4},{8,9},{9,10},{10,1... | collective-permute-start | bytes 104 | tf_op jit(solution)/shard_map/ppermute | solution.py:455
  5.2 4.8 %collective-permute-start = (s32[1,4,2]{2,1,0:T(4,128)S(1)}, s32[1,4,2]{2,1,0:T(4,128)S(1)}, u32[]{:S(2)}, u32[]{:S(2)}) collective-permute-start(s32[1,4,2]{2,1,0:T(4,128)S(1)} %multiply_add_fusion.tab_ref), channel_id=1, source_target_pairs={{0,3},{1,0},{2,1},{3,2},{4,7},{5,4},{6,5},{7,6},{8,11},{9,8},{10,9... | collective-permute-start | bytes 104 | tf_op jit(solution)/shard_map/ppermute | solution.py:455
  10.0 1.2 copy-start
  13.2 59.2 %collective-permute-start.4 = (bf16[2,64,2048]{2,1,0:T(8,128)(2,1)}, bf16[2,64,2048]{2,1,0:T(8,128)(2,1)}, u32[]{:S(2)}, u32[]{:S(2)}) collective-permute-start(bf16[2,64,2048]{2,1,0:T(8,128)(2,1)} %get-tuple-element.23.token_ref), channel_id=1, source_target_pairs={{0,1},{1,2},{2,3},{3,0},{4,5},{5,6},{6,7},{7,4},{8,9},{9,10},{10,1... | collective-permute-start | bytes 1572872 | tf_op jit(solution)/shard_map/ppermute | solution.py:462
  13.3 59.2 %collective-permute-start.5 = (bf16[2,64,2048]{2,1,0:T(8,128)(2,1)}, bf16[2,64,2048]{2,1,0:T(8,128)(2,1)}, u32[]{:S(2)}, u32[]{:S(2)}) collective-permute-start(bf16[2,64,2048]{2,1,0:T(8,128)(2,1)} %get-tuple-element.28), channel_id=1, source_target_pairs={{0,3},{1,0},{2,1},{3,2},{4,7},{5,4},{6,5},{7,6},{8,11},{9,8},{10,9... | collective-permute-start | bytes 1572872 | tf_op jit(solution)/shard_map/ppermute | solution.py:462
  15.3 57.2 %collective-permute-start.6 = (bf16[2,64,2048]{2,1,0:T(8,128)(2,1)}, bf16[2,64,2048]{2,1,0:T(8,128)(2,1)}, u32[]{:S(2)}, u32[]{:S(2)}) collective-permute-start(bf16[2,64,2048]{2,1,0:T(8,128)(2,1)} %get-tuple-element.31), channel_id=1, source_target_pairs={{0,2},{1,3},{2,0},{3,1},{4,6},{5,7},{6,4},{7,5},{8,10},{9,11},{10,... | collective-permute-start | bytes 1572872 | tf_op jit(solution)/shard_map/ppermute | solution.py:462
  15.3 1.2 copy-start.1
  16.5 1.2 copy-start.5
  17.7 1.2 copy-start.6
  19.0 0.7 copy-start.9
  22.2 109.5 %all-to-all-start = ((bf16[16,784,128]{2,1,0:T(8,128)(2,1)}), bf16[16,784,128]{2,1,0:T(8,128)(2,1)S(1)}, u32[]{:S(2)}, u32[]{:S(2)}) async-start(bf16[16,784,128]{2,1,0:T(8,128)(2,1)} %pack_heads.1.after_ref), calls=%async_computation | async-start | bytes 6422528 | tf_op jit(solution)/shard_map/all_to_all | solution.py:463
  27.4 38.3 %collective-permute-start.3 = (s32[4,4,2]{2,1,0:T(4,128)S(1)}, s32[4,4,2]{2,1,0:T(4,128)S(1)}, u32[]{:S(2)}, u32[]{:S(2)}) collective-permute-start(s32[4,4,2]{2,1,0:T(4,128)S(1)} %pad_add_fusion.tab_ref), channel_id=1, source_target_pairs={{0,4},{1,5},{2,6},{3,7},{4,0},{5,1},{6,2},{7,3},{8,12},{9,13},{10,... | collective-permute-start | bytes 392 | tf_op jit(solution)/shard_map/ppermute | solution.py:457
  65.7 26.7 %collective-permute-start.10 = (bf16[256,2048]{1,0:T(8,128)(2,1)}, bf16[256,2048]{1,0:T(8,128)(2,1)S(1)}, u32[]{:S(2)}, u32[]{:S(2)}) collective-permute-start(bf16[256,2048]{1,0:T(8,128)(2,1)} %bitcast.7), channel_id=1, source_target_pairs={{0,4},{1,5},{2,6},{3,7},{4,0},{5,1},{6,2},{7,3},{8,12},{9,13},{10,... | collective-permute-start | bytes 3145736 | tf_op jit(solution)/shard_map/ppermute | solution.py:460
  68.4 1.6 copy-start.3
  70.0 8.1 %copy-start.2 = (bf16[1,256,2048]{2,1,0:T(8,128)(2,1)S(1)}, bf16[1,256,2048]{2,1,0:T(8,128)(2,1)}, u32[]{:S(2)}) copy-start(bf16[1,256,2048]{2,1,0:T(8,128)(2,1)} %param.8) | copy-start | bytes 3145732
  72.5 48.6 %collective-permute-start.11 = (bf16[2,2,64,2048]{3,2,1,0:T(8,128)(2,1)S(1)}, bf16[2,2,64,2048]{3,2,1,0:T(8,128)(2,1)S(1)}, u32[]{:S(2)}, u32[]{:S(2)}) collective-permute-start(bf16[2,2,64,2048]{3,2,1,0:T(8,128)(2,1)S(1)} %get-tuple-element.41), channel_id=1, source_target_pairs={{0,1},{1,2},{2,3},{3,0},{4,5},{5,6},{6,7},{7,4},{8,9},{9,10},{10,1... | collective-permute-start | bytes 3145736 | tf_op jit(solution)/shard_map/ppermute | solution.py:468
  75.2 49.8 %collective-permute-start.12 = (bf16[2,2,64,2048]{3,2,1,0:T(8,128)(2,1)S(1)}, bf16[2,2,64,2048]{3,2,1,0:T(8,128)(2,1)S(1)}, u32[]{:S(2)}, u32[]{:S(2)}) collective-permute-start(bf16[2,2,64,2048]{3,2,1,0:T(8,128)(2,1)S(1)} %get-tuple-element.42), channel_id=1, source_target_pairs={{0,3},{1,0},{2,1},{3,2},{4,7},{5,4},{6,5},{7,6},{8,11},{9,8},{10,9... | collective-permute-start | bytes 3145736 | tf_op jit(solution)/shard_map/ppermute | solution.py:468
  75.2 49.8 %collective-permute-start.13 = (bf16[2,2,64,2048]{3,2,1,0:T(8,128)(2,1)S(1)}, bf16[2,2,64,2048]{3,2,1,0:T(8,128)(2,1)S(1)}, u32[]{:S(2)}, u32[]{:S(2)}) collective-permute-start(bf16[2,2,64,2048]{3,2,1,0:T(8,128)(2,1)S(1)} %get-tuple-element.43), channel_id=1, source_target_pairs={{0,2},{1,3},{2,0},{3,1},{4,6},{5,7},{6,4},{7,5},{8,10},{9,11},{10,... | collective-permute-start | bytes 3145736 | tf_op jit(solution)/shard_map/ppermute | solution.py:468
  84.9 0.8 copy-start.7
  85.7 72.9 %collective-permute-start.7 = (bf16[2,64,2176]{2,1,0:T(8,128)(2,1)}, bf16[2,64,2176]{2,1,0:T(8,128)(2,1)}, u32[]{:S(2)}, u32[]{:S(2)}) collective-permute-start(bf16[2,64,2176]{2,1,0:T(8,128)(2,1)} %get-tuple-element.33), channel_id=1, source_target_pairs={{0,3},{1,0},{2,1},{3,2},{4,7},{5,4},{6,5},{7,6},{8,11},{9,8},{10,9... | collective-permute-start | bytes 1671176 | tf_op jit(solution)/shard_map/ppermute | solution.py:470
  92.4 66.3 %collective-permute-start.8 = (bf16[2,64,2176]{2,1,0:T(8,128)(2,1)}, bf16[2,64,2176]{2,1,0:T(8,128)(2,1)}, u32[]{:S(2)}, u32[]{:S(2)}) collective-permute-start(bf16[2,64,2176]{2,1,0:T(8,128)(2,1)} %get-tuple-element.34), channel_id=1, source_target_pairs={{0,1},{1,2},{2,3},{3,0},{4,5},{5,6},{6,7},{7,4},{8,9},{9,10},{10,1... | collective-permute-start | bytes 1671176 | tf_op jit(solution)/shard_map/ppermute | solution.py:470
  121.1 37.6 %collective-permute-start.9 = (bf16[2,64,2176]{2,1,0:T(8,128)(2,1)}, bf16[2,64,2176]{2,1,0:T(8,128)(2,1)}, u32[]{:S(2)}, u32[]{:S(2)}) collective-permute-start(bf16[2,64,2176]{2,1,0:T(8,128)(2,1)} %get-tuple-element.35), channel_id=1, source_target_pairs={{0,2},{1,3},{2,0},{3,1},{4,6},{5,7},{6,4},{7,5},{8,10},{9,11},{10,... | collective-permute-start | bytes 1671176 | tf_op jit(solution)/shard_map/ppermute | solution.py:470
  130.6 28.1 %collective-permute-start.14 = (bf16[256,2176]{1,0:T(8,128)(2,1)}, bf16[256,2176]{1,0:T(8,128)(2,1)}, u32[]{:S(2)}, u32[]{:S(2)}) collective-permute-start(bf16[256,2176]{1,0:T(8,128)(2,1)} %cross_far.1), channel_id=1, source_target_pairs={{0,4},{1,5},{2,6},{3,7},{4,0},{5,1},{6,2},{7,3},{8,12},{9,13},{10,... | collective-permute-start | bytes 3342344 | tf_op jit(solution)/shard_map/ppermute | solution.py:471
  152.3 1.0 copy-start.4
  153.3 21.9 %all-to-all-start.1 = ((bf16[16,256,128]{2,1,0:T(8,128)(2,1)}), bf16[16,256,128]{2,1,0:T(8,128)(2,1)S(1)}, u32[]{:S(2)}, u32[]{:S(2)}) async-start(bf16[16,256,128]{2,1,0:T(8,128)(2,1)} %copy-done.4), calls=%async_computation.1 | async-start | bytes 2097152 | tf_op jit(solution)/shard_map/all_to_all | solution.py:474
  158.6 1.1 copy-start.8

commit v9 on v6

--- a/solution.py
+++ b/solution.py
@@ -202,7 +202,7 @@
             pltpu.SemaphoreType.DMA((3, 2, 2)),
             pltpu.SemaphoreType.DMA((3, 2, 2)),
         ],
-        compiler_params=params(),
+        compiler_params=pltpu.CompilerParams(vmem_limit_bytes=60 << 20),
         cost_estimate=cost(0, 7 << 20),
         name="pack_far" if far else "pack_near",
     )(*tables, keys, values)

time: 129 us -> 126 us (0.977)
  starting transfers between devices: 42.4 us -> 41.1 us
    all_to_all x1, waiting for transfers between devices: 7.43 us -> 3.74 us  [per_device(): lax.all_to_all(self_rows, 'ctx', split_axis=0, concat_axis=0, tiled=True)]
    ppermute x3, waiting for transfers between devices: 0.45 us -> 3.76 us  [per_device(): near_got.append(lax.ppermute(near[i], 'db', turn(k)))]
    pallas_call x1, Pallas kernels: 21.4 us -> 18.5 us  [self_attention(): pl.pallas_call(self_kernel, in_specs=[pl.BlockSpec(memory_space=pltpu.VME...]
    pallas_call x2, Pallas kernels: 8.24 us -> 9.92 us  [pack_spans(): pl.pallas_call(functools.partial(pack_spans_kernel, int(far)), in_specs=[...]
    unnamed x14 -> x20, local copies, waits for them, and re-layouts: 3.14 us -> 3.1 us
where the time goes in v9:
time: 126 us
  Pallas kernels  47.4 us (38%)
  starting transfers between devices  41.1 us (33%)
  waiting for transfers between devices  33.4 us (27%)
  local copies, waits for them, and re-layouts  3.1 us (2%)
    ppermute x3, waiting for transfers between devices, per_device(): far_got = [lax.ppermute(x, 'db', turn(k)) for x, k in zip(far, SHIFTS)]  23.6 us
    pallas_call x1, Pallas kernels, self_attention(): pl.pallas_call(self_kernel, in_specs=[pl.BlockSpec(memory_space=pltpu.VME...  18.5 us
    pallas_call x2, Pallas kernels, cross(): pl.pallas_call(functools.partial(cross_kernel, far), in_specs=[pl.BlockSp...  14.9 us
    all_to_all x1, starting transfers between devices, per_device(): lax.all_to_all(self_rows, 'ctx', split_axis=0, concat_axis=0, tiled=True)  12.8 us
    pallas_call x2, Pallas kernels, pack_spans(): pl.pallas_call(functools.partial(pack_spans_kernel, int(far)), in_specs=[...  9.92 us
    all_to_all x1, starting transfers between devices, per_device(): lax.all_to_all(heads, 'ctx', split_axis=0, concat_axis=0, tiled=True)  8.93 us
    ppermute x3, starting transfers between devices, per_device(): tables = [lax.ppermute(table, 'db', turn(NZ - k)) for k in SHIFTS]  6.5 us
    ppermute x3, starting transfers between devices, per_device(): far_got = [lax.ppermute(x, 'db', turn(k)) for x, k in zip(far, SHIFTS)]  3.86 us
  transfers between devices with their start and end apart: 14, of which 6 were waited for; matrix products, arithmetic and copies ran while one was open for 0% of the time, Pallas kernels for 36%

profile of v9, /device:TPU:1, one launch (start us, length us, event | category | flops | bytes accessed | tf_op | source)
XLA Modules:
  0.0 125.8 jit_solution(1656427595416363859)
XLA Ops:
  0.6 0.8 copy.13
  1.4 0.8 copy.14
  2.2 3.6 %collective-permute-start = (s32[1,4,2]{2,1,0:T(4,128)S(1)}, s32[1,4,2]{2,1,0:T(4,128)S(1)}, u32[]{:S(2)}, u32[]{:S(2)}) collective-permute-start(s32[1,4,2]{2,1,0:T(4,128)S(1)} %multiply_add_fusion), channel_id=1, source_target_pairs={{0,4},{1,5},{2,6},{3,7},{4,0},{5,1},{6,2},{7,3},{8,12},{9,13},{10,... | collective-permute-start | bytes 104 | tf_op jit(solution)/shard_map/ppermute | solution.py:339
  5.7 0.1 collective-permute-start.7
  5.8 0.9 collective-permute-done
  6.7 3.8 %collective-permute-start.3 = (s32[2,4,2]{2,1,0:T(4,128)S(1)}, s32[2,4,2]{2,1,0:T(4,128)S(1)}, u32[]{:S(2)}, u32[]{:S(2)}) collective-permute-start(s32[2,4,2]{2,1,0:T(4,128)S(1)} %pad_add_fusion.token_ref.tab_ref), channel_id=1, source_target_pairs={{0,2},{1,3},{2,0},{3,1},{4,6},{5,7},{6,4},{7,5},{8,10},{9,11},{10,... | collective-permute-start | bytes 200 | tf_op jit(solution)/shard_map/ppermute | solution.py:340
  10.5 0.7 collective-permute-start.2
  11.3 1.9 %collective-permute-start.1 = (s32[2,4,2]{2,1,0:T(4,128)S(1)}, s32[2,4,2]{2,1,0:T(4,128)S(1)}, u32[]{:S(2)}, u32[]{:S(2)}) collective-permute-start(s32[2,4,2]{2,1,0:T(4,128)S(1)} %pad_add_fusion.token_ref.tab_ref), channel_id=1, source_target_pairs={{0,3},{1,0},{2,1},{3,2},{4,7},{5,4},{6,5},{7,6},{8,11},{9,8},{10,9... | collective-permute-start | bytes 200 | tf_op jit(solution)/shard_map/ppermute | solution.py:340
  13.2 0.0 collective-permute-done.3.refs_2_
  13.2 1.4 %collective-permute-done.2.refs_1_ = s32[2,4,2]{2,1,0:T(4,128)S(1)} collective-permute-done((s32[2,4,2]{2,1,0:T(4,128)S(1)}, s32[2,4,2]{2,1,0:T(4,128)S(1)}, u32[]{:S(2)}, u32[]{:S(2)}) %collective-permute-start.2) | collective-permute-done | bytes 96 | tf_op jit(solution)/shard_map/ppermute | solution.py:340
  14.6 0.0 collective-permute-done.1.refs_0_
  14.6 0.0 copy-done.6
  14.6 0.6 copy-done.7
  15.2 0.0 copy-done.8
  15.2 0.0 copy-start.5
  15.2 5.0 %pack_far.1 = (bf16[2,2,64,2048]{3,2,1,0:T(8,128)(2,1)}, bf16[2,2,64,2048]{3,2,1,0:T(8,128)(2,1)}, bf16[2,2,64,2048]{3,2,1,0:T(8,128)(2,1)}) custom-call(s32[2,4,2]{2,1,0:T(4,128)} %copy-done.8, s32[2,4,2]{2,1,0:T(4,128)} %copy-done.7, s32[2,4,2]{2,1,0:T(4,128)} %copy-done.6, bf16[8,64,2048]{2,1,0:T(8,128)(2,1)} %bitcast.12, bf16[8,64,2048]{2,1,0:T(8,128)(2,1)} %bitcast.16), custom_call_target="tpu_custom_call" | custom-call | bytes 458752 | tf_op jit(solution)/shard_map/pack_far/pallas_call | solution.py:195
  20.2 0.1 collective-permute-start.8
  20.3 2.7 %collective-permute-start.9 = (bf16[2,2,64,2048]{3,2,1,0:T(8,128)(2,1)}, bf16[2,2,64,2048]{3,2,1,0:T(8,128)(2,1)}, u32[]{:S(2)}, u32[]{:S(2)}) collective-permute-start(bf16[2,2,64,2048]{3,2,1,0:T(8,128)(2,1)} %get-tuple-element.18), channel_id=1, source_target_pairs={{0,3},{1,0},{2,1},{3,2},{4,7},{5,4},{6,5},{7,6},{8,11},{9,8},{10,9... | collective-permute-start | bytes 3145736 | tf_op jit(solution)/shard_map/ppermute | solution.py:342
  23.0 1.1 collective-permute-start.10
  24.1 0.0 copy-done
  24.1 0.0 copy-done.3
  24.1 0.0 copy-done.4
  24.1 0.0 copy-done.5
  24.1 2.5 %pack_heads.1 = bf16[16,784,128]{2,1,0:T(8,128)(2,1)} custom-call(s32[2,4,2]{2,1,0:T(4,128)S(1)} %pad_add_fusion.token_ref.tab_ref, s32[1,256]{1,0:T(1,128)S(1)} %copy-done.5, bf16[256,2048]{1,0:T(8,128)(2,1)S(1)} %bitcast.8, bf16[256,2048]{1,0:T(8,128)(2,1)S(1)} %bitcast.10, bf16[256,2048]{1,0:T(8,128)(2,1)S(1)} %bitcast.11), custom_call_target="tpu_custom_call" | custom-call | bytes 393216 | tf_op jit(solution)/shard_map/pack_heads/pallas_call | solution.py:51
  26.6 8.9 %all-to-all-start = ((bf16[16,784,128]{2,1,0:T(8,128)(2,1)}), bf16[16,784,128]{2,1,0:T(8,128)(2,1)S(1)}, u32[]{:S(2)}, u32[]{:S(2)}) async-start(bf16[16,784,128]{2,1,0:T(8,128)(2,1)} %pack_heads.1), calls=%async_computation | async-start | bytes 6422528 | tf_op jit(solution)/shard_map/all_to_all | solution.py:345
  35.6 4.9 %pack_near.1 = (bf16[2,2,64,2048]{3,2,1,0:T(8,128)(2,1)}, bf16[2,2,64,2048]{3,2,1,0:T(8,128)(2,1)}, bf16[2,2,64,2048]{3,2,1,0:T(8,128)(2,1)}) custom-call(s32[2,4,2]{2,1,0:T(4,128)} %copy-done.8, s32[2,4,2]{2,1,0:T(4,128)} %copy-done.7, s32[2,4,2]{2,1,0:T(4,128)} %copy-done.6, bf16[8,64,2048]{2,1,0:T(8,128)(2,1)} %bitcast.13, bf16[8,64,2048]{2,1,0:T(8,128)(2,1)} %bitcast.17), custom_call_target="tpu_custom_call" | custom-call | bytes 458752 | tf_op jit(solution)/shard_map/pack_near/pallas_call | solution.py:195
  40.5 1.0 collective-permute-start.4
  41.5 0.0 collective-permute-done.7.q_ref
  41.5 1.8 %collective-permute-start.5 = (bf16[2,2,64,2048]{3,2,1,0:T(8,128)(2,1)}, bf16[2,2,64,2048]{3,2,1,0:T(8,128)(2,1)}, u32[]{:S(2)}, u32[]{:S(2)}) collective-permute-start(bf16[2,2,64,2048]{3,2,1,0:T(8,128)(2,1)} %get-tuple-element.12), channel_id=1, source_target_pairs={{0,3},{1,0},{2,1},{3,2},{4,7},{5,4},{6,5},{7,6},{8,11},{9,8},{10,9... | collective-permute-start | bytes 3145736 | tf_op jit(solution)/shard_map/ppermute | solution.py:350
  43.2 0.3 collective-permute-done.8.refs_2_
  43.6 0.4 collective-permute-start.6
  43.9 0.0 collective-permute-done.9.refs_3_
  43.9 23.2 %collective-permute-done.10.refs_4_ = bf16[2,2,64,2048]{3,2,1,0:T(8,128)(2,1)} collective-permute-done((bf16[2,2,64,2048]{3,2,1,0:T(8,128)(2,1)}, bf16[2,2,64,2048]{3,2,1,0:T(8,128)(2,1)}, u32[]{:S(2)}, u32[]{:S(2)}) %collective-permute-start.10) | collective-permute-done | bytes 1048608 | tf_op jit(solution)/shard_map/ppermute | solution.py:342
  67.2 6.6 %cross_far.1 = bf16[256,2176]{1,0:T(8,128)(2,1)} custom-call(s32[2,4,2]{2,1,0:T(4,128)S(1)} %pad_add_fusion.token_ref.tab_ref, bf16[256,2048]{1,0:T(8,128)(2,1)} %collective-permute-done.7.q_ref, bf16[8,64,2048]{2,1,0:T(8,128)(2,1)} %bitcast.14, bf16[8,64,2048]{2,1,0:T(8,128)(2,1)} %bitcast.18, bf16[2,2,64,2048]{3,2,1,0:T(8,128)(2,1)} %collective-permute-done.8.refs_2_, ...), custom_call_target="tpu_custom_call" | custom-call | flops 34359738368 | tf_op jit(solution)/shard_map/cross_far/pallas_call | solution.py:296
  73.8 2.2 %collective-permute-start.11 = (bf16[256,2176]{1,0:T(8,128)(2,1)}, bf16[256,2176]{1,0:T(8,128)(2,1)}, u32[]{:S(2)}, u32[]{:S(2)}) collective-permute-start(bf16[256,2176]{1,0:T(8,128)(2,1)} %cross_far.1), channel_id=1, source_target_pairs={{0,4},{1,5},{2,6},{3,7},{4,0},{5,1},{6,2},{7,3},{8,12},{9,13},{10,... | collective-permute-start | bytes 3342344 | tf_op jit(solution)/shard_map/ppermute | solution.py:351
  76.0 0.0 all-to-all-done.x_ref
  76.0 18.5 %self_attention.1 = bf16[16,256,128]{2,1,0:T(8,128)(2,1)S(1)} custom-call(bf16[16,784,128]{2,1,0:T(8,128)(2,1)S(1)} %all-to-all-done.x_ref), custom_call_target="tpu_custom_call" | custom-call | flops 268435456 | bytes 262144 | tf_op jit(solution)/shard_map/self_attention/pallas_call | solution.py:152
  94.5 0.0 copy-start.2
  94.6 1.0 copy-done.2
  95.5 12.8 %all-to-all-start.1 = ((bf16[16,256,128]{2,1,0:T(8,128)(2,1)}), bf16[16,256,128]{2,1,0:T(8,128)(2,1)S(1)}, u32[]{:S(2)}, u32[]{:S(2)}) async-start(bf16[16,256,128]{2,1,0:T(8,128)(2,1)} %copy-done.2), calls=%async_computation.1 | async-start | bytes 2097152 | tf_op jit(solution)/shard_map/all_to_all | solution.py:354
  108.4 0.0 collective-permute-done.4.refs_0_
  108.4 0.0 collective-permute-done.5.refs_1_
  108.4 3.8 %collective-permute-done.6.refs_2_ = bf16[2,2,64,2048]{3,2,1,0:T(8,128)(2,1)} collective-permute-done((bf16[2,2,64,2048]{3,2,1,0:T(8,128)(2,1)}, bf16[2,2,64,2048]{3,2,1,0:T(8,128)(2,1)}, u32[]{:S(2)}, u32[]{:S(2)}) %collective-permute-start.6) | collective-permute-done | bytes 1048608 | tf_op jit(solution)/shard_map/ppermute | solution.py:350
  112.1 0.0 collective-permute-done.11.refs_5_
  112.1 0.0 copy-done.1
  112.1 8.3 %cross_near.1 = bf16[256,2048]{1,0:T(8,128)(2,1)} custom-call(s32[2,4,2]{2,1,0:T(4,128)S(1)} %pad_add_fusion.token_ref.tab_ref, bf16[256,2048]{1,0:T(8,128)(2,1)S(1)} %bitcast.9, bf16[8,64,2048]{2,1,0:T(8,128)(2,1)} %bitcast.15, bf16[8,64,2048]{2,1,0:T(8,128)(2,1)} %bitcast.19, bf16[2,2,64,2048]{3,2,1,0:T(8,128)(2,1)} %get-tuple-element.14.refs_2_, ...), custom_call_target="tpu_custom_call" | custom-call | flops 67108864 | tf_op jit(solution)/shard_map/cross_near/pallas_call | solution.py:296
  120.4 3.7 %all-to-all-done.1.x_ref = bf16[16,256,128]{2,1,0:T(8,128)(2,1)S(1)} async-done(((bf16[16,256,128]{2,1,0:T(8,128)(2,1)}), bf16[16,256,128]{2,1,0:T(8,128)(2,1)S(1)}, u32[]{:S(2)}, u32[]{:S(2)}) %all-to-all-start.1) | async-done | bytes 1048608 | tf_op jit(solution)/shard_map/all_to_all | solution.py:354
  124.2 1.6 %unpack_heads.1 = bf16[256,2048]{1,0:T(8,128)(2,1)} custom-call(bf16[16,256,128]{2,1,0:T(8,128)(2,1)S(1)} %all-to-all-done.1.x_ref), custom_call_target="tpu_custom_call" | custom-call | bytes 131072 | tf_op jit(solution)/shard_map/unpack_heads/pallas_call | solution.py:75
  (10 shorter events, 0.0 us)
Async XLA Ops:
  2.2 4.5 %collective-permute-start = (s32[1,4,2]{2,1,0:T(4,128)S(1)}, s32[1,4,2]{2,1,0:T(4,128)S(1)}, u32[]{:S(2)}, u32[]{:S(2)}) collective-permute-start(s32[1,4,2]{2,1,0:T(4,128)S(1)} %multiply_add_fusion), channel_id=1, source_target_pairs={{0,4},{1,5},{2,6},{3,7},{4,0},{5,1},{6,2},{7,3},{8,12},{9,13},{10,... | collective-permute-start | bytes 104 | tf_op jit(solution)/shard_map/ppermute | solution.py:339
  5.7 35.7 %collective-permute-start.7 = (bf16[256,2048]{1,0:T(8,128)(2,1)}, bf16[256,2048]{1,0:T(8,128)(2,1)}, u32[]{:S(2)}, u32[]{:S(2)}) collective-permute-start(bf16[256,2048]{1,0:T(8,128)(2,1)} %bitcast.7), channel_id=1, source_target_pairs={{0,4},{1,5},{2,6},{3,7},{4,0},{5,1},{6,2},{7,3},{8,12},{9,13},{10,... | collective-permute-start | bytes 3145736 | tf_op jit(solution)/shard_map/ppermute | solution.py:336
  6.7 6.5 %collective-permute-start.3 = (s32[2,4,2]{2,1,0:T(4,128)S(1)}, s32[2,4,2]{2,1,0:T(4,128)S(1)}, u32[]{:S(2)}, u32[]{:S(2)}) collective-permute-start(s32[2,4,2]{2,1,0:T(4,128)S(1)} %pad_add_fusion.token_ref.tab_ref), channel_id=1, source_target_pairs={{0,2},{1,3},{2,0},{3,1},{4,6},{5,7},{6,4},{7,5},{8,10},{9,11},{10,... | collective-permute-start | bytes 200 | tf_op jit(solution)/shard_map/ppermute | solution.py:340
  10.5 4.1 %collective-permute-start.2 = (s32[2,4,2]{2,1,0:T(4,128)S(1)}, s32[2,4,2]{2,1,0:T(4,128)S(1)}, u32[]{:S(2)}, u32[]{:S(2)}) collective-permute-start(s32[2,4,2]{2,1,0:T(4,128)S(1)} %pad_add_fusion.token_ref.tab_ref), channel_id=1, source_target_pairs={{0,1},{1,2},{2,3},{3,0},{4,5},{5,6},{6,7},{7,4},{8,9},{9,10},{10,1... | collective-permute-start | bytes 200 | tf_op jit(solution)/shard_map/ppermute | solution.py:340
  11.3 3.3 %collective-permute-start.1 = (s32[2,4,2]{2,1,0:T(4,128)S(1)}, s32[2,4,2]{2,1,0:T(4,128)S(1)}, u32[]{:S(2)}, u32[]{:S(2)}) collective-permute-start(s32[2,4,2]{2,1,0:T(4,128)S(1)} %pad_add_fusion.token_ref.tab_ref), channel_id=1, source_target_pairs={{0,3},{1,0},{2,1},{3,2},{4,7},{5,4},{6,5},{7,6},{8,11},{9,8},{10,9... | collective-permute-start | bytes 200 | tf_op jit(solution)/shard_map/ppermute | solution.py:340
  13.2 1.4 %copy-start.6 = (s32[2,4,2]{2,1,0:T(4,128)}, s32[2,4,2]{2,1,0:T(4,128)S(1)}, u32[]{:S(2)}) copy-start(s32[2,4,2]{2,1,0:T(4,128)S(1)} %collective-permute-done.3.refs_2_) | copy-start | bytes 196
  14.6 0.6 copy-start.7
  14.6 0.6 copy-start.8
  15.2 8.9 %copy-start = (bf16[1,256,2048]{2,1,0:T(8,128)(2,1)S(1)}, bf16[1,256,2048]{2,1,0:T(8,128)(2,1)}, u32[]{:S(2)}) copy-start(bf16[1,256,2048]{2,1,0:T(8,128)(2,1)} %param.8) | copy-start | bytes 3145732
  15.2 8.9 %copy-start.3 = (bf16[1,256,2048]{2,1,0:T(8,128)(2,1)S(1)}, bf16[1,256,2048]{2,1,0:T(8,128)(2,1)}, u32[]{:S(2)}) copy-start(bf16[1,256,2048]{2,1,0:T(8,128)(2,1)} %param.9) | copy-start | bytes 3145732
  15.2 8.9 %copy-start.4 = (bf16[1,256,2048]{2,1,0:T(8,128)(2,1)S(1)}, bf16[1,256,2048]{2,1,0:T(8,128)(2,1)}, u32[]{:S(2)}) copy-start(bf16[1,256,2048]{2,1,0:T(8,128)(2,1)} %param.10) | copy-start | bytes 3145732
  15.2 8.9 %copy-start.5 = (s32[1,256]{1,0:T(1,128)S(1)}, s32[1,256]{1,0:T(1,128)}, u32[]{:S(2)}) copy-start(s32[1,256]{1,0:T(1,128)} %docs_ref.1) | copy-start | bytes 3076
  20.2 23.3 %collective-permute-start.8 = (bf16[2,2,64,2048]{3,2,1,0:T(8,128)(2,1)}, bf16[2,2,64,2048]{3,2,1,0:T(8,128)(2,1)}, u32[]{:S(2)}, u32[]{:S(2)}) collective-permute-start(bf16[2,2,64,2048]{3,2,1,0:T(8,128)(2,1)} %get-tuple-element.17), channel_id=1, source_target_pairs={{0,1},{1,2},{2,3},{3,0},{4,5},{5,6},{6,7},{7,4},{8,9},{9,10},{10,1... | collective-permute-start | bytes 3145736 | tf_op jit(solution)/shard_map/ppermute | solution.py:342
  20.3 23.6 %collective-permute-start.9 = (bf16[2,2,64,2048]{3,2,1,0:T(8,128)(2,1)}, bf16[2,2,64,2048]{3,2,1,0:T(8,128)(2,1)}, u32[]{:S(2)}, u32[]{:S(2)}) collective-permute-start(bf16[2,2,64,2048]{3,2,1,0:T(8,128)(2,1)} %get-tuple-element.18), channel_id=1, source_target_pairs={{0,3},{1,0},{2,1},{3,2},{4,7},{5,4},{6,5},{7,6},{8,11},{9,8},{10,9... | collective-permute-start | bytes 3145736 | tf_op jit(solution)/shard_map/ppermute | solution.py:342
  23.0 44.2 %collective-permute-start.10 = (bf16[2,2,64,2048]{3,2,1,0:T(8,128)(2,1)}, bf16[2,2,64,2048]{3,2,1,0:T(8,128)(2,1)}, u32[]{:S(2)}, u32[]{:S(2)}) collective-permute-start(bf16[2,2,64,2048]{3,2,1,0:T(8,128)(2,1)} %get-tuple-element.19), channel_id=1, source_target_pairs={{0,2},{1,3},{2,0},{3,1},{4,6},{5,7},{6,4},{7,5},{8,10},{9,11},{10,... | collective-permute-start | bytes 3145736 | tf_op jit(solution)/shard_map/ppermute | solution.py:342
  26.6 49.4 %all-to-all-start = ((bf16[16,784,128]{2,1,0:T(8,128)(2,1)}), bf16[16,784,128]{2,1,0:T(8,128)(2,1)S(1)}, u32[]{:S(2)}, u32[]{:S(2)}) async-start(bf16[16,784,128]{2,1,0:T(8,128)(2,1)} %pack_heads.1), calls=%async_computation | async-start | bytes 6422528 | tf_op jit(solution)/shard_map/all_to_all | solution.py:345
  40.5 67.9 %collective-permute-start.4 = (bf16[2,2,64,2048]{3,2,1,0:T(8,128)(2,1)}, bf16[2,2,64,2048]{3,2,1,0:T(8,128)(2,1)}, u32[]{:S(2)}, u32[]{:S(2)}) collective-permute-start(bf16[2,2,64,2048]{3,2,1,0:T(8,128)(2,1)} %get-tuple-element.11), channel_id=1, source_target_pairs={{0,1},{1,2},{2,3},{3,0},{4,5},{5,6},{6,7},{7,4},{8,9},{9,10},{10,1... | collective-permute-start | bytes 3145736 | tf_op jit(solution)/shard_map/ppermute | solution.py:350
  41.5 66.9 %collective-permute-start.5 = (bf16[2,2,64,2048]{3,2,1,0:T(8,128)(2,1)}, bf16[2,2,64,2048]{3,2,1,0:T(8,128)(2,1)}, u32[]{:S(2)}, u32[]{:S(2)}) collective-permute-start(bf16[2,2,64,2048]{3,2,1,0:T(8,128)(2,1)} %get-tuple-element.12), channel_id=1, source_target_pairs={{0,3},{1,0},{2,1},{3,2},{4,7},{5,4},{6,5},{7,6},{8,11},{9,8},{10,9... | collective-permute-start | bytes 3145736 | tf_op jit(solution)/shard_map/ppermute | solution.py:350
  43.6 68.6 %collective-permute-start.6 = (bf16[2,2,64,2048]{3,2,1,0:T(8,128)(2,1)}, bf16[2,2,64,2048]{3,2,1,0:T(8,128)(2,1)}, u32[]{:S(2)}, u32[]{:S(2)}) collective-permute-start(bf16[2,2,64,2048]{3,2,1,0:T(8,128)(2,1)} %get-tuple-element.13), channel_id=1, source_target_pairs={{0,2},{1,3},{2,0},{3,1},{4,6},{5,7},{6,4},{7,5},{8,10},{9,11},{10,... | collective-permute-start | bytes 3145736 | tf_op jit(solution)/shard_map/ppermute | solution.py:350
  73.8 38.4 %collective-permute-start.11 = (bf16[256,2176]{1,0:T(8,128)(2,1)}, bf16[256,2176]{1,0:T(8,128)(2,1)}, u32[]{:S(2)}, u32[]{:S(2)}) collective-permute-start(bf16[256,2176]{1,0:T(8,128)(2,1)} %cross_far.1), channel_id=1, source_target_pairs={{0,4},{1,5},{2,6},{3,7},{4,0},{5,1},{6,2},{7,3},{8,12},{9,13},{10,... | collective-permute-start | bytes 3342344 | tf_op jit(solution)/shard_map/ppermute | solution.py:351
  94.5 1.0 copy-start.2
  95.5 28.7 %all-to-all-start.1 = ((bf16[16,256,128]{2,1,0:T(8,128)(2,1)}), bf16[16,256,128]{2,1,0:T(8,128)(2,1)S(1)}, u32[]{:S(2)}, u32[]{:S(2)}) async-start(bf16[16,256,128]{2,1,0:T(8,128)(2,1)} %copy-done.2), calls=%async_computation.1 | async-start | bytes 2097152 | tf_op jit(solution)/shard_map/all_to_all | solution.py:354
  108.4 3.8 %copy-start.1 = (bf16[1,256,2048]{2,1,0:T(8,128)(2,1)S(1)}, bf16[1,256,2048]{2,1,0:T(8,128)(2,1)}, u32[]{:S(2)}) copy-start(bf16[1,256,2048]{2,1,0:T(8,128)(2,1)} %param.8) | copy-start | bytes 3145732

commit v10 on v9

--- a/solution.py
+++ b/solution.py
@@ -164,16 +164,16 @@
 
 
 def pack_spans_kernel(far, *refs):
-    tabs, keys_ref, values_ref = refs[:3], refs[3], refs[4]
-    outs, hold, loads, stores = refs[5:8], refs[8], refs[9], refs[10]
+    tab_ref, keys_ref, values_ref = refs[:3]
+    outs, hold, loads, stores = refs[3:6], refs[6], refs[7], refs[8]
     me = lax.axis_index("db")
     moves = []
     for i in range(3):
         first, second, seen = jnp.int32(0), jnp.int32(0), jnp.int32(0)
         for r in range(8):
-            entry = tabs[i][far, r // 2, r % 2]
-            hit = entry // 8 == me
-            span = entry % 8
+            entry = tab_ref[2 * i + far, r // 2, r % 2]
+            hit = (entry >> 3) == me
+            span = entry & 7
             first = jnp.where(hit & (seen == 0), span, first)
             second = jnp.where(hit & (seen == 1), span, second)
             seen = seen + jnp.where(hit, 1, 0)
@@ -190,11 +190,11 @@
         store.wait()
 
 
-def pack_spans(far, tables, keys, values):
+def pack_spans(far, table, keys, values):
     anywhere = pl.BlockSpec(memory_space=pl.ANY)
     return pl.pallas_call(
         functools.partial(pack_spans_kernel, int(far)),
-        in_specs=[pl.BlockSpec(memory_space=pltpu.SMEM)] * 3 + [anywhere, anywhere],
+        in_specs=[pl.BlockSpec(memory_space=pltpu.SMEM), anywhere, anywhere],
         out_specs=[anywhere] * 3,
         out_shape=[jax.ShapeDtypeStruct((2, 2, CH, HD), bf16)] * 3,
         scratch_shapes=[
@@ -205,7 +205,7 @@
         compiler_params=pltpu.CompilerParams(vmem_limit_bytes=60 << 20),
         cost_estimate=cost(0, 7 << 20),
         name="pack_far" if far else "pack_near",
-    )(*tables, keys, values)
+    )(table, keys, values)
 
 
 def cross_kernel(far, tab_ref, q_ref, *refs):
@@ -216,18 +216,20 @@
     else:
         part_ref, out_ref, kbuf, vbuf, sems = refs[5:]
     me = lax.axis_index("db")
-    plane, z = me // NZ, me % NZ
+    plane, z = me >> 2, me & 3
     row = 1 if far else 0
     here = []
+    entries = [tab_ref[row, r // 2, r % 2] for r in range(8)]
+    owners = [entry >> 3 for entry in entries]
     for r in range(8):
-        owner = tab_ref[row, r // 2, r % 2] // 8
+        owner = owners[r]
         slot = jnp.int32(0)
         for earlier in range(r):
-            slot = slot + jnp.where(tab_ref[row, earlier // 2, earlier % 2] // 8 == owner, 1, 0)
-        here.append(jnp.where(owner // NZ == plane, 1, 0))
-        shift = (z - owner % NZ + NZ) % NZ
+            slot = slot + jnp.where(owners[earlier] == owner, 1, 0)
+        here.append(jnp.where((owner >> 2) == plane, 1, 0))
+        shift = (z - owner) & 3
         place = pl.ds((r % 2) * CH, CH)
-        span = tab_ref[row, r // 2, r % 2] % 8
+        span = entries[r] & 7
 
         @pl.when(shift == 0)
         def _(span=span, place=place, r=r):
@@ -337,7 +339,7 @@
 
     asked = lax.optimization_barrier(nbr_owner * 8 + nbr_local)
     table = jnp.concatenate([asked, lax.ppermute(asked, "db", swap)], axis=0)
-    tables = [lax.ppermute(table, "db", turn(NZ - k)) for k in SHIFTS]
+    tables = jnp.concatenate([lax.ppermute(table, "db", turn(NZ - k)) for k in SHIFTS], axis=0)
     far = pack_spans(True, tables, db_k, db_v)
     far_got = [lax.ppermute(x, "db", turn(k)) for x, k in zip(far, SHIFTS)]
 

time: 126 us -> 126 us (level)
    all_to_all x1, waiting for transfers between devices: 3.74 us -> 6.22 us  [per_device(): lax.all_to_all(self_rows, 'ctx', split_axis=0, concat_axis=0, tiled=True)]
    ppermute x3, waiting for transfers between devices: 3.76 us -> 1.59 us  [per_device(): near_got.append(lax.ppermute(near[i], 'db', turn(k)))]
    ppermute x3, waiting for transfers between devices: 23.6 us -> 21.9 us  [per_device(): far_got = [lax.ppermute(x, 'db', turn(k)) for x, k in zip(far, SHIFTS)]]
    ppermute x3, waiting for transfers between devices: 1.39 us -> 3.04 us  [per_device(): lax.ppermute(table, 'db', turn(NZ - k))]
    all_to_all x1, starting transfers between devices: 12.8 us -> 14.4 us  [per_device(): lax.all_to_all(self_rows, 'ctx', split_axis=0, concat_axis=0, tiled=True)]
    unnamed x20 -> x18, local copies, waits for them, and re-layouts: 3.1 us -> 3.11 us
  transfers between devices with their start and end apart: 14 -> 14, of which waited for: 6 -> 7; matrix products, arithmetic and copies ran while one was open for 0% -> 0% of each run, Pallas kernels for 36% -> 36%
where the time goes in v10:
time: 126 us; the launch traced here: 125 us
  Pallas kernels  47.3 us (38%)
  starting transfers between devices  40.5 us (32%)
  waiting for transfers between devices  33.7 us (27%)
  local copies, waits for them, and re-layouts  3.12 us (2%)
    ppermute x3, waiting for transfers between devices, per_device(): far_got = [lax.ppermute(x, 'db', turn(k)) for x, k in zip(far, SHIFTS)]  21.9 us
    pallas_call x1, Pallas kernels, self_attention(): pl.pallas_call(self_kernel, in_specs=[pl.BlockSpec(memory_space=pltpu.VME...  18.5 us
    pallas_call x2, Pallas kernels, cross(): pl.pallas_call(functools.partial(cross_kernel, far), in_specs=[pl.BlockSp...  14.7 us
    all_to_all x1, starting transfers between devices, per_device(): lax.all_to_all(self_rows, 'ctx', split_axis=0, concat_axis=0, tiled=True)  14.4 us
    pallas_call x2, Pallas kernels, pack_spans(): pl.pallas_call(functools.partial(pack_spans_kernel, int(far)), in_specs=[...  9.94 us
    all_to_all x1, starting transfers between devices, per_device(): lax.all_to_all(heads, 'ctx', split_axis=0, concat_axis=0, tiled=True)  8.91 us
    all_to_all x1, waiting for transfers between devices, per_device(): lax.all_to_all(self_rows, 'ctx', split_axis=0, concat_axis=0, tiled=True)  6.22 us
    ppermute x3, starting transfers between devices, per_device(): lax.ppermute(table, 'db', turn(NZ - k))  5.29 us
  transfers between devices with their start and end apart: 14, of which 7 were waited for; matrix products, arithmetic and copies ran while one was open for 0% of the time, Pallas kernels for 36%

profile of v10, /device:TPU:1, one launch (start us, length us, event | category | flops | bytes accessed | tf_op | source)
XLA Modules:
  0.0 125.3 jit_solution(1665077518374941638)
XLA Ops:
  0.6 0.8 copy.22
  1.4 0.8 copy.23
  2.2 3.6 %collective-permute-start = (s32[1,4,2]{2,1,0:T(4,128)S(1)}, s32[1,4,2]{2,1,0:T(4,128)S(1)}, u32[]{:S(2)}, u32[]{:S(2)}) collective-permute-start(s32[1,4,2]{2,1,0:T(4,128)S(1)} %multiply_add_fusion), channel_id=1, source_target_pairs={{0,4},{1,5},{2,6},{3,7},{4,0},{5,1},{6,2},{7,3},{8,12},{9,13},{10,... | collective-permute-start | bytes 104 | tf_op jit(solution)/shard_map/ppermute | solution.py:341
  5.7 0.1 collective-permute-start.7
  5.8 0.9 collective-permute-done
  6.7 3.8 %collective-permute-start.3 = (s32[2,4,2]{2,1,0:T(4,128)S(1)}, s32[2,4,2]{2,1,0:T(4,128)S(1)}, u32[]{:S(2)}, u32[]{:S(2)}) collective-permute-start(s32[2,4,2]{2,1,0:T(4,128)S(1)} %pad_add_fusion.token_ref.tab_ref), channel_id=1, source_target_pairs={{0,2},{1,3},{2,0},{3,1},{4,6},{5,7},{6,4},{7,5},{8,10},{9,11},{10,... | collective-permute-start | bytes 200 | tf_op jit(solution)/shard_map/ppermute | solution.py:342
  10.5 0.4 collective-permute-start.1
  11.0 1.0 collective-permute-start.2
  12.0 1.4 %collective-permute-done.1 = s32[2,4,2]{2,1,0:T(4,128)S(1)} collective-permute-done((s32[2,4,2]{2,1,0:T(4,128)S(1)}, s32[2,4,2]{2,1,0:T(4,128)S(1)}, u32[]{:S(2)}, u32[]{:S(2)}) %collective-permute-start.1) | collective-permute-done | bytes 96 | tf_op jit(solution)/shard_map/ppermute | solution.py:342
  13.4 1.6 %collective-permute-done.2 = s32[2,4,2]{2,1,0:T(4,128)S(1)} collective-permute-done((s32[2,4,2]{2,1,0:T(4,128)S(1)}, s32[2,4,2]{2,1,0:T(4,128)S(1)}, u32[]{:S(2)}, u32[]{:S(2)}) %collective-permute-start.2) | collective-permute-done | bytes 96 | tf_op jit(solution)/shard_map/ppermute | solution.py:342
  15.0 0.0 collective-permute-done.3
  15.1 0.0 copy-start.6
  15.1 0.6 copy-done.6
  15.7 0.0 copy-start
  15.7 0.0 copy-start.3
  15.7 5.0 %pack_far.1 = (bf16[2,2,64,2048]{3,2,1,0:T(8,128)(2,1)}, bf16[2,2,64,2048]{3,2,1,0:T(8,128)(2,1)}, bf16[2,2,64,2048]{3,2,1,0:T(8,128)(2,1)}) custom-call(s32[6,4,2]{2,1,0:T(4,128)} %copy-done.6, bf16[8,64,2048]{2,1,0:T(8,128)(2,1)} %bitcast.12, bf16[8,64,2048]{2,1,0:T(8,128)(2,1)} %bitcast.16), custom_call_target="tpu_custom_call" | custom-call | bytes 458752 | tf_op jit(solution)/shard_map/pack_far/pallas_call | solution.py:195
  20.7 0.1 collective-permute-start.8
  20.8 2.7 %collective-permute-start.9 = (bf16[2,2,64,2048]{3,2,1,0:T(8,128)(2,1)}, bf16[2,2,64,2048]{3,2,1,0:T(8,128)(2,1)}, u32[]{:S(2)}, u32[]{:S(2)}) collective-permute-start(bf16[2,2,64,2048]{3,2,1,0:T(8,128)(2,1)} %get-tuple-element.18), channel_id=1, source_target_pairs={{0,3},{1,0},{2,1},{3,2},{4,7},{5,4},{6,5},{7,6},{8,11},{9,8},{10,9... | collective-permute-start | bytes 3145736 | tf_op jit(solution)/shard_map/ppermute | solution.py:344
  23.4 0.0 collective-permute-start.10
  23.5 0.0 copy-done
  23.5 0.0 copy-done.3
  23.5 0.0 copy-done.4
  23.5 0.0 copy-done.5
  23.5 2.5 %pack_heads.1 = bf16[16,784,128]{2,1,0:T(8,128)(2,1)} custom-call(s32[2,4,2]{2,1,0:T(4,128)S(1)} %pad_add_fusion.token_ref.tab_ref, s32[1,256]{1,0:T(1,128)S(1)} %copy-done.5, bf16[256,2048]{1,0:T(8,128)(2,1)S(1)} %bitcast.8, bf16[256,2048]{1,0:T(8,128)(2,1)S(1)} %bitcast.10, bf16[256,2048]{1,0:T(8,128)(2,1)S(1)} %bitcast.11), custom_call_target="tpu_custom_call" | custom-call | bytes 393216 | tf_op jit(solution)/shard_map/pack_heads/pallas_call | solution.py:51
  26.0 8.9 %all-to-all-start = ((bf16[16,784,128]{2,1,0:T(8,128)(2,1)}), bf16[16,784,128]{2,1,0:T(8,128)(2,1)S(1)}, u32[]{:S(2)}, u32[]{:S(2)}) async-start(bf16[16,784,128]{2,1,0:T(8,128)(2,1)} %pack_heads.1), calls=%async_computation | async-start | bytes 6422528 | tf_op jit(solution)/shard_map/all_to_all | solution.py:347
  34.9 4.9 %pack_near.1 = (bf16[2,2,64,2048]{3,2,1,0:T(8,128)(2,1)}, bf16[2,2,64,2048]{3,2,1,0:T(8,128)(2,1)}, bf16[2,2,64,2048]{3,2,1,0:T(8,128)(2,1)}) custom-call(s32[6,4,2]{2,1,0:T(4,128)} %copy-done.6, bf16[8,64,2048]{2,1,0:T(8,128)(2,1)} %bitcast.13, bf16[8,64,2048]{2,1,0:T(8,128)(2,1)} %bitcast.17), custom_call_target="tpu_custom_call" | custom-call | bytes 458752 | tf_op jit(solution)/shard_map/pack_near/pallas_call | solution.py:195
  39.8 0.2 collective-permute-start.4
  40.1 0.0 collective-permute-done.7.q_ref
  40.1 2.5 %collective-permute-start.5 = (bf16[2,2,64,2048]{3,2,1,0:T(8,128)(2,1)}, bf16[2,2,64,2048]{3,2,1,0:T(8,128)(2,1)}, u32[]{:S(2)}, u32[]{:S(2)}) collective-permute-start(bf16[2,2,64,2048]{3,2,1,0:T(8,128)(2,1)} %get-tuple-element.12), channel_id=1, source_target_pairs={{0,3},{1,0},{2,1},{3,2},{4,7},{5,4},{6,5},{7,6},{8,11},{9,8},{10,9... | collective-permute-start | bytes 3145736 | tf_op jit(solution)/shard_map/ppermute | solution.py:352
  42.6 3.7 %collective-permute-done.8.refs_2_ = bf16[2,2,64,2048]{3,2,1,0:T(8,128)(2,1)} collective-permute-done((bf16[2,2,64,2048]{3,2,1,0:T(8,128)(2,1)}, bf16[2,2,64,2048]{3,2,1,0:T(8,128)(2,1)}, u32[]{:S(2)}, u32[]{:S(2)}) %collective-permute-start.8) | collective-permute-done | bytes 1048608 | tf_op jit(solution)/shard_map/ppermute | solution.py:344
  46.3 0.0 collective-permute-start.6
  46.3 0.0 collective-permute-done.9.refs_3_
  46.3 18.2 %collective-permute-done.10.refs_4_ = bf16[2,2,64,2048]{3,2,1,0:T(8,128)(2,1)} collective-permute-done((bf16[2,2,64,2048]{3,2,1,0:T(8,128)(2,1)}, bf16[2,2,64,2048]{3,2,1,0:T(8,128)(2,1)}, u32[]{:S(2)}, u32[]{:S(2)}) %collective-permute-start.10) | collective-permute-done | bytes 1048608 | tf_op jit(solution)/shard_map/ppermute | solution.py:344
  64.5 6.7 %cross_far.1 = bf16[256,2176]{1,0:T(8,128)(2,1)} custom-call(s32[2,4,2]{2,1,0:T(4,128)S(1)} %pad_add_fusion.token_ref.tab_ref, bf16[256,2048]{1,0:T(8,128)(2,1)} %collective-permute-done.7.q_ref, bf16[8,64,2048]{2,1,0:T(8,128)(2,1)} %bitcast.14, bf16[8,64,2048]{2,1,0:T(8,128)(2,1)} %bitcast.18, bf16[2,2,64,2048]{3,2,1,0:T(8,128)(2,1)} %collective-permute-done.8.refs_2_, ...), custom_call_target="tpu_custom_call" | custom-call | flops 34359738368 | tf_op jit(solution)/shard_map/cross_far/pallas_call | solution.py:298
  71.2 2.7 %collective-permute-start.11 = (bf16[256,2176]{1,0:T(8,128)(2,1)}, bf16[256,2176]{1,0:T(8,128)(2,1)}, u32[]{:S(2)}, u32[]{:S(2)}) collective-permute-start(bf16[256,2176]{1,0:T(8,128)(2,1)} %cross_far.1), channel_id=1, source_target_pairs={{0,4},{1,5},{2,6},{3,7},{4,0},{5,1},{6,2},{7,3},{8,12},{9,13},{10,... | collective-permute-start | bytes 3342344 | tf_op jit(solution)/shard_map/ppermute | solution.py:353
  74.0 0.0 all-to-all-done.x_ref
  74.0 18.5 %self_attention.1 = bf16[16,256,128]{2,1,0:T(8,128)(2,1)S(1)} custom-call(bf16[16,784,128]{2,1,0:T(8,128)(2,1)S(1)} %all-to-all-done.x_ref), custom_call_target="tpu_custom_call" | custom-call | flops 268435456 | bytes 262144 | tf_op jit(solution)/shard_map/self_attention/pallas_call | solution.py:152
  92.5 0.0 copy-start.2
  92.5 1.0 copy-done.2
  93.5 14.4 %all-to-all-start.1 = ((bf16[16,256,128]{2,1,0:T(8,128)(2,1)}), bf16[16,256,128]{2,1,0:T(8,128)(2,1)S(1)}, u32[]{:S(2)}, u32[]{:S(2)}) async-start(bf16[16,256,128]{2,1,0:T(8,128)(2,1)} %copy-done.2), calls=%async_computation.1 | async-start | bytes 2097152 | tf_op jit(solution)/shard_map/all_to_all | solution.py:356
  107.9 0.0 collective-permute-done.4.refs_0_
  107.9 0.0 collective-permute-done.5.refs_1_
  107.9 1.6 %collective-permute-done.6.refs_2_ = bf16[2,2,64,2048]{3,2,1,0:T(8,128)(2,1)} collective-permute-done((bf16[2,2,64,2048]{3,2,1,0:T(8,128)(2,1)}, bf16[2,2,64,2048]{3,2,1,0:T(8,128)(2,1)}, u32[]{:S(2)}, u32[]{:S(2)}) %collective-permute-start.6) | collective-permute-done | bytes 1048608 | tf_op jit(solution)/shard_map/ppermute | solution.py:352
  109.5 0.0 collective-permute-done.11.refs_5_
  109.5 0.0 copy-done.1
  109.5 8.0 %cross_near.1 = bf16[256,2048]{1,0:T(8,128)(2,1)} custom-call(s32[2,4,2]{2,1,0:T(4,128)S(1)} %pad_add_fusion.token_ref.tab_ref, bf16[256,2048]{1,0:T(8,128)(2,1)S(1)} %bitcast.9, bf16[8,64,2048]{2,1,0:T(8,128)(2,1)} %bitcast.15, bf16[8,64,2048]{2,1,0:T(8,128)(2,1)} %bitcast.19, bf16[2,2,64,2048]{3,2,1,0:T(8,128)(2,1)} %get-tuple-element.14.refs_2_, ...), custom_call_target="tpu_custom_call" | custom-call | flops 67108864 | tf_op jit(solution)/shard_map/cross_near/pallas_call | solution.py:298
  117.5 6.2 %all-to-all-done.1.x_ref = bf16[16,256,128]{2,1,0:T(8,128)(2,1)S(1)} async-done(((bf16[16,256,128]{2,1,0:T(8,128)(2,1)}), bf16[16,256,128]{2,1,0:T(8,128)(2,1)S(1)}, u32[]{:S(2)}, u32[]{:S(2)}) %all-to-all-start.1) | async-done | bytes 1048608 | tf_op jit(solution)/shard_map/all_to_all | solution.py:356
  123.7 1.6 %unpack_heads.1 = bf16[256,2048]{1,0:T(8,128)(2,1)} custom-call(bf16[16,256,128]{2,1,0:T(8,128)(2,1)S(1)} %all-to-all-done.1.x_ref), custom_call_target="tpu_custom_call" | custom-call | bytes 131072 | tf_op jit(solution)/shard_map/unpack_heads/pallas_call | solution.py:75
  (9 shorter events, 0.0 us)
Async XLA Ops:
  2.2 4.5 %collective-permute-start = (s32[1,4,2]{2,1,0:T(4,128)S(1)}, s32[1,4,2]{2,1,0:T(4,128)S(1)}, u32[]{:S(2)}, u32[]{:S(2)}) collective-permute-start(s32[1,4,2]{2,1,0:T(4,128)S(1)} %multiply_add_fusion), channel_id=1, source_target_pairs={{0,4},{1,5},{2,6},{3,7},{4,0},{5,1},{6,2},{7,3},{8,12},{9,13},{10,... | collective-permute-start | bytes 104 | tf_op jit(solution)/shard_map/ppermute | solution.py:341
  5.7 34.4 %collective-permute-start.7 = (bf16[256,2048]{1,0:T(8,128)(2,1)}, bf16[256,2048]{1,0:T(8,128)(2,1)}, u32[]{:S(2)}, u32[]{:S(2)}) collective-permute-start(bf16[256,2048]{1,0:T(8,128)(2,1)} %bitcast.7), channel_id=1, source_target_pairs={{0,4},{1,5},{2,6},{3,7},{4,0},{5,1},{6,2},{7,3},{8,12},{9,13},{10,... | collective-permute-start | bytes 3145736 | tf_op jit(solution)/shard_map/ppermute | solution.py:338
  6.7 8.3 %collective-permute-start.3 = (s32[2,4,2]{2,1,0:T(4,128)S(1)}, s32[2,4,2]{2,1,0:T(4,128)S(1)}, u32[]{:S(2)}, u32[]{:S(2)}) collective-permute-start(s32[2,4,2]{2,1,0:T(4,128)S(1)} %pad_add_fusion.token_ref.tab_ref), channel_id=1, source_target_pairs={{0,2},{1,3},{2,0},{3,1},{4,6},{5,7},{6,4},{7,5},{8,10},{9,11},{10,... | collective-permute-start | bytes 200 | tf_op jit(solution)/shard_map/ppermute | solution.py:342
  10.5 2.9 %collective-permute-start.1 = (s32[2,4,2]{2,1,0:T(4,128)S(1)}, s32[2,4,2]{2,1,0:T(4,128)S(1)}, u32[]{:S(2)}, u32[]{:S(2)}) collective-permute-start(s32[2,4,2]{2,1,0:T(4,128)S(1)} %pad_add_fusion.token_ref.tab_ref), channel_id=1, source_target_pairs={{0,3},{1,0},{2,1},{3,2},{4,7},{5,4},{6,5},{7,6},{8,11},{9,8},{10,9... | collective-permute-start | bytes 200 | tf_op jit(solution)/shard_map/ppermute | solution.py:342
  11.0 4.1 %collective-permute-start.2 = (s32[2,4,2]{2,1,0:T(4,128)S(1)}, s32[2,4,2]{2,1,0:T(4,128)S(1)}, u32[]{:S(2)}, u32[]{:S(2)}) collective-permute-start(s32[2,4,2]{2,1,0:T(4,128)S(1)} %pad_add_fusion.token_ref.tab_ref), channel_id=1, source_target_pairs={{0,1},{1,2},{2,3},{3,0},{4,5},{5,6},{6,7},{7,4},{8,9},{9,10},{10,1... | collective-permute-start | bytes 200 | tf_op jit(solution)/shard_map/ppermute | solution.py:342
  15.1 0.6 copy-start.6
  15.7 7.8 %copy-start = (bf16[1,256,2048]{2,1,0:T(8,128)(2,1)S(1)}, bf16[1,256,2048]{2,1,0:T(8,128)(2,1)}, u32[]{:S(2)}) copy-start(bf16[1,256,2048]{2,1,0:T(8,128)(2,1)} %param.8) | copy-start | bytes 3145732
  15.7 7.8 %copy-start.3 = (bf16[1,256,2048]{2,1,0:T(8,128)(2,1)S(1)}, bf16[1,256,2048]{2,1,0:T(8,128)(2,1)}, u32[]{:S(2)}) copy-start(bf16[1,256,2048]{2,1,0:T(8,128)(2,1)} %param.9) | copy-start | bytes 3145732
  15.7 7.8 %copy-start.4 = (bf16[1,256,2048]{2,1,0:T(8,128)(2,1)S(1)}, bf16[1,256,2048]{2,1,0:T(8,128)(2,1)}, u32[]{:S(2)}) copy-start(bf16[1,256,2048]{2,1,0:T(8,128)(2,1)} %param.10) | copy-start | bytes 3145732
  15.7 7.8 %copy-start.5 = (s32[1,256]{1,0:T(1,128)S(1)}, s32[1,256]{1,0:T(1,128)}, u32[]{:S(2)}) copy-start(s32[1,256]{1,0:T(1,128)} %docs_ref.1) | copy-start | bytes 3076
  20.7 25.6 %collective-permute-start.8 = (bf16[2,2,64,2048]{3,2,1,0:T(8,128)(2,1)}, bf16[2,2,64,2048]{3,2,1,0:T(8,128)(2,1)}, u32[]{:S(2)}, u32[]{:S(2)}) collective-permute-start(bf16[2,2,64,2048]{3,2,1,0:T(8,128)(2,1)} %get-tuple-element.17), channel_id=1, source_target_pairs={{0,1},{1,2},{2,3},{3,0},{4,5},{5,6},{6,7},{7,4},{8,9},{9,10},{10,1... | collective-permute-start | bytes 3145736 | tf_op jit(solution)/shard_map/ppermute | solution.py:344
  20.8 25.6 %collective-permute-start.9 = (bf16[2,2,64,2048]{3,2,1,0:T(8,128)(2,1)}, bf16[2,2,64,2048]{3,2,1,0:T(8,128)(2,1)}, u32[]{:S(2)}, u32[]{:S(2)}) collective-permute-start(bf16[2,2,64,2048]{3,2,1,0:T(8,128)(2,1)} %get-tuple-element.18), channel_id=1, source_target_pairs={{0,3},{1,0},{2,1},{3,2},{4,7},{5,4},{6,5},{7,6},{8,11},{9,8},{10,9... | collective-permute-start | bytes 3145736 | tf_op jit(solution)/shard_map/ppermute | solution.py:344
  23.4 41.1 %collective-permute-start.10 = (bf16[2,2,64,2048]{3,2,1,0:T(8,128)(2,1)}, bf16[2,2,64,2048]{3,2,1,0:T(8,128)(2,1)}, u32[]{:S(2)}, u32[]{:S(2)}) collective-permute-start(bf16[2,2,64,2048]{3,2,1,0:T(8,128)(2,1)} %get-tuple-element.19), channel_id=1, source_target_pairs={{0,2},{1,3},{2,0},{3,1},{4,6},{5,7},{6,4},{7,5},{8,10},{9,11},{10,... | collective-permute-start | bytes 3145736 | tf_op jit(solution)/shard_map/ppermute | solution.py:344
  26.0 48.0 %all-to-all-start = ((bf16[16,784,128]{2,1,0:T(8,128)(2,1)}), bf16[16,784,128]{2,1,0:T(8,128)(2,1)S(1)}, u32[]{:S(2)}, u32[]{:S(2)}) async-start(bf16[16,784,128]{2,1,0:T(8,128)(2,1)} %pack_heads.1), calls=%async_computation | async-start | bytes 6422528 | tf_op jit(solution)/shard_map/all_to_all | solution.py:347
  39.8 68.1 %collective-permute-start.4 = (bf16[2,2,64,2048]{3,2,1,0:T(8,128)(2,1)}, bf16[2,2,64,2048]{3,2,1,0:T(8,128)(2,1)}, u32[]{:S(2)}, u32[]{:S(2)}) collective-permute-start(bf16[2,2,64,2048]{3,2,1,0:T(8,128)(2,1)} %get-tuple-element.11), channel_id=1, source_target_pairs={{0,1},{1,2},{2,3},{3,0},{4,5},{5,6},{6,7},{7,4},{8,9},{9,10},{10,1... | collective-permute-start | bytes 3145736 | tf_op jit(solution)/shard_map/ppermute | solution.py:352
  40.1 67.8 %collective-permute-start.5 = (bf16[2,2,64,2048]{3,2,1,0:T(8,128)(2,1)}, bf16[2,2,64,2048]{3,2,1,0:T(8,128)(2,1)}, u32[]{:S(2)}, u32[]{:S(2)}) collective-permute-start(bf16[2,2,64,2048]{3,2,1,0:T(8,128)(2,1)} %get-tuple-element.12), channel_id=1, source_target_pairs={{0,3},{1,0},{2,1},{3,2},{4,7},{5,4},{6,5},{7,6},{8,11},{9,8},{10,9... | collective-permute-start | bytes 3145736 | tf_op jit(solution)/shard_map/ppermute | solution.py:352
  46.3 63.2 %collective-permute-start.6 = (bf16[2,2,64,2048]{3,2,1,0:T(8,128)(2,1)}, bf16[2,2,64,2048]{3,2,1,0:T(8,128)(2,1)}, u32[]{:S(2)}, u32[]{:S(2)}) collective-permute-start(bf16[2,2,64,2048]{3,2,1,0:T(8,128)(2,1)} %get-tuple-element.13), channel_id=1, source_target_pairs={{0,2},{1,3},{2,0},{3,1},{4,6},{5,7},{6,4},{7,5},{8,10},{9,11},{10,... | collective-permute-start | bytes 3145736 | tf_op jit(solution)/shard_map/ppermute | solution.py:352
  71.2 38.3 %collective-permute-start.11 = (bf16[256,2176]{1,0:T(8,128)(2,1)}, bf16[256,2176]{1,0:T(8,128)(2,1)}, u32[]{:S(2)}, u32[]{:S(2)}) collective-permute-start(bf16[256,2176]{1,0:T(8,128)(2,1)} %cross_far.1), channel_id=1, source_target_pairs={{0,4},{1,5},{2,6},{3,7},{4,0},{5,1},{6,2},{7,3},{8,12},{9,13},{10,... | collective-permute-start | bytes 3342344 | tf_op jit(solution)/shard_map/ppermute | solution.py:353
  92.5 1.0 copy-start.2
  93.5 30.2 %all-to-all-start.1 = ((bf16[16,256,128]{2,1,0:T(8,128)(2,1)}), bf16[16,256,128]{2,1,0:T(8,128)(2,1)S(1)}, u32[]{:S(2)}, u32[]{:S(2)}) async-start(bf16[16,256,128]{2,1,0:T(8,128)(2,1)} %copy-done.2), calls=%async_computation.1 | async-start | bytes 2097152 | tf_op jit(solution)/shard_map/all_to_all | solution.py:356
  107.9 1.6 %copy-start.1 = (bf16[1,256,2048]{2,1,0:T(8,128)(2,1)S(1)}, bf16[1,256,2048]{2,1,0:T(8,128)(2,1)}, u32[]{:S(2)}) copy-start(bf16[1,256,2048]{2,1,0:T(8,128)(2,1)} %param.8) | copy-start | bytes 3145732

commit v11 on v10

--- a/solution.py
+++ b/solution.py
@@ -20,6 +20,7 @@
 NEG = -1e30
 SCALE = math.log2(math.e) / math.sqrt(DH)
 VMEM = 48 << 20
+GRANT = 60
 
 f32, bf16, i32 = jnp.float32, jnp.bfloat16, jnp.int32
 
@@ -163,26 +164,23 @@
 SHIFTS = (1, 3, 2)
 
 
-def pack_spans_kernel(far, *refs):
-    tab_ref, keys_ref, values_ref = refs[:3]
-    outs, hold, loads, stores = refs[3:6], refs[6], refs[7], refs[8]
+def pack_spans_kernel(far, tab_ref, keys_ref, values_ref, out_ref, hold, loads, stores):
     me = lax.axis_index("db")
+    first, second, seen = jnp.int32(0), jnp.int32(0), jnp.int32(0)
+    for r in range(8):
+        entry = tab_ref[far, r // 2, r % 2]
+        hit = (entry >> 3) == me
+        span = entry & 7
+        first = jnp.where(hit & (seen == 0), span, first)
+        second = jnp.where(hit & (seen == 1), span, second)
+        seen = seen + jnp.where(hit, 1, 0)
     moves = []
-    for i in range(3):
-        first, second, seen = jnp.int32(0), jnp.int32(0), jnp.int32(0)
-        for r in range(8):
-            entry = tab_ref[2 * i + far, r // 2, r % 2]
-            hit = (entry >> 3) == me
-            span = entry & 7
-            first = jnp.where(hit & (seen == 0), span, first)
-            second = jnp.where(hit & (seen == 1), span, second)
-            seen = seen + jnp.where(hit, 1, 0)
-        for slot, span in ((0, first), (1, second)):
-            for kind, src in ((0, keys_ref), (1, values_ref)):
-                at = (i, slot, kind)
-                load = pltpu.make_async_copy(src.at[span], hold.at[at], loads.at[at])
-                load.start()
-                moves.append((load, pltpu.make_async_copy(hold.at[at], outs[i].at[slot, kind], stores.at[at])))
+    for slot, span in ((0, first), (1, second)):
+        for kind, src in ((0, keys_ref), (1, values_ref)):
+            at = (slot, kind)
+            load = pltpu.make_async_copy(src.at[span], hold.at[at], loads.at[at])
+            load.start()
+            moves.append((load, pltpu.make_async_copy(hold.at[at], out_ref.at[at], stores.at[at])))
     for load, store in moves:
         load.wait()
         store.start()
@@ -195,15 +193,15 @@
     return pl.pallas_call(
         functools.partial(pack_spans_kernel, int(far)),
         in_specs=[pl.BlockSpec(memory_space=pltpu.SMEM), anywhere, anywhere],
-        out_specs=[anywhere] * 3,
-        out_shape=[jax.ShapeDtypeStruct((2, 2, CH, HD), bf16)] * 3,
+        out_specs=anywhere,
+        out_shape=jax.ShapeDtypeStruct((2, 2, CH, HD), bf16),
         scratch_shapes=[
-            pltpu.VMEM((3, 2, 2, CH, HD), bf16),
-            pltpu.SemaphoreType.DMA((3, 2, 2)),
-            pltpu.SemaphoreType.DMA((3, 2, 2)),
+            pltpu.VMEM((2, 2, CH, HD), bf16),
+            pltpu.SemaphoreType.DMA((2, 2)),
+            pltpu.SemaphoreType.DMA((2, 2)),
         ],
-        compiler_params=pltpu.CompilerParams(vmem_limit_bytes=60 << 20),
-        cost_estimate=cost(0, 7 << 20),
+        compiler_params=pltpu.CompilerParams(vmem_limit_bytes=GRANT << 20),
+        cost_estimate=cost(0, 3 << 20),
         name="pack_far" if far else "pack_near",
     )(table, keys, values)
 
@@ -339,14 +337,14 @@
 
     asked = lax.optimization_barrier(nbr_owner * 8 + nbr_local)
     table = jnp.concatenate([asked, lax.ppermute(asked, "db", swap)], axis=0)
-    tables = jnp.concatenate([lax.ppermute(table, "db", turn(NZ - k)) for k in SHIFTS], axis=0)
-    far = pack_spans(True, tables, db_k, db_v)
+    tables = [lax.ppermute(table, "db", turn(NZ - k)) for k in SHIFTS]
+    far = [pack_spans(True, t, db_k, db_v) for t in tables]
     far_got = [lax.ppermute(x, "db", turn(k)) for x, k in zip(far, SHIFTS)]
 
     heads = pack_heads(table, doc_ids, q, keys[0], values[0])
     heads = lax.all_to_all(heads, "ctx", split_axis=0, concat_axis=0, tiled=True)
 
-    near = pack_spans(False, tables, db_k, db_v)
+    near = [pack_spans(False, t, db_k, db_v) for t in tables]
     near_got = []
     for i, k in enumerate(SHIFTS):
         near_got.append(lax.ppermute(near[i], "db", turn(k)))

time: 126 us -> 121 us (0.960)
  Pallas kernels: 47.3 us -> 53.7 us
  waiting for transfers between devices: 33.7 us -> 27.4 us
  starting transfers between devices: 40.5 us -> 34.3 us
    all_to_all x1, starting transfers between devices: 14.4 us -> 4.84 us  [per_device(): lax.all_to_all(self_rows, 'ctx', split_axis=0, concat_axis=0, tiled=True)]
    ppermute x3, waiting for transfers between devices: 21.9 us -> 14.1 us  [per_device(): far_got = [lax.ppermute(x, 'db', turn(k)) for x, k in zip(far, SHIFTS)]]
    pallas_call x2 -> x6, Pallas kernels: 9.94 us -> 16.5 us  [pack_spans(): pl.pallas_call(functools.partial(pack_spans_kernel, int(far)), in_specs=[...]
    all_to_all x1, waiting for transfers between devices: 0.01 us -> 4.45 us  [per_device(): lax.all_to_all(heads, 'ctx', split_axis=0, concat_axis=0, tiled=True)]
    ppermute x3, waiting for transfers between devices: 3.04 us -> 0.01 us  [per_device(): tables = [lax.ppermute(table, 'db', turn(NZ - k)) for k in SHIFTS]]
    ppermute x3, starting transfers between devices: 2.74 us -> 5.39 us  [per_device(): far_got = [lax.ppermute(x, 'db', turn(k)) for x, k in zip(far, SHIFTS)]]
    ppermute x3, waiting for transfers between devices: 1.59 us -> 3.7 us  [per_device(): near_got.append(lax.ppermute(near[i], 'db', turn(k)))]
    all_to_all x1, waiting for transfers between devices: 6.22 us -> 4.2 us  [per_device(): lax.all_to_all(self_rows, 'ctx', split_axis=0, concat_axis=0, tiled=True)]
  transfers between devices with their start and end apart: 14 -> 14, of which waited for: 7 -> 5; matrix products, arithmetic and copies ran while one was open for 0% -> 0% of each run, Pallas kernels for 36% -> 43%
where the time goes in v11:
time: 121 us; the launch traced here: 120 us
  Pallas kernels  53.7 us (44%)
  starting transfers between devices  34.3 us (28%)
  waiting for transfers between devices  27.4 us (23%)
  local copies, waits for them, and re-layouts  4.3 us (4%)
    pallas_call x1, Pallas kernels, self_attention(): pl.pallas_call(self_kernel, in_specs=[pl.BlockSpec(memory_space=pltpu.VME...  18.5 us
    pallas_call x6, Pallas kernels, pack_spans(): pl.pallas_call(functools.partial(pack_spans_kernel, int(far)), in_specs=[...  16.5 us
    pallas_call x2, Pallas kernels, cross(): pl.pallas_call(functools.partial(cross_kernel, far), in_specs=[pl.BlockSp...  14.4 us
    ppermute x3, waiting for transfers between devices, per_device(): far_got = [lax.ppermute(x, 'db', turn(k)) for x, k in zip(far, SHIFTS)]  14.1 us
    all_to_all x1, starting transfers between devices, per_device(): lax.all_to_all(heads, 'ctx', split_axis=0, concat_axis=0, tiled=True)  9.47 us
    ppermute x3, starting transfers between devices, per_device(): far_got = [lax.ppermute(x, 'db', turn(k)) for x, k in zip(far, SHIFTS)]  5.39 us
    ppermute x3, starting transfers between devices, per_device(): tables = [lax.ppermute(table, 'db', turn(NZ - k)) for k in SHIFTS]  5.29 us
    all_to_all x1, starting transfers between devices, per_device(): lax.all_to_all(self_rows, 'ctx', split_axis=0, concat_axis=0, tiled=True)  4.84 us
  transfers between devices with their start and end apart: 14, of which 5 were waited for; matrix products, arithmetic and copies ran while one was open for 0% of the time, Pallas kernels for 43%

profile of v11, /device:TPU:1, one launch (start us, length us, event | category | flops | bytes accessed | tf_op | source)
XLA Modules:
  0.0 120.4 jit_solution(2241199819012846455)
XLA Ops:
  0.6 0.8 copy.13
  1.4 0.8 copy.14
  2.2 3.6 %collective-permute-start = (s32[1,4,2]{2,1,0:T(4,128)S(1)}, s32[1,4,2]{2,1,0:T(4,128)S(1)}, u32[]{:S(2)}, u32[]{:S(2)}) collective-permute-start(s32[1,4,2]{2,1,0:T(4,128)S(1)} %multiply_add_fusion), channel_id=1, source_target_pairs={{0,4},{1,5},{2,6},{3,7},{4,0},{5,1},{6,2},{7,3},{8,12},{9,13},{10,... | collective-permute-start | bytes 104 | tf_op jit(solution)/shard_map/ppermute | solution.py:339
  5.7 0.1 collective-permute-start.7
  5.8 0.9 collective-permute-done
  6.7 3.8 %collective-permute-start.5 = (s32[2,4,2]{2,1,0:T(4,128)S(1)}, s32[2,4,2]{2,1,0:T(4,128)S(1)}, u32[]{:S(2)}, u32[]{:S(2)}) collective-permute-start(s32[2,4,2]{2,1,0:T(4,128)S(1)} %pad_add_fusion.token_ref.tab_ref), channel_id=1, source_target_pairs={{0,2},{1,3},{2,0},{3,1},{4,6},{5,7},{6,4},{7,5},{8,10},{9,11},{10,... | collective-permute-start | bytes 200 | tf_op jit(solution)/shard_map/ppermute | solution.py:340
  10.5 0.4 collective-permute-start.1
  11.0 1.0 collective-permute-start.3
  12.0 0.0 collective-permute-done.5.tab_ref
  12.0 0.6 copy-done.6
  12.6 2.8 %pack_far.5 = bf16[2,2,64,2048]{3,2,1,0:T(8,128)(2,1)} custom-call(s32[2,4,2]{2,1,0:T(4,128)} %copy-done.6, bf16[8,64,2048]{2,1,0:T(8,128)(2,1)} %bitcast.12, bf16[8,64,2048]{2,1,0:T(8,128)(2,1)} %bitcast.20), custom_call_target="tpu_custom_call" | custom-call | bytes 196608 | tf_op jit(solution)/shard_map/pack_far/pallas_call | solution.py:193
  15.4 2.6 %collective-permute-start.10 = (bf16[2,2,64,2048]{3,2,1,0:T(8,128)(2,1)}, bf16[2,2,64,2048]{3,2,1,0:T(8,128)(2,1)}, u32[]{:S(2)}, u32[]{:S(2)}) collective-permute-start(bf16[2,2,64,2048]{3,2,1,0:T(8,128)(2,1)} %pack_far.5), channel_id=1, source_target_pairs={{0,2},{1,3},{2,0},{3,1},{4,6},{5,7},{6,4},{7,5},{8,10},{9,11},{10,... | collective-permute-start | bytes 3145736 | tf_op jit(solution)/shard_map/ppermute | solution.py:342
  17.9 0.0 collective-permute-done.1.tab_ref
  17.9 0.6 copy-done.8
  18.5 2.7 %pack_far.3 = bf16[2,2,64,2048]{3,2,1,0:T(8,128)(2,1)} custom-call(s32[2,4,2]{2,1,0:T(4,128)} %copy-done.8, bf16[8,64,2048]{2,1,0:T(8,128)(2,1)} %bitcast.13, bf16[8,64,2048]{2,1,0:T(8,128)(2,1)} %bitcast.21), custom_call_target="tpu_custom_call" | custom-call | bytes 196608 | tf_op jit(solution)/shard_map/pack_far/pallas_call | solution.py:193
  21.3 0.0 copy-start
  21.3 0.0 copy-start.3
  21.3 0.0 copy-start.4
  21.3 0.0 copy-start.5
  21.3 0.8 collective-permute-start.8
  22.1 0.0 collective-permute-done.3.tab_ref
  22.2 0.6 copy-done.7
  22.7 2.7 %pack_far.4 = bf16[2,2,64,2048]{3,2,1,0:T(8,128)(2,1)} custom-call(s32[2,4,2]{2,1,0:T(4,128)} %copy-done.7, bf16[8,64,2048]{2,1,0:T(8,128)(2,1)} %bitcast.14, bf16[8,64,2048]{2,1,0:T(8,128)(2,1)} %bitcast.22), custom_call_target="tpu_custom_call" | custom-call | bytes 196608 | tf_op jit(solution)/shard_map/pack_far/pallas_call | solution.py:193
  25.5 2.0 %collective-permute-start.9 = (bf16[2,2,64,2048]{3,2,1,0:T(8,128)(2,1)}, bf16[2,2,64,2048]{3,2,1,0:T(8,128)(2,1)}, u32[]{:S(2)}, u32[]{:S(2)}) collective-permute-start(bf16[2,2,64,2048]{3,2,1,0:T(8,128)(2,1)} %pack_far.4), channel_id=1, source_target_pairs={{0,3},{1,0},{2,1},{3,2},{4,7},{5,4},{6,5},{7,6},{8,11},{9,8},{10,9... | collective-permute-start | bytes 3145736 | tf_op jit(solution)/shard_map/ppermute | solution.py:342
  27.5 2.6 %pack_heads.1 = bf16[16,784,128]{2,1,0:T(8,128)(2,1)} custom-call(s32[2,4,2]{2,1,0:T(4,128)S(1)} %pad_add_fusion.token_ref.tab_ref, s32[1,256]{1,0:T(1,128)S(1)} %copy-done.5, bf16[256,2048]{1,0:T(8,128)(2,1)S(1)} %bitcast.8, bf16[256,2048]{1,0:T(8,128)(2,1)S(1)} %bitcast.10, bf16[256,2048]{1,0:T(8,128)(2,1)S(1)} %bitcast.11), custom_call_target="tpu_custom_call" | custom-call | bytes 393216 | tf_op jit(solution)/shard_map/pack_heads/pallas_call | solution.py:52
  30.1 9.5 %all-to-all-start = ((bf16[16,784,128]{2,1,0:T(8,128)(2,1)}), bf16[16,784,128]{2,1,0:T(8,128)(2,1)S(1)}, u32[]{:S(2)}, u32[]{:S(2)}) async-start(bf16[16,784,128]{2,1,0:T(8,128)(2,1)} %pack_heads.1), calls=%async_computation | async-start | bytes 6422528 | tf_op jit(solution)/shard_map/all_to_all | solution.py:345
  39.6 2.7 %pack_near.3 = bf16[2,2,64,2048]{3,2,1,0:T(8,128)(2,1)} custom-call(s32[2,4,2]{2,1,0:T(4,128)} %copy-done.8, bf16[8,64,2048]{2,1,0:T(8,128)(2,1)} %bitcast.15, bf16[8,64,2048]{2,1,0:T(8,128)(2,1)} %bitcast.23), custom_call_target="tpu_custom_call" | custom-call | bytes 196608 | tf_op jit(solution)/shard_map/pack_near/pallas_call | solution.py:193
  42.3 0.1 collective-permute-start.2
  42.4 2.8 %pack_near.4 = bf16[2,2,64,2048]{3,2,1,0:T(8,128)(2,1)} custom-call(s32[2,4,2]{2,1,0:T(4,128)} %copy-done.7, bf16[8,64,2048]{2,1,0:T(8,128)(2,1)} %bitcast.16, bf16[8,64,2048]{2,1,0:T(8,128)(2,1)} %bitcast.24), custom_call_target="tpu_custom_call" | custom-call | bytes 196608 | tf_op jit(solution)/shard_map/pack_near/pallas_call | solution.py:193
  45.2 2.8 %pack_near.5 = bf16[2,2,64,2048]{3,2,1,0:T(8,128)(2,1)} custom-call(s32[2,4,2]{2,1,0:T(4,128)} %copy-done.6, bf16[8,64,2048]{2,1,0:T(8,128)(2,1)} %bitcast.17, bf16[8,64,2048]{2,1,0:T(8,128)(2,1)} %bitcast.25), custom_call_target="tpu_custom_call" | custom-call | bytes 196608 | tf_op jit(solution)/shard_map/pack_near/pallas_call | solution.py:193
  48.0 2.7 %collective-permute-start.4 = (bf16[2,2,64,2048]{3,2,1,0:T(8,128)(2,1)}, bf16[2,2,64,2048]{3,2,1,0:T(8,128)(2,1)}, u32[]{:S(2)}, u32[]{:S(2)}) collective-permute-start(bf16[2,2,64,2048]{3,2,1,0:T(8,128)(2,1)} %pack_near.4), channel_id=1, source_target_pairs={{0,3},{1,0},{2,1},{3,2},{4,7},{5,4},{6,5},{7,6},{8,11},{9,8},{10,9... | collective-permute-start | bytes 3145736 | tf_op jit(solution)/shard_map/ppermute | solution.py:350
  50.7 0.0 collective-permute-done.10.refs_4_
  50.7 0.0 collective-permute-start.6
  50.7 14.1 %collective-permute-done.8.refs_2_ = bf16[2,2,64,2048]{3,2,1,0:T(8,128)(2,1)} collective-permute-done((bf16[2,2,64,2048]{3,2,1,0:T(8,128)(2,1)}, bf16[2,2,64,2048]{3,2,1,0:T(8,128)(2,1)}, u32[]{:S(2)}, u32[]{:S(2)}) %collective-permute-start.8) | collective-permute-done | bytes 1048608 | tf_op jit(solution)/shard_map/ppermute | solution.py:342
  64.8 0.0 collective-permute-done.9.refs_3_
  64.8 6.5 %cross_far.1 = bf16[256,2176]{1,0:T(8,128)(2,1)} custom-call(s32[2,4,2]{2,1,0:T(4,128)S(1)} %pad_add_fusion.token_ref.tab_ref, bf16[256,2048]{1,0:T(8,128)(2,1)} %collective-permute-done.7.q_ref, bf16[8,64,2048]{2,1,0:T(8,128)(2,1)} %bitcast.18, bf16[8,64,2048]{2,1,0:T(8,128)(2,1)} %bitcast.26, bf16[2,2,64,2048]{3,2,1,0:T(8,128)(2,1)} %collective-permute-done.8.refs_2_, ...), custom_call_target="tpu_custom_call" | custom-call | flops 34359738368 | tf_op jit(solution)/shard_map/cross_far/pallas_call | solution.py:296
  71.4 2.8 %collective-permute-start.11 = (bf16[256,2176]{1,0:T(8,128)(2,1)}, bf16[256,2176]{1,0:T(8,128)(2,1)}, u32[]{:S(2)}, u32[]{:S(2)}) collective-permute-start(bf16[256,2176]{1,0:T(8,128)(2,1)} %cross_far.1), channel_id=1, source_target_pairs={{0,4},{1,5},{2,6},{3,7},{4,0},{5,1},{6,2},{7,3},{8,12},{9,13},{10,... | collective-permute-start | bytes 3342344 | tf_op jit(solution)/shard_map/ppermute | solution.py:351
  74.2 4.5 %all-to-all-done.x_ref = bf16[16,784,128]{2,1,0:T(8,128)(2,1)S(1)} async-done(((bf16[16,784,128]{2,1,0:T(8,128)(2,1)}), bf16[16,784,128]{2,1,0:T(8,128)(2,1)S(1)}, u32[]{:S(2)}, u32[]{:S(2)}) %all-to-all-start) | async-done | bytes 3211296 | tf_op jit(solution)/shard_map/all_to_all | solution.py:345
  78.6 18.5 %self_attention.1 = bf16[16,256,128]{2,1,0:T(8,128)(2,1)S(1)} custom-call(bf16[16,784,128]{2,1,0:T(8,128)(2,1)S(1)} %all-to-all-done.x_ref), custom_call_target="tpu_custom_call" | custom-call | flops 268435456 | bytes 262144 | tf_op jit(solution)/shard_map/self_attention/pallas_call | solution.py:153
  97.2 0.0 copy-start.2
  97.2 1.0 copy-done.2
  98.2 4.8 %all-to-all-start.1 = ((bf16[16,256,128]{2,1,0:T(8,128)(2,1)}), bf16[16,256,128]{2,1,0:T(8,128)(2,1)S(1)}, u32[]{:S(2)}, u32[]{:S(2)}) async-start(bf16[16,256,128]{2,1,0:T(8,128)(2,1)} %copy-done.2), calls=%async_computation.1 | async-start | bytes 2097152 | tf_op jit(solution)/shard_map/all_to_all | solution.py:354
  103.0 0.0 collective-permute-done.2.refs_0_
  103.0 3.7 %collective-permute-done.6.refs_2_ = bf16[2,2,64,2048]{3,2,1,0:T(8,128)(2,1)} collective-permute-done((bf16[2,2,64,2048]{3,2,1,0:T(8,128)(2,1)}, bf16[2,2,64,2048]{3,2,1,0:T(8,128)(2,1)}, u32[]{:S(2)}, u32[]{:S(2)}) %collective-permute-start.6) | collective-permute-done | bytes 1048608 | tf_op jit(solution)/shard_map/ppermute | solution.py:350
  106.7 0.0 collective-permute-done.11.refs_5_
  106.7 7.9 %cross_near.1 = bf16[256,2048]{1,0:T(8,128)(2,1)} custom-call(s32[2,4,2]{2,1,0:T(4,128)S(1)} %pad_add_fusion.token_ref.tab_ref, bf16[256,2048]{1,0:T(8,128)(2,1)S(1)} %bitcast.9, bf16[8,64,2048]{2,1,0:T(8,128)(2,1)} %bitcast.19, bf16[8,64,2048]{2,1,0:T(8,128)(2,1)} %bitcast.27, bf16[2,2,64,2048]{3,2,1,0:T(8,128)(2,1)} %get-tuple-element.5.refs_2_, ...), custom_call_target="tpu_custom_call" | custom-call | flops 67108864 | tf_op jit(solution)/shard_map/cross_near/pallas_call | solution.py:296
  114.6 4.2 %all-to-all-done.1.x_ref = bf16[16,256,128]{2,1,0:T(8,128)(2,1)S(1)} async-done(((bf16[16,256,128]{2,1,0:T(8,128)(2,1)}), bf16[16,256,128]{2,1,0:T(8,128)(2,1)S(1)}, u32[]{:S(2)}, u32[]{:S(2)}) %all-to-all-start.1) | async-done | bytes 1048608 | tf_op jit(solution)/shard_map/all_to_all | solution.py:354
  118.8 1.6 %unpack_heads.1 = bf16[256,2048]{1,0:T(8,128)(2,1)} custom-call(bf16[16,256,128]{2,1,0:T(8,128)(2,1)S(1)} %all-to-all-done.1.x_ref), custom_call_target="tpu_custom_call" | custom-call | bytes 131072 | tf_op jit(solution)/shard_map/unpack_heads/pallas_call | solution.py:76
  (14 shorter events, 0.0 us)
Async XLA Ops:
  2.2 4.5 %collective-permute-start = (s32[1,4,2]{2,1,0:T(4,128)S(1)}, s32[1,4,2]{2,1,0:T(4,128)S(1)}, u32[]{:S(2)}, u32[]{:S(2)}) collective-permute-start(s32[1,4,2]{2,1,0:T(4,128)S(1)} %multiply_add_fusion), channel_id=1, source_target_pairs={{0,4},{1,5},{2,6},{3,7},{4,0},{5,1},{6,2},{7,3},{8,12},{9,13},{10,... | collective-permute-start | bytes 104 | tf_op jit(solution)/shard_map/ppermute | solution.py:339
  5.7 42.2 %collective-permute-start.7 = (bf16[256,2048]{1,0:T(8,128)(2,1)}, bf16[256,2048]{1,0:T(8,128)(2,1)}, u32[]{:S(2)}, u32[]{:S(2)}) collective-permute-start(bf16[256,2048]{1,0:T(8,128)(2,1)} %bitcast.7), channel_id=1, source_target_pairs={{0,4},{1,5},{2,6},{3,7},{4,0},{5,1},{6,2},{7,3},{8,12},{9,13},{10,... | collective-permute-start | bytes 3145736 | tf_op jit(solution)/shard_map/ppermute | solution.py:336
  6.7 5.3 %collective-permute-start.5 = (s32[2,4,2]{2,1,0:T(4,128)S(1)}, s32[2,4,2]{2,1,0:T(4,128)S(1)}, u32[]{:S(2)}, u32[]{:S(2)}) collective-permute-start(s32[2,4,2]{2,1,0:T(4,128)S(1)} %pad_add_fusion.token_ref.tab_ref), channel_id=1, source_target_pairs={{0,2},{1,3},{2,0},{3,1},{4,6},{5,7},{6,4},{7,5},{8,10},{9,11},{10,... | collective-permute-start | bytes 200 | tf_op jit(solution)/shard_map/ppermute | solution.py:340
  10.5 7.4 %collective-permute-start.1 = (s32[2,4,2]{2,1,0:T(4,128)S(1)}, s32[2,4,2]{2,1,0:T(4,128)S(1)}, u32[]{:S(2)}, u32[]{:S(2)}) collective-permute-start(s32[2,4,2]{2,1,0:T(4,128)S(1)} %pad_add_fusion.token_ref.tab_ref), channel_id=1, source_target_pairs={{0,3},{1,0},{2,1},{3,2},{4,7},{5,4},{6,5},{7,6},{8,11},{9,8},{10,9... | collective-permute-start | bytes 200 | tf_op jit(solution)/shard_map/ppermute | solution.py:340
  11.0 11.2 %collective-permute-start.3 = (s32[2,4,2]{2,1,0:T(4,128)S(1)}, s32[2,4,2]{2,1,0:T(4,128)S(1)}, u32[]{:S(2)}, u32[]{:S(2)}) collective-permute-start(s32[2,4,2]{2,1,0:T(4,128)S(1)} %pad_add_fusion.token_ref.tab_ref), channel_id=1, source_target_pairs={{0,1},{1,2},{2,3},{3,0},{4,5},{5,6},{6,7},{7,4},{8,9},{9,10},{10,1... | collective-permute-start | bytes 200 | tf_op jit(solution)/shard_map/ppermute | solution.py:340
  12.0 0.6 copy-start.6
  15.4 35.3 %collective-permute-start.10 = (bf16[2,2,64,2048]{3,2,1,0:T(8,128)(2,1)}, bf16[2,2,64,2048]{3,2,1,0:T(8,128)(2,1)}, u32[]{:S(2)}, u32[]{:S(2)}) collective-permute-start(bf16[2,2,64,2048]{3,2,1,0:T(8,128)(2,1)} %pack_far.5), channel_id=1, source_target_pairs={{0,2},{1,3},{2,0},{3,1},{4,6},{5,7},{6,4},{7,5},{8,10},{9,11},{10,... | collective-permute-start | bytes 3145736 | tf_op jit(solution)/shard_map/ppermute | solution.py:342
  17.9 0.6 copy-start.8
  21.3 6.2 %copy-start = (bf16[1,256,2048]{2,1,0:T(8,128)(2,1)S(1)}, bf16[1,256,2048]{2,1,0:T(8,128)(2,1)}, u32[]{:S(2)}) copy-start(bf16[1,256,2048]{2,1,0:T(8,128)(2,1)} %param.8) | copy-start | bytes 3145732
  21.3 6.2 %copy-start.3 = (bf16[1,256,2048]{2,1,0:T(8,128)(2,1)S(1)}, bf16[1,256,2048]{2,1,0:T(8,128)(2,1)}, u32[]{:S(2)}) copy-start(bf16[1,256,2048]{2,1,0:T(8,128)(2,1)} %param.9) | copy-start | bytes 3145732
  21.3 6.2 %copy-start.4 = (bf16[1,256,2048]{2,1,0:T(8,128)(2,1)S(1)}, bf16[1,256,2048]{2,1,0:T(8,128)(2,1)}, u32[]{:S(2)}) copy-start(bf16[1,256,2048]{2,1,0:T(8,128)(2,1)} %param.10) | copy-start | bytes 3145732
  21.3 6.2 %copy-start.5 = (s32[1,256]{1,0:T(1,128)S(1)}, s32[1,256]{1,0:T(1,128)}, u32[]{:S(2)}) copy-start(s32[1,256]{1,0:T(1,128)} %docs_ref.1) | copy-start | bytes 3076
  21.3 43.5 %collective-permute-start.8 = (bf16[2,2,64,2048]{3,2,1,0:T(8,128)(2,1)}, bf16[2,2,64,2048]{3,2,1,0:T(8,128)(2,1)}, u32[]{:S(2)}, u32[]{:S(2)}) collective-permute-start(bf16[2,2,64,2048]{3,2,1,0:T(8,128)(2,1)} %pack_far.3), channel_id=1, source_target_pairs={{0,1},{1,2},{2,3},{3,0},{4,5},{5,6},{6,7},{7,4},{8,9},{9,10},{10,1... | collective-permute-start | bytes 3145736 | tf_op jit(solution)/shard_map/ppermute | solution.py:342
  22.2 0.6 copy-start.7
  25.5 39.3 %collective-permute-start.9 = (bf16[2,2,64,2048]{3,2,1,0:T(8,128)(2,1)}, bf16[2,2,64,2048]{3,2,1,0:T(8,128)(2,1)}, u32[]{:S(2)}, u32[]{:S(2)}) collective-permute-start(bf16[2,2,64,2048]{3,2,1,0:T(8,128)(2,1)} %pack_far.4), channel_id=1, source_target_pairs={{0,3},{1,0},{2,1},{3,2},{4,7},{5,4},{6,5},{7,6},{8,11},{9,8},{10,9... | collective-permute-start | bytes 3145736 | tf_op jit(solution)/shard_map/ppermute | solution.py:342
  30.1 48.5 %all-to-all-start = ((bf16[16,784,128]{2,1,0:T(8,128)(2,1)}), bf16[16,784,128]{2,1,0:T(8,128)(2,1)S(1)}, u32[]{:S(2)}, u32[]{:S(2)}) async-start(bf16[16,784,128]{2,1,0:T(8,128)(2,1)} %pack_heads.1), calls=%async_computation | async-start | bytes 6422528 | tf_op jit(solution)/shard_map/all_to_all | solution.py:345
  42.3 60.7 %collective-permute-start.2 = (bf16[2,2,64,2048]{3,2,1,0:T(8,128)(2,1)}, bf16[2,2,64,2048]{3,2,1,0:T(8,128)(2,1)}, u32[]{:S(2)}, u32[]{:S(2)}) collective-permute-start(bf16[2,2,64,2048]{3,2,1,0:T(8,128)(2,1)} %pack_near.3), channel_id=1, source_target_pairs={{0,1},{1,2},{2,3},{3,0},{4,5},{5,6},{6,7},{7,4},{8,9},{9,10},{10,1... | collective-permute-start | bytes 3145736 | tf_op jit(solution)/shard_map/ppermute | solution.py:350
  48.0 55.0 %collective-permute-start.4 = (bf16[2,2,64,2048]{3,2,1,0:T(8,128)(2,1)}, bf16[2,2,64,2048]{3,2,1,0:T(8,128)(2,1)}, u32[]{:S(2)}, u32[]{:S(2)}) collective-permute-start(bf16[2,2,64,2048]{3,2,1,0:T(8,128)(2,1)} %pack_near.4), channel_id=1, source_target_pairs={{0,3},{1,0},{2,1},{3,2},{4,7},{5,4},{6,5},{7,6},{8,11},{9,8},{10,9... | collective-permute-start | bytes 3145736 | tf_op jit(solution)/shard_map/ppermute | solution.py:350
  50.7 56.0 %collective-permute-start.6 = (bf16[2,2,64,2048]{3,2,1,0:T(8,128)(2,1)}, bf16[2,2,64,2048]{3,2,1,0:T(8,128)(2,1)}, u32[]{:S(2)}, u32[]{:S(2)}) collective-permute-start(bf16[2,2,64,2048]{3,2,1,0:T(8,128)(2,1)} %pack_near.5), channel_id=1, source_target_pairs={{0,2},{1,3},{2,0},{3,1},{4,6},{5,7},{6,4},{7,5},{8,10},{9,11},{10,... | collective-permute-start | bytes 3145736 | tf_op jit(solution)/shard_map/ppermute | solution.py:350
  71.4 35.4 %collective-permute-start.11 = (bf16[256,2176]{1,0:T(8,128)(2,1)}, bf16[256,2176]{1,0:T(8,128)(2,1)}, u32[]{:S(2)}, u32[]{:S(2)}) collective-permute-start(bf16[256,2176]{1,0:T(8,128)(2,1)} %cross_far.1), channel_id=1, source_target_pairs={{0,4},{1,5},{2,6},{3,7},{4,0},{5,1},{6,2},{7,3},{8,12},{9,13},{10,... | collective-permute-start | bytes 3342344 | tf_op jit(solution)/shard_map/ppermute | solution.py:351
  97.2 1.0 copy-start.2
  98.2 20.7 %all-to-all-start.1 = ((bf16[16,256,128]{2,1,0:T(8,128)(2,1)}), bf16[16,256,128]{2,1,0:T(8,128)(2,1)S(1)}, u32[]{:S(2)}, u32[]{:S(2)}) async-start(bf16[16,256,128]{2,1,0:T(8,128)(2,1)} %copy-done.2), calls=%async_computation.1 | async-start | bytes 2097152 | tf_op jit(solution)/shard_map/all_to_all | solution.py:354
  103.0 3.7 %copy-start.1 = (bf16[1,256,2048]{2,1,0:T(8,128)(2,1)S(1)}, bf16[1,256,2048]{2,1,0:T(8,128)(2,1)}, u32[]{:S(2)}) copy-start(bf16[1,256,2048]{2,1,0:T(8,128)(2,1)} %param.8) | copy-start | bytes 3145732

commit v12 on v11

--- a/solution.py
+++ b/solution.py
@@ -164,7 +164,8 @@
 SHIFTS = (1, 3, 2)
 
 
-def pack_spans_kernel(far, tab_ref, keys_ref, values_ref, out_ref, hold, loads, stores):
+def pack_spans_kernel(far, tab_ref, keys_ref, values_ref, *refs):
+    out_ref, hold, loads, stores = refs[-4:]
     me = lax.axis_index("db")
     first, second, seen = jnp.int32(0), jnp.int32(0), jnp.int32(0)
     for r in range(8):
@@ -188,11 +189,11 @@
         store.wait()
 
 
-def pack_spans(far, table, keys, values):
+def pack_spans(far, table, keys, values, *after):
     anywhere = pl.BlockSpec(memory_space=pl.ANY)
     return pl.pallas_call(
         functools.partial(pack_spans_kernel, int(far)),
-        in_specs=[pl.BlockSpec(memory_space=pltpu.SMEM), anywhere, anywhere],
+        in_specs=[pl.BlockSpec(memory_space=pltpu.SMEM)] + [anywhere] * (2 + len(after)),
         out_specs=anywhere,
         out_shape=jax.ShapeDtypeStruct((2, 2, CH, HD), bf16),
         scratch_shapes=[
@@ -203,7 +204,7 @@
         compiler_params=pltpu.CompilerParams(vmem_limit_bytes=GRANT << 20),
         cost_estimate=cost(0, 3 << 20),
         name="pack_far" if far else "pack_near",
-    )(table, keys, values)
+    )(table, keys, values, *after)
 
 
 def cross_kernel(far, tab_ref, q_ref, *refs):
@@ -338,10 +339,11 @@
     asked = lax.optimization_barrier(nbr_owner * 8 + nbr_local)
     table = jnp.concatenate([asked, lax.ppermute(asked, "db", swap)], axis=0)
     tables = [lax.ppermute(table, "db", turn(NZ - k)) for k in SHIFTS]
-    far = [pack_spans(True, t, db_k, db_v) for t in tables]
+    heads = pack_heads(table, doc_ids, q, keys[0], values[0])
+    far = [pack_spans(True, t, db_k, db_v, heads) for t in tables[:2]]
+    far.append(pack_spans(True, tables[2], db_k, db_v))
     far_got = [lax.ppermute(x, "db", turn(k)) for x, k in zip(far, SHIFTS)]
 
-    heads = pack_heads(table, doc_ids, q, keys[0], values[0])
     heads = lax.all_to_all(heads, "ctx", split_axis=0, concat_axis=0, tiled=True)
 
     near = [pack_spans(False, t, db_k, db_v) for t in tables]

time: 121 us -> 130 us (1.074)
  the two profiles are of different devices: /device:TPU:1 before, /device:TPU:96 now
where the time goes in v12:
time: 130 us; the launch traced here: 129 us
  Pallas kernels  53.6 us (41%)
  waiting for transfers between devices  37.5 us (29%)
  starting transfers between devices  28.7 us (22%)
  local copies, waits for them, and re-layouts  8.62 us (7%)
    ppermute x3, waiting for transfers between devices, per_device(): far_got = [lax.ppermute(x, 'db', turn(k)) for x, k in zip(far, SHIFTS)]  27.3 us
    pallas_call x1, Pallas kernels, self_attention(): pl.pallas_call(self_kernel, in_specs=[pl.BlockSpec(memory_space=pltpu.VME...  18.5 us
    pallas_call x6, Pallas kernels, pack_spans(): pl.pallas_call(functools.partial(pack_spans_kernel, int(far)), in_specs=[...  16.5 us
    pallas_call x2, Pallas kernels, cross(): pl.pallas_call(functools.partial(cross_kernel, far), in_specs=[pl.BlockSp...  14.5 us
    unnamed x20, local copies, waits for them, and re-layouts  8.62 us
    ppermute x3, waiting for transfers between devices, per_device(): near_got.append(lax.ppermute(near[i], 'db', turn(k)))  7.15 us
    ppermute x3, starting transfers between devices, per_device(): far_got = [lax.ppermute(x, 'db', turn(k)) for x, k in zip(far, SHIFTS)]  5.97 us
    all_to_all x1, starting transfers between devices, per_device(): lax.all_to_all(heads, 'ctx', split_axis=0, concat_axis=0, tiled=True)  5.33 us
  transfers between devices with their start and end apart: 14, of which 6 were waited for; matrix products, arithmetic and copies ran while one was open for 0% of the time, Pallas kernels for 40%

profile of v12, /device:TPU:96, one launch (start us, length us, event | category | flops | bytes accessed | tf_op | source)
XLA Modules:
  0.0 129.1 jit_solution(12749119791229744145)
XLA Ops:
  0.6 0.8 copy.14
  1.4 0.8 copy.13
  2.2 3.0 %collective-permute-start = (s32[1,4,2]{2,1,0:T(4,128)S(1)}, s32[1,4,2]{2,1,0:T(4,128)S(1)}, u32[]{:S(2)}, u32[]{:S(2)}) collective-permute-start(s32[1,4,2]{2,1,0:T(4,128)S(1)} %multiply_add_fusion), channel_id=1, source_target_pairs={{0,4},{1,5},{2,6},{3,7},{4,0},{5,1},{6,2},{7,3},{8,12},{9,13},{10,... | collective-permute-start | bytes 104 | tf_op jit(solution)/shard_map/ppermute | solution.py:340
  5.2 0.5 collective-permute-start.7
  5.7 1.6 %collective-permute-done = s32[1,4,2]{2,1,0:T(4,128)S(1)} collective-permute-done((s32[1,4,2]{2,1,0:T(4,128)S(1)}, s32[1,4,2]{2,1,0:T(4,128)S(1)}, u32[]{:S(2)}, u32[]{:S(2)}) %collective-permute-start) | collective-permute-done | bytes 64 | tf_op jit(solution)/shard_map/ppermute | solution.py:340
  7.3 0.4 collective-permute-start.1
  7.7 2.8 %collective-permute-start.3 = (s32[2,4,2]{2,1,0:T(4,128)S(1)}, s32[2,4,2]{2,1,0:T(4,128)S(1)}, u32[]{:S(2)}, u32[]{:S(2)}) collective-permute-start(s32[2,4,2]{2,1,0:T(4,128)S(1)} %pad_add_fusion.token_ref.tab_ref), channel_id=1, source_target_pairs={{0,1},{1,2},{2,3},{3,0},{4,5},{5,6},{6,7},{7,4},{8,9},{9,10},{10,1... | collective-permute-start | bytes 200 | tf_op jit(solution)/shard_map/ppermute | solution.py:341
  10.5 0.0 collective-permute-start.5
  10.5 1.2 copy-done
  11.7 1.2 copy-done.3
  13.0 1.2 copy-done.4
  14.2 0.7 copy-done.5
  14.9 2.5 %pack_heads.1.refs_0_ = bf16[16,784,128]{2,1,0:T(8,128)(2,1)} custom-call(s32[2,4,2]{2,1,0:T(4,128)S(1)} %pad_add_fusion.token_ref.tab_ref, s32[1,256]{1,0:T(1,128)S(1)} %copy-done.5, bf16[256,2048]{1,0:T(8,128)(2,1)S(1)} %bitcast.8, bf16[256,2048]{1,0:T(8,128)(2,1)S(1)} %bitcast.10, bf16[256,2048]{1,0:T(8,128)(2,1)S(1)} %bitcast.11), custom_call_target="tpu_custom_call" | custom-call | bytes 393216 | tf_op jit(solution)/shard_map/pack_heads/pallas_call | solution.py:52
  17.4 0.0 collective-permute-done.1.tab_ref
  17.4 0.6 copy-done.7
  18.0 2.7 %pack_far.3 = bf16[2,2,64,2048]{3,2,1,0:T(8,128)(2,1)} custom-call(s32[2,4,2]{2,1,0:T(4,128)} %copy-done.7, bf16[8,64,2048]{2,1,0:T(8,128)(2,1)} %bitcast.12, bf16[8,64,2048]{2,1,0:T(8,128)(2,1)} %bitcast.20, bf16[16,784,128]{2,1,0:T(8,128)(2,1)} %pack_heads.1.refs_0_), custom_call_target="tpu_custom_call" | custom-call | bytes 196608 | tf_op jit(solution)/shard_map/pack_far/pallas_call | solution.py:194
  20.7 1.9 %collective-permute-start.8 = (bf16[2,2,64,2048]{3,2,1,0:T(8,128)(2,1)}, bf16[2,2,64,2048]{3,2,1,0:T(8,128)(2,1)}, u32[]{:S(2)}, u32[]{:S(2)}) collective-permute-start(bf16[2,2,64,2048]{3,2,1,0:T(8,128)(2,1)} %pack_far.3), channel_id=1, source_target_pairs={{0,1},{1,2},{2,3},{3,0},{4,5},{5,6},{6,7},{7,4},{8,9},{9,10},{10,1... | collective-permute-start | bytes 3145736 | tf_op jit(solution)/shard_map/ppermute | solution.py:345
  22.6 0.0 collective-permute-done.3.tab_ref
  22.7 0.6 copy-done.6
  23.2 2.8 %pack_far.4 = bf16[2,2,64,2048]{3,2,1,0:T(8,128)(2,1)} custom-call(s32[2,4,2]{2,1,0:T(4,128)} %copy-done.6, bf16[8,64,2048]{2,1,0:T(8,128)(2,1)} %bitcast.13, bf16[8,64,2048]{2,1,0:T(8,128)(2,1)} %bitcast.21, bf16[16,784,128]{2,1,0:T(8,128)(2,1)} %pack_heads.1.refs_0_), custom_call_target="tpu_custom_call" | custom-call | bytes 196608 | tf_op jit(solution)/shard_map/pack_far/pallas_call | solution.py:194
  26.0 0.2 collective-permute-start.9
  26.2 0.0 collective-permute-done.5.tab_ref
  26.2 0.6 copy-done.8
  26.8 2.8 %pack_far.5 = bf16[2,2,64,2048]{3,2,1,0:T(8,128)(2,1)} custom-call(s32[2,4,2]{2,1,0:T(4,128)} %copy-done.8, bf16[8,64,2048]{2,1,0:T(8,128)(2,1)} %bitcast.14, bf16[8,64,2048]{2,1,0:T(8,128)(2,1)} %bitcast.22), custom_call_target="tpu_custom_call" | custom-call | bytes 196608 | tf_op jit(solution)/shard_map/pack_far/pallas_call | solution.py:194
  29.6 3.8 %collective-permute-start.10 = (bf16[2,2,64,2048]{3,2,1,0:T(8,128)(2,1)}, bf16[2,2,64,2048]{3,2,1,0:T(8,128)(2,1)}, u32[]{:S(2)}, u32[]{:S(2)}) collective-permute-start(bf16[2,2,64,2048]{3,2,1,0:T(8,128)(2,1)} %pack_far.5), channel_id=1, source_target_pairs={{0,2},{1,3},{2,0},{3,1},{4,6},{5,7},{6,4},{7,5},{8,10},{9,11},{10,... | collective-permute-start | bytes 3145736 | tf_op jit(solution)/shard_map/ppermute | solution.py:345
  33.4 5.3 %all-to-all-start = ((bf16[16,784,128]{2,1,0:T(8,128)(2,1)}), bf16[16,784,128]{2,1,0:T(8,128)(2,1)S(1)}, u32[]{:S(2)}, u32[]{:S(2)}) async-start(bf16[16,784,128]{2,1,0:T(8,128)(2,1)} %pack_heads.1.refs_0_), calls=%async_computation | async-start | bytes 6422528 | tf_op jit(solution)/shard_map/all_to_all | solution.py:347
  38.8 2.7 %pack_near.3 = bf16[2,2,64,2048]{3,2,1,0:T(8,128)(2,1)} custom-call(s32[2,4,2]{2,1,0:T(4,128)} %copy-done.7, bf16[8,64,2048]{2,1,0:T(8,128)(2,1)} %bitcast.15, bf16[8,64,2048]{2,1,0:T(8,128)(2,1)} %bitcast.23), custom_call_target="tpu_custom_call" | custom-call | bytes 196608 | tf_op jit(solution)/shard_map/pack_near/pallas_call | solution.py:194
  41.5 1.1 collective-permute-start.2
  42.5 2.7 %pack_near.4 = bf16[2,2,64,2048]{3,2,1,0:T(8,128)(2,1)} custom-call(s32[2,4,2]{2,1,0:T(4,128)} %copy-done.6, bf16[8,64,2048]{2,1,0:T(8,128)(2,1)} %bitcast.16, bf16[8,64,2048]{2,1,0:T(8,128)(2,1)} %bitcast.24), custom_call_target="tpu_custom_call" | custom-call | bytes 196608 | tf_op jit(solution)/shard_map/pack_near/pallas_call | solution.py:194
  45.3 2.8 %pack_near.5 = bf16[2,2,64,2048]{3,2,1,0:T(8,128)(2,1)} custom-call(s32[2,4,2]{2,1,0:T(4,128)} %copy-done.8, bf16[8,64,2048]{2,1,0:T(8,128)(2,1)} %bitcast.17, bf16[8,64,2048]{2,1,0:T(8,128)(2,1)} %bitcast.25), custom_call_target="tpu_custom_call" | custom-call | bytes 196608 | tf_op jit(solution)/shard_map/pack_near/pallas_call | solution.py:194
  48.1 0.0 collective-permute-done.7.q_ref
  48.1 1.3 %collective-permute-start.4 = (bf16[2,2,64,2048]{3,2,1,0:T(8,128)(2,1)}, bf16[2,2,64,2048]{3,2,1,0:T(8,128)(2,1)}, u32[]{:S(2)}, u32[]{:S(2)}) collective-permute-start(bf16[2,2,64,2048]{3,2,1,0:T(8,128)(2,1)} %pack_near.4), channel_id=1, source_target_pairs={{0,3},{1,0},{2,1},{3,2},{4,7},{5,4},{6,5},{7,6},{8,11},{9,8},{10,9... | collective-permute-start | bytes 3145736 | tf_op jit(solution)/shard_map/ppermute | solution.py:352
  49.4 15.4 %collective-permute-done.8.refs_2_ = bf16[2,2,64,2048]{3,2,1,0:T(8,128)(2,1)} collective-permute-done((bf16[2,2,64,2048]{3,2,1,0:T(8,128)(2,1)}, bf16[2,2,64,2048]{3,2,1,0:T(8,128)(2,1)}, u32[]{:S(2)}, u32[]{:S(2)}) %collective-permute-start.8) | collective-permute-done | bytes 1048608 | tf_op jit(solution)/shard_map/ppermute | solution.py:345
  64.8 0.0 collective-permute-start.6
  64.8 5.2 %collective-permute-done.9.refs_3_ = bf16[2,2,64,2048]{3,2,1,0:T(8,128)(2,1)} collective-permute-done((bf16[2,2,64,2048]{3,2,1,0:T(8,128)(2,1)}, bf16[2,2,64,2048]{3,2,1,0:T(8,128)(2,1)}, u32[]{:S(2)}, u32[]{:S(2)}) %collective-permute-start.9) | collective-permute-done | bytes 1048608 | tf_op jit(solution)/shard_map/ppermute | solution.py:345
  70.0 6.7 %collective-permute-done.10.refs_4_ = bf16[2,2,64,2048]{3,2,1,0:T(8,128)(2,1)} collective-permute-done((bf16[2,2,64,2048]{3,2,1,0:T(8,128)(2,1)}, bf16[2,2,64,2048]{3,2,1,0:T(8,128)(2,1)}, u32[]{:S(2)}, u32[]{:S(2)}) %collective-permute-start.10) | collective-permute-done | bytes 1048608 | tf_op jit(solution)/shard_map/ppermute | solution.py:345
  76.7 6.6 %cross_far.1 = bf16[256,2176]{1,0:T(8,128)(2,1)} custom-call(s32[2,4,2]{2,1,0:T(4,128)S(1)} %pad_add_fusion.token_ref.tab_ref, bf16[256,2048]{1,0:T(8,128)(2,1)} %collective-permute-done.7.q_ref, bf16[8,64,2048]{2,1,0:T(8,128)(2,1)} %bitcast.18, bf16[8,64,2048]{2,1,0:T(8,128)(2,1)} %bitcast.26, bf16[2,2,64,2048]{3,2,1,0:T(8,128)(2,1)} %collective-permute-done.8.refs_2_, ...), custom_call_target="tpu_custom_call" | custom-call | flops 34359738368 | tf_op jit(solution)/shard_map/cross_far/pallas_call | solution.py:297
  83.2 3.1 %collective-permute-start.11 = (bf16[256,2176]{1,0:T(8,128)(2,1)}, bf16[256,2176]{1,0:T(8,128)(2,1)}, u32[]{:S(2)}, u32[]{:S(2)}) collective-permute-start(bf16[256,2176]{1,0:T(8,128)(2,1)} %cross_far.1), channel_id=1, source_target_pairs={{0,4},{1,5},{2,6},{3,7},{4,0},{5,1},{6,2},{7,3},{8,12},{9,13},{10,... | collective-permute-start | bytes 3342344 | tf_op jit(solution)/shard_map/ppermute | solution.py:353
  86.3 18.5 %self_attention.1 = bf16[16,256,128]{2,1,0:T(8,128)(2,1)S(1)} custom-call(bf16[16,784,128]{2,1,0:T(8,128)(2,1)S(1)} %all-to-all-done.x_ref), custom_call_target="tpu_custom_call" | custom-call | flops 268435456 | bytes 262144 | tf_op jit(solution)/shard_map/self_attention/pallas_call | solution.py:153
  104.9 0.0 copy-start.2
  104.9 1.0 copy-done.2
  105.8 5.1 %all-to-all-start.1 = ((bf16[16,256,128]{2,1,0:T(8,128)(2,1)}), bf16[16,256,128]{2,1,0:T(8,128)(2,1)S(1)}, u32[]{:S(2)}, u32[]{:S(2)}) async-start(bf16[16,256,128]{2,1,0:T(8,128)(2,1)} %copy-done.2), calls=%async_computation.1 | async-start | bytes 2097152 | tf_op jit(solution)/shard_map/all_to_all | solution.py:356
  111.0 0.0 copy-start.1
  111.0 0.0 collective-permute-done.4.refs_1_
  111.0 7.1 %collective-permute-done.6.refs_2_ = bf16[2,2,64,2048]{3,2,1,0:T(8,128)(2,1)} collective-permute-done((bf16[2,2,64,2048]{3,2,1,0:T(8,128)(2,1)}, bf16[2,2,64,2048]{3,2,1,0:T(8,128)(2,1)}, u32[]{:S(2)}, u32[]{:S(2)}) %collective-permute-start.6) | collective-permute-done | bytes 1048608 | tf_op jit(solution)/shard_map/ppermute | solution.py:352
  118.1 7.9 %cross_near.1 = bf16[256,2048]{1,0:T(8,128)(2,1)} custom-call(s32[2,4,2]{2,1,0:T(4,128)S(1)} %pad_add_fusion.token_ref.tab_ref, bf16[256,2048]{1,0:T(8,128)(2,1)S(1)} %bitcast.9, bf16[8,64,2048]{2,1,0:T(8,128)(2,1)} %bitcast.19, bf16[8,64,2048]{2,1,0:T(8,128)(2,1)} %bitcast.27, bf16[2,2,64,2048]{3,2,1,0:T(8,128)(2,1)} %get-tuple-element.5.refs_2_, ...), custom_call_target="tpu_custom_call" | custom-call | flops 67108864 | tf_op jit(solution)/shard_map/cross_near/pallas_call | solution.py:297
  126.1 1.5 %all-to-all-done.1.x_ref = bf16[16,256,128]{2,1,0:T(8,128)(2,1)S(1)} async-done(((bf16[16,256,128]{2,1,0:T(8,128)(2,1)}), bf16[16,256,128]{2,1,0:T(8,128)(2,1)S(1)}, u32[]{:S(2)}, u32[]{:S(2)}) %all-to-all-start.1) | async-done | bytes 1048608 | tf_op jit(solution)/shard_map/all_to_all | solution.py:356
  127.6 1.6 %unpack_heads.1 = bf16[256,2048]{1,0:T(8,128)(2,1)} custom-call(bf16[16,256,128]{2,1,0:T(8,128)(2,1)S(1)} %all-to-all-done.1.x_ref), custom_call_target="tpu_custom_call" | custom-call | bytes 131072 | tf_op jit(solution)/shard_map/unpack_heads/pallas_call | solution.py:76
  (14 shorter events, 0.0 us)
Async XLA Ops:
  2.2 5.1 %collective-permute-start = (s32[1,4,2]{2,1,0:T(4,128)S(1)}, s32[1,4,2]{2,1,0:T(4,128)S(1)}, u32[]{:S(2)}, u32[]{:S(2)}) collective-permute-start(s32[1,4,2]{2,1,0:T(4,128)S(1)} %multiply_add_fusion), channel_id=1, source_target_pairs={{0,4},{1,5},{2,6},{3,7},{4,0},{5,1},{6,2},{7,3},{8,12},{9,13},{10,... | collective-permute-start | bytes 104 | tf_op jit(solution)/shard_map/ppermute | solution.py:340
  5.2 42.9 %collective-permute-start.7 = (bf16[256,2048]{1,0:T(8,128)(2,1)}, bf16[256,2048]{1,0:T(8,128)(2,1)}, u32[]{:S(2)}, u32[]{:S(2)}) collective-permute-start(bf16[256,2048]{1,0:T(8,128)(2,1)} %bitcast.7), channel_id=1, source_target_pairs={{0,4},{1,5},{2,6},{3,7},{4,0},{5,1},{6,2},{7,3},{8,12},{9,13},{10,... | collective-permute-start | bytes 3145736 | tf_op jit(solution)/shard_map/ppermute | solution.py:337
  7.3 10.1 %collective-permute-start.1 = (s32[2,4,2]{2,1,0:T(4,128)S(1)}, s32[2,4,2]{2,1,0:T(4,128)S(1)}, u32[]{:S(2)}, u32[]{:S(2)}) collective-permute-start(s32[2,4,2]{2,1,0:T(4,128)S(1)} %pad_add_fusion.token_ref.tab_ref), channel_id=1, source_target_pairs={{0,3},{1,0},{2,1},{3,2},{4,7},{5,4},{6,5},{7,6},{8,11},{9,8},{10,9... | collective-permute-start | bytes 200 | tf_op jit(solution)/shard_map/ppermute | solution.py:341
  7.7 15.0 %collective-permute-start.3 = (s32[2,4,2]{2,1,0:T(4,128)S(1)}, s32[2,4,2]{2,1,0:T(4,128)S(1)}, u32[]{:S(2)}, u32[]{:S(2)}) collective-permute-start(s32[2,4,2]{2,1,0:T(4,128)S(1)} %pad_add_fusion.token_ref.tab_ref), channel_id=1, source_target_pairs={{0,1},{1,2},{2,3},{3,0},{4,5},{5,6},{6,7},{7,4},{8,9},{9,10},{10,1... | collective-permute-start | bytes 200 | tf_op jit(solution)/shard_map/ppermute | solution.py:341
  10.5 15.7 %collective-permute-start.5 = (s32[2,4,2]{2,1,0:T(4,128)S(1)}, s32[2,4,2]{2,1,0:T(4,128)S(1)}, u32[]{:S(2)}, u32[]{:S(2)}) collective-permute-start(s32[2,4,2]{2,1,0:T(4,128)S(1)} %pad_add_fusion.token_ref.tab_ref), channel_id=1, source_target_pairs={{0,2},{1,3},{2,0},{3,1},{4,6},{5,7},{6,4},{7,5},{8,10},{9,11},{10,... | collective-permute-start | bytes 200 | tf_op jit(solution)/shard_map/ppermute | solution.py:341
  10.5 1.2 copy-start
  11.7 1.2 copy-start.3
  13.0 1.2 copy-start.4
  14.2 0.7 copy-start.5
  17.4 0.6 copy-start.7
  20.7 44.1 %collective-permute-start.8 = (bf16[2,2,64,2048]{3,2,1,0:T(8,128)(2,1)}, bf16[2,2,64,2048]{3,2,1,0:T(8,128)(2,1)}, u32[]{:S(2)}, u32[]{:S(2)}) collective-permute-start(bf16[2,2,64,2048]{3,2,1,0:T(8,128)(2,1)} %pack_far.3), channel_id=1, source_target_pairs={{0,1},{1,2},{2,3},{3,0},{4,5},{5,6},{6,7},{7,4},{8,9},{9,10},{10,1... | collective-permute-start | bytes 3145736 | tf_op jit(solution)/shard_map/ppermute | solution.py:345
  22.6 0.6 copy-start.6
  26.0 44.0 %collective-permute-start.9 = (bf16[2,2,64,2048]{3,2,1,0:T(8,128)(2,1)}, bf16[2,2,64,2048]{3,2,1,0:T(8,128)(2,1)}, u32[]{:S(2)}, u32[]{:S(2)}) collective-permute-start(bf16[2,2,64,2048]{3,2,1,0:T(8,128)(2,1)} %pack_far.4), channel_id=1, source_target_pairs={{0,3},{1,0},{2,1},{3,2},{4,7},{5,4},{6,5},{7,6},{8,11},{9,8},{10,9... | collective-permute-start | bytes 3145736 | tf_op jit(solution)/shard_map/ppermute | solution.py:345
  26.2 0.6 copy-start.8
  29.6 47.1 %collective-permute-start.10 = (bf16[2,2,64,2048]{3,2,1,0:T(8,128)(2,1)}, bf16[2,2,64,2048]{3,2,1,0:T(8,128)(2,1)}, u32[]{:S(2)}, u32[]{:S(2)}) collective-permute-start(bf16[2,2,64,2048]{3,2,1,0:T(8,128)(2,1)} %pack_far.5), channel_id=1, source_target_pairs={{0,2},{1,3},{2,0},{3,1},{4,6},{5,7},{6,4},{7,5},{8,10},{9,11},{10,... | collective-permute-start | bytes 3145736 | tf_op jit(solution)/shard_map/ppermute | solution.py:345
  33.4 52.9 %all-to-all-start = ((bf16[16,784,128]{2,1,0:T(8,128)(2,1)}), bf16[16,784,128]{2,1,0:T(8,128)(2,1)S(1)}, u32[]{:S(2)}, u32[]{:S(2)}) async-start(bf16[16,784,128]{2,1,0:T(8,128)(2,1)} %pack_heads.1.refs_0_), calls=%async_computation | async-start | bytes 6422528 | tf_op jit(solution)/shard_map/all_to_all | solution.py:347
  41.5 69.5 %collective-permute-start.2 = (bf16[2,2,64,2048]{3,2,1,0:T(8,128)(2,1)}, bf16[2,2,64,2048]{3,2,1,0:T(8,128)(2,1)}, u32[]{:S(2)}, u32[]{:S(2)}) collective-permute-start(bf16[2,2,64,2048]{3,2,1,0:T(8,128)(2,1)} %pack_near.3), channel_id=1, source_target_pairs={{0,1},{1,2},{2,3},{3,0},{4,5},{5,6},{6,7},{7,4},{8,9},{9,10},{10,1... | collective-permute-start | bytes 3145736 | tf_op jit(solution)/shard_map/ppermute | solution.py:352
  48.1 62.9 %collective-permute-start.4 = (bf16[2,2,64,2048]{3,2,1,0:T(8,128)(2,1)}, bf16[2,2,64,2048]{3,2,1,0:T(8,128)(2,1)}, u32[]{:S(2)}, u32[]{:S(2)}) collective-permute-start(bf16[2,2,64,2048]{3,2,1,0:T(8,128)(2,1)} %pack_near.4), channel_id=1, source_target_pairs={{0,3},{1,0},{2,1},{3,2},{4,7},{5,4},{6,5},{7,6},{8,11},{9,8},{10,9... | collective-permute-start | bytes 3145736 | tf_op jit(solution)/shard_map/ppermute | solution.py:352
  64.8 53.4 %collective-permute-start.6 = (bf16[2,2,64,2048]{3,2,1,0:T(8,128)(2,1)}, bf16[2,2,64,2048]{3,2,1,0:T(8,128)(2,1)}, u32[]{:S(2)}, u32[]{:S(2)}) collective-permute-start(bf16[2,2,64,2048]{3,2,1,0:T(8,128)(2,1)} %pack_near.5), channel_id=1, source_target_pairs={{0,2},{1,3},{2,0},{3,1},{4,6},{5,7},{6,4},{7,5},{8,10},{9,11},{10,... | collective-permute-start | bytes 3145736 | tf_op jit(solution)/shard_map/ppermute | solution.py:352
  83.2 34.9 %collective-permute-start.11 = (bf16[256,2176]{1,0:T(8,128)(2,1)}, bf16[256,2176]{1,0:T(8,128)(2,1)}, u32[]{:S(2)}, u32[]{:S(2)}) collective-permute-start(bf16[256,2176]{1,0:T(8,128)(2,1)} %cross_far.1), channel_id=1, source_target_pairs={{0,4},{1,5},{2,6},{3,7},{4,0},{5,1},{6,2},{7,3},{8,12},{9,13},{10,... | collective-permute-start | bytes 3342344 | tf_op jit(solution)/shard_map/ppermute | solution.py:353
  104.9 1.0 copy-start.2
  105.8 21.7 %all-to-all-start.1 = ((bf16[16,256,128]{2,1,0:T(8,128)(2,1)}), bf16[16,256,128]{2,1,0:T(8,128)(2,1)S(1)}, u32[]{:S(2)}, u32[]{:S(2)}) async-start(bf16[16,256,128]{2,1,0:T(8,128)(2,1)} %copy-done.2), calls=%async_computation.1 | async-start | bytes 2097152 | tf_op jit(solution)/shard_map/all_to_all | solution.py:356
  111.0 7.2 %copy-start.1 = (bf16[1,256,2048]{2,1,0:T(8,128)(2,1)S(1)}, bf16[1,256,2048]{2,1,0:T(8,128)(2,1)}, u32[]{:S(2)}) copy-start(bf16[1,256,2048]{2,1,0:T(8,128)(2,1)} %param.8) | copy-start | bytes 3145732
